TPU v7x, 32 devices: a whole 2x2x4 slice. The times are simulated.
32 devices in a mesh: rve: 2 (over x), sub: 16 (over z, y, core).
Axes of the slice: x: 2, y: 2, z: 4, core: 2. Of those that a mesh axis runs over, the one named last changes fastest.
Arguments:
- condensed: float32 [49152, 1536], P(('rve', 'sub')), parts along dimension 0, may hold values from -0.15625 to 0.15625
- eigen_loads: float32 [49152, 128], P(('rve', 'sub')), parts along dimension 0, may hold values from -6 to 6
- coarse_inverse: float32 [1536, 768], P(('rve', 'sub')), parts along dimension 0, may hold values from -0.21875 to 0.21875
- face_rows: int32 [16, 2, 128], P('sub'), may hold values from 0 to 1535, as said below
- primal_rows: int32 [16, 96], P('sub'), may hold values from 0 to 1535, as said below
- primal_slot: int32 [16, 96], P('sub'), may hold values from 0 to 95, each once within a row
Outputs:
- displaced: float32 [49152, 128], P(('rve', 'sub')), parts along dimension 0
- multipliers: float32 [4096, 128], P(('rve', 'sub')), parts along dimension 0
There are 2 independent parts, one for each index of `rve`. A program takes and returns all parts, laid end to end along the dimension named above; an argument that names none is the same for every part. Nothing has to cross between parts.
Inputs may be any that keep to these rules, and one draw needn't show every extreme that they name: `face_rows`: in each subdomain the 128 left-face rows, the 128 right-face rows and the 96 primal rows in primal_rows are all distinct. `primal_rows`: distinct from that subdomain's face rows.
All inputs are finite; a program needn't handle non-finite values.
Results may differ from a plain program's by a relative error of at most 0.0001.
Values sent between devices are 32-bit elements; how exact they have to be, the bound alone decides.
No kernel may reach another device: no remote copies, remote signals or barrier semaphores. Data moves between devices by JAX's collectives and lax.ppermute only.
A program may use at most 64 MiB of HBM per device.

v0:
```python
import jax
import jax.numpy as jnp
from jax import lax
from jax.sharding import PartitionSpec as P

ITERS = 3


DAMPING = 0.5


def passed_along(value, axis, steps):
    count = lax.axis_size(axis)
    pairs = [(source, (source + steps) % count) for source in range(count)]
    return lax.ppermute(value, axis, pairs)


def local(condensed, eigen_loads, coarse_inverse, face_rows, primal_rows, primal_slot):
    columns = eigen_loads.shape[1]
    owned = coarse_inverse.shape[0]
    width = face_rows.shape[2]
    left_rows = face_rows[0, 0]
    right_rows = face_rows[0, 1]
    prim_rows = primal_rows[0]
    slots = primal_slot[0]
    prolong = condensed[:, prim_rows]
    multipliers = jnp.zeros((width, columns), jnp.float32)
    previous = jnp.zeros((width, columns), jnp.float32)
    displaced = eigen_loads
    for step in range(ITERS):
        loads = eigen_loads.at[right_rows].add(-multipliers).at[left_rows].add(previous)
        displaced = jnp.dot(
            condensed, loads, precision=lax.Precision.HIGHEST, preferred_element_type=jnp.float32
        )
        slotted = jnp.zeros((2 * owned, columns), jnp.float32).at[slots].set(displaced[prim_rows])
        extended = jnp.concatenate([coarse_inverse, coarse_inverse[:, :owned]], axis=1)
        piece = lax.all_gather(slotted, "sub", axis=0, tiled=True)
        count = piece.shape[0] // (2 * owned)
        pieces = piece.reshape(count, 2, owned, columns)
        own_part = pieces[:, 0].reshape(count * owned, columns)
        sent_part = pieces[:, 1].reshape(count * owned, columns)
        next_cols = lax.dynamic_slice_in_dim(extended, owned, count * owned, 1)
        total = jnp.dot(
            coarse_inverse,
            own_part,
            precision=lax.Precision.HIGHEST,
            preferred_element_type=jnp.float32,
        )
        coarse_sol = total + jnp.dot(
            next_cols,
            sent_part,
            precision=lax.Precision.HIGHEST,
            preferred_element_type=jnp.float32,
        )
        coarse_next = passed_along(coarse_sol, "sub", -1)
        paired = jnp.concatenate([coarse_sol, coarse_next], axis=0)
        displaced = displaced - jnp.dot(
            prolong,
            paired[slots],
            precision=lax.Precision.HIGHEST,
            preferred_element_type=jnp.float32,
        )
        right_vals = displaced[right_rows]
        left_vals = displaced[left_rows]
        beyond = passed_along(left_vals, "sub", -1)
        multipliers = multipliers + DAMPING * (right_vals - beyond)
        if step + 1 < ITERS:
            previous = passed_along(multipliers, "sub", 1)
    return (displaced, multipliers)


def solution(mesh):
    placed = (
        P(("rve", "sub"), None),
        P(("rve", "sub"), None),
        P(("rve", "sub"), None),
        P("sub", None, None),
        P("sub", None),
        P("sub", None),
    )
    return jax.shard_map(
        local,
        mesh=mesh,
        in_specs=placed,
        out_specs=(P(("rve", "sub"), None), P(("rve", "sub"), None)),
        check_vma=False,
    )
```

profile of v0, /device:TPU:0, one launch (start us, length us, event | category | flops | bytes accessed | tf_op | source)
XLA Modules:
  0.0 172.6 jit_solution(9518307290389604258)
XLA Ops:
  0.6 1.1 copy.46
  1.8 0.1 copy.43
  1.8 0.1 copy.41
  1.9 0.8 fusion.18
  2.7 0.7 fusion.19
  3.3 0.7 fusion.20
  4.0 1.5 scatter_custom_fusion
  5.5 1.6 scatter_custom_fusion.1
  7.1 10.4 %convolution_bitcast_fusion.2 = f32[1536,128]{0,1:T(8,128)S(1)} fusion(f32[1536,128]{1,0:T(8,128)S(1)} %scatter_custom_fusion.1, f32[1536,1536]{1,0:T(8,128)} %param.6), kind=kOutput, calls=%fused_computation.27 | convolution fusion | flops 3623878656 | bytes 11010048 | tf_op jit(solution)/shard_map/dot_general | solution.py:32
  17.5 0.3 copy.23
  17.8 1.1 scatter_custom_fusion.2
  18.9 25.5 %all_gather.9 = f32[1536,128]{1,0:T(8,128)S(1)} all-gather(f32[96,128]{1,0:T(8,128)S(1)} %scatter_custom_fusion.2), channel_id=1, replica_groups=mesh['rve'=2,'sub'=16] {'sub'}, dimensions={0}, use_global_device_ids=true | all-gather | bytes 835584 | tf_op jit(solution)/shard_map/all_gather | solution.py:37
  44.4 0.1 fusion.26
  44.5 0.3 convolution_bitcast_fusion.5
  44.8 0.4 convolution_add_fusion.2
  45.2 0.1 collective-permute-start
  45.3 9.6 %copy.22 = f32[1536,1536]{0,1:T(8,128)} copy(f32[1536,1536]{1,0:T(8,128)} %param.6) | data formatting | bytes 18874368 | tf_op args[0]
  54.9 4.8 %gather_fusion = f32[96,1536]{1,0:T(8,128)S(1)} fusion(f32[1536,1536]{0,1:T(8,128)} %copy.22, s32[1024]{0:T(1024)S(1)} %pad_clamp_fusion.3), kind=kCustom, calls=%fused_computation | custom fusion | bytes 1180032 | tf_op jit(solution)/shard_map/gather | solution.py:26
  59.7 0.6 gather_fusion.1
  60.3 1.7 convolution_subtract_fusion.2
  62.0 1.4 copy.25
  63.4 0.6 gather_fusion.3
  64.1 0.1 collective-permute-start.1
  64.1 0.6 gather_fusion.2
  64.8 1.2 collective-permute-done.1
  66.0 2.3 %collective-permute-start.2 = (f32[128,128]{1,0:T(8,128)S(1)}, f32[128,128]{1,0:T(8,128)S(1)}, u32[]{:S(2)}, u32[]{:S(2)}) collective-permute-start(f32[128,128]{1,0:T(8,128)S(1)} %subtract_multiply_fusion), channel_id=1, source_target_pairs={{0,1},{1,2},{2,3},{3,4},{4,5},{5,6},{6,7},{7,8},{8,9},{9,10},{10,1... | collective-permute-start | bytes 196616 | tf_op jit(solution)/shard_map/ppermute | solution.py:15
  68.3 1.5 scatter_custom_fusion.3
  69.9 2.6 %collective-permute-done.2 = f32[128,128]{1,0:T(8,128)S(1)} collective-permute-done((f32[128,128]{1,0:T(8,128)S(1)}, f32[128,128]{1,0:T(8,128)S(1)}, u32[]{:S(2)}, u32[]{:S(2)}) %collective-permute-start.2) | collective-permute-done | bytes 65568 | tf_op jit(solution)/shard_map/ppermute | solution.py:15
  72.5 1.7 scatter_fusion
  74.2 10.4 %convolution_bitcast_fusion.1 = f32[1536,128]{0,1:T(8,128)S(1)} fusion(f32[1536,128]{1,0:T(8,128)S(1)} %scatter_fusion, f32[1536,1536]{1,0:T(8,128)} %param.6), kind=kOutput, calls=%fused_computation.26 | convolution fusion | flops 3623878656 | bytes 11010048 | tf_op jit(solution)/shard_map/dot_general | solution.py:32
  84.7 0.3 copy.27
  84.9 1.1 scatter_custom_fusion.5
  86.1 19.7 %all_gather.10 = f32[1536,128]{1,0:T(8,128)S(1)} all-gather(f32[96,128]{1,0:T(8,128)S(1)} %scatter_custom_fusion.5), channel_id=1, replica_groups=mesh['rve'=2,'sub'=16] {'sub'}, dimensions={0}, use_global_device_ids=true | all-gather | bytes 835584 | tf_op jit(solution)/shard_map/all_gather | solution.py:37
  105.8 0.3 convolution_bitcast_fusion.4
  106.2 0.4 convolution_add_fusion.1
  106.5 1.7 collective-permute-start.3
  108.2 1.5 collective-permute-done.3
  109.7 0.6 gather_fusion.4
  110.4 0.8 convolution_subtract_fusion.1
  111.2 0.3 copy.29
  111.5 0.7 gather_fusion.6
  112.1 4.5 %collective-permute-start.4 = (f32[128,128]{1,0:T(8,128)S(1)}, f32[128,128]{1,0:T(8,128)S(1)}, u32[]{:S(2)}, u32[]{:S(2)}) collective-permute-start(f32[128,128]{1,0:T(8,128)S(1)} %gather_fusion.6), channel_id=1, source_target_pairs={{0,15},{1,0},{2,1},{3,2},{4,3},{5,4},{6,5},{7,6},{8,7},{9,8},{10,9... | collective-permute-start | bytes 196616 | tf_op jit(solution)/shard_map/ppermute | solution.py:15
  116.6 0.6 gather_fusion.5
  117.2 1.3 collective-permute-done.4
  118.5 0.1 collective-permute-start.5
  118.6 1.6 scatter_custom_fusion.6
  120.1 4.9 %collective-permute-done.5 = f32[128,128]{1,0:T(8,128)S(1)} collective-permute-done((f32[128,128]{1,0:T(8,128)S(1)}, f32[128,128]{1,0:T(8,128)S(1)}, u32[]{:S(2)}, u32[]{:S(2)}) %collective-permute-start.5) | collective-permute-done | bytes 65568 | tf_op jit(solution)/shard_map/ppermute | solution.py:15
  125.0 1.8 %scatter_fusion.1 = f32[1536,128]{1,0:T(8,128)S(1)} fusion(f32[1536,128]{1,0:T(8,128)S(1)} %scatter_custom_fusion.6, s32[128]{0:T(128)S(1)} %get-tuple-element.12, f32[128,128]{1,0:T(8,128)S(1)} %collective-permute-done.5), kind=kCustom, calls=%fused_computation.20 | custom fusion | flops 16384 | bytes 197120 | tf_op jit(solution)/shard_map/scatter-add | solution.py:31
  126.8 10.4 %convolution_bitcast_fusion = f32[1536,128]{0,1:T(8,128)S(1)} fusion(f32[1536,128]{1,0:T(8,128)S(1)} %scatter_fusion.1, f32[1536,1536]{1,0:T(8,128)} %param.6), kind=kOutput, calls=%fused_computation.25 | convolution fusion | flops 3623878656 | bytes 11010048 | tf_op jit(solution)/shard_map/dot_general | solution.py:32
  137.2 0.3 copy.31
  137.5 1.1 scatter_custom_fusion.8
  138.6 19.6 %all_gather.11 = f32[1536,128]{1,0:T(8,128)S(1)} all-gather(f32[96,128]{1,0:T(8,128)S(1)} %scatter_custom_fusion.8), channel_id=1, replica_groups=mesh['rve'=2,'sub'=16] {'sub'}, dimensions={0}, use_global_device_ids=true | all-gather | bytes 835584 | tf_op jit(solution)/shard_map/all_gather | solution.py:37
  158.2 0.3 convolution_bitcast_fusion.3
  158.6 0.4 convolution_add_fusion
  158.9 2.7 %collective-permute-start.6 = (f32[48,128]{1,0:T(8,128)S(1)}, f32[48,128]{1,0:T(8,128)S(1)}, u32[]{:S(2)}, u32[]{:S(2)}) collective-permute-start(f32[48,128]{1,0:T(8,128)S(1)} %convolution_add_fusion), channel_id=1, source_target_pairs={{0,15},{1,0},{2,1},{3,2},{4,3},{5,4},{6,5},{7,6},{8,7},{9,8},{10,9... | collective-permute-start | bytes 73736 | tf_op jit(solution)/shard_map/ppermute | solution.py:15
  161.7 1.5 collective-permute-done.6
  163.2 0.6 gather_fusion.7
  163.8 0.8 convolution_subtract_fusion
  164.6 0.3 copy.35
  164.9 0.6 gather_fusion.9
  165.5 4.5 %collective-permute-start.7 = (f32[128,128]{1,0:T(8,128)S(1)}, f32[128,128]{1,0:T(8,128)S(1)}, u32[]{:S(2)}, u32[]{:S(2)}) collective-permute-start(f32[128,128]{1,0:T(8,128)S(1)} %gather_fusion.9), channel_id=1, source_target_pairs={{0,15},{1,0},{2,1},{3,2},{4,3},{5,4},{6,5},{7,6},{8,7},{9,8},{10,9... | collective-permute-start | bytes 196616 | tf_op jit(solution)/shard_map/ppermute | solution.py:15
  170.0 0.6 gather_fusion.8
  170.7 1.3 collective-permute-done.7
  171.9 0.6 multiply_add_fusion
  (17 shorter events, 0.2 us)
Async XLA Ops:
  1.8 42.6 %copy-start = (f32[48,768]{1,0:T(8,128)S(1)}, f32[48,768]{1,0:T(8,128)}, u32[]{:S(2)}) copy-start(f32[48,768]{1,0:T(8,128)} %param.8) | copy-start | bytes 442372
  45.2 14.5 %collective-permute-start = (f32[48,128]{1,0:T(8,128)S(1)}, f32[48,128]{1,0:T(8,128)S(1)}, u32[]{:S(2)}, u32[]{:S(2)}) collective-permute-start(f32[48,128]{1,0:T(8,128)S(1)} %convolution_add_fusion.2), channel_id=1, source_target_pairs={{0,15},{1,0},{2,1},{3,2},{4,3},{5,4},{6,5},{7,6},{8,7},{9,8},{10,9... | collective-permute-start | bytes 73736 | tf_op jit(solution)/shard_map/ppermute | solution.py:15
  64.1 2.0 %collective-permute-start.1 = (f32[128,128]{1,0:T(8,128)S(1)}, f32[128,128]{1,0:T(8,128)S(1)}, u32[]{:S(2)}, u32[]{:S(2)}) collective-permute-start(f32[128,128]{1,0:T(8,128)S(1)} %gather_fusion.3), channel_id=1, source_target_pairs={{0,15},{1,0},{2,1},{3,2},{4,3},{5,4},{6,5},{7,6},{8,7},{9,8},{10,9... | collective-permute-start | bytes 196616 | tf_op jit(solution)/shard_map/ppermute | solution.py:15
  66.0 6.5 %collective-permute-start.2 = (f32[128,128]{1,0:T(8,128)S(1)}, f32[128,128]{1,0:T(8,128)S(1)}, u32[]{:S(2)}, u32[]{:S(2)}) collective-permute-start(f32[128,128]{1,0:T(8,128)S(1)} %subtract_multiply_fusion), channel_id=1, source_target_pairs={{0,1},{1,2},{2,3},{3,4},{4,5},{5,6},{6,7},{7,8},{8,9},{9,10},{10,1... | collective-permute-start | bytes 196616 | tf_op jit(solution)/shard_map/ppermute | solution.py:15
  106.5 3.2 %collective-permute-start.3 = (f32[48,128]{1,0:T(8,128)S(1)}, f32[48,128]{1,0:T(8,128)S(1)}, u32[]{:S(2)}, u32[]{:S(2)}) collective-permute-start(f32[48,128]{1,0:T(8,128)S(1)} %convolution_add_fusion.1), channel_id=1, source_target_pairs={{0,15},{1,0},{2,1},{3,2},{4,3},{5,4},{6,5},{7,6},{8,7},{9,8},{10,9... | collective-permute-start | bytes 73736 | tf_op jit(solution)/shard_map/ppermute | solution.py:15
  112.1 6.4 %collective-permute-start.4 = (f32[128,128]{1,0:T(8,128)S(1)}, f32[128,128]{1,0:T(8,128)S(1)}, u32[]{:S(2)}, u32[]{:S(2)}) collective-permute-start(f32[128,128]{1,0:T(8,128)S(1)} %gather_fusion.6), channel_id=1, source_target_pairs={{0,15},{1,0},{2,1},{3,2},{4,3},{5,4},{6,5},{7,6},{8,7},{9,8},{10,9... | collective-permute-start | bytes 196616 | tf_op jit(solution)/shard_map/ppermute | solution.py:15
  118.5 6.5 %collective-permute-start.5 = (f32[128,128]{1,0:T(8,128)S(1)}, f32[128,128]{1,0:T(8,128)S(1)}, u32[]{:S(2)}, u32[]{:S(2)}) collective-permute-start(f32[128,128]{1,0:T(8,128)S(1)} %multiply_add_fusion.1), channel_id=1, source_target_pairs={{0,1},{1,2},{2,3},{3,4},{4,5},{5,6},{6,7},{7,8},{8,9},{9,10},{10,1... | collective-permute-start | bytes 196616 | tf_op jit(solution)/shard_map/ppermute | solution.py:15
  158.9 4.2 %collective-permute-start.6 = (f32[48,128]{1,0:T(8,128)S(1)}, f32[48,128]{1,0:T(8,128)S(1)}, u32[]{:S(2)}, u32[]{:S(2)}) collective-permute-start(f32[48,128]{1,0:T(8,128)S(1)} %convolution_add_fusion), channel_id=1, source_target_pairs={{0,15},{1,0},{2,1},{3,2},{4,3},{5,4},{6,5},{7,6},{8,7},{9,8},{10,9... | collective-permute-start | bytes 73736 | tf_op jit(solution)/shard_map/ppermute | solution.py:15
  164.9 7.7 %copy-start.1 = (f32[1536,128]{1,0:T(8,128)}, f32[1536,128]{1,0:T(8,128)S(1)}, u32[]{:S(2)}) copy-start(f32[1536,128]{1,0:T(8,128)S(1)} %copy.35) | copy-start | bytes 2359300
  165.5 6.4 %collective-permute-start.7 = (f32[128,128]{1,0:T(8,128)S(1)}, f32[128,128]{1,0:T(8,128)S(1)}, u32[]{:S(2)}, u32[]{:S(2)}) collective-permute-start(f32[128,128]{1,0:T(8,128)S(1)} %gather_fusion.9), channel_id=1, source_target_pairs={{0,15},{1,0},{2,1},{3,2},{4,3},{5,4},{6,5},{7,6},{8,7},{9,8},{10,9... | collective-permute-start | bytes 196616 | tf_op jit(solution)/shard_map/ppermute | solution.py:15
where the time goes:
time: 173 us
  blocking collectives  64.8 us (37%)
  matrix products  36.7 us (21%)
  local copies, waits for them, and re-layouts  27.5 us (16%)
  starting transfers between devices  15.8 us (9%)
  waiting for transfers between devices  14.3 us (8%)
  other arithmetic  12.5 us (7%)
    all_gather x3, blocking collectives, local(): piece = lax.all_gather(slotted, 'sub', axis=0, tiled=True)  64.8 us
    dot_general x3, matrix products, local(): jnp.dot(condensed, loads, precision=lax.Precision.HIGHEST, preferred_elem...  31.3 us
    ppermute x8, starting transfers between devices, passed_along(): return lax.ppermute(value, axis, pairs)  15.8 us
    ppermute x8, waiting for transfers between devices, passed_along(): return lax.ppermute(value, axis, pairs)  14.3 us
    unnamed x9, local copies, waits for them, and re-layouts  11.1 us
    scatter-add x6, other arithmetic, local(): eigen_loads.at[right_rows].add(-multipliers).at[left_rows].add(previous)  9.69 us
    gather x1, local copies, waits for them, and re-layouts, local(): prolong = condensed[:, prim_rows]  4.76 us
  transfers between devices with their start and end apart: 8, of which 7 were waited for; matrix products, arithmetic and copies ran while one was open for 11% of the time, Pallas kernels for 0%

commit v1 on v0

v1 whole, which is shorter than its diff:
```python
import functools

import jax
import jax.numpy as jnp
from jax import lax
from jax.experimental import pallas as pl
from jax.experimental.pallas import tpu as pltpu
from jax.sharding import PartitionSpec as P

ITERS = 3
DAMPING = 0.5
GROUP = 4
LANES = 128
BF16 = jnp.bfloat16
F32 = jnp.float32


def call(kernel, out_shapes, args, in_specs=None, grid=None, out_specs=None, scratch=(), flops=0, size=0):
    vmem = pl.BlockSpec(memory_space=pltpu.VMEM)
    if in_specs is None:
        in_specs = [pl.BlockSpec(memory_space=pltpu.SMEM)] + [vmem] * (len(args) - 1)
    if out_specs is None:
        out_specs = [vmem] * len(out_shapes)
    options = {} if grid is None else {"grid": grid}
    return pl.pallas_call(
        kernel,
        out_shape=[jax.ShapeDtypeStruct(s, F32) for s in out_shapes],
        in_specs=in_specs,
        out_specs=out_specs,
        scratch_shapes=list(scratch),
        compiler_params=pltpu.CompilerParams(vmem_limit_bytes=48 * 1024 * 1024),
        cost_estimate=pl.CostEstimate(flops=flops, bytes_accessed=size, transcendentals=0),
        **options,
    )(*args)


def halves(x):
    high = x.astype(BF16)
    return high, (x - high.astype(F32)).astype(BF16)


def dot(a, b):
    return jnp.dot(a, b, preferred_element_type=F32)


def product(a, b):
    ah, al = halves(a)
    bh, bl = halves(b)
    n = b.shape[1]
    both = dot(ah, jnp.concatenate([bh, bl], axis=1))
    return both[:, :n] + both[:, n:] + dot(al, bh)


def lane_block(rows):
    return lax.broadcasted_iota(jnp.int32, (rows, LANES), 1) // (LANES // GROUP)


def turned(x, blocks):
    width = LANES // GROUP
    if isinstance(blocks, int):
        shift = (blocks % GROUP) * width
        return x if shift == 0 else pltpu.roll(x, shift, 1)
    return pltpu.roll(x, lax.rem(blocks + 2 * GROUP, GROUP) * width, 1)


def cut(x, member, out_refs):
    rows = x.shape[0] // GROUP
    block = lane_block(rows)
    parts = [x[q * rows:(q + 1) * rows] for q in range(GROUP)]
    for k, out in enumerate(out_refs):
        to = member ^ k
        packed = jnp.zeros((rows, LANES), F32)
        for q in range(GROUP):
            packed = jnp.where(block == q, turned(parts[q], q - to), packed)
        out[...] = packed


def joined(pieces, member):
    rows = pieces[0].shape[0]
    block = lane_block(rows)
    out = []
    for q in range(GROUP):
        part = jnp.zeros((rows, LANES), F32)
        for k, piece in enumerate(pieces):
            came = member ^ k
            part = jnp.where(block == came, turned(piece, came - q), part)
        out.append(part)
    return jnp.concatenate(out, axis=0)


def packed(x, chunk):
    first = lane_block(chunk) == 0
    out = None
    for q in range(x.shape[0] // chunk):
        part = turned(jnp.where(first, x[q * chunk:(q + 1) * chunk], 0.0), q)
        out = part if out is None else out + part
    return out


def unpacked(x, count):
    return jnp.concatenate([turned(x, -q) for q in range(count)], axis=0)


def chunk_of(owned):
    return -(-owned // (GROUP * 8)) * 8


def payload(v, width, owned, out):
    chunk = chunk_of(owned)
    first = lane_block(owned) == 0
    coarse = v[2 * width:]
    below = turned(coarse[owned:], 1)
    out[0:owned] = coarse[:owned] + jnp.where(first, 0.0, below)
    out[owned:owned + chunk] = packed(below, chunk)
    small = width // GROUP
    at = owned + chunk
    out[at:at + small] = packed(v[:width], small)
    out[at + small:at + 2 * small] = packed(turned(v[width:2 * width], 1), small)


def selector(rows_ref, et_ref):
    sets, width = rows_ref.shape
    for group in range(sets):
        row = rows_ref[group:group + 1, :].astype(F32)
        column = jnp.broadcast_to(row, (width, width)).T
        for c in range(et_ref.shape[1] // width):
            lane = lax.broadcasted_iota(jnp.int32, (width, width), 1) + c * width
            hit = column == lane.astype(F32)
            et_ref[group * width:(group + 1) * width, c * width:(c + 1) * width] = jnp.where(hit, 1.0, 0.0).astype(BF16)


def first_kernel(kept, pos, rows_ref, k_ref, f_ref, u_ref, *rest):
    pieces, (et, loads) = rest[:GROUP], rest[GROUP:]
    step = pl.program_id(0)
    rows, columns = k_ref.shape[0], f_ref.shape[1]

    @pl.when(step == 0)
    def _():
        selector(rows_ref, et)
        high, low = halves(f_ref[...])
        loads[:, :columns] = high
        loads[:, columns:] = low

    high, low = halves(k_ref[...])
    both = dot(high, loads[...])
    u = both[:, :columns] + both[:, columns:] + dot(low, loads[:, :columns])
    u_ref[pl.ds(pl.multiple_of(step * rows, rows), rows), :] = u

    @pl.when(step == pl.num_programs(0) - 1)
    def _():
        high, low = halves(u_ref[...])
        v = dot(et[...], jnp.concatenate([high, low], axis=1))
        v = v[:, :columns] + v[:, columns:]
        cut(v[:kept], pos[0], pieces)


def columns_kernel(rows_ref, k_ref, ks_ref, a_ref, et):
    step = pl.program_id(0)
    rows = k_ref.shape[0]

    @pl.when(step == 0)
    def _():
        selector(rows_ref, et)

    high, low = halves(k_ref[...])
    dims = (((1,), (1,)), ((), ()))
    picked = lax.dot_general(high, et[...], dims, preferred_element_type=F32)
    picked = picked + lax.dot_general(low, et[...], dims, preferred_element_type=F32)
    ks_ref[pl.ds(pl.multiple_of(step * rows, rows), rows), :] = picked

    @pl.when(step == pl.num_programs(0) - 1)
    def _():
        high, low = halves(ks_ref[...])
        a_ref[...] = (dot(et[...], high) + dot(et[...], low))[:a_ref.shape[0]]


def coarse_kernel(pos, c0, c1, c2, c3, plane, up, down):
    owned = c0.shape[0]
    for k, piece in enumerate((c0, c1, c2, c3)):
        member = pos[0] ^ k
        plane[pl.ds(pl.multiple_of(member * owned, 8), owned), :] = piece[...]
    up[...] = plane[(GROUP - 1) * owned:, :]
    down[...] = plane[:2 * owned, :]


def edges_kernel(width, pos, a0, a1, a2, a3, up, down):
    for k, piece in enumerate((a0, a1, a2, a3)):
        member = pos[0] ^ k

        @pl.when(member == GROUP - 1)
        def _():
            up[...] = piece[width:2 * width, 2 * width:]

        @pl.when(member == 0)
        def _():
            down[...] = piece[:width, 2 * width:]


def start_kernel(width, owned, pos, p0, p1, p2, p3, v_ref, pay_ref):
    v = joined([p0[...], p1[...], p2[...], p3[...]], pos[0])
    v_ref[...] = v
    payload(v, width, owned, pay_ref)


def turn_kernel(width, owned, kind, pos, pays, above, plane, below, a0, a1, a2, a3, edge_up, edge_down, v0, *rest):
    if kind == "first":
        now = v0
    else:
        now, left_ref, right_ref = rest[:3]
        rest = rest[3:]
    outs, (stack,) = rest[:-1], rest[-1:]
    member, group = pos[0], pos[1]
    groups = pays.shape[0]
    chunk = chunk_of(owned)
    small = width // GROUP
    at = owned + chunk
    blocks = (a0, a1, a2, a3)
    first = lane_block(owned) == 0

    for h in range(groups):
        extra = unpacked(pays[(h - 1) % groups, owned:at, :], -(-owned // chunk))[:owned]
        whole = pays[h, :owned, :] + jnp.where(first, extra, 0.0)
        for i in range(GROUP):
            high, low = halves(turned(whole, -i))
            place = slice((h * GROUP + i) * owned, (h * GROUP + i + 1) * owned)
            stack[place, :LANES] = high
            stack[place, LANES:] = low

    def solved(c_ref):
        high, low = halves(c_ref[...])
        both = dot(high, stack[...])
        return both[:, :LANES] + both[:, LANES:] + dot(low, stack[:, :LANES])

    w = jnp.concatenate([solved(above), solved(plane), solved(below)], axis=0)
    pair = lane_block(2 * owned)
    q = jnp.zeros((2 * owned, LANES), F32)
    for i in range(GROUP):
        q = jnp.where(pair == i, turned(w[(i + 1) * owned:(i + 3) * owned], i), q)
    filler = jnp.zeros((width - 2 * owned, LANES), F32)

    def applied(cols, rows, x):
        block = lane_block(x.shape[0])
        total = None
        for k in range(GROUP):
            mine = jnp.where(block == (member ^ k), x, 0.0)
            part = product(blocks[k][rows, cols], mine)
            total = part if total is None else total + part
        return total

    padded = jnp.concatenate([q, filler], axis=0)
    faces = now[:2 * width, :] - applied(slice(2 * width, 3 * width), slice(0, 2 * width), padded)
    left, right = faces[:width], faces[width:]
    before = jnp.concatenate([w[:2 * owned], filler], axis=0)
    after = jnp.concatenate([w[(GROUP + 1) * owned:], filler], axis=0)
    previous = lax.rem(group + groups - 1, groups)
    following = lax.rem(group + 1, groups)
    right_before = unpacked(pays[previous, at + small:at + 2 * small, :], GROUP) - product(edge_up[...], before)
    left_after = unpacked(pays[following, at:at + small, :], GROUP) - product(edge_down[...], after)
    block = lane_block(width)
    beyond = jnp.where(block == GROUP - 1, turned(left_after, GROUP - 1), turned(left, -1))
    behind = jnp.where(block == 0, right_before, turned(right, 1))
    lam_right = DAMPING * (right - beyond)
    lam_left = DAMPING * (behind - left)
    if kind != "first":
        lam_right = lam_right + right_ref[...]
        lam_left = lam_left + left_ref[...]
    if kind == "last":
        cut(jnp.concatenate([q, lam_right], axis=0), member, outs)
        return
    v_ref, left_out, right_out, pay_ref = outs[:4]
    left_out[...] = lam_left
    right_out[...] = lam_right
    v = v0[...] + applied(slice(0, 2 * width), slice(None), jnp.concatenate([lam_left, -lam_right], axis=0))
    v_ref[...] = v
    payload(v, width, owned, pay_ref)
    if kind == "middle":
        cut(jnp.concatenate([lam_left, lam_right], axis=0), member, outs[4:])


def spread_kernel(width, pos, p0, p1, p2, p3, u_ref, ks_ref, out_ref):
    lam = joined([p0[...], p1[...], p2[...], p3[...]], pos[0])
    rows = lax.broadcasted_iota(jnp.int32, lam.shape, 0)
    out_ref[...] = u_ref[...] + product(ks_ref[:, :2 * width], jnp.where(rows < width, lam, -lam))


def final_kernel(width, owned, pos, p0, p1, p2, p3, u_ref, ks_ref, out_ref, lam_ref):
    x = joined([p0[...], p1[...], p2[...], p3[...]], pos[0])
    lam_ref[...] = x[2 * owned:]
    filler = jnp.zeros((width - 2 * owned, LANES), F32)
    q = jnp.concatenate([x[:2 * owned], filler], axis=0)
    out_ref[...] = u_ref[...] - product(ks_ref[:, 2 * width:], q)


def local(condensed, eigen_loads, coarse_inverse, face_rows, primal_rows, primal_slot):
    order, columns = eigen_loads.shape
    owned, coarse = coarse_inverse.shape
    width = face_rows.shape[2]
    kept = 2 * width + 2 * owned
    count = lax.axis_size("sub")
    groups = count // GROUP
    me = lax.axis_index("sub")
    pos = jnp.stack([me % GROUP, me // GROUP]).astype(jnp.int32)

    def mate(x, k):
        return lax.ppermute(x, "sub", [(s, s ^ k) for s in range(count)])

    def planes(x, by):
        return lax.ppermute(x, "sub", [(s, (s + by * GROUP) % count) for s in range(count)])

    def along(x):
        lines = [[h * GROUP + m for h in range(groups)] for m in range(GROUP)]
        return lax.all_gather(x, "sub", axis_index_groups=lines)

    def traded(pieces):
        return [pieces[0]] + [mate(pieces[k], k) for k in range(1, GROUP)]

    def plane_all(x):
        second = mate(x, 2)
        return [x, mate(x, 1), second, mate(second, 1)]

    slots = lax.broadcasted_iota(jnp.int32, (2 * owned, width), 1)
    by_slot = jnp.max(jnp.where(primal_slot[0][:, None] == slots, primal_rows[0][:, None], -1), axis=0)
    rows = jnp.concatenate([face_rows[0], by_slot[None]], axis=0)

    c_blocks = plane_all(coarse_inverse)

    block = 256 if order % 256 == 0 else order
    k_spec = pl.BlockSpec((block, order), lambda i: (i, 0))
    smem = pl.BlockSpec(memory_space=pltpu.SMEM)

    def whole(*shape):
        return pl.BlockSpec(shape, lambda i: (0,) * len(shape))

    small = kept // GROUP
    u0, *pieces = call(
        functools.partial(first_kernel, kept),
        [(order, columns)] + [(small, LANES)] * GROUP,
        (pos, rows, condensed, eigen_loads),
        in_specs=[smem, whole(3, width), k_spec, whole(order, columns)],
        grid=(order // block,),
        out_specs=[whole(order, columns)] + [whole(small, LANES)] * GROUP,
        scratch=[pltpu.VMEM((3 * width, order), BF16), pltpu.VMEM((order, 2 * columns), BF16)],
        flops=6 * order * order * columns,
        size=4 * order * order,
    )
    pieces = traded(pieces)
    ks, a_own = call(
        columns_kernel,
        [(order, 3 * width), (kept, 3 * width)],
        (rows, condensed),
        in_specs=[whole(3, width), k_spec],
        grid=(order // block,),
        out_specs=[whole(order, 3 * width), whole(kept, 3 * width)],
        scratch=[pltpu.VMEM((3 * width, order), BF16)],
        flops=4 * order * order * 3 * width,
        size=4 * order * order,
    )
    plane, c_up, c_down = call(
        coarse_kernel,
        [(GROUP * owned, coarse), (owned, coarse), (2 * owned, coarse)],
        (pos, *c_blocks),
    )
    above, below = planes(c_up, 1), planes(c_down, -1)
    chunk = chunk_of(owned)
    pay_rows = owned + chunk + 2 * (width // GROUP)
    v0, pay = call(
        functools.partial(start_kernel, width, owned),
        [(kept, LANES), (pay_rows, LANES)],
        (pos, *pieces),
    )
    a_blocks = plane_all(a_own)
    a_up, a_down = call(functools.partial(edges_kernel, width), [(width, width)] * 2, (pos, *a_blocks))
    edge_up, edge_down = planes(a_up, 1), planes(a_down, -1)

    fixed = (above, plane, below, *a_blocks, edge_up, edge_down, v0)
    stack = [pltpu.VMEM((coarse, 2 * LANES), BF16)]
    state = ()
    for step in range(ITERS):
        kind = "first" if step == 0 else "last" if step == ITERS - 1 else "middle"
        shapes = [(kept, LANES), (width, LANES), (width, LANES), (pay_rows, LANES)]
        if kind == "middle":
            shapes = shapes + [(2 * width // GROUP, LANES)] * GROUP
        if kind == "last":
            shapes = [((2 * owned + width) // GROUP, LANES)] * GROUP
        outs = call(
            functools.partial(turn_kernel, width, owned, kind),
            shapes,
            (pos, along(pay), *fixed, *state),
            scratch=stack,
        )
        if kind != "last":
            state, pay = outs[:3], outs[3]
        if kind == "middle":
            lam_pieces = traded(outs[4:])
            (spread,) = call(
                functools.partial(spread_kernel, width),
                [(order, columns)],
                (pos, *lam_pieces, u0, ks),
                flops=6 * order * 2 * width * columns,
                size=4 * order * 5 * width,
            )
    displaced, multipliers = call(
        functools.partial(final_kernel, width, owned),
        [(order, columns), (width, columns)],
        (pos, *traded(outs), spread, ks),
    )
    return displaced, multipliers


def solution(mesh):
    placed = (
        P(("rve", "sub"), None),
        P(("rve", "sub"), None),
        P(("rve", "sub"), None),
        P("sub", None, None),
        P("sub", None),
        P("sub", None),
    )
    return jax.shard_map(
        local,
        mesh=mesh,
        in_specs=placed,
        out_specs=(P(("rve", "sub"), None), P(("rve", "sub"), None)),
        check_vma=False,
    )
```

time: 173 us -> 121 us (0.70)
  matrix products: 36.7 us -> 0 us
  Pallas kernels: 0 us -> 33.5 us
  local copies, waits for them, and re-layouts: 27.5 us -> 1.13 us
  blocking collectives: 64.8 us -> 42.5 us
  other arithmetic: 12.5 us -> 1.54 us
  waiting for transfers between devices: 14.3 us -> 23.7 us
    dot_general x12 -> x0, matrix products: 36.7 us -> none  [the longest x3 31.3 us: local(): jnp.dot(condensed, loads, precision=lax.Precision.HIGHEST, preferred_elem...]
    pallas_call x0 -> x10, Pallas kernels: none -> 33.5 us  [call(): pl.pallas_call(kernel, out_shape=[jax.ShapeDtypeStruct(s, F32) for s in o...]
    all_gather x3, blocking collectives: 64.8 us -> 42.5 us  [along(): return lax.all_gather(x, 'sub', axis_index_groups=lines)]
    gather x10 -> x0, local copies, waits for them, and re-layouts: 10.5 us -> none  [the longest x1 4.76 us: local(): prolong = condensed[:, prim_rows]]
    unnamed x9 -> x2, local copies, waits for them, and re-layouts: 11.1 us -> 1.13 us
    scatter-add x6 -> x0, other arithmetic: 9.69 us -> none  [local(): eigen_loads.at[right_rows].add(-multipliers).at[left_rows].add(previous)]
    ppermute x8 -> x19, waiting for transfers between devices: 14.3 us -> 23.7 us  [the longest x15 23.7 us: mate(): return lax.ppermute(x, 'sub', [(s, s ^ k) for s in range(count)])]
    scatter x3 -> x0, local copies, waits for them, and re-layouts: 3.3 us -> none  [local(): jnp.zeros((2 * owned, columns), jnp.float32).at[slots]]
  transfers between devices with their start and end apart: 8 -> 19, of which waited for: 7 -> 7; matrix products, arithmetic and copies ran while one was open for 11% -> 0% of each run, Pallas kernels for 0% -> 13%
where the time goes in v1:
time: 121 us; the launch traced here: 120 us
  blocking collectives  42.5 us (35%)
  Pallas kernels  33.5 us (28%)
  waiting for transfers between devices  23.7 us (20%)
  starting transfers between devices  17.3 us (14%)
  other arithmetic  1.54 us (1%)
    all_gather x3, blocking collectives, along(): return lax.all_gather(x, 'sub', axis_index_groups=lines)  42.5 us
    pallas_call x10, Pallas kernels, call(): pl.pallas_call(kernel, out_shape=[jax.ShapeDtypeStruct(s, F32) for s in o...  33.5 us
    ppermute x15, waiting for transfers between devices, mate(): return lax.ppermute(x, 'sub', [(s, s ^ k) for s in range(count)])  23.7 us
    ppermute x15, starting transfers between devices, mate(): return lax.ppermute(x, 'sub', [(s, s ^ k) for s in range(count)])  9.56 us
    ppermute x4, starting transfers between devices, planes(): lax.ppermute(x, 'sub', [(s, (s + by * GROUP) % count) for s in range(coun...  7.76 us
  transfers between devices with their start and end apart: 19, of which 7 were waited for; matrix products, arithmetic and copies ran while one was open for 0% of the time, Pallas kernels for 13%

profile of v1, /device:TPU:0, one launch (start us, length us, event | category | flops | bytes accessed | tf_op | source)
XLA Modules:
  0.0 120.5 jit_solution(5063435674854377234)
XLA Ops:
  0.6 0.8 select_reduce_fusion
  1.4 0.7 pad_add_fusion.rows_ref
  2.1 10.1 %shard_map.80 = (f32[1536,384]{1,0:T(8,128)S(1)}, f32[352,384]{1,0:T(8,128)S(1)}) custom-call(s32[3,128]{1,0:T(4,128)S(1)} %pad_add_fusion.rows_ref, f32[1536,1536]{1,0:T(8,128)} %k_ref.3), custom_call_target="tpu_custom_call" | custom-call | flops 3623878656 | bytes 9437184 | tf_op jit(solution)/shard_map/pallas_call | solution.py:25
  12.2 3.0 %collective-permute-start.9 = (f32[352,384]{1,0:T(8,128)S(1)}, f32[352,384]{1,0:T(8,128)S(1)}, u32[]{:S(2)}, u32[]{:S(2)}) collective-permute-start(f32[352,384]{1,0:T(8,128)S(1)} %get-tuple-element.40.a0), channel_id=1, source_target_pairs={{0,2},{1,3},{2,0},{3,1},{4,6},{5,7},{6,4},{7,5},{8,10},{9,11},{10,... | collective-permute-start | bytes 1622024 | tf_op jit(solution)/shard_map/ppermute | solution.py:305
  15.3 0.1 collective-permute-start.4
  15.4 0.0 collective-permute-start.8
  15.4 13.0 %collective-permute-done.9.a2 = f32[352,384]{1,0:T(8,128)S(1)} collective-permute-done((f32[352,384]{1,0:T(8,128)S(1)}, f32[352,384]{1,0:T(8,128)S(1)}, u32[]{:S(2)}, u32[]{:S(2)}) %collective-permute-start.9) | collective-permute-done | bytes 540704 | tf_op jit(solution)/shard_map/ppermute | solution.py:305
  28.4 0.0 collective-permute-start.10
  28.4 0.5 collective-permute-start.3
  28.9 1.9 %collective-permute-done.4.c2 = f32[48,768]{1,0:T(8,128)} collective-permute-done((f32[48,768]{1,0:T(8,128)}, f32[48,768]{1,0:T(8,128)}, u32[]{:S(2)}, u32[]{:S(2)}) %collective-permute-start.4) | collective-permute-done | bytes 147488 | tf_op jit(solution)/shard_map/ppermute | solution.py:305
  30.8 0.0 collective-permute-start.5
  30.8 0.1 pad_add_fusion.1.pos
  30.9 0.0 collective-permute-done.3.c1
  30.9 1.6 %collective-permute-done.5.c3 = f32[48,768]{1,0:T(8,128)} collective-permute-done((f32[48,768]{1,0:T(8,128)}, f32[48,768]{1,0:T(8,128)}, u32[]{:S(2)}, u32[]{:S(2)}) %collective-permute-start.5) | collective-permute-done | bytes 147488 | tf_op jit(solution)/shard_map/ppermute | solution.py:305
  32.5 1.2 %shard_map.79 = (f32[192,768]{1,0:T(8,128)S(1)}, f32[48,768]{1,0:T(8,128)S(1)}, f32[96,768]{1,0:T(8,128)S(1)}) custom-call(s32[2]{0:T(128)S(1)} %pad_add_fusion.1.pos, f32[48,768]{1,0:T(8,128)} %c0.1, f32[48,768]{1,0:T(8,128)} %collective-permute-done.3.c1, f32[48,768]{1,0:T(8,128)} %collective-permute-done.4.c2, f32[48,768]{1,0:T(8,128)} %collective-permute-done.5.c3), custom_call_target="tpu_custom_call" | custom-call | tf_op jit(solution)/shard_map/pallas_call | solution.py:25
  33.7 3.9 %collective-permute-start.7 = (f32[96,768]{1,0:T(8,128)S(1)}, f32[96,768]{1,0:T(8,128)S(1)}, u32[]{:S(2)}, u32[]{:S(2)}) collective-permute-start(f32[96,768]{1,0:T(8,128)S(1)} %get-tuple-element.39), channel_id=1, source_target_pairs={{0,12},{1,13},{2,14},{3,15},{4,0},{5,1},{6,2},{7,3},{8,4},{9,5},{1... | collective-permute-start | bytes 884744 | tf_op jit(solution)/shard_map/ppermute | solution.py:308
  37.6 0.0 copy-start
  37.6 1.1 copy-done
  38.8 8.0 %shard_map.77 = (f32[1536,128]{1,0:T(8,128)S(1)}, f32[88,128]{1,0:T(8,128)S(1)}, f32[88,128]{1,0:T(8,128)S(1)}, f32[88,128]{1,0:T(8,128)S(1)}, f32[88,128]{1,0:T(8,128)S(1)}) custom-call(s32[2]{0:T(128)S(1)} %pad_add_fusion.1.pos, s32[3,128]{1,0:T(4,128)S(1)} %pad_add_fusion.rows_ref, f32[1536,1536]{1,0:T(8,128)} %k_ref.3, f32[1536,128]{1,0:T(8,128)S(1)} %copy-done), custom_call_target="tpu_custom_call" | custom-call | flops 1811939328 | bytes 9437184 | tf_op jit(solution)/shard_map/pallas_call | solution.py:25
  46.8 0.1 collective-permute-start
  46.9 1.6 %collective-permute-start.1 = (f32[88,128]{1,0:T(8,128)S(1)}, f32[88,128]{1,0:T(8,128)S(1)}, u32[]{:S(2)}, u32[]{:S(2)}) collective-permute-start(f32[88,128]{1,0:T(8,128)S(1)} %get-tuple-element.34), channel_id=1, source_target_pairs={{0,2},{1,3},{2,0},{3,1},{4,6},{5,7},{6,4},{7,5},{8,10},{9,11},{10,... | collective-permute-start | bytes 135176 | tf_op jit(solution)/shard_map/ppermute | solution.py:305
  48.4 0.0 collective-permute-done.p1
  48.4 0.0 collective-permute-start.6
  48.5 2.5 %collective-permute-done.1.p2 = f32[88,128]{1,0:T(8,128)S(1)} collective-permute-done((f32[88,128]{1,0:T(8,128)S(1)}, f32[88,128]{1,0:T(8,128)S(1)}, u32[]{:S(2)}, u32[]{:S(2)}) %collective-permute-start.1) | collective-permute-done | bytes 45088 | tf_op jit(solution)/shard_map/ppermute | solution.py:305
  51.0 0.4 collective-permute-start.2
  51.4 3.5 %collective-permute-done.2.p3 = f32[88,128]{1,0:T(8,128)S(1)} collective-permute-done((f32[88,128]{1,0:T(8,128)S(1)}, f32[88,128]{1,0:T(8,128)S(1)}, u32[]{:S(2)}, u32[]{:S(2)}) %collective-permute-start.2) | collective-permute-done | bytes 45088 | tf_op jit(solution)/shard_map/ppermute | solution.py:305
  54.9 0.9 shard_map.78
  55.8 0.0 collective-permute-done.8.a1
  55.8 0.0 collective-permute-done.10.a3
  55.8 1.3 %shard_map.81 = (f32[128,128]{1,0:T(8,128)S(1)}, f32[128,128]{1,0:T(8,128)S(1)}) custom-call(s32[2]{0:T(128)S(1)} %pad_add_fusion.1.pos, f32[352,384]{1,0:T(8,128)S(1)} %get-tuple-element.40.a0, f32[352,384]{1,0:T(8,128)} %collective-permute-done.8.a1, f32[352,384]{1,0:T(8,128)S(1)} %collective-permute-done.9.a2, f32[352,384]{1,0:T(8,128)} %collective-permute-done.10.a3), custom_call_target="tpu_custom_call" | custom-call | tf_op jit(solution)/shard_map/pallas_call | solution.py:25
  57.1 0.1 collective-permute-start.11
  57.1 3.8 %collective-permute-start.12 = (f32[128,128]{1,0:T(8,128)S(1)}, f32[128,128]{1,0:T(8,128)S(1)}, u32[]{:S(2)}, u32[]{:S(2)}) collective-permute-start(f32[128,128]{1,0:T(8,128)S(1)} %get-tuple-element.42), channel_id=1, source_target_pairs={{0,12},{1,13},{2,14},{3,15},{4,0},{5,1},{6,2},{7,3},{8,4},{9,5},{1... | collective-permute-start | bytes 196616 | tf_op jit(solution)/shard_map/ppermute | solution.py:308
  61.0 14.3 %all-gather = f32[512,128]{1,0:T(8,128)S(1)} all-gather(f32[128,128]{1,0:T(8,128)S(1)} %get-tuple-element.36), channel_id=2, replica_groups={{0,4,8,12},{1,5,9,13},{2,6,10,14},{3,7,11,15},{16,20,24,28},{17,21,25,2..., dimensions={0}, use_global_device_ids=true | all-gather | bytes 327680 | tf_op jit(solution)/shard_map/all_gather | solution.py:312
  75.2 0.0 collective-permute-done.6.above
  75.2 0.0 collective-permute-done.7.below
  75.2 0.0 collective-permute-done.11.edge_up
  75.2 0.0 collective-permute-done.12.edge_down
  75.2 3.1 %shard_map.82 = (f32[352,128]{1,0:T(8,128)S(1)}, f32[128,128]{1,0:T(8,128)S(1)}, f32[128,128]{1,0:T(8,128)S(1)}, f32[128,128]{1,0:T(8,128)S(1)}) custom-call(s32[2]{0:T(128)S(1)} %pad_add_fusion.1.pos, f32[4,128,128]{2,1,0:T(8,128)S(1)} %bitcast.9, f32[48,768]{1,0:T(8,128)S(1)} %collective-permute-done.6.above, f32[192,768]{1,0:T(8,128)S(1)} %get-tuple-element.38.plane, ...), custom_call_target="tpu_custom_call" | custom-call | tf_op jit(solution)/shard_map/pallas_call | solution.py:25
  78.3 13.8 %all-gather.1 = f32[512,128]{1,0:T(8,128)S(1)} all-gather(f32[128,128]{1,0:T(8,128)S(1)} %get-tuple-element.44), channel_id=3, replica_groups={{0,4,8,12},{1,5,9,13},{2,6,10,14},{3,7,11,15},{16,20,24,28},{17,21,25,2..., dimensions={0}, use_global_device_ids=true | all-gather | bytes 327680 | tf_op jit(solution)/shard_map/all_gather | solution.py:312
  92.2 3.1 %shard_map.83 = (f32[352,128]{1,0:T(8,128)S(1)}, f32[128,128]{1,0:T(8,128)S(1)}, f32[128,128]{1,0:T(8,128)S(1)}, f32[128,128]{1,0:T(8,128)S(1)}, f32[64,128]{1,0...) custom-call(s32[2]{0:T(128)S(1)} %pad_add_fusion.1.pos, ...), custom_call_target="tpu_custom_call" | custom-call | tf_op jit(solution)/shard_map/pallas_call | solution.py:25
  95.3 0.1 collective-permute-start.16
  95.3 0.7 collective-permute-start.17
  96.0 1.1 collective-permute-start.18
  97.2 14.4 %all-gather.2 = f32[512,128]{1,0:T(8,128)S(1)} all-gather(f32[128,128]{1,0:T(8,128)S(1)} %get-tuple-element.48), channel_id=4, replica_groups={{0,4,8,12},{1,5,9,13},{2,6,10,14},{3,7,11,15},{16,20,24,28},{17,21,25,2..., dimensions={0}, use_global_device_ids=true | all-gather | bytes 327680 | tf_op jit(solution)/shard_map/all_gather | solution.py:312
  111.6 2.5 %shard_map.84 = (f32[56,128]{1,0:T(8,128)S(1)}, f32[56,128]{1,0:T(8,128)S(1)}, f32[56,128]{1,0:T(8,128)S(1)}, f32[56,128]{1,0:T(8,128)S(1)}) custom-call(s32[2]{0:T(128)S(1)} %pad_add_fusion.1.pos, f32[4,128,128]{2,1,0:T(8,128)S(1)} %bitcast.10, f32[48,768]{1,0:T(8,128)S(1)} %collective-permute-done.6.above, f32[192,768]{1,0:T(8,128)S(1)} %get-tuple-element.38.plane, ...), custom_call_target="tpu_custom_call" | custom-call | tf_op jit(solution)/shard_map/pallas_call | solution.py:25
  114.1 0.1 collective-permute-start.13
  114.2 0.7 collective-permute-start.14
  114.9 0.0 collective-permute-done.16.p1
  114.9 1.1 collective-permute-start.15
  116.0 0.0 collective-permute-done.17.p2
  116.0 0.0 collective-permute-done.18.p3
  116.0 1.3 %shard_map.85.u_ref = f32[1536,128]{1,0:T(8,128)S(1)} custom-call(s32[2]{0:T(128)S(1)} %pad_add_fusion.1.pos, f32[64,128]{1,0:T(8,128)S(1)} %get-tuple-element.56.p0, f32[64,128]{1,0:T(8,128)S(1)} %collective-permute-done.16.p1, f32[64,128]{1,0:T(8,128)S(1)} %collective-permute-done.17.p2, f32[64,128]{1,0:T(8,128)S(1)} %collective-permute-done.18.p3, ...), custom_call_target="tpu_custom_call" | custom-call | flops 301989888 | bytes 3932160 | tf_op jit(solution)/shard_map/pallas_call | solution.py:25
  117.3 0.0 collective-permute-done.13.p1
  117.3 1.0 collective-permute-done.14.p2
  118.3 0.2 collective-permute-done.15.p3
  118.5 2.0 %shard_map.86 = (f32[1536,128]{1,0:T(8,128)}, f32[128,128]{1,0:T(8,128)}) custom-call(s32[2]{0:T(128)S(1)} %pad_add_fusion.1.pos, f32[56,128]{1,0:T(8,128)S(1)} %get-tuple-element.52.p0, f32[56,128]{1,0:T(8,128)S(1)} %collective-permute-done.13.p1, f32[56,128]{1,0:T(8,128)S(1)} %collective-permute-done.14.p2, f32[56,128]{1,0:T(8,128)S(1)} %collective-permute-done.15.p3, ...), custom_call_target="tpu_custom_call" | custom-call | tf_op jit(solution)/shard_map/pallas_call | solution.py:25
Async XLA Ops:
  12.2 16.1 %collective-permute-start.9 = (f32[352,384]{1,0:T(8,128)S(1)}, f32[352,384]{1,0:T(8,128)S(1)}, u32[]{:S(2)}, u32[]{:S(2)}) collective-permute-start(f32[352,384]{1,0:T(8,128)S(1)} %get-tuple-element.40.a0), channel_id=1, source_target_pairs={{0,2},{1,3},{2,0},{3,1},{4,6},{5,7},{6,4},{7,5},{8,10},{9,11},{10,... | collective-permute-start | bytes 1622024 | tf_op jit(solution)/shard_map/ppermute | solution.py:305
  15.3 15.5 %collective-permute-start.4 = (f32[48,768]{1,0:T(8,128)}, f32[48,768]{1,0:T(8,128)}, u32[]{:S(2)}, u32[]{:S(2)}) collective-permute-start(f32[48,768]{1,0:T(8,128)} %c0.1), channel_id=1, source_target_pairs={{0,2},{1,3},{2,0},{3,1},{4,6},{5,7},{6,4},{7,5},{8,10},{9,11},{10,... | collective-permute-start | bytes 442376 | tf_op jit(solution)/shard_map/ppermute | solution.py:305
  15.4 40.4 %collective-permute-start.8 = (f32[352,384]{1,0:T(8,128)S(1)}, f32[352,384]{1,0:T(8,128)}, u32[]{:S(2)}, u32[]{:S(2)}) collective-permute-start(f32[352,384]{1,0:T(8,128)S(1)} %get-tuple-element.40.a0), channel_id=1, source_target_pairs={{0,1},{1,0},{2,3},{3,2},{4,5},{5,4},{6,7},{7,6},{8,9},{9,8},{10,11... | collective-permute-start | bytes 1622024 | tf_op jit(solution)/shard_map/ppermute | solution.py:305
  28.4 27.4 %collective-permute-start.10 = (f32[352,384]{1,0:T(8,128)S(1)}, f32[352,384]{1,0:T(8,128)}, u32[]{:S(2)}, u32[]{:S(2)}) collective-permute-start(f32[352,384]{1,0:T(8,128)S(1)} %collective-permute-done.9.a2), channel_id=1, source_target_pairs={{0,1},{1,0},{2,3},{3,2},{4,5},{5,4},{6,7},{7,6},{8,9},{9,8},{10,11... | collective-permute-start | bytes 1622024 | tf_op jit(solution)/shard_map/ppermute | solution.py:305
  28.4 2.5 %collective-permute-start.3 = (f32[48,768]{1,0:T(8,128)}, f32[48,768]{1,0:T(8,128)}, u32[]{:S(2)}, u32[]{:S(2)}) collective-permute-start(f32[48,768]{1,0:T(8,128)} %c0.1), channel_id=1, source_target_pairs={{0,1},{1,0},{2,3},{3,2},{4,5},{5,4},{6,7},{7,6},{8,9},{9,8},{10,11... | collective-permute-start | bytes 442376 | tf_op jit(solution)/shard_map/ppermute | solution.py:305
  30.8 1.7 %collective-permute-start.5 = (f32[48,768]{1,0:T(8,128)}, f32[48,768]{1,0:T(8,128)}, u32[]{:S(2)}, u32[]{:S(2)}) collective-permute-start(f32[48,768]{1,0:T(8,128)} %collective-permute-done.4.c2), channel_id=1, source_target_pairs={{0,1},{1,0},{2,3},{3,2},{4,5},{5,4},{6,7},{7,6},{8,9},{9,8},{10,11... | collective-permute-start | bytes 442376 | tf_op jit(solution)/shard_map/ppermute | solution.py:305
  33.7 41.5 %collective-permute-start.7 = (f32[96,768]{1,0:T(8,128)S(1)}, f32[96,768]{1,0:T(8,128)S(1)}, u32[]{:S(2)}, u32[]{:S(2)}) collective-permute-start(f32[96,768]{1,0:T(8,128)S(1)} %get-tuple-element.39), channel_id=1, source_target_pairs={{0,12},{1,13},{2,14},{3,15},{4,0},{5,1},{6,2},{7,3},{8,4},{9,5},{1... | collective-permute-start | bytes 884744 | tf_op jit(solution)/shard_map/ppermute | solution.py:308
  37.6 1.1 copy-start
  46.8 1.7 %collective-permute-start = (f32[88,128]{1,0:T(8,128)S(1)}, f32[88,128]{1,0:T(8,128)S(1)}, u32[]{:S(2)}, u32[]{:S(2)}) collective-permute-start(f32[88,128]{1,0:T(8,128)S(1)} %get-tuple-element.33), channel_id=1, source_target_pairs={{0,1},{1,0},{2,3},{3,2},{4,5},{5,4},{6,7},{7,6},{8,9},{9,8},{10,11... | collective-permute-start | bytes 135176 | tf_op jit(solution)/shard_map/ppermute | solution.py:305
  46.9 4.1 %collective-permute-start.1 = (f32[88,128]{1,0:T(8,128)S(1)}, f32[88,128]{1,0:T(8,128)S(1)}, u32[]{:S(2)}, u32[]{:S(2)}) collective-permute-start(f32[88,128]{1,0:T(8,128)S(1)} %get-tuple-element.34), channel_id=1, source_target_pairs={{0,2},{1,3},{2,0},{3,1},{4,6},{5,7},{6,4},{7,5},{8,10},{9,11},{10,... | collective-permute-start | bytes 135176 | tf_op jit(solution)/shard_map/ppermute | solution.py:305
  48.4 26.8 %collective-permute-start.6 = (f32[48,768]{1,0:T(8,128)S(1)}, f32[48,768]{1,0:T(8,128)S(1)}, u32[]{:S(2)}, u32[]{:S(2)}) collective-permute-start(f32[48,768]{1,0:T(8,128)S(1)} %get-tuple-element.37), channel_id=1, source_target_pairs={{0,4},{1,5},{2,6},{3,7},{4,8},{5,9},{6,10},{7,11},{8,12},{9,13},{1... | collective-permute-start | bytes 442376 | tf_op jit(solution)/shard_map/ppermute | solution.py:308
  51.0 3.9 %collective-permute-start.2 = (f32[88,128]{1,0:T(8,128)S(1)}, f32[88,128]{1,0:T(8,128)S(1)}, u32[]{:S(2)}, u32[]{:S(2)}) collective-permute-start(f32[88,128]{1,0:T(8,128)S(1)} %get-tuple-element.35), channel_id=1, source_target_pairs={{0,3},{1,2},{2,1},{3,0},{4,7},{5,6},{6,5},{7,4},{8,11},{9,10},{10,... | collective-permute-start | bytes 135176 | tf_op jit(solution)/shard_map/ppermute | solution.py:305
  57.1 18.1 %collective-permute-start.11 = (f32[128,128]{1,0:T(8,128)S(1)}, f32[128,128]{1,0:T(8,128)S(1)}, u32[]{:S(2)}, u32[]{:S(2)}) collective-permute-start(f32[128,128]{1,0:T(8,128)S(1)} %get-tuple-element.41), channel_id=1, source_target_pairs={{0,4},{1,5},{2,6},{3,7},{4,8},{5,9},{6,10},{7,11},{8,12},{9,13},{1... | collective-permute-start | bytes 196616 | tf_op jit(solution)/shard_map/ppermute | solution.py:308
  57.1 18.1 %collective-permute-start.12 = (f32[128,128]{1,0:T(8,128)S(1)}, f32[128,128]{1,0:T(8,128)S(1)}, u32[]{:S(2)}, u32[]{:S(2)}) collective-permute-start(f32[128,128]{1,0:T(8,128)S(1)} %get-tuple-element.42), channel_id=1, source_target_pairs={{0,12},{1,13},{2,14},{3,15},{4,0},{5,1},{6,2},{7,3},{8,4},{9,5},{1... | collective-permute-start | bytes 196616 | tf_op jit(solution)/shard_map/ppermute | solution.py:308
  95.3 19.6 %collective-permute-start.16 = (f32[64,128]{1,0:T(8,128)S(1)}, f32[64,128]{1,0:T(8,128)S(1)}, u32[]{:S(2)}, u32[]{:S(2)}) collective-permute-start(f32[64,128]{1,0:T(8,128)S(1)} %get-tuple-element.57), channel_id=1, source_target_pairs={{0,1},{1,0},{2,3},{3,2},{4,5},{5,4},{6,7},{7,6},{8,9},{9,8},{10,11... | collective-permute-start | bytes 98312 | tf_op jit(solution)/shard_map/ppermute | solution.py:305
  95.3 20.7 %collective-permute-start.17 = (f32[64,128]{1,0:T(8,128)S(1)}, f32[64,128]{1,0:T(8,128)S(1)}, u32[]{:S(2)}, u32[]{:S(2)}) collective-permute-start(f32[64,128]{1,0:T(8,128)S(1)} %get-tuple-element.58), channel_id=1, source_target_pairs={{0,2},{1,3},{2,0},{3,1},{4,6},{5,7},{6,4},{7,5},{8,10},{9,11},{10,... | collective-permute-start | bytes 98312 | tf_op jit(solution)/shard_map/ppermute | solution.py:305
  96.0 20.0 %collective-permute-start.18 = (f32[64,128]{1,0:T(8,128)S(1)}, f32[64,128]{1,0:T(8,128)S(1)}, u32[]{:S(2)}, u32[]{:S(2)}) collective-permute-start(f32[64,128]{1,0:T(8,128)S(1)} %get-tuple-element.59), channel_id=1, source_target_pairs={{0,3},{1,2},{2,1},{3,0},{4,7},{5,6},{6,5},{7,4},{8,11},{9,10},{10,... | collective-permute-start | bytes 98312 | tf_op jit(solution)/shard_map/ppermute | solution.py:305
  114.1 3.3 %collective-permute-start.13 = (f32[56,128]{1,0:T(8,128)S(1)}, f32[56,128]{1,0:T(8,128)S(1)}, u32[]{:S(2)}, u32[]{:S(2)}) collective-permute-start(f32[56,128]{1,0:T(8,128)S(1)} %get-tuple-element.53), channel_id=1, source_target_pairs={{0,1},{1,0},{2,3},{3,2},{4,5},{5,4},{6,7},{7,6},{8,9},{9,8},{10,11... | collective-permute-start | bytes 86024 | tf_op jit(solution)/shard_map/ppermute | solution.py:305
  114.2 4.2 %collective-permute-start.14 = (f32[56,128]{1,0:T(8,128)S(1)}, f32[56,128]{1,0:T(8,128)S(1)}, u32[]{:S(2)}, u32[]{:S(2)}) collective-permute-start(f32[56,128]{1,0:T(8,128)S(1)} %get-tuple-element.54), channel_id=1, source_target_pairs={{0,2},{1,3},{2,0},{3,1},{4,6},{5,7},{6,4},{7,5},{8,10},{9,11},{10,... | collective-permute-start | bytes 86024 | tf_op jit(solution)/shard_map/ppermute | solution.py:305
  114.9 3.6 %collective-permute-start.15 = (f32[56,128]{1,0:T(8,128)S(1)}, f32[56,128]{1,0:T(8,128)S(1)}, u32[]{:S(2)}, u32[]{:S(2)}) collective-permute-start(f32[56,128]{1,0:T(8,128)S(1)} %get-tuple-element.55), channel_id=1, source_target_pairs={{0,3},{1,2},{2,1},{3,0},{4,7},{5,6},{6,5},{7,4},{8,11},{9,10},{10,... | collective-permute-start | bytes 86024 | tf_op jit(solution)/shard_map/ppermute | solution.py:305

commit v2 on v0

v2 whole, which is shorter than its diff:
```python
import functools

import jax
import jax.numpy as jnp
from jax import lax
from jax.experimental import pallas as pl
from jax.experimental.pallas import tpu as pltpu
from jax.sharding import PartitionSpec as P

ITERS = 3
DAMPING = 0.5
GROUP = 4
LANES = 128
BF16 = jnp.bfloat16
F32 = jnp.float32


def call(kernel, outs, args, smem=1, hbm=(), scratch=(), vmem=24):
    in_specs = [
        pl.BlockSpec(memory_space=pltpu.SMEM if i < smem else pltpu.HBM if i in hbm else pltpu.VMEM)
        for i in range(len(args))
    ]
    shapes = [o if isinstance(o[0], tuple) else (o, F32) for o in outs]
    return pl.pallas_call(
        kernel,
        out_shape=[jax.ShapeDtypeStruct(s, d) for s, d in shapes],
        in_specs=in_specs,
        out_specs=[pl.BlockSpec(memory_space=pltpu.VMEM)] * len(shapes),
        scratch_shapes=list(scratch),
        compiler_params=pltpu.CompilerParams(vmem_limit_bytes=vmem * 1024 * 1024),
    )(*args)


def halves(x):
    high = x.astype(BF16)
    return high, (x - high.astype(F32)).astype(BF16)


def dot(a, b):
    return jnp.dot(a, b, preferred_element_type=F32)


def product(a, b):
    ah, al = halves(a)
    bh, bl = halves(b)
    n = b.shape[1]
    both = dot(ah, jnp.concatenate([bh, bl], axis=1))
    return both[:, :n] + both[:, n:] + dot(al, bh)


def lane_block(rows):
    return lax.broadcasted_iota(jnp.int32, (rows, LANES), 1) // (LANES // GROUP)


def turned(x, blocks):
    width = LANES // GROUP
    if isinstance(blocks, int):
        shift = (blocks % GROUP) * width
        return x if shift == 0 else pltpu.roll(x, shift, 1)
    return pltpu.roll(x, lax.rem(blocks + 2 * GROUP, GROUP) * width, 1)


def cut(x, member, out_refs):
    rows = x.shape[0] // GROUP
    block = lane_block(rows)
    parts = [x[q * rows:(q + 1) * rows] for q in range(GROUP)]
    for k, out in enumerate(out_refs):
        to = member ^ k
        packed = jnp.zeros((rows, LANES), F32)
        for q in range(GROUP):
            packed = jnp.where(block == q, turned(parts[q], q - to), packed)
        out[...] = packed


def joined(pieces, member):
    rows = pieces[0].shape[0]
    block = lane_block(rows)
    out = []
    for q in range(GROUP):
        part = jnp.zeros((rows, LANES), F32)
        for k, piece in enumerate(pieces):
            came = member ^ k
            part = jnp.where(block == came, turned(piece, came - q), part)
        out.append(part)
    return jnp.concatenate(out, axis=0)


def packed(x, chunk):
    first = lane_block(chunk) == 0
    out = None
    for q in range(x.shape[0] // chunk):
        part = turned(jnp.where(first, x[q * chunk:(q + 1) * chunk], 0.0), q)
        out = part if out is None else out + part
    return out


def unpacked(x, count):
    return jnp.concatenate([turned(x, -q) for q in range(count)], axis=0)


def chunk_of(owned):
    return -(-owned // (GROUP * 8)) * 8


def stacked(x):
    return jnp.concatenate(halves(x), axis=0)


def beside(x):
    return jnp.concatenate(halves(x), axis=1)


def combined(p, n):
    m = p.shape[0] // 2
    return p[:m, :n] + p[:m, n:] + p[m:, :n]


def payload(c, out):
    owned = c.shape[0] // 2
    below = turned(c[owned:], 1)
    out[:owned] = c[:owned] + jnp.where(lane_block(owned) == 0, 0.0, below)
    out[owned:] = packed(below, chunk_of(owned))


def fetch(source, count, rows, target, places, sem):
    def one(j, carry):
        pltpu.make_async_copy(source.at[pl.ds(rows(j), 1)], target.at[pl.ds(places(j), 1)], sem).start()
        return carry

    lax.fori_loop(0, count, one, 0, unroll=8)


def rows_kernel(pos, face, prim, slot, k_ref, f_ref, facev, primv, slotv, *rest):
    pieces, (ks, near, edge, right_side, sem) = rest[:GROUP], rest[GROUP:]
    width, count, order, columns = face.shape[1], prim.shape[1], ks.shape[1], f_ref.shape[1]
    side = 2 * width
    fetch(k_ref, prim.shape[1], lambda j: prim[0, j], ks, lambda j: side + slot[0, j], sem)
    fetch(k_ref, side, lambda j: face[j // width, j % width], ks, lambda j: j, sem)
    def indicator(row):
        place = lax.broadcasted_iota(jnp.int32, (order, row.shape[1]), 0).astype(F32)
        return jnp.where(place == row, 1.0, 0.0).astype(BF16)

    slots = jnp.broadcast_to(slotv[...].astype(F32), (count, count)).T
    prims = jnp.broadcast_to(primv[...].astype(F32), (count, count)).T
    wanted = lax.broadcasted_iota(jnp.int32, (count, count), 1).astype(F32)
    by_slot = jnp.sum(jnp.where(slots == wanted, prims, 0.0), axis=0, keepdims=True)
    right_side[:, :width] = indicator(facev[0:1].astype(F32))
    right_side[:, width:side] = indicator(facev[1:2].astype(F32))
    right_side[:, side:side + count] = indicator(by_slot)
    right_side[:, side + count:side + width] = jnp.zeros((order, width - count), BF16)
    right_side[:, side + width:] = beside(f_ref[...])
    pltpu.make_async_copy(k_ref.at[pl.ds(0, ks.shape[0])], ks, sem).wait()
    cut(combined(dot(stacked(ks[...]), right_side[:, side + width:]), columns), pos[0], pieces)

    def picked(rows, columns):
        high, low = halves(ks[rows])
        return dot(high, right_side[:, columns]) + dot(low, right_side[:, columns])

    cross = picked(slice(0, side), slice(side, side + width))
    near[:side] = cross
    edge[...] = jnp.where(pos[0] == GROUP - 1, cross[width:], cross[:width])
    own = picked(slice(side, side + count), slice(0, side))
    near[side:side + count] = own[:, :width]
    near[side + count:] = own[:, width:]


def far_kernel(pos, ks, right_side, far):
    side = far.shape[1]
    high, low = halves(ks[:side])
    far[...] = dot(high, right_side[:, :side]) + dot(low, right_side[:, :side])


def sweep_kernel(first, pos, right_side, k_ref, u_ref, ks_ref):
    rows, columns = u_ref.shape
    at = right_side.shape[1] - 2 * columns
    high, low = halves(k_ref[first:first + rows])
    both = dot(high, right_side[...])
    part = dot(low, right_side[:, :at + columns])
    u_ref[...] = both[:, at:at + columns] + both[:, at + columns:] + part[:, at:]
    ks_ref[...] = both[:, :at] + part[:, :at]


GOT = (-1, None, 5, 4)
GOT_NEXT = (5, 4, -1, None)


def solver_kernel(pos, mine, next_mine, got, next_got, theirs, out):
    owned = mine.shape[0]
    half = out.shape[0] // 2
    other = [theirs[i * owned:(i + 1) * owned] for i in range(4)]
    for m in range(GROUP):

        @pl.when(pos[0] == m)
        def _():
            p = m ^ 1
            held = [(m, mine[...]), (m ^ 2, next_mine[...]), (GOT[m], got[...]), (GOT_NEXT[m], next_got[...])]
            held += list(zip((p, p ^ 2, GOT[p], GOT_NEXT[p]), other))
            for block, values in held:
                if block is not None:
                    at = (block + 1) * owned
                    high, low = halves(values)
                    out[at:at + owned] = high
                    out[half + at:half + at + owned] = low


def blocks_kernel(width, pos, n0, n2, came, came_next, theirs, cross, own, edge_up, edge_down):
    side, size = 2 * width, n0.shape[0]
    count = (size - side) // 2
    other = [theirs[:size], theirs[size:2 * size], theirs[2 * size:2 * size + width], theirs[2 * size + width:]]
    for k, values in enumerate((n0[...], other[0], n2[...], other[1])):
        cross[:, k * width:(k + 1) * width] = stacked(values[:side])
        own[:, k * side:k * side + width] = stacked(values[side:side + count])
        own[:, k * side + width:(k + 1) * side] = stacked(values[side + count:])
    for m in range(GROUP):

        @pl.when(pos[0] == m)
        def _():
            held = {GOT[m]: came, GOT_NEXT[m]: came_next}
            for block, values in zip((GOT[m ^ 1], GOT_NEXT[m ^ 1]), other[2:]):
                held.setdefault(block, values)
            edge_up[...] = stacked(held[-1][...])
            edge_down[...] = stacked(held[4][...])


def spans_kernel(pos, n0, n1, n2, n3, out):
    side = n0.shape[1]
    for k, ref in enumerate((n0, n1, n2, n3)):
        out[:, k * side:(k + 1) * side] = stacked(ref[...])


def halos(v, up, down):
    width = v.shape[0] // 2
    down[...] = packed(v[:width], width // GROUP)
    up[...] = packed(turned(v[width:], 1), width // GROUP)


def start_kernel(pos, p0, p1, p2, p3, c_ref, v_ref, pay_ref, pay_up, pay_down):
    v = joined([p0[...], p1[...], p2[...], p3[...]], pos[0])
    side = v_ref.shape[0]
    v_ref[...] = v[:side]
    c_ref[...] = v[side:]
    payload(v[side:], pay_ref)
    size = pay_ref.shape[0]
    pay_up[:size] = pay_ref[...]
    pay_down[:size] = pay_ref[...]
    halos(v[:side], pay_up.at[size:], pay_down.at[size:])


def shared(x, member):
    block = lane_block(x.shape[0])
    high, low = halves(x)
    high, low = high.astype(F32), low.astype(F32)
    out = []
    for k in range(GROUP):
        mine = block == (member ^ k)
        pair = [jnp.where(mine, half, 0.0).astype(BF16) for half in (high, low)]
        out.append(jnp.concatenate(pair, axis=1))
    return jnp.concatenate(out, axis=0)


def again_kernel(pos, far, v0, left, right, v_ref, up, down):
    lam = jnp.concatenate([left[...], -right[...]], axis=0)
    v = v0[...] + combined(dot(far[...], shared(lam, pos[0])), LANES)
    v_ref[...] = v
    halos(v, up, down)


def turn_kernel(kind, groups, pos, *refs):
    pays, refs = refs[:groups], refs[groups:]
    solver, cross, own, edge_up, edge_down, c0, faces_ref = refs[:7]
    refs = refs[7:]
    size = pays[0].shape[0]
    if kind == "first":
        halo_up, halo_down = pays[1].at[size:], pays[groups - 1].at[size:]
    else:
        (halo_up, halo_down), refs = refs[:2], refs[2:]
    if kind != "first":
        left_ref, right_ref = refs[:2]
        refs = refs[2:]
    outs, stack = refs[:-1], refs[-1]
    member, group = pos[0], pos[1]
    owned, width = c0.shape[0] // 2, faces_ref.shape[0] // 2
    first = lane_block(owned) == 0

    for k in range(groups):
        h = lax.rem(group - k + groups, groups)
        extra = unpacked(pays[(k + 1) % groups][owned:size, :], -(-owned // chunk_of(owned)))[:owned]
        whole = pays[k][:owned, :] + jnp.where(first, extra, 0.0)
        for i in range(GROUP):
            place = pl.multiple_of((h * GROUP + i) * owned, 16)
            stack[pl.ds(place, owned), :] = beside(turned(whole, -i))

    w = combined(dot(solver[...], stack[...]), LANES)
    pair = lane_block(2 * owned)
    q = jnp.zeros((2 * owned, LANES), F32)
    for i in range(GROUP):
        q = jnp.where(pair == i, turned(w[(i + 1) * owned:(i + 3) * owned], i), q)
    filler = jnp.zeros((width - 2 * owned, LANES), F32)

    def padded(x):
        return jnp.concatenate([x, filler], axis=0)

    faces = faces_ref[...] - combined(dot(cross[...], shared(padded(q), member)), LANES)
    left, right = faces[:width], faces[width:]
    before, after = beside(padded(w[:2 * owned])), beside(padded(w[(GROUP + 1) * owned:]))
    right_before = unpacked(halo_up[...], GROUP) - combined(dot(edge_up[...], before), LANES)
    left_after = unpacked(halo_down[...], GROUP) - combined(dot(edge_down[...], after), LANES)
    block = lane_block(width)
    beyond = jnp.where(block == GROUP - 1, turned(left_after, GROUP - 1), turned(left, -1))
    behind = jnp.where(block == 0, right_before, turned(right, 1))
    lam_right = DAMPING * (right - beyond)
    lam_left = DAMPING * (behind - left)
    if kind != "first":
        lam_right = lam_right + right_ref[...]
        lam_left = lam_left + left_ref[...]
    if kind == "last":
        cut(jnp.concatenate([q, lam_right], axis=0), member, outs)
        return
    left_out, right_out, pay_ref = outs[:3]
    left_out[...] = lam_left
    right_out[...] = lam_right
    lam = jnp.concatenate([lam_left, -lam_right], axis=0)
    payload(c0[...] + combined(dot(own[...], shared(lam, member)), LANES), pay_ref)
    if kind == "middle":
        cut(jnp.concatenate([lam_left, lam_right], axis=0), member, outs[3:])


def spread_kernel(parts, pos, p0, p1, p2, p3, *refs):
    lam = joined([p0[...], p1[...], p2[...], p3[...]], pos[0])
    side = lam.shape[0]
    rows = lax.broadcasted_iota(jnp.int32, lam.shape, 0)
    lam = beside(jnp.where(rows < side // 2, lam, -lam))
    us, kss, out = refs[:parts], refs[parts:2 * parts], refs[2 * parts]
    at = 0
    for u, ks in zip(us, kss):
        out[at:at + u.shape[0]] = u[...] + combined(dot(stacked(ks[:, :side]), lam), LANES)
        at += u.shape[0]


def final_kernel(parts, owned, pos, p0, p1, p2, p3, u_ref, *refs):
    x = joined([p0[...], p1[...], p2[...], p3[...]], pos[0])
    kss, (out, lam_ref) = refs[:parts], refs[parts:]
    lam_ref[...] = x[2 * owned:]
    width = lam_ref.shape[0]
    q = beside(jnp.concatenate([x[:2 * owned], jnp.zeros((width - 2 * owned, LANES), F32)], axis=0))
    at = 0
    for ks in kss:
        rows = slice(at, at + ks.shape[0])
        out[rows] = u_ref[rows] - combined(dot(stacked(ks[:, 2 * width:]), q), LANES)
        at += ks.shape[0]


def local(condensed, eigen_loads, coarse_inverse, face_rows, primal_rows, primal_slot):
    order, columns = eigen_loads.shape
    owned, coarse = coarse_inverse.shape
    width = face_rows.shape[2]
    side, count = 2 * width, 2 * owned
    kept = side + count
    total = lax.axis_size("sub")
    groups = total // GROUP
    me = lax.axis_index("sub")
    pos = jnp.stack([me % GROUP, me // GROUP]).astype(jnp.int32)
    faces = face_rows[0]

    def mate(x, k):
        return lax.ppermute(x, "sub", [(s, s ^ k) for s in range(total)])

    def planes(x, by):
        return lax.ppermute(x, "sub", [(s, (s + by * GROUP) % total) for s in range(total)])

    def traded(pieces):
        return [pieces[0]] + [mate(pieces[k], k) for k in range(1, GROUP)]

    def after(x, other):
        return lax.optimization_barrier((x, other))[0]

    def crossing(pairs):
        return [(g * GROUP + a, (g * GROUP + b) % total) for g in range(groups) for a, b in pairs]

    ends = crossing([(GROUP - 1, GROUP), (0, -1), (1, -2)])
    ends_next = crossing([(GROUP - 1, GROUP + 2), (0, -3), (1, -4)])
    got = lax.ppermute(coarse_inverse, "sub", ends)
    got_next = lax.ppermute(coarse_inverse, "sub", ends_next)
    c_next = mate(coarse_inverse, 2)

    *pieces, ks, near, edge, right_side = call(
        rows_kernel,
        [(kept // GROUP, LANES)] * GROUP
        + [(kept, order), (side + 2 * count, width), (width, width), ((order, side + width + 2 * columns), BF16)],
        (pos, faces, primal_rows, primal_slot, condensed, eigen_loads, faces, primal_rows, primal_slot),
        smem=4,
        hbm=(4,),
        scratch=[pltpu.SemaphoreType.DMA],
        vmem=52,
    )
    parts = 4 if order % 64 == 0 else 1
    block = order // parts

    def swept(part, right_side):
        return call(
            functools.partial(sweep_kernel, part * block),
            [(block, columns), (block, side + width)],
            (pos, right_side, condensed),
        )

    *pieces, got, got_next, c_next = lax.optimization_barrier((*pieces, got, got_next, c_next))
    pieces = traded(pieces)
    near_next = mate(near, 2)
    came = lax.ppermute(edge, "sub", ends)
    sweeps = [swept(0, right_side)]
    pieces[0] = after(pieces[0], sweeps[0])
    small = (width // GROUP, LANES)
    pay_rows = owned + chunk_of(owned)
    c0, v0, pay, pay_up, pay_down = call(
        start_kernel,
        [(count, LANES), (side, LANES), (pay_rows, LANES)] + [(pay_rows + width // GROUP, LANES)] * 2,
        (pos, *pieces),
    )
    came_next = mate(after(came, pay), 2)
    for part in range(1, parts):
        sweeps.append(swept(part, after(right_side, (pay, sweeps[-1]))))
    arrived = [planes(pay_up, 1)] + [planes(pay, k) for k in range(2, groups - 1)] + [planes(pay_down, -1)]
    near_late, near_next, came_late, came_next, got, got_next, c_next, arrived, _ = lax.optimization_barrier(
        (near, near_next, came, came_next, got, got_next, c_next, arrived, sweeps[-2])
    )
    theirs_c = mate(jnp.concatenate([coarse_inverse, c_next, got, got_next], axis=0), 1)
    theirs = mate(jnp.concatenate([near_late, near_next, came_late, came_next], axis=0), 1)
    us, kss = [x[0] for x in sweeps], [x[1] for x in sweeps]
    (solver,) = call(
        solver_kernel,
        [((2 * (GROUP + 3) * owned, coarse), BF16)],
        (pos, coarse_inverse, c_next, got, got_next, theirs_c),
    )
    cross, own, edge_up, edge_down = call(
        functools.partial(blocks_kernel, width),
        [((2 * side, GROUP * width), BF16), ((2 * count, GROUP * side), BF16)] + [((side, width), BF16)] * 2,
        (pos, near, near_next, came, came_next, theirs),
    )
    (far,) = call(far_kernel, [(side, side)], (pos, after(ks, sweeps[1]), right_side))
    far_next = mate(after(far, near_next), 2)

    now, state, sides = v0, (), []
    for step in range(ITERS):
        kind = "first" if step == 0 else "last" if step == ITERS - 1 else "middle"
        if kind == "first":
            pays = [after(pay, sweeps), *arrived]
        else:
            pays = [pay] + [planes(pay, k) for k in range(1, groups)]
            sides = [planes(up, 1), planes(down, -1)]
        if step == ITERS - 1:
            lam_pieces = traded(lax.optimization_barrier((*lam_pieces, *sides))[:GROUP])
        shapes = [(width, LANES), (width, LANES), (pay_rows, LANES)]
        if kind == "middle":
            shapes = shapes + [(side // GROUP, LANES)] * GROUP
        if kind == "last":
            shapes = [((count + width) // GROUP, LANES)] * GROUP
        outs = call(
            functools.partial(turn_kernel, kind, groups),
            shapes,
            (pos, *pays, solver, cross, own, edge_up, edge_down, c0, now, *sides, *state),
            scratch=[pltpu.VMEM((coarse, 2 * LANES), BF16)],
        )
        if kind == "first":
            (far_all,) = call(
                spans_kernel,
                [((2 * side, GROUP * side), BF16)],
                (pos, far, mate(far, 1), far_next, mate(far_next, 1)),
            )
        if kind != "last":
            state, pay = outs[:2], outs[2]
            now, up, down = call(again_kernel, [(side, LANES), small, small], (pos, far_all, v0, *state))
        if kind == "middle":
            lam_pieces = outs[3:]
    (spread,) = call(
        functools.partial(spread_kernel, parts),
        [(order, columns)],
        (pos, *lam_pieces, *us, *kss),
    )
    displaced, multipliers = call(
        functools.partial(final_kernel, parts, owned),
        [(order, columns), (width, columns)],
        (pos, *traded(outs), spread, *kss),
    )
    return displaced, multipliers


def solution(mesh):
    placed = (
        P(("rve", "sub"), None),
        P(("rve", "sub"), None),
        P(("rve", "sub"), None),
        P("sub", None, None),
        P("sub", None),
        P("sub", None),
    )
    return jax.shard_map(
        local,
        mesh=mesh,
        in_specs=placed,
        out_specs=(P(("rve", "sub"), None), P(("rve", "sub"), None)),
        check_vma=False,
    )
```

time: 173 us -> 98 us (0.57)
  blocking collectives: 64.8 us -> 0 us
  matrix products: 36.7 us -> 0 us
  Pallas kernels: 0 us -> 34.7 us
  starting transfers between devices: 15.8 us -> 43.4 us
  local copies, waits for them, and re-layouts: 27.5 us -> 5.34 us
  other arithmetic: 12.5 us -> 0.16 us
    all_gather x3 -> x0, blocking collectives: 64.8 us -> none  [local(): piece = lax.all_gather(slotted, 'sub', axis=0, tiled=True)]
    dot_general x12 -> x0, matrix products: 36.7 us -> none  [the longest x3 31.3 us: local(): jnp.dot(condensed, loads, precision=lax.Precision.HIGHEST, preferred_elem...]
    pallas_call x0 -> x17, Pallas kernels: none -> 34.7 us  [call(): pl.pallas_call(kernel, out_shape=[jax.ShapeDtypeStruct(s, d) for s, d in...]
    ppermute x8 -> x33, starting transfers between devices: 15.8 us -> 43.4 us  [the longest x13 18.9 us: planes(): lax.ppermute(x, 'sub', [(s, (s + by * GROUP) % total) for s in range(tota...]
    gather x10 -> x0, local copies, waits for them, and re-layouts: 10.5 us -> none  [the longest x1 4.76 us: local(): prolong = condensed[:, prim_rows]]
    scatter-add x6 -> x0, other arithmetic: 9.69 us -> none  [local(): eigen_loads.at[right_rows].add(-multipliers).at[left_rows].add(previous)]
    unnamed x9 -> x18, local copies, waits for them, and re-layouts: 11.1 us -> 5.34 us
    scatter x3 -> x0, local copies, waits for them, and re-layouts: 3.3 us -> none  [local(): jnp.zeros((2 * owned, columns), jnp.float32).at[slots]]
  transfers between devices with their start and end apart: 8 -> 33, of which waited for: 7 -> 7; matrix products, arithmetic and copies ran while one was open for 11% -> 0% of each run, Pallas kernels for 0% -> 30%
where the time goes in v2:
time: 98 us; the launch traced here: 97.6 us
  starting transfers between devices  43.4 us (44%)
  Pallas kernels  34.7 us (35%)
  waiting for transfers between devices  13.1 us (13%)
  local copies, waits for them, and re-layouts  5.34 us (5%)
  between operations  0.99 us (1%)
    pallas_call x17, Pallas kernels, call(): pl.pallas_call(kernel, out_shape=[jax.ShapeDtypeStruct(s, d) for s, d in...  34.7 us
    ppermute x13, starting transfers between devices, planes(): lax.ppermute(x, 'sub', [(s, (s + by * GROUP) % total) for s in range(tota...  18.9 us
    ppermute x17, starting transfers between devices, mate(): return lax.ppermute(x, 'sub', [(s, s ^ k) for s in range(total)])  11.6 us
    ppermute x17, waiting for transfers between devices, mate(): return lax.ppermute(x, 'sub', [(s, s ^ k) for s in range(total)])  7.91 us
    ppermute x1, starting transfers between devices, local(): came = lax.ppermute(edge, 'sub', ends)  6.09 us
    unnamed x18, local copies, waits for them, and re-layouts  5.34 us
    ppermute x13, waiting for transfers between devices, planes(): lax.ppermute(x, 'sub', [(s, (s + by * GROUP) % total) for s in range(tota...  5.16 us
    ppermute x1, starting transfers between devices, local(): got_next = lax.ppermute(coarse_inverse, 'sub', ends_next)  4.66 us
  transfers between devices with their start and end apart: 33, of which 7 were waited for; matrix products, arithmetic and copies ran while one was open for 0% of the time, Pallas kernels for 30%

profile of v2, /device:TPU:0, one launch (start us, length us, event | category | flops | bytes accessed | tf_op | source)
XLA Modules:
  0.0 97.6 jit_solution(15745223520562478256)
XLA Ops:
  0.6 3.0 %collective-permute-start.2 = (f32[48,768]{1,0:T(8,128)}, f32[48,768]{1,0:T(8,128)S(1)}, u32[]{:S(2)}, u32[]{:S(2)}) collective-permute-start(f32[48,768]{1,0:T(8,128)} %mine.1), channel_id=1, source_target_pairs={{0,2},{1,3},{2,0},{3,1},{4,6},{5,7},{6,4},{7,5},{8,10},{9,11},{10,... | collective-permute-start | bytes 442376 | tf_op jit(solution)/shard_map/ppermute | solution.py:366
  3.7 4.7 %collective-permute-start.1 = (f32[48,768]{1,0:T(8,128)}, f32[48,768]{1,0:T(8,128)S(1)}, u32[]{:S(2)}, u32[]{:S(2)}) collective-permute-start(f32[48,768]{1,0:T(8,128)} %mine.1), channel_id=1, source_target_pairs={{3,6},{0,13},{1,12},{7,10},{4,1},{5,0},{11,14},{8,5},{9,4},{15,2},... | collective-permute-start | bytes 442376 | tf_op jit(solution)/shard_map/ppermute | solution.py:383
  8.3 2.2 %collective-permute-start = (f32[48,768]{1,0:T(8,128)}, f32[48,768]{1,0:T(8,128)S(1)}, u32[]{:S(2)}, u32[]{:S(2)}) collective-permute-start(f32[48,768]{1,0:T(8,128)} %mine.1), channel_id=1, source_target_pairs={{3,4},{0,15},{1,14},{7,8},{4,3},{5,2},{11,12},{8,7},{9,6},{15,0},{... | collective-permute-start | bytes 442376 | tf_op jit(solution)/shard_map/ppermute | solution.py:382
  10.5 0.1 pad_add_fusion.pos
  10.6 1.1 %copy-done.4 = f32[1536,128]{1,0:T(8,128)S(1)} copy-done((f32[1536,128]{1,0:T(8,128)S(1)}, f32[1536,128]{1,0:T(8,128)}, u32[]{:S(2)}) %copy-start.4) | copy-done | bytes 786456
  11.7 0.7 copy-done.6
  12.4 0.7 copy-done.7
  13.1 0.7 copy-done.8
  13.7 8.3 %shard_map.77 = (f32[88,128]{1,0:T(8,128)S(1)}, f32[88,128]{1,0:T(8,128)S(1)}, f32[88,128]{1,0:T(8,128)S(1)}, f32[88,128]{1,0:T(8,128)S(1)}, f32[352,1536]{1,0:T...) custom-call(s32[2]{0:T(128)S(1)} %pad_add_fusion.pos, s32[2,128]{1,0:T(2,128)S(1)} %bitcast.3, ...), custom_call_target="tpu_custom_call" | custom-call | tf_op jit(solution)/shard_map/pallas_call | solution.py:24
  22.0 0.1 collective-permute-start.6
  22.1 6.1 %collective-permute-start.7 = (f32[128,128]{1,0:T(8,128)S(1)}, f32[128,128]{1,0:T(8,128)S(1)}, u32[]{:S(2)}, u32[]{:S(2)}) collective-permute-start(f32[128,128]{1,0:T(8,128)S(1)} %get-tuple-element.100), channel_id=1, source_target_pairs={{3,4},{0,15},{1,14},{7,8},{4,3},{5,2},{11,12},{8,7},{9,6},{15,0},{... | collective-permute-start | bytes 196616 | tf_op jit(solution)/shard_map/ppermute | solution.py:409
  28.2 0.0 collective-permute-done.2.next_mine
  28.2 0.1 collective-permute-start.3
  28.3 0.1 collective-permute-start.4
  28.4 1.8 %collective-permute-start.5 = (f32[88,128]{1,0:T(8,128)S(1)}, f32[88,128]{1,0:T(8,128)S(1)}, u32[]{:S(2)}, u32[]{:S(2)}) collective-permute-start(f32[88,128]{1,0:T(8,128)S(1)} %get-tuple-element.87), channel_id=1, source_target_pairs={{0,3},{1,2},{2,1},{3,0},{4,7},{5,6},{6,5},{7,4},{8,11},{9,10},{10,... | collective-permute-start | bytes 135176 | tf_op jit(solution)/shard_map/ppermute | solution.py:366
  30.2 1.5 %copy-done.1 = bf16[1536,640]{1,0:T(8,128)(2,1)S(1)} copy-done((bf16[1536,640]{1,0:T(8,128)(2,1)S(1)}, bf16[1536,640]{1,0:T(8,128)(2,1)}, u32[]{:S(2)}) %copy-start.1) | copy-done | bytes 1966104
  31.7 2.3 %shard_map.78 = (f32[384,128]{1,0:T(8,128)S(1)}, f32[384,384]{1,0:T(8,128)S(1)}) custom-call(s32[2]{0:T(128)S(1)} %pad_add_fusion.pos, bf16[1536,640]{1,0:T(8,128)(2,1)S(1)} %copy-done.1, f32[1536,1536]{1,0:T(8,128)S(1)} %copy-done), custom_call_target="tpu_custom_call" | custom-call | tf_op jit(solution)/shard_map/pallas_call | solution.py:24
  34.1 0.0 collective-permute-done.4.p2
  34.1 0.0 collective-permute-done.5.p3
  34.1 0.9 shard_map.79
  35.0 0.0 collective-permute-done.7.came
  35.0 0.4 collective-permute-start.8
  35.4 0.0 collective-permute-start.9
  35.4 3.8 %collective-permute-start.11 = (f32[96,128]{1,0:T(8,128)S(1)}, f32[96,128]{1,0:T(8,128)S(1)}, u32[]{:S(2)}, u32[]{:S(2)}) collective-permute-start(f32[96,128]{1,0:T(8,128)S(1)} %get-tuple-element.106), channel_id=1, source_target_pairs={{0,12},{1,13},{2,14},{3,15},{4,0},{5,1},{6,2},{7,3},{8,4},{9,5},{1... | collective-permute-start | bytes 147464 | tf_op jit(solution)/shard_map/ppermute | solution.py:369
  39.2 2.3 %shard_map.80 = (f32[384,128]{1,0:T(8,128)S(1)}, f32[384,384]{1,0:T(8,128)S(1)}) custom-call(s32[2]{0:T(128)S(1)} %pad_add_fusion.pos, bf16[1536,640]{1,0:T(8,128)(2,1)S(1)} %copy-done.2, f32[1536,1536]{1,0:T(8,128)S(1)} %copy-done), custom_call_target="tpu_custom_call" | custom-call | tf_op jit(solution)/shard_map/pallas_call | solution.py:24
  41.5 0.0 copy-start.5
  41.5 2.3 %shard_map.81 = (f32[384,128]{1,0:T(8,128)S(1)}, f32[384,384]{1,0:T(8,128)S(1)}) custom-call(s32[2]{0:T(128)S(1)} %pad_add_fusion.pos, bf16[1536,640]{1,0:T(8,128)(2,1)S(1)} %copy-done.2, f32[1536,1536]{1,0:T(8,128)S(1)} %copy-done), custom_call_target="tpu_custom_call" | custom-call | tf_op jit(solution)/shard_map/pallas_call | solution.py:24
  43.8 0.2 collective-permute-done.10.refs_2_
  44.1 0.1 collective-permute-start.12
  44.2 0.6 collective-permute-start.13
  44.8 0.7 copy-done.3
  45.4 1.1 %shard_map.86.n0 = f32[256,256]{1,0:T(8,128)S(1)} custom-call(s32[2]{0:T(128)S(1)} %pad_add_fusion.pos, f32[352,1536]{1,0:T(8,128)S(1)} %copy-done.3, bf16[1536,640]{1,0:T(8,128)(2,1)S(1)} %copy-done.2), custom_call_target="tpu_custom_call" | custom-call | tf_op jit(solution)/shard_map/pallas_call | solution.py:24
  46.6 1.8 %collective-permute-start.18 = (f32[256,256]{1,0:T(8,128)S(1)}, f32[256,256]{1,0:T(8,128)S(1)}, u32[]{:S(2)}, u32[]{:S(2)}) collective-permute-start(f32[256,256]{1,0:T(8,128)S(1)} %shard_map.86.n0), channel_id=1, source_target_pairs={{0,2},{1,3},{2,0},{3,1},{4,6},{5,7},{6,4},{7,5},{8,10},{9,11},{10,... | collective-permute-start | bytes 786440 | tf_op jit(solution)/shard_map/ppermute | solution.py:366
  48.4 6.0 %collective-permute-done.18.n2 = f32[256,256]{1,0:T(8,128)S(1)} collective-permute-done((f32[256,256]{1,0:T(8,128)S(1)}, f32[256,256]{1,0:T(8,128)S(1)}, u32[]{:S(2)}, u32[]{:S(2)}) %collective-permute-start.18) | collective-permute-done | bytes 262176 | tf_op jit(solution)/shard_map/ppermute | solution.py:366
  54.4 2.3 %shard_map.82 = (f32[384,128]{1,0:T(8,128)S(1)}, f32[384,384]{1,0:T(8,128)S(1)}) custom-call(s32[2]{0:T(128)S(1)} %pad_add_fusion.pos, bf16[1536,640]{1,0:T(8,128)(2,1)S(1)} %copy-done.2, f32[1536,1536]{1,0:T(8,128)S(1)} %copy-done), custom_call_target="tpu_custom_call" | custom-call | tf_op jit(solution)/shard_map/pallas_call | solution.py:24
  56.7 0.7 shard_map.83.refs_4_
  57.4 0.9 shard_map.84
  58.4 2.5 %shard_map.85 = (f32[128,128]{1,0:T(8,128)S(1)}, f32[128,128]{1,0:T(8,128)S(1)}, f32[64,128]{1,0:T(8,128)S(1)}) custom-call(s32[2]{0:T(128)S(1)} %pad_add_fusion.pos, f32[64,128]{1,0:T(8,128)S(1)} %get-tuple-element.98.refs_0_, f32[96,128]{1,0:T(8,128)S(1)} %collective-permute-done.9.refs_1_, f32[64,128]{1,0:T(8,128)S(1)} %collective-permute-done.10.refs_2_, ...), custom_call_target="tpu_custom_call" | custom-call | tf_op jit(solution)/shard_map/pallas_call | solution.py:24
  60.9 1.4 %collective-permute-start.16 = (f32[64,128]{1,0:T(8,128)S(1)}, f32[64,128]{1,0:T(8,128)S(1)}, u32[]{:S(2)}, u32[]{:S(2)}) collective-permute-start(f32[64,128]{1,0:T(8,128)S(1)} %get-tuple-element.123.refs_0_), channel_id=1, source_target_pairs={{0,12},{1,13},{2,14},{3,15},{4,0},{5,1},{6,2},{7,3},{8,4},{9,5},{1... | collective-permute-start | bytes 98312 | tf_op jit(solution)/shard_map/ppermute | solution.py:369
  62.3 1.4 %collective-permute-start.15 = (f32[64,128]{1,0:T(8,128)S(1)}, f32[64,128]{1,0:T(8,128)S(1)}, u32[]{:S(2)}, u32[]{:S(2)}) collective-permute-start(f32[64,128]{1,0:T(8,128)S(1)} %get-tuple-element.123.refs_0_), channel_id=1, source_target_pairs={{0,8},{1,9},{2,10},{3,11},{4,12},{5,13},{6,14},{7,15},{8,0},{9,1},... | collective-permute-start | bytes 98312 | tf_op jit(solution)/shard_map/ppermute | solution.py:369
  63.6 2.0 %collective-permute-start.14 = (f32[64,128]{1,0:T(8,128)S(1)}, f32[64,128]{1,0:T(8,128)S(1)}, u32[]{:S(2)}, u32[]{:S(2)}) collective-permute-start(f32[64,128]{1,0:T(8,128)S(1)} %get-tuple-element.123.refs_0_), channel_id=1, source_target_pairs={{0,4},{1,5},{2,6},{3,7},{4,8},{5,9},{6,10},{7,11},{8,12},{9,13},{1... | collective-permute-start | bytes 98312 | tf_op jit(solution)/shard_map/ppermute | solution.py:369
  65.6 0.7 shard_map.87.far
  66.3 1.1 %shard_map.88 = (f32[256,128]{1,0:T(8,128)S(1)}, f32[32,128]{1,0:T(8,128)S(1)}, f32[32,128]{1,0:T(8,128)S(1)}) custom-call(s32[2]{0:T(128)S(1)} %pad_add_fusion.pos, bf16[512,1024]{1,0:T(8,128)(2,1)S(1)} %shard_map.87.far, f32[256,128]{1,0:T(8,128)S(1)} %get-tuple-element.122.refs_10_.v0, f32[128,128]{1,0:T(8,128)S(1)} %get-tuple-element.127.left.refs_13_, ...), custom_call_target="tpu_custom_call" | custom-call | tf_op jit(solution)/shard_map/pallas_call | solution.py:24
  67.5 0.2 collective-permute-start.20
  67.7 3.7 %collective-permute-start.21 = (f32[32,128]{1,0:T(8,128)S(1)}, f32[32,128]{1,0:T(8,128)S(1)}, u32[]{:S(2)}, u32[]{:S(2)}) collective-permute-start(f32[32,128]{1,0:T(8,128)S(1)} %get-tuple-element.131), channel_id=1, source_target_pairs={{0,12},{1,13},{2,14},{3,15},{4,0},{5,1},{6,2},{7,3},{8,4},{9,5},{1... | collective-permute-start | bytes 49160 | tf_op jit(solution)/shard_map/ppermute | solution.py:369
  71.3 1.7 %collective-permute-done.20.refs_11_ = f32[32,128]{1,0:T(8,128)S(1)} collective-permute-done((f32[32,128]{1,0:T(8,128)S(1)}, f32[32,128]{1,0:T(8,128)S(1)}, u32[]{:S(2)}, u32[]{:S(2)}) %collective-permute-start.20) | collective-permute-done | bytes 16416 | tf_op jit(solution)/shard_map/ppermute | solution.py:369
  73.1 2.5 %shard_map.89 = (f32[128,128]{1,0:T(8,128)S(1)}, f32[128,128]{1,0:T(8,128)S(1)}, f32[64,128]{1,0:T(8,128)S(1)}, f32[64,128]{1,0:T(8,128)S(1)}, f32[64,128]{1,0:T...) custom-call(s32[2]{0:T(128)S(1)} %pad_add_fusion.pos, f32[64,128]{1,0:T(8,128)S(1)} %get-tuple-element.123.refs_0_, ...), custom_call_target="tpu_custom_call" | custom-call | tf_op jit(solution)/shard_map/pallas_call | solution.py:24
  75.6 1.1 %shard_map.90 = (f32[256,128]{1,0:T(8,128)S(1)}, f32[32,128]{1,0:T(8,128)S(1)}, f32[32,128]{1,0:T(8,128)S(1)}) custom-call(s32[2]{0:T(128)S(1)} %pad_add_fusion.pos, bf16[512,1024]{1,0:T(8,128)(2,1)S(1)} %shard_map.87.far, f32[256,128]{1,0:T(8,128)S(1)} %get-tuple-element.122.refs_10_.v0, f32[128,128]{1,0:T(8,128)S(1)} %get-tuple-element.133.left.refs_13_, ...), custom_call_target="tpu_custom_call" | custom-call | tf_op jit(solution)/shard_map/pallas_call | solution.py:24
  76.7 0.1 collective-permute-start.25
  76.8 3.9 %collective-permute-start.26 = (f32[32,128]{1,0:T(8,128)S(1)}, f32[32,128]{1,0:T(8,128)S(1)}, u32[]{:S(2)}, u32[]{:S(2)}) collective-permute-start(f32[32,128]{1,0:T(8,128)S(1)} %get-tuple-element.137), channel_id=1, source_target_pairs={{0,12},{1,13},{2,14},{3,15},{4,0},{5,1},{6,2},{7,3},{8,4},{9,5},{1... | collective-permute-start | bytes 49160 | tf_op jit(solution)/shard_map/ppermute | solution.py:369
  80.7 2.0 %collective-permute-start.24 = (f32[64,128]{1,0:T(8,128)S(1)}, f32[64,128]{1,0:T(8,128)S(1)}, u32[]{:S(2)}, u32[]{:S(2)}) collective-permute-start(f32[64,128]{1,0:T(8,128)S(1)} %get-tuple-element.132.refs_0_), channel_id=1, source_target_pairs={{0,12},{1,13},{2,14},{3,15},{4,0},{5,1},{6,2},{7,3},{8,4},{9,5},{1... | collective-permute-start | bytes 98312 | tf_op jit(solution)/shard_map/ppermute | solution.py:369
  82.7 0.6 collective-permute-start.22
  83.3 1.7 %collective-permute-start.31 = (f32[64,128]{1,0:T(8,128)S(1)}, f32[64,128]{1,0:T(8,128)S(1)}, u32[]{:S(2)}, u32[]{:S(2)}) collective-permute-start(f32[64,128]{1,0:T(8,128)S(1)} %get-tuple-element.148), channel_id=1, source_target_pairs={{0,2},{1,3},{2,0},{3,1},{4,6},{5,7},{6,4},{7,5},{8,10},{9,11},{10,... | collective-permute-start | bytes 98312 | tf_op jit(solution)/shard_map/ppermute | solution.py:366
  85.0 0.1 collective-permute-start.32
  85.1 2.3 %collective-permute-done.23.refs_2_ = f32[64,128]{1,0:T(8,128)S(1)} collective-permute-done((f32[64,128]{1,0:T(8,128)S(1)}, f32[64,128]{1,0:T(8,128)S(1)}, u32[]{:S(2)}, u32[]{:S(2)}) %collective-permute-start.23) | collective-permute-done | bytes 32800 | tf_op jit(solution)/shard_map/ppermute | solution.py:369
  87.5 0.9 collective-permute-done.22.refs_1_
  88.4 2.0 %shard_map.91 = (f32[56,128]{1,0:T(8,128)S(1)}, f32[56,128]{1,0:T(8,128)S(1)}, f32[56,128]{1,0:T(8,128)S(1)}, f32[56,128]{1,0:T(8,128)S(1)}) custom-call(s32[2]{0:T(128)S(1)} %pad_add_fusion.pos, f32[64,128]{1,0:T(8,128)S(1)} %get-tuple-element.132.refs_0_, f32[64,128]{1,0:T(8,128)S(1)} %collective-permute-done.22.refs_1_, ...), custom_call_target="tpu_custom_call" | custom-call | tf_op jit(solution)/shard_map/pallas_call | solution.py:24
  90.4 0.1 collective-permute-start.27
  90.5 1.7 %collective-permute-start.28 = (f32[56,128]{1,0:T(8,128)S(1)}, f32[56,128]{1,0:T(8,128)S(1)}, u32[]{:S(2)}, u32[]{:S(2)}) collective-permute-start(f32[56,128]{1,0:T(8,128)S(1)} %get-tuple-element.140), channel_id=1, source_target_pairs={{0,2},{1,3},{2,0},{3,1},{4,6},{5,7},{6,4},{7,5},{8,10},{9,11},{10,... | collective-permute-start | bytes 86024 | tf_op jit(solution)/shard_map/ppermute | solution.py:366
  92.2 0.1 collective-permute-start.29
  92.4 1.3 %shard_map.92.u_ref = f32[1536,128]{1,0:T(8,128)S(1)} custom-call(s32[2]{0:T(128)S(1)} %pad_add_fusion.pos, f32[64,128]{1,0:T(8,128)S(1)} %get-tuple-element.146.p0, f32[64,128]{1,0:T(8,128)S(1)} %collective-permute-done.30.p1, f32[64,128]{1,0:T(8,128)S(1)} %collective-permute-done.31.p2, f32[64,128]{1,0:T(8,128)S(1)} %collective-permute-done.32.p3, ...), custom_call_target="tpu_custom_call" | custom-call | tf_op jit(solution)/shard_map/pallas_call | solution.py:24
  93.7 0.7 collective-permute-done.28.p2
  94.4 1.1 %collective-permute-done.29.p3 = f32[56,128]{1,0:T(8,128)S(1)} collective-permute-done((f32[56,128]{1,0:T(8,128)S(1)}, f32[56,128]{1,0:T(8,128)S(1)}, u32[]{:S(2)}, u32[]{:S(2)}) %collective-permute-start.29) | collective-permute-done | bytes 28704 | tf_op jit(solution)/shard_map/ppermute | solution.py:366
  95.5 2.1 %shard_map.93 = (f32[1536,128]{1,0:T(8,128)}, f32[128,128]{1,0:T(8,128)}) custom-call(s32[2]{0:T(128)S(1)} %pad_add_fusion.pos, f32[56,128]{1,0:T(8,128)S(1)} %get-tuple-element.138.p0, f32[56,128]{1,0:T(8,128)S(1)} %collective-permute-done.27.p1, f32[56,128]{1,0:T(8,128)S(1)} %collective-permute-done.28.p2, f32[56,128]{1,0:T(8,128)S(1)} %collective-permute-done.29.p3, ...), custom_call_target="tpu_custom_call" | custom-call | tf_op jit(solution)/shard_map/pallas_call | solution.py:24
  (40 shorter events, 0.2 us)
Async XLA Ops:
  0.6 27.6 %collective-permute-start.2 = (f32[48,768]{1,0:T(8,128)}, f32[48,768]{1,0:T(8,128)S(1)}, u32[]{:S(2)}, u32[]{:S(2)}) collective-permute-start(f32[48,768]{1,0:T(8,128)} %mine.1), channel_id=1, source_target_pairs={{0,2},{1,3},{2,0},{3,1},{4,6},{5,7},{6,4},{7,5},{8,10},{9,11},{10,... | collective-permute-start | bytes 442376 | tf_op jit(solution)/shard_map/ppermute | solution.py:366
  3.7 24.6 %collective-permute-start.1 = (f32[48,768]{1,0:T(8,128)}, f32[48,768]{1,0:T(8,128)S(1)}, u32[]{:S(2)}, u32[]{:S(2)}) collective-permute-start(f32[48,768]{1,0:T(8,128)} %mine.1), channel_id=1, source_target_pairs={{3,6},{0,13},{1,12},{7,10},{4,1},{5,0},{11,14},{8,5},{9,4},{15,2},... | collective-permute-start | bytes 442376 | tf_op jit(solution)/shard_map/ppermute | solution.py:383
  8.3 19.9 %collective-permute-start = (f32[48,768]{1,0:T(8,128)}, f32[48,768]{1,0:T(8,128)S(1)}, u32[]{:S(2)}, u32[]{:S(2)}) collective-permute-start(f32[48,768]{1,0:T(8,128)} %mine.1), channel_id=1, source_target_pairs={{3,4},{0,15},{1,14},{7,8},{4,3},{5,2},{11,12},{8,7},{9,6},{15,0},{... | collective-permute-start | bytes 442376 | tf_op jit(solution)/shard_map/ppermute | solution.py:382
  10.6 1.1 %copy-start.4 = (f32[1536,128]{1,0:T(8,128)S(1)}, f32[1536,128]{1,0:T(8,128)}, u32[]{:S(2)}) copy-start(f32[1536,128]{1,0:T(8,128)} %f_ref.1) | copy-start | bytes 2359300
  11.7 0.7 copy-start.6
  12.4 0.7 copy-start.7
  13.1 0.7 copy-start.8
  13.7 16.5 %copy-start = (f32[1536,1536]{1,0:T(8,128)S(1)}, f32[1536,1536]{1,0:T(8,128)}, u32[]{:S(2)}) copy-start(f32[1536,1536]{1,0:T(8,128)} %k_ref.9) | copy-start | bytes 28311556
  22.0 22.0 %collective-permute-start.6 = (f32[448,128]{1,0:T(8,128)S(1)}, f32[448,128]{1,0:T(8,128)S(1)}, u32[]{:S(2)}, u32[]{:S(2)}) collective-permute-start(f32[448,128]{1,0:T(8,128)S(1)} %get-tuple-element.115.n0), channel_id=1, source_target_pairs={{0,2},{1,3},{2,0},{3,1},{4,6},{5,7},{6,4},{7,5},{8,10},{9,11},{10,... | collective-permute-start | bytes 688136 | tf_op jit(solution)/shard_map/ppermute | solution.py:366
  22.1 12.9 %collective-permute-start.7 = (f32[128,128]{1,0:T(8,128)S(1)}, f32[128,128]{1,0:T(8,128)S(1)}, u32[]{:S(2)}, u32[]{:S(2)}) collective-permute-start(f32[128,128]{1,0:T(8,128)S(1)} %get-tuple-element.100), channel_id=1, source_target_pairs={{3,4},{0,15},{1,14},{7,8},{4,3},{5,2},{11,12},{8,7},{9,6},{15,0},{... | collective-permute-start | bytes 196616 | tf_op jit(solution)/shard_map/ppermute | solution.py:409
  28.2 5.8 %collective-permute-start.3 = (f32[88,128]{1,0:T(8,128)S(1)}, f32[88,128]{1,0:T(8,128)S(1)}, u32[]{:S(2)}, u32[]{:S(2)}) collective-permute-start(f32[88,128]{1,0:T(8,128)S(1)} %get-tuple-element.85), channel_id=1, source_target_pairs={{0,1},{1,0},{2,3},{3,2},{4,5},{5,4},{6,7},{7,6},{8,9},{9,8},{10,11... | collective-permute-start | bytes 135176 | tf_op jit(solution)/shard_map/ppermute | solution.py:366
  28.3 5.7 %collective-permute-start.4 = (f32[88,128]{1,0:T(8,128)S(1)}, f32[88,128]{1,0:T(8,128)S(1)}, u32[]{:S(2)}, u32[]{:S(2)}) collective-permute-start(f32[88,128]{1,0:T(8,128)S(1)} %get-tuple-element.86), channel_id=1, source_target_pairs={{0,2},{1,3},{2,0},{3,1},{4,6},{5,7},{6,4},{7,5},{8,10},{9,11},{10,... | collective-permute-start | bytes 135176 | tf_op jit(solution)/shard_map/ppermute | solution.py:366
  28.4 5.7 %collective-permute-start.5 = (f32[88,128]{1,0:T(8,128)S(1)}, f32[88,128]{1,0:T(8,128)S(1)}, u32[]{:S(2)}, u32[]{:S(2)}) collective-permute-start(f32[88,128]{1,0:T(8,128)S(1)} %get-tuple-element.87), channel_id=1, source_target_pairs={{0,3},{1,2},{2,1},{3,0},{4,7},{5,6},{6,5},{7,4},{8,11},{9,10},{10,... | collective-permute-start | bytes 135176 | tf_op jit(solution)/shard_map/ppermute | solution.py:366
  30.2 1.5 %copy-start.1 = (bf16[1536,640]{1,0:T(8,128)(2,1)S(1)}, bf16[1536,640]{1,0:T(8,128)(2,1)}, u32[]{:S(2)}) copy-start(bf16[1536,640]{1,0:T(8,128)(2,1)} %get-tuple-element.95.right_side) | copy-start | bytes 5898244
  31.7 7.5 %copy-start.2 = (bf16[1536,640]{1,0:T(8,128)(2,1)S(1)}, bf16[1536,640]{1,0:T(8,128)(2,1)}, u32[]{:S(2)}) copy-start(bf16[1536,640]{1,0:T(8,128)(2,1)} %get-tuple-element.95.right_side) | copy-start | bytes 5898244
  35.0 9.0 %collective-permute-start.8 = (f32[128,128]{1,0:T(8,128)S(1)}, f32[128,128]{1,0:T(8,128)S(1)}, u32[]{:S(2)}, u32[]{:S(2)}) collective-permute-start(f32[128,128]{1,0:T(8,128)S(1)} %collective-permute-done.7.came), channel_id=1, source_target_pairs={{0,2},{1,3},{2,0},{3,1},{4,6},{5,7},{6,4},{7,5},{8,10},{9,11},{10,... | collective-permute-start | bytes 196616 | tf_op jit(solution)/shard_map/ppermute | solution.py:366
  35.4 8.6 %collective-permute-start.9 = (f32[96,128]{1,0:T(8,128)S(1)}, f32[96,128]{1,0:T(8,128)S(1)}, u32[]{:S(2)}, u32[]{:S(2)}) collective-permute-start(f32[96,128]{1,0:T(8,128)S(1)} %get-tuple-element.105), channel_id=1, source_target_pairs={{0,4},{1,5},{2,6},{3,7},{4,8},{5,9},{6,10},{7,11},{8,12},{9,13},{1... | collective-permute-start | bytes 147464 | tf_op jit(solution)/shard_map/ppermute | solution.py:369
  35.4 8.6 %collective-permute-start.11 = (f32[96,128]{1,0:T(8,128)S(1)}, f32[96,128]{1,0:T(8,128)S(1)}, u32[]{:S(2)}, u32[]{:S(2)}) collective-permute-start(f32[96,128]{1,0:T(8,128)S(1)} %get-tuple-element.106), channel_id=1, source_target_pairs={{0,12},{1,13},{2,14},{3,15},{4,0},{5,1},{6,2},{7,3},{8,4},{9,5},{1... | collective-permute-start | bytes 147464 | tf_op jit(solution)/shard_map/ppermute | solution.py:369
  39.2 4.8 %collective-permute-start.10 = (f32[64,128]{1,0:T(8,128)S(1)}, f32[64,128]{1,0:T(8,128)S(1)}, u32[]{:S(2)}, u32[]{:S(2)}) collective-permute-start(f32[64,128]{1,0:T(8,128)S(1)} %get-tuple-element.98.refs_0_), channel_id=1, source_target_pairs={{0,8},{1,9},{2,10},{3,11},{4,12},{5,13},{6,14},{7,15},{8,0},{9,1},... | collective-permute-start | bytes 98312 | tf_op jit(solution)/shard_map/ppermute | solution.py:369
  41.5 2.5 %copy-start.5 = (f32[48,768]{1,0:T(8,128)S(1)}, f32[48,768]{1,0:T(8,128)}, u32[]{:S(2)}) copy-start(f32[48,768]{1,0:T(8,128)} %mine.1) | copy-start | bytes 442372
  43.8 1.6 %copy-start.3 = (f32[352,1536]{1,0:T(8,128)S(1)}, f32[352,1536]{1,0:T(8,128)}, u32[]{:S(2)}) copy-start(f32[352,1536]{1,0:T(8,128)} %get-tuple-element.125.ks) | copy-start | bytes 6488068
  44.1 12.6 %collective-permute-start.12 = (f32[192,768]{1,0:T(8,128)S(1)}, f32[192,768]{1,0:T(8,128)S(1)}, u32[]{:S(2)}, u32[]{:S(2)}) collective-permute-start(f32[192,768]{1,0:T(8,128)S(1)} %pad_maximum_fusion), channel_id=1, source_target_pairs={{0,1},{1,0},{2,3},{3,2},{4,5},{5,4},{6,7},{7,6},{8,9},{9,8},{10,11... | collective-permute-start | bytes 1769480 | tf_op jit(solution)/shard_map/ppermute | solution.py:366
  44.2 13.2 %collective-permute-start.13 = (f32[1152,128]{1,0:T(8,128)S(1)}, f32[1152,128]{1,0:T(8,128)S(1)}, u32[]{:S(2)}, u32[]{:S(2)}) collective-permute-start(f32[1152,128]{1,0:T(8,128)S(1)} %pad_maximum_fusion.1), channel_id=1, source_target_pairs={{0,1},{1,0},{2,3},{3,2},{4,5},{5,4},{6,7},{7,6},{8,9},{9,8},{10,11... | collective-permute-start | bytes 1769480 | tf_op jit(solution)/shard_map/ppermute | solution.py:366
  46.6 7.8 %collective-permute-start.18 = (f32[256,256]{1,0:T(8,128)S(1)}, f32[256,256]{1,0:T(8,128)S(1)}, u32[]{:S(2)}, u32[]{:S(2)}) collective-permute-start(f32[256,256]{1,0:T(8,128)S(1)} %shard_map.86.n0), channel_id=1, source_target_pairs={{0,2},{1,3},{2,0},{3,1},{4,6},{5,7},{6,4},{7,5},{8,10},{9,11},{10,... | collective-permute-start | bytes 786440 | tf_op jit(solution)/shard_map/ppermute | solution.py:366
  48.4 17.3 %collective-permute-start.17 = (f32[256,256]{1,0:T(8,128)S(1)}, f32[256,256]{1,0:T(8,128)S(1)}, u32[]{:S(2)}, u32[]{:S(2)}) collective-permute-start(f32[256,256]{1,0:T(8,128)S(1)} %shard_map.86.n0), channel_id=1, source_target_pairs={{0,1},{1,0},{2,3},{3,2},{4,5},{5,4},{6,7},{7,6},{8,9},{9,8},{10,11... | collective-permute-start | bytes 786440 | tf_op jit(solution)/shard_map/ppermute | solution.py:366
  54.4 11.2 %collective-permute-start.19 = (f32[256,256]{1,0:T(8,128)S(1)}, f32[256,256]{1,0:T(8,128)S(1)}, u32[]{:S(2)}, u32[]{:S(2)}) collective-permute-start(f32[256,256]{1,0:T(8,128)S(1)} %collective-permute-done.18.n2), channel_id=1, source_target_pairs={{0,1},{1,0},{2,3},{3,2},{4,5},{5,4},{6,7},{7,6},{8,9},{9,8},{10,11... | collective-permute-start | bytes 786440 | tf_op jit(solution)/shard_map/ppermute | solution.py:366
  60.9 12.2 %collective-permute-start.16 = (f32[64,128]{1,0:T(8,128)S(1)}, f32[64,128]{1,0:T(8,128)S(1)}, u32[]{:S(2)}, u32[]{:S(2)}) collective-permute-start(f32[64,128]{1,0:T(8,128)S(1)} %get-tuple-element.123.refs_0_), channel_id=1, source_target_pairs={{0,12},{1,13},{2,14},{3,15},{4,0},{5,1},{6,2},{7,3},{8,4},{9,5},{1... | collective-permute-start | bytes 98312 | tf_op jit(solution)/shard_map/ppermute | solution.py:369
  62.3 10.8 %collective-permute-start.15 = (f32[64,128]{1,0:T(8,128)S(1)}, f32[64,128]{1,0:T(8,128)S(1)}, u32[]{:S(2)}, u32[]{:S(2)}) collective-permute-start(f32[64,128]{1,0:T(8,128)S(1)} %get-tuple-element.123.refs_0_), channel_id=1, source_target_pairs={{0,8},{1,9},{2,10},{3,11},{4,12},{5,13},{6,14},{7,15},{8,0},{9,1},... | collective-permute-start | bytes 98312 | tf_op jit(solution)/shard_map/ppermute | solution.py:369
  63.6 9.4 %collective-permute-start.14 = (f32[64,128]{1,0:T(8,128)S(1)}, f32[64,128]{1,0:T(8,128)S(1)}, u32[]{:S(2)}, u32[]{:S(2)}) collective-permute-start(f32[64,128]{1,0:T(8,128)S(1)} %get-tuple-element.123.refs_0_), channel_id=1, source_target_pairs={{0,4},{1,5},{2,6},{3,7},{4,8},{5,9},{6,10},{7,11},{8,12},{9,13},{1... | collective-permute-start | bytes 98312 | tf_op jit(solution)/shard_map/ppermute | solution.py:369
  67.5 5.6 %collective-permute-start.20 = (f32[32,128]{1,0:T(8,128)S(1)}, f32[32,128]{1,0:T(8,128)S(1)}, u32[]{:S(2)}, u32[]{:S(2)}) collective-permute-start(f32[32,128]{1,0:T(8,128)S(1)} %get-tuple-element.130), channel_id=1, source_target_pairs={{0,4},{1,5},{2,6},{3,7},{4,8},{5,9},{6,10},{7,11},{8,12},{9,13},{1... | collective-permute-start | bytes 49160 | tf_op jit(solution)/shard_map/ppermute | solution.py:369
  67.7 5.4 %collective-permute-start.21 = (f32[32,128]{1,0:T(8,128)S(1)}, f32[32,128]{1,0:T(8,128)S(1)}, u32[]{:S(2)}, u32[]{:S(2)}) collective-permute-start(f32[32,128]{1,0:T(8,128)S(1)} %get-tuple-element.131), channel_id=1, source_target_pairs={{0,12},{1,13},{2,14},{3,15},{4,0},{5,1},{6,2},{7,3},{8,4},{9,5},{1... | collective-permute-start | bytes 49160 | tf_op jit(solution)/shard_map/ppermute | solution.py:369
  76.7 6.5 %collective-permute-start.25 = (f32[32,128]{1,0:T(8,128)S(1)}, f32[32,128]{1,0:T(8,128)S(1)}, u32[]{:S(2)}, u32[]{:S(2)}) collective-permute-start(f32[32,128]{1,0:T(8,128)S(1)} %get-tuple-element.136), channel_id=1, source_target_pairs={{0,4},{1,5},{2,6},{3,7},{4,8},{5,9},{6,10},{7,11},{8,12},{9,13},{1... | collective-permute-start | bytes 49160 | tf_op jit(solution)/shard_map/ppermute | solution.py:369
  76.8 6.4 %collective-permute-start.26 = (f32[32,128]{1,0:T(8,128)S(1)}, f32[32,128]{1,0:T(8,128)S(1)}, u32[]{:S(2)}, u32[]{:S(2)}) collective-permute-start(f32[32,128]{1,0:T(8,128)S(1)} %get-tuple-element.137), channel_id=1, source_target_pairs={{0,12},{1,13},{2,14},{3,15},{4,0},{5,1},{6,2},{7,3},{8,4},{9,5},{1... | collective-permute-start | bytes 49160 | tf_op jit(solution)/shard_map/ppermute | solution.py:369
  80.7 4.3 %collective-permute-start.24 = (f32[64,128]{1,0:T(8,128)S(1)}, f32[64,128]{1,0:T(8,128)S(1)}, u32[]{:S(2)}, u32[]{:S(2)}) collective-permute-start(f32[64,128]{1,0:T(8,128)S(1)} %get-tuple-element.132.refs_0_), channel_id=1, source_target_pairs={{0,12},{1,13},{2,14},{3,15},{4,0},{5,1},{6,2},{7,3},{8,4},{9,5},{1... | collective-permute-start | bytes 98312 | tf_op jit(solution)/shard_map/ppermute | solution.py:369
  82.7 4.8 %collective-permute-start.23 = (f32[64,128]{1,0:T(8,128)S(1)}, f32[64,128]{1,0:T(8,128)S(1)}, u32[]{:S(2)}, u32[]{:S(2)}) collective-permute-start(f32[64,128]{1,0:T(8,128)S(1)} %get-tuple-element.132.refs_0_), channel_id=1, source_target_pairs={{0,8},{1,9},{2,10},{3,11},{4,12},{5,13},{6,14},{7,15},{8,0},{9,1},... | collective-permute-start | bytes 98312 | tf_op jit(solution)/shard_map/ppermute | solution.py:369
  82.7 5.7 %collective-permute-start.22 = (f32[64,128]{1,0:T(8,128)S(1)}, f32[64,128]{1,0:T(8,128)S(1)}, u32[]{:S(2)}, u32[]{:S(2)}) collective-permute-start(f32[64,128]{1,0:T(8,128)S(1)} %get-tuple-element.132.refs_0_), channel_id=1, source_target_pairs={{0,4},{1,5},{2,6},{3,7},{4,8},{5,9},{6,10},{7,11},{8,12},{9,13},{1... | collective-permute-start | bytes 98312 | tf_op jit(solution)/shard_map/ppermute | solution.py:369
  83.3 9.0 %collective-permute-start.30 = (f32[64,128]{1,0:T(8,128)S(1)}, f32[64,128]{1,0:T(8,128)S(1)}, u32[]{:S(2)}, u32[]{:S(2)}) collective-permute-start(f32[64,128]{1,0:T(8,128)S(1)} %get-tuple-element.147), channel_id=1, source_target_pairs={{0,1},{1,0},{2,3},{3,2},{4,5},{5,4},{6,7},{7,6},{8,9},{9,8},{10,11... | collective-permute-start | bytes 98312 | tf_op jit(solution)/shard_map/ppermute | solution.py:366
  83.3 9.1 %collective-permute-start.31 = (f32[64,128]{1,0:T(8,128)S(1)}, f32[64,128]{1,0:T(8,128)S(1)}, u32[]{:S(2)}, u32[]{:S(2)}) collective-permute-start(f32[64,128]{1,0:T(8,128)S(1)} %get-tuple-element.148), channel_id=1, source_target_pairs={{0,2},{1,3},{2,0},{3,1},{4,6},{5,7},{6,4},{7,5},{8,10},{9,11},{10,... | collective-permute-start | bytes 98312 | tf_op jit(solution)/shard_map/ppermute | solution.py:366
  85.0 7.3 %collective-permute-start.32 = (f32[64,128]{1,0:T(8,128)S(1)}, f32[64,128]{1,0:T(8,128)S(1)}, u32[]{:S(2)}, u32[]{:S(2)}) collective-permute-start(f32[64,128]{1,0:T(8,128)S(1)} %get-tuple-element.149), channel_id=1, source_target_pairs={{0,3},{1,2},{2,1},{3,0},{4,7},{5,6},{6,5},{7,4},{8,11},{9,10},{10,... | collective-permute-start | bytes 98312 | tf_op jit(solution)/shard_map/ppermute | solution.py:366
  90.4 3.3 %collective-permute-start.27 = (f32[56,128]{1,0:T(8,128)S(1)}, f32[56,128]{1,0:T(8,128)S(1)}, u32[]{:S(2)}, u32[]{:S(2)}) collective-permute-start(f32[56,128]{1,0:T(8,128)S(1)} %get-tuple-element.139), channel_id=1, source_target_pairs={{0,1},{1,0},{2,3},{3,2},{4,5},{5,4},{6,7},{7,6},{8,9},{9,8},{10,11... | collective-permute-start | bytes 86024 | tf_op jit(solution)/shard_map/ppermute | solution.py:366
  90.5 3.9 %collective-permute-start.28 = (f32[56,128]{1,0:T(8,128)S(1)}, f32[56,128]{1,0:T(8,128)S(1)}, u32[]{:S(2)}, u32[]{:S(2)}) collective-permute-start(f32[56,128]{1,0:T(8,128)S(1)} %get-tuple-element.140), channel_id=1, source_target_pairs={{0,2},{1,3},{2,0},{3,1},{4,6},{5,7},{6,4},{7,5},{8,10},{9,11},{10,... | collective-permute-start | bytes 86024 | tf_op jit(solution)/shard_map/ppermute | solution.py:366
  92.2 3.3 %collective-permute-start.29 = (f32[56,128]{1,0:T(8,128)S(1)}, f32[56,128]{1,0:T(8,128)S(1)}, u32[]{:S(2)}, u32[]{:S(2)}) collective-permute-start(f32[56,128]{1,0:T(8,128)S(1)} %get-tuple-element.141), channel_id=1, source_target_pairs={{0,3},{1,2},{2,1},{3,0},{4,7},{5,6},{6,5},{7,4},{8,11},{9,10},{10,... | collective-permute-start | bytes 86024 | tf_op jit(solution)/shard_map/ppermute | solution.py:366

commit v3 on v0

v3 whole, which is shorter than its diff:
```python
import functools

import jax
import jax.numpy as jnp
from jax import lax
from jax.experimental import pallas as pl
from jax.experimental.pallas import tpu as pltpu
from jax.sharding import PartitionSpec as P

ITERS = 3
DAMPING = 0.5
GROUP = 4
LANES = 128
BF16 = jnp.bfloat16
F32 = jnp.float32


def call(kernel, outs, args, smem=1, hbm=(), scratch=(), vmem=24):
    in_specs = [
        pl.BlockSpec(memory_space=pltpu.SMEM if i < smem else pltpu.HBM if i in hbm else pltpu.VMEM)
        for i in range(len(args))
    ]
    shapes = [o if isinstance(o[0], tuple) else (o, F32) for o in outs]
    return pl.pallas_call(
        kernel,
        out_shape=[jax.ShapeDtypeStruct(s, d) for s, d in shapes],
        in_specs=in_specs,
        out_specs=[pl.BlockSpec(memory_space=pltpu.VMEM)] * len(shapes),
        scratch_shapes=list(scratch),
        compiler_params=pltpu.CompilerParams(vmem_limit_bytes=vmem * 1024 * 1024),
    )(*args)


def halves(x):
    high = x.astype(BF16)
    return high, (x - high.astype(F32)).astype(BF16)


def dot(a, b):
    return jnp.dot(a, b, preferred_element_type=F32)


def product(a, b):
    ah, al = halves(a)
    bh, bl = halves(b)
    n = b.shape[1]
    both = dot(ah, jnp.concatenate([bh, bl], axis=1))
    return both[:, :n] + both[:, n:] + dot(al, bh)


def lane_block(rows):
    return lax.broadcasted_iota(jnp.int32, (rows, LANES), 1) // (LANES // GROUP)


def turned(x, blocks):
    shift = (blocks % GROUP) * (LANES // GROUP)
    return x if shift == 0 else pltpu.roll(x, shift, 1)


def transposed(parts):
    block = lane_block(parts[0].shape[0])
    out = []
    for j in range(GROUP):
        total = turned(parts[0], -j)
        for q in range(1, GROUP):
            total = jnp.where(block == q, turned(parts[q], q - j), total)
        out.append(total)
    return out


def cut(x, out):
    rows = x.shape[0] // GROUP
    for j, part in enumerate(transposed([x[q * rows:(q + 1) * rows] for q in range(GROUP)])):
        out[j] = part


def joined(pieces):
    return jnp.concatenate(transposed([pieces[i] for i in range(GROUP)]), axis=0)


def packed(x, chunk):
    first = lane_block(chunk) == 0
    out = None
    for q in range(x.shape[0] // chunk):
        part = turned(jnp.where(first, x[q * chunk:(q + 1) * chunk], 0.0), q)
        out = part if out is None else out + part
    return out


def unpacked(x, count):
    return jnp.concatenate([turned(x, -q) for q in range(count)], axis=0)


def chunk_of(owned):
    return -(-owned // (GROUP * 8)) * 8


def stacked(x):
    return jnp.concatenate(halves(x), axis=0)


def beside(x):
    return jnp.concatenate(halves(x), axis=1)


def combined(p, n):
    m = p.shape[0] // 2
    return p[:m, :n] + p[:m, n:] + p[m:, :n]


def payload(v, width, group, out):
    groups, faces = out.shape[0], v[:2 * width]
    coarse = v[2 * width:]
    owned = coarse.shape[0] // 2
    below = turned(coarse[owned:], 1)
    rows = jnp.concatenate(
        [coarse[:owned] + jnp.where(lane_block(owned) == 0, 0.0, below), packed(below, chunk_of(owned))], axis=0
    )
    at = rows.shape[0]
    down, up = packed(faces[:width], width // GROUP), packed(turned(faces[width:], 1), width // GROUP)
    for h in range(groups):
        out[h, :at] = rows
        out[h, at:] = down
    out[lax.rem(group + 1, groups), at:] = up


def fetch(source, count, rows, target, places, sem):
    def one(j, carry):
        pltpu.make_async_copy(source.at[pl.ds(rows(j), 1)], target.at[pl.ds(places(j), 1)], sem).start()
        return carry

    lax.fori_loop(0, count, one, 0, unroll=8)


def rows_kernel(pos, face, prim, slot, k_ref, f_ref, c_ref, facev, primv, slotv, *rest):
    pieces, spans, edge, right_side, ks, sem = rest
    width, count, order, columns = face.shape[1], prim.shape[1], ks.shape[1], f_ref.shape[1]
    side = 2 * width
    fetch(k_ref, count, lambda j: prim[0, j], ks, lambda j: side + slot[0, j], sem)
    fetch(k_ref, side, lambda j: face[j // width, j % width], ks, lambda j: j, sem)

    def indicator(row):
        place = lax.broadcasted_iota(jnp.int32, (order, row.shape[1]), 0).astype(F32)
        return jnp.where(place == row, 1.0, 0.0).astype(BF16)

    slots = jnp.broadcast_to(slotv[...].astype(F32), (count, count)).T
    prims = jnp.broadcast_to(primv[...].astype(F32), (count, count)).T
    wanted = lax.broadcasted_iota(jnp.int32, (count, count), 1).astype(F32)
    by_slot = jnp.sum(jnp.where(slots == wanted, prims, 0.0), axis=0, keepdims=True)
    right_side[:, :width] = indicator(facev[0:1].astype(F32))
    right_side[:, width:side] = indicator(facev[1:2].astype(F32))
    right_side[:, side:side + count] = indicator(by_slot)
    right_side[:, side + count:side + width] = jnp.zeros((order, width - count), BF16)
    right_side[:, side + width:] = beside(f_ref[...])
    tall = c_ref.shape[1] // LANES
    owned = c_ref.shape[0]
    for i in range(tall):
        edge[width + i * owned:width + (i + 1) * owned] = c_ref[:, i * LANES:(i + 1) * LANES]
    pltpu.make_async_copy(k_ref.at[pl.ds(0, ks.shape[0])], ks, sem).wait()

    at = side + width
    high, low = halves(ks[...])
    both = dot(high, right_side[...])
    part = dot(low, right_side[:, :at + columns])
    cut(both[:, at:at + columns] + both[:, at + columns:] + part[:, at:], pieces)
    block = both[:, :at] + part[:, :at]
    rows = side + count
    for i in range(3):
        kept = side if i == 2 else rows
        spans[i * rows:i * rows + kept] = block[:kept, i * width:(i + 1) * width]
    edge[:width] = jnp.where(pos[0] == GROUP - 1, block[width:side, side:], block[:width, side:])


def sweep_kernel(first, pos, right_side, k_ref, u_ref, ks_ref):
    rows, columns = u_ref.shape
    at = right_side.shape[1] - 2 * columns
    high, low = halves(k_ref[first:first + rows])
    both = dot(high, right_side[...])
    part = dot(low, right_side[:, :at + columns])
    u_ref[...] = both[:, at:at + columns] + both[:, at + columns:] + part[:, at:]
    ks_ref[...] = both[:, :at] + part[:, :at]


GOT = (-1, None, 5, 4)
GOT_NEXT = (5, 4, -1, None)


GOT = (-1, None, 5, 4)
GOT_NEXT = (5, 4, -1, None)


def blocks_kernel(width, pos, c0, c2, s0, s2, came, came_next, theirs, solver, cross, own, edge_up, edge_down):
    side, size, edge_size = 2 * width, s0.shape[0], came.shape[0]
    kept = (size - side) // 2
    owned, tall = c0.shape[0], c0.shape[1] // LANES
    half = solver.shape[0] // 2
    other, at = [], 0
    for rows in (size, size, edge_size, edge_size, edge_size - width, edge_size - width):
        other.append(theirs.at[at:at + rows])
        at += rows
    for k, ref in enumerate((s0, other[0], s2, other[1])):
        own[:, k * side:k * side + width] = stacked(ref[:kept])
        own[:, k * side + width:(k + 1) * side] = stacked(ref[kept:2 * kept])
        cross[:, k * width:(k + 1) * width] = stacked(ref[2 * kept:])

    def placed(block, tile):
        at = (block + 1) * owned
        for i in range(tall):
            high, low = halves(tile(i))
            solver[at:at + owned, i * LANES:(i + 1) * LANES] = high
            solver[half + at:half + at + owned, i * LANES:(i + 1) * LANES] = low

    def wide(ref):
        return lambda i: ref[:, i * LANES:(i + 1) * LANES]

    def high_up(ref, first):
        return lambda i: ref[first + i * owned:first + (i + 1) * owned]

    for m in range(GROUP):

        @pl.when(pos[0] == m)
        def _():
            p = m ^ 1
            placed(m, wide(c0))
            placed(m ^ 2, wide(c2))
            placed(p, high_up(other[4], 0))
            placed(p ^ 2, high_up(other[5], 0))
            held = {}
            for block, ref in zip((GOT[m], GOT_NEXT[m], GOT[p], GOT_NEXT[p]), (came, came_next, other[2], other[3])):
                held.setdefault(block, ref)
            for block in (-1, 4, 5):
                placed(block, high_up(held[block], width))
            edge_up[...] = stacked(held[-1][:width])
            edge_down[...] = stacked(held[4][:width])


def start_kernel(pos, pieces, v_ref, pay_ref):
    v = joined(pieces)
    v_ref[...] = v
    payload(v, v.shape[1], pos[1], pay_ref)


def shared(x, member):
    block = lane_block(x.shape[0])
    high, low = halves(x)
    high, low = high.astype(F32), low.astype(F32)
    out = []
    for k in range(GROUP):
        mine = block == (member ^ k)
        pair = [jnp.where(mine, half, 0.0).astype(BF16) for half in (high, low)]
        out.append(jnp.concatenate(pair, axis=1))
    return jnp.concatenate(out, axis=0)


def turn_kernel(kind, pos, pays, solver, cross, own, edge_up, edge_down, v0, *refs):
    if kind == "first":
        now = v0
    else:
        (now, left_ref, right_ref), refs = refs[:3], refs[3:]
    outs, stack = refs[:-1], refs[-1]
    member, group = pos[0], pos[1]
    groups, width = pays.shape[0], edge_down.shape[1]
    owned = (v0.shape[0] - 2 * width) // 2
    size = owned + chunk_of(owned)
    first = lane_block(owned) == 0

    for h in range(groups):
        extra = unpacked(pays[(h - 1) % groups, owned:size], -(-owned // chunk_of(owned)))[:owned]
        whole = pays[h, :owned] + jnp.where(first, extra, 0.0)
        for i in range(GROUP):
            place = (h * GROUP + i) * owned
            stack[place:place + owned, :] = beside(turned(whole, -i))

    w = combined(dot(solver[...], stack[...]), LANES)
    pair = lane_block(2 * owned)
    q = w[owned:3 * owned]
    for i in range(1, GROUP):
        q = jnp.where(pair == i, turned(w[(i + 1) * owned:(i + 3) * owned], i), q)
    filler = jnp.zeros((width - 2 * owned, LANES), F32)

    def padded(x):
        return jnp.concatenate([x, filler], axis=0)

    faces = now[:2 * width] - combined(dot(cross[...], shared(padded(q), member)), LANES)
    left, right = faces[:width], faces[width:]
    before, after = beside(padded(w[:2 * owned])), beside(padded(w[(GROUP + 1) * owned:]))
    halo_up = pays[lax.rem(group + groups - 1, groups), size:]
    halo_down = pays[lax.rem(group + 1, groups), size:]
    right_before = unpacked(halo_up, GROUP) - combined(dot(edge_up[...], before), LANES)
    left_after = unpacked(halo_down, GROUP) - combined(dot(edge_down[...], after), LANES)
    block = lane_block(width)
    beyond = jnp.where(block == GROUP - 1, turned(left_after, GROUP - 1), turned(left, -1))
    behind = jnp.where(block == 0, right_before, turned(right, 1))
    lam_right = DAMPING * (right - beyond)
    lam_left = DAMPING * (behind - left)
    if kind != "first":
        lam_right = lam_right + right_ref[...]
        lam_left = lam_left + left_ref[...]
    if kind == "last":
        cut(jnp.concatenate([q, lam_right, left_ref[...], right_ref[...]], axis=0), outs[0])
        return
    v_ref, left_out, right_out, pay_ref = outs[:4]
    left_out[...] = lam_left
    right_out[...] = lam_right
    lam = jnp.concatenate([lam_left, -lam_right], axis=0)
    v = v0[...] + combined(dot(own[...], shared(lam, member)), LANES)
    v_ref[...] = v
    payload(v, width, group, pay_ref)


def final_kernel(parts, count, pos, pieces, *refs):
    x = joined(pieces)
    us, kss, (out, lam_ref) = refs[:parts], refs[parts:2 * parts], refs[2 * parts:]
    width = lam_ref.shape[0]
    lam_ref[...] = x[count:count + width]
    at = count + width
    filler = jnp.zeros((width - count, LANES), F32)
    change = beside(jnp.concatenate([x[at:at + width], -x[at + width:], -x[:count], filler], axis=0))
    at = 0
    for u, ks in zip(us, kss):
        out[at:at + u.shape[0]] = u[...] + combined(dot(stacked(ks[...]), change), LANES)
        at += u.shape[0]


def local(condensed, eigen_loads, coarse_inverse, face_rows, primal_rows, primal_slot):
    order, columns = eigen_loads.shape
    owned, coarse = coarse_inverse.shape
    width = face_rows.shape[2]
    side, count = 2 * width, 2 * owned
    kept = side + count
    total = lax.axis_size("sub")
    groups = total // GROUP
    me = lax.axis_index("sub")
    pos = jnp.stack([me % GROUP, me // GROUP]).astype(jnp.int32)
    faces = face_rows[0]

    def mate(x, k):
        return lax.ppermute(x, "sub", [(s, s ^ k) for s in range(total)])

    def crossing(x, pairs):
        pairs = [(g * GROUP + a, (g * GROUP + b) % total) for g in range(groups) for a, b in pairs]
        return lax.ppermute(x, "sub", pairs)

    def traded(x):
        planes = [[g * GROUP + m for m in range(GROUP)] for g in range(groups)]
        return lax.all_to_all(x, "sub", 0, 0, axis_index_groups=planes)

    def along(x):
        lines = [[g * GROUP + m for g in range(groups)] for m in range(GROUP)]
        return lax.all_to_all(x, "sub", 0, 0, axis_index_groups=lines)

    def after(x, other):
        return lax.optimization_barrier((x, other))[0]

    c_next = mate(coarse_inverse, 2)
    tall = owned * coarse // LANES
    pieces, spans, edge, right_side = call(
        rows_kernel,
        [
            (GROUP, kept // GROUP, LANES),
            (2 * kept + side, width),
            (width + tall, width),
            ((order, side + width + 2 * columns), BF16),
        ],
        (pos, faces, primal_rows, primal_slot, condensed, eigen_loads, coarse_inverse, faces, primal_rows, primal_slot),
        smem=4,
        hbm=(4,),
        scratch=[pltpu.VMEM((kept, order), F32), pltpu.SemaphoreType.DMA],
        vmem=52,
    )
    spans_next = mate(spans, 2)
    pieces = traded(after(pieces, c_next))
    pay_shape = (groups, owned + chunk_of(owned) + width // GROUP, LANES)
    v0, pay = call(start_kernel, [(kept, LANES), pay_shape], (pos, pieces))
    edge = after(edge, pay)
    came = crossing(edge, [(GROUP - 1, GROUP), (0, -1), (1, -2)])
    came_next = crossing(edge, [(GROUP - 1, GROUP + 2), (0, -3), (1, -4)])
    got = along(pay)

    parts = 4 if order % 64 == 0 else 1
    block = order // parts
    sweeps, later = [], after(right_side, pay)
    for part in range(parts):
        sweeps.append(call(
            functools.partial(sweep_kernel, part * block),
            [(block, columns), (block, side + width)],
            (pos, later, condensed),
        ))
        later = after(right_side, sweeps[-1])
    us, kss = [x[0] for x in sweeps], [x[1] for x in sweeps]
    spans_next, came, came_next, got = lax.optimization_barrier((spans_next, came, came_next, got, sweeps[:3]))[:4]

    def high_up(x):
        return jnp.concatenate([x[:, i:i + LANES] for i in range(0, coarse, LANES)], axis=0)

    theirs = [spans, spans_next, came, came_next, edge[width:], high_up(c_next)]
    theirs = mate(jnp.concatenate(theirs, axis=0), 1)
    blocks = call(
        functools.partial(blocks_kernel, width),
        [
            ((2 * (GROUP + 3) * owned, coarse), BF16),
            ((2 * side, GROUP * width), BF16),
            ((2 * kept, GROUP * side), BF16),
            ((side, width), BF16),
            ((side, width), BF16),
        ],
        (pos, coarse_inverse, c_next, spans, spans_next, came, came_next, theirs),
    )

    state = ()
    for step in range(ITERS):
        kind = "first" if step == 0 else "last" if step == ITERS - 1 else "middle"
        shapes = [(kept, LANES), (width, LANES), (width, LANES), pay_shape]
        if kind == "last":
            shapes = [(GROUP, (count + 3 * width) // GROUP, LANES)]
        outs = call(
            functools.partial(turn_kernel, kind),
            shapes,
            (pos, got, *blocks, v0, *state),
            scratch=[pltpu.VMEM((coarse, 2 * LANES), BF16)],
        )
        if kind != "last":
            state = outs[:3]
            got = along(outs[3])
    displaced, multipliers = call(
        functools.partial(final_kernel, parts, count),
        [(order, columns), (width, columns)],
        (pos, traded(outs[0]), *us, *kss),
    )
    return displaced, multipliers


def solution(mesh):
    placed = (
        P(("rve", "sub"), None),
        P(("rve", "sub"), None),
        P(("rve", "sub"), None),
        P("sub", None, None),
        P("sub", None),
        P("sub", None),
    )
    return jax.shard_map(
        local,
        mesh=mesh,
        in_specs=placed,
        out_specs=(P(("rve", "sub"), None), P(("rve", "sub"), None)),
        check_vma=False,
    )
```

time: 173 us -> 121 us (0.70)
  matrix products: 36.7 us -> 0 us
  Pallas kernels: 0 us -> 30 us
  blocking collectives: 64.8 us -> 35.6 us
  other arithmetic: 12.5 us -> 0.07 us
  waiting for transfers between devices: 14.3 us -> 3.82 us
  local copies, waits for them, and re-layouts: 27.5 us -> 30.7 us
  starting transfers between devices: 15.8 us -> 19 us
    all_gather x3 -> x0, blocking collectives: 64.8 us -> none  [local(): piece = lax.all_gather(slotted, 'sub', axis=0, tiled=True)]
    dot_general x12 -> x0, matrix products: 36.7 us -> none  [the longest x3 31.3 us: local(): jnp.dot(condensed, loads, precision=lax.Precision.HIGHEST, preferred_elem...]
    all_to_all x0 -> x3, blocking collectives: none -> 35.6 us  [the longest x2 21 us: along(): return lax.all_to_all(x, 'sub', 0, 0, axis_index_groups=lines)]
    pallas_call x0 -> x11, Pallas kernels: none -> 30 us  [call(): pl.pallas_call(kernel, out_shape=[jax.ShapeDtypeStruct(s, d) for s, d in...]
    unnamed x9 -> x54, local copies, waits for them, and re-layouts: 11.1 us -> 30.1 us
    gather x10 -> x0, local copies, waits for them, and re-layouts: 10.5 us -> none  [the longest x1 4.76 us: local(): prolong = condensed[:, prim_rows]]
    ppermute x8 -> x5, waiting for transfers between devices: 14.3 us -> 3.82 us  [the longest x3 3.81 us: mate(): return lax.ppermute(x, 'sub', [(s, s ^ k) for s in range(total)])]
    scatter-add x6 -> x0, other arithmetic: 9.69 us -> none  [local(): eigen_loads.at[right_rows].add(-multipliers).at[left_rows].add(previous)]
  transfers between devices with their start and end apart: 8 -> 7, of which waited for: 7 -> 1; matrix products, arithmetic and copies ran while one was open for 11% -> 1% of each run, Pallas kernels for 0% -> 15%
where the time goes in v3:
time: 121 us; the launch traced here: 120 us
  blocking collectives  35.6 us (29%)
  local copies, waits for them, and re-layouts  30.7 us (25%)
  Pallas kernels  30 us (25%)
  starting transfers between devices  19 us (16%)
  waiting for transfers between devices  3.82 us (3%)
    unnamed x54, local copies, waits for them, and re-layouts  30.1 us
    pallas_call x11, Pallas kernels, call(): pl.pallas_call(kernel, out_shape=[jax.ShapeDtypeStruct(s, d) for s, d in...  30 us
    all_to_all x2, blocking collectives, along(): return lax.all_to_all(x, 'sub', 0, 0, axis_index_groups=lines)  21 us
    all_to_all x1, blocking collectives, traded(): return lax.all_to_all(x, 'sub', 0, 0, axis_index_groups=planes)  14.6 us
    ppermute x2, starting transfers between devices, crossing(): return lax.ppermute(x, 'sub', pairs)  7.3 us
    all_to_all x1, starting transfers between devices, along(): return lax.all_to_all(x, 'sub', 0, 0, axis_index_groups=lines)  4.87 us
    ppermute x3, waiting for transfers between devices, mate(): return lax.ppermute(x, 'sub', [(s, s ^ k) for s in range(total)])  3.81 us
    all_to_all x1, starting transfers between devices, traded(): return lax.all_to_all(x, 'sub', 0, 0, axis_index_groups=planes)  3.73 us
  transfers between devices with their start and end apart: 7, of which 1 were waited for; matrix products, arithmetic and copies ran while one was open for 1% of the time, Pallas kernels for 15%

profile of v3, /device:TPU:0, one launch (start us, length us, event | category | flops | bytes accessed | tf_op | source)
XLA Modules:
  0.0 120.0 jit_solution(8794584282844266582)
XLA Ops:
  0.6 3.0 %collective-permute-start.1 = (f32[48,768]{1,0:T(8,128)}, f32[48,768]{1,0:T(8,128)S(1)}, u32[]{:S(2)}, u32[]{:S(2)}) collective-permute-start(f32[48,768]{1,0:T(8,128)} %c0.1), channel_id=1, source_target_pairs={{0,2},{1,3},{2,0},{3,1},{4,6},{5,7},{6,4},{7,5},{8,10},{9,11},{10,... | collective-permute-start | bytes 442376 | tf_op jit(solution)/shard_map/ppermute | solution.py:338
  3.7 0.1 pad_add_fusion.pos
  3.7 1.1 copy-done.4
  4.9 0.9 copy-done.9
  5.8 0.7 copy-done.19
  6.5 0.7 copy-done.20
  7.1 0.7 copy-done.21
  7.8 7.3 %shard_map.77 = (f32[4,88,128]{2,1,0:T(8,128)S(1)}, f32[960,128]{1,0:T(8,128)S(1)}, f32[416,128]{1,0:T(8,128)}, bf16[1536,640]{1,0:T(8,128)(2,1)}) custom-call(s32[2]{0:T(128)S(1)} %pad_add_fusion.pos, s32[2,128]{1,0:T(2,128)S(1)} %bitcast.3, s32[1,96]{1,0:T(1,128)S(1)} %copy-done.20, s32[1,96]{1,0:T(1,128)S(1)} %copy-done.21, f32[1536,1536]{1,0:T(8,128)} %k_ref.9, ...), custom_call_target="tpu_custom_call" | custom-call | tf_op jit(solution)/shard_map/pallas_call | solution.py:24
  15.1 0.1 collective-permute-start
  15.2 0.0 collective-permute-done.1.c2
  15.2 14.6 %all_to_all.25.pieces = f32[4,88,128]{2,1,0:T(8,128)S(1)} all-to-all(f32[4,88,128]{2,1,0:T(8,128)S(1)} %get-tuple-element.42), channel_id=1, replica_groups={{0,1,2,3},{4,5,6,7},{8,9,10,11},{12,13,14,15},{16,17,18,19},{20,21,22,2..., dimensions={0} | all-to-all | bytes 360448 | tf_op jit(solution)/shard_map/all_to_all | solution.py:346
  29.8 1.6 %shard_map.78 = (f32[352,128]{1,0:T(8,128)S(1)}, f32[4,96,128]{2,1,0:T(8,128)}) custom-call(s32[2]{0:T(128)S(1)} %pad_add_fusion.pos, f32[4,88,128]{2,1,0:T(8,128)S(1)} %all_to_all.25.pieces), custom_call_target="tpu_custom_call" | custom-call | tf_op jit(solution)/shard_map/pallas_call | solution.py:24
  31.3 4.9 %all-to-all-start.1 = ((f32[4,96,128]{2,1,0:T(8,128)}), f32[4,96,128]{2,1,0:T(8,128)S(1)}, u32[]{:S(2)}, u32[]{:S(2)}) async-start(f32[4,96,128]{2,1,0:T(8,128)} %get-tuple-element.43), calls=%async_computation.1 | async-start | bytes 393216 | tf_op jit(solution)/shard_map/all_to_all | solution.py:350
  36.2 4.6 %collective-permute-start.3 = (f32[416,128]{1,0:T(8,128)}, f32[416,128]{1,0:T(8,128)S(1)}, u32[]{:S(2)}, u32[]{:S(2)}) collective-permute-start(f32[416,128]{1,0:T(8,128)} %get-tuple-element.44), channel_id=1, source_target_pairs={{3,6},{0,13},{1,12},{7,10},{4,1},{5,0},{11,14},{8,5},{9,4},{15,2},... | collective-permute-start | bytes 638984 | tf_op jit(solution)/shard_map/ppermute | solution.py:342
  40.8 2.7 %collective-permute-start.2 = (f32[416,128]{1,0:T(8,128)}, f32[416,128]{1,0:T(8,128)S(1)}, u32[]{:S(2)}, u32[]{:S(2)}) collective-permute-start(f32[416,128]{1,0:T(8,128)} %get-tuple-element.44), channel_id=1, source_target_pairs={{3,4},{0,15},{1,14},{7,8},{4,3},{5,2},{11,12},{8,7},{9,6},{15,0},{... | collective-permute-start | bytes 638984 | tf_op jit(solution)/shard_map/ppermute | solution.py:342
  43.5 0.8 constant_dynamic-update-slice_fusion.3
  44.4 3.7 %copy-done = f32[1536,1536]{1,0:T(8,128)S(1)} copy-done((f32[1536,1536]{1,0:T(8,128)S(1)}, f32[1536,1536]{1,0:T(8,128)}, u32[]{:S(2)}) %copy-start) | copy-done | bytes 9437208
  48.0 1.5 %copy-done.2 = bf16[1536,640]{1,0:T(8,128)(2,1)S(1)} copy-done((bf16[1536,640]{1,0:T(8,128)(2,1)S(1)}, bf16[1536,640]{1,0:T(8,128)(2,1)}, u32[]{:S(2)}) %copy-start.2) | copy-done | bytes 1966104
  49.6 2.3 %shard_map.79 = (f32[384,128]{1,0:T(8,128)S(1)}, f32[384,384]{1,0:T(8,128)S(1)}) custom-call(s32[2]{0:T(128)S(1)} %pad_add_fusion.pos, bf16[1536,640]{1,0:T(8,128)(2,1)S(1)} %copy-done.2, f32[1536,1536]{1,0:T(8,128)S(1)} %copy-done), custom_call_target="tpu_custom_call" | custom-call | tf_op jit(solution)/shard_map/pallas_call | solution.py:24
  51.8 0.0 copy-start.11
  51.9 2.3 %shard_map.80 = (f32[384,128]{1,0:T(8,128)S(1)}, f32[384,384]{1,0:T(8,128)S(1)}) custom-call(s32[2]{0:T(128)S(1)} %pad_add_fusion.pos, bf16[1536,640]{1,0:T(8,128)(2,1)S(1)} %copy-done.2, f32[1536,1536]{1,0:T(8,128)S(1)} %copy-done), custom_call_target="tpu_custom_call" | custom-call | tf_op jit(solution)/shard_map/pallas_call | solution.py:24
  54.1 0.0 copy-done.11
  54.1 0.0 copy-start.13
  54.1 0.7 copy-done.13
  54.8 2.3 %shard_map.81 = (f32[384,128]{1,0:T(8,128)S(1)}, f32[384,384]{1,0:T(8,128)S(1)}) custom-call(s32[2]{0:T(128)S(1)} %pad_add_fusion.pos, bf16[1536,640]{1,0:T(8,128)(2,1)S(1)} %copy-done.2, f32[1536,1536]{1,0:T(8,128)S(1)} %copy-done), custom_call_target="tpu_custom_call" | custom-call | tf_op jit(solution)/shard_map/pallas_call | solution.py:24
  57.1 0.0 copy-start.5
  57.1 0.8 copy-done.5
  57.9 0.7 copy-done.15
  58.6 0.0 collective-permute-done.s2
  58.6 0.0 collective-permute-done.3.came_next
  58.6 0.0 collective-permute-done.2.came
  58.6 0.0 all-to-all-done.1.pays
  58.6 0.8 constant_dynamic-update-slice_fusion.2
  59.4 0.7 constant_dynamic-update-slice_fusion.1
  60.1 0.7 constant_dynamic-update-slice_fusion
  60.8 1.6 %slice_dynamic-update-slice_fusion = f32[3328,128]{1,0:T(8,128)} fusion(f32[3328,128]{1,0:T(8,128)} %constant_dynamic-update-slice_fusion, f32[416,128]{1,0:T(8,128)} %get-tuple-element.44), kind=kLoop, calls=%fused_computation | loop fusion | bytes 294912
  62.4 0.6 slice_dynamic-update-slice_fusion.6
  63.0 0.6 slice_dynamic-update-slice_fusion.5
  63.6 0.6 slice_dynamic-update-slice_fusion.4
  64.2 0.6 slice_dynamic-update-slice_fusion.3
  64.8 0.6 slice_dynamic-update-slice_fusion.2
  65.4 0.6 slice_dynamic-update-slice_fusion.1
  66.0 0.0 collective-permute-start.4
  66.0 3.8 %collective-permute-done.4.theirs = f32[3328,128]{1,0:T(8,128)S(1)} collective-permute-done((f32[3328,128]{1,0:T(8,128)}, f32[3328,128]{1,0:T(8,128)S(1)}, u32[]{:S(2)}, u32[]{:S(2)}) %collective-permute-start.4) | collective-permute-done | bytes 1703968 | tf_op jit(solution)/shard_map/ppermute | solution.py:338
  69.8 0.0 copy-done.10
  69.8 1.2 %shard_map.82 = (bf16[672,768]{1,0:T(8,128)(2,1)S(1)}, bf16[512,512]{1,0:T(8,128)(2,1)S(1)}, bf16[704,1024]{1,0:T(8,128)(2,1)S(1)}, bf16[256,128]{1,0:T(8,128)(2,1)S(1)}, bf16[256,128]{1,0:T(8,128)(2,1)S(1)}) custom-call(s32[2]{0:T(128)S(1)} %pad_add_fusion.pos, f32[48,768]{1,0:T(8,128)S(1)} %copy-done.10, f32[48,768]{1,0:T(8,128)S(1)} %collective-permute-done.1.c2, ...), custom_call_target="tpu_custom_call" | custom-call | tf_op jit(solution)/shard_map/pallas_call | solution.py:24
  71.1 2.8 %shard_map.83 = (f32[352,128]{1,0:T(8,128)S(1)}, f32[128,128]{1,0:T(8,128)S(1)}, f32[128,128]{1,0:T(8,128)S(1)}, f32[4,96,128]{2,1,0:T(8,128)S(1)}) custom-call(s32[2]{0:T(128)S(1)} %pad_add_fusion.pos, f32[4,96,128]{2,1,0:T(8,128)S(1)} %all-to-all-done.1.pays, bf16[672,768]{1,0:T(8,128)(2,1)S(1)} %get-tuple-element.59.solver, ...), custom_call_target="tpu_custom_call" | custom-call | tf_op jit(solution)/shard_map/pallas_call | solution.py:24
  73.8 10.9 %all_to_all.26.pays = f32[4,96,128]{2,1,0:T(8,128)S(1)} all-to-all(f32[4,96,128]{2,1,0:T(8,128)S(1)} %get-tuple-element.65), channel_id=1, replica_groups={{0,4,8,12},{1,5,9,13},{2,6,10,14},{3,7,11,15},{16,20,24,28},{17,21,25,2..., dimensions={0} | all-to-all | bytes 393216 | tf_op jit(solution)/shard_map/all_to_all | solution.py:350
  84.7 2.8 %shard_map.84 = (f32[352,128]{1,0:T(8,128)S(1)}, f32[128,128]{1,0:T(8,128)S(1)}, f32[128,128]{1,0:T(8,128)S(1)}, f32[4,96,128]{2,1,0:T(8,128)S(1)}) custom-call(s32[2]{0:T(128)S(1)} %pad_add_fusion.pos, f32[4,96,128]{2,1,0:T(8,128)S(1)} %all_to_all.26.pays, bf16[672,768]{1,0:T(8,128)(2,1)S(1)} %get-tuple-element.59.solver, ...), custom_call_target="tpu_custom_call" | custom-call | tf_op jit(solution)/shard_map/pallas_call | solution.py:24
  87.4 10.2 %all_to_all.27.pays = f32[4,96,128]{2,1,0:T(8,128)S(1)} all-to-all(f32[4,96,128]{2,1,0:T(8,128)S(1)} %get-tuple-element.69), channel_id=1, replica_groups={{0,4,8,12},{1,5,9,13},{2,6,10,14},{3,7,11,15},{16,20,24,28},{17,21,25,2..., dimensions={0} | all-to-all | bytes 393216 | tf_op jit(solution)/shard_map/all_to_all | solution.py:350
  97.6 2.7 %shard_map.85 = f32[4,120,128]{2,1,0:T(8,128)} custom-call(s32[2]{0:T(128)S(1)} %pad_add_fusion.pos, f32[4,96,128]{2,1,0:T(8,128)S(1)} %all_to_all.27.pays, bf16[672,768]{1,0:T(8,128)(2,1)S(1)} %get-tuple-element.59.solver, bf16[512,512]{1,0:T(8,128)(2,1)S(1)} %get-tuple-element.60.cross, bf16[704,1024]{1,0:T(8,128)(2,1)S(1)} %get-tuple-element.61.own, ...), custom_call_target="tpu_custom_call" | custom-call | tf_op jit(solution)/shard_map/pallas_call | solution.py:24
  100.3 3.7 %all-to-all-start.4 = ((f32[4,120,128]{2,1,0:T(8,128)}), f32[4,120,128]{2,1,0:T(8,128)S(1)}, u32[]{:S(2)}, u32[]{:S(2)}) async-start(f32[4,120,128]{2,1,0:T(8,128)} %shard_map.85), calls=%async_computation.4 | async-start | bytes 491520 | tf_op jit(solution)/shard_map/all_to_all | solution.py:346
  104.1 3.7 %copy-done.1 = f32[1536,1536]{1,0:T(8,128)S(1)} copy-done((f32[1536,1536]{1,0:T(8,128)S(1)}, f32[1536,1536]{1,0:T(8,128)}, u32[]{:S(2)}) %copy-start.1) | copy-done | bytes 9437208
  107.7 2.3 %shard_map.86 = (f32[384,128]{1,0:T(8,128)S(1)}, f32[384,384]{1,0:T(8,128)S(1)}) custom-call(s32[2]{0:T(128)S(1)} %pad_add_fusion.pos, bf16[1536,640]{1,0:T(8,128)(2,1)S(1)} %copy-done.3, f32[1536,1536]{1,0:T(8,128)S(1)} %copy-done.1), custom_call_target="tpu_custom_call" | custom-call | tf_op jit(solution)/shard_map/pallas_call | solution.py:24
  110.0 0.8 copy-done.7
  110.9 0.7 copy-done.17
  111.5 0.0 all-to-all-done.4.pieces
  111.5 1.1 copy-done.6
  112.6 1.1 copy-done.8
  113.7 0.9 copy-done.12
  114.6 0.9 copy-done.14
  115.5 0.9 copy-done.16
  116.4 0.9 copy-done.18
  117.4 2.6 %shard_map.87 = (f32[1536,128]{1,0:T(8,128)}, f32[128,128]{1,0:T(8,128)}) custom-call(s32[2]{0:T(128)S(1)} %pad_add_fusion.pos, f32[4,120,128]{2,1,0:T(8,128)S(1)} %all-to-all-done.4.pieces, f32[384,128]{1,0:T(8,128)S(1)} %copy-done.12, f32[384,128]{1,0:T(8,128)S(1)} %copy-done.14, f32[384,128]{1,0:T(8,128)S(1)} %copy-done.16, f32[384,128]{1,0:T(8,128)S(1)} %copy-done.18, ...), custom_call_target="tpu_custom_call" | custom-call | tf_op jit(solution)/shard_map/pallas_call | solution.py:24
  (20 shorter events, 0.0 us)
Async XLA Ops:
  0.6 14.6 %collective-permute-start.1 = (f32[48,768]{1,0:T(8,128)}, f32[48,768]{1,0:T(8,128)S(1)}, u32[]{:S(2)}, u32[]{:S(2)}) collective-permute-start(f32[48,768]{1,0:T(8,128)} %c0.1), channel_id=1, source_target_pairs={{0,2},{1,3},{2,0},{3,1},{4,6},{5,7},{6,4},{7,5},{8,10},{9,11},{10,... | collective-permute-start | bytes 442376 | tf_op jit(solution)/shard_map/ppermute | solution.py:338
  3.7 1.1 copy-start.4
  4.9 0.9 copy-start.9
  5.8 0.7 copy-start.19
  6.5 0.7 copy-start.20
  7.1 0.7 copy-start.21
  15.1 43.5 %collective-permute-start = (f32[960,128]{1,0:T(8,128)S(1)}, f32[960,128]{1,0:T(8,128)S(1)}, u32[]{:S(2)}, u32[]{:S(2)}) collective-permute-start(f32[960,128]{1,0:T(8,128)S(1)} %get-tuple-element.39.s0), channel_id=1, source_target_pairs={{0,2},{1,3},{2,0},{3,1},{4,6},{5,7},{6,4},{7,5},{8,10},{9,11},{10,... | collective-permute-start | bytes 1474568 | tf_op jit(solution)/shard_map/ppermute | solution.py:338
  31.3 27.3 %all-to-all-start.1 = ((f32[4,96,128]{2,1,0:T(8,128)}), f32[4,96,128]{2,1,0:T(8,128)S(1)}, u32[]{:S(2)}, u32[]{:S(2)}) async-start(f32[4,96,128]{2,1,0:T(8,128)} %get-tuple-element.43), calls=%async_computation.1 | async-start | bytes 393216 | tf_op jit(solution)/shard_map/all_to_all | solution.py:350
  36.2 22.4 %collective-permute-start.3 = (f32[416,128]{1,0:T(8,128)}, f32[416,128]{1,0:T(8,128)S(1)}, u32[]{:S(2)}, u32[]{:S(2)}) collective-permute-start(f32[416,128]{1,0:T(8,128)} %get-tuple-element.44), channel_id=1, source_target_pairs={{3,6},{0,13},{1,12},{7,10},{4,1},{5,0},{11,14},{8,5},{9,4},{15,2},... | collective-permute-start | bytes 638984 | tf_op jit(solution)/shard_map/ppermute | solution.py:342
  40.8 17.7 %collective-permute-start.2 = (f32[416,128]{1,0:T(8,128)}, f32[416,128]{1,0:T(8,128)S(1)}, u32[]{:S(2)}, u32[]{:S(2)}) collective-permute-start(f32[416,128]{1,0:T(8,128)} %get-tuple-element.44), channel_id=1, source_target_pairs={{3,4},{0,15},{1,14},{7,8},{4,3},{5,2},{11,12},{8,7},{9,6},{15,0},{... | collective-permute-start | bytes 638984 | tf_op jit(solution)/shard_map/ppermute | solution.py:342
  44.4 3.7 %copy-start = (f32[1536,1536]{1,0:T(8,128)S(1)}, f32[1536,1536]{1,0:T(8,128)}, u32[]{:S(2)}) copy-start(f32[1536,1536]{1,0:T(8,128)} %k_ref.9) | copy-start | bytes 28311556
  48.0 1.5 %copy-start.2 = (bf16[1536,640]{1,0:T(8,128)(2,1)S(1)}, bf16[1536,640]{1,0:T(8,128)(2,1)}, u32[]{:S(2)}) copy-start(bf16[1536,640]{1,0:T(8,128)(2,1)} %get-tuple-element.73.right_side) | copy-start | bytes 5898244
  51.8 2.3 %copy-start.11 = (f32[384,128]{1,0:T(8,128)}, f32[384,128]{1,0:T(8,128)S(1)}, u32[]{:S(2)}) copy-start(f32[384,128]{1,0:T(8,128)S(1)} %get-tuple-element.47.refs_0_) | copy-start | bytes 589828
  54.1 0.7 copy-start.13
  57.1 0.8 copy-start.5
  57.9 0.7 copy-start.15
  58.6 11.3 %copy-start.10 = (f32[48,768]{1,0:T(8,128)S(1)}, f32[48,768]{1,0:T(8,128)}, u32[]{:S(2)}) copy-start(f32[48,768]{1,0:T(8,128)} %c0.1) | copy-start | bytes 442372
  66.0 3.8 %collective-permute-start.4 = (f32[3328,128]{1,0:T(8,128)}, f32[3328,128]{1,0:T(8,128)S(1)}, u32[]{:S(2)}, u32[]{:S(2)}) collective-permute-start(f32[3328,128]{1,0:T(8,128)} %slice_dynamic-update-slice_fusion.1), channel_id=1, source_target_pairs={{0,1},{1,0},{2,3},{3,2},{4,5},{5,4},{6,7},{7,6},{8,9},{9,8},{10,11... | collective-permute-start | bytes 5111816 | tf_op jit(solution)/shard_map/ppermute | solution.py:338
  97.6 6.4 %copy-start.3 = (bf16[1536,640]{1,0:T(8,128)(2,1)S(1)}, bf16[1536,640]{1,0:T(8,128)(2,1)}, u32[]{:S(2)}) copy-start(bf16[1536,640]{1,0:T(8,128)(2,1)} %get-tuple-element.73.right_side) | copy-start | bytes 5898244
  100.3 11.2 %all-to-all-start.4 = ((f32[4,120,128]{2,1,0:T(8,128)}), f32[4,120,128]{2,1,0:T(8,128)S(1)}, u32[]{:S(2)}, u32[]{:S(2)}) async-start(f32[4,120,128]{2,1,0:T(8,128)} %shard_map.85), calls=%async_computation.4 | async-start | bytes 491520 | tf_op jit(solution)/shard_map/all_to_all | solution.py:346
  104.1 3.7 %copy-start.1 = (f32[1536,1536]{1,0:T(8,128)S(1)}, f32[1536,1536]{1,0:T(8,128)}, u32[]{:S(2)}) copy-start(f32[1536,1536]{1,0:T(8,128)} %k_ref.9) | copy-start | bytes 28311556
  110.0 0.8 copy-start.7
  110.9 0.7 copy-start.17
  111.5 1.1 copy-start.6
  112.6 1.1 copy-start.8
  113.7 0.9 copy-start.12
  114.6 0.9 copy-start.14
  115.5 0.9 copy-start.16
  116.4 0.9 copy-start.18

commit v4 on v3

v4 whole, which is shorter than its diff:
```python
import functools

import jax
import jax.numpy as jnp
from jax import lax
from jax.experimental import pallas as pl
from jax.experimental.pallas import tpu as pltpu
from jax.sharding import PartitionSpec as P

ITERS = 3
DAMPING = 0.5
GROUP = 4
LANES = 128
BF16 = jnp.bfloat16
F32 = jnp.float32


def call(kernel, outs, args, smem=1, hbm=(), scratch=(), vmem=24):
    in_specs = [
        pl.BlockSpec(memory_space=pltpu.SMEM if i < smem else pltpu.HBM if i in hbm else pltpu.VMEM)
        for i in range(len(args))
    ]
    shapes = [o if isinstance(o[0], tuple) else (o, F32) for o in outs]
    return pl.pallas_call(
        kernel,
        out_shape=[jax.ShapeDtypeStruct(s, d) for s, d in shapes],
        in_specs=in_specs,
        out_specs=[pl.BlockSpec(memory_space=pltpu.VMEM)] * len(shapes),
        scratch_shapes=list(scratch),
        compiler_params=pltpu.CompilerParams(vmem_limit_bytes=vmem * 1024 * 1024),
    )(*args)


def halves(x):
    high = x.astype(BF16)
    return high, (x - high.astype(F32)).astype(BF16)


def dot(a, b):
    return jnp.dot(a, b, preferred_element_type=F32)


def product(a, b):
    ah, al = halves(a)
    bh, bl = halves(b)
    n = b.shape[1]
    both = dot(ah, jnp.concatenate([bh, bl], axis=1))
    return both[:, :n] + both[:, n:] + dot(al, bh)


def lane_block(rows):
    return lax.broadcasted_iota(jnp.int32, (rows, LANES), 1) // (LANES // GROUP)


def turned(x, blocks):
    width = LANES // GROUP
    if isinstance(blocks, int):
        shift = (blocks % GROUP) * width
        return x if shift == 0 else pltpu.roll(x, shift, 1)
    return pltpu.roll(x, lax.rem(blocks + 2 * GROUP, GROUP) * width, 1)


def cut(x, member, out_refs):
    rows = x.shape[0] // GROUP
    block = lane_block(rows)
    parts = [x[q * rows:(q + 1) * rows] for q in range(GROUP)]
    for k, out in enumerate(out_refs):
        to = member ^ k
        packed = jnp.zeros((rows, LANES), F32)
        for q in range(GROUP):
            packed = jnp.where(block == q, turned(parts[q], q - to), packed)
        out[...] = packed


def joined(pieces, member):
    rows = pieces[0].shape[0]
    block = lane_block(rows)
    out = []
    for q in range(GROUP):
        part = jnp.zeros((rows, LANES), F32)
        for k, piece in enumerate(pieces):
            came = member ^ k
            part = jnp.where(block == came, turned(piece, came - q), part)
        out.append(part)
    return jnp.concatenate(out, axis=0)


def packed(x, chunk):
    first = lane_block(chunk) == 0
    out = None
    for q in range(x.shape[0] // chunk):
        part = turned(jnp.where(first, x[q * chunk:(q + 1) * chunk], 0.0), q)
        out = part if out is None else out + part
    return out


def unpacked(x, count):
    return jnp.concatenate([turned(x, -q) for q in range(count)], axis=0)


def chunk_of(owned):
    return -(-owned // (GROUP * 8)) * 8


def stacked(x):
    return jnp.concatenate(halves(x), axis=0)


def beside(x):
    return jnp.concatenate(halves(x), axis=1)


def combined(p, n):
    m = p.shape[0] // 2
    return p[:m, :n] + p[:m, n:] + p[m:, :n]


def payload(v, width, out, out_up, out_down):
    coarse = v[2 * width:]
    owned = coarse.shape[0] // 2
    below = turned(coarse[owned:], 1)
    own = coarse[:owned] + jnp.where(lane_block(owned) == 0, 0.0, below)
    rows = jnp.concatenate([own, packed(below, chunk_of(owned))], axis=0)
    size = rows.shape[0]
    for ref in (out, out_up, out_down):
        ref[:size] = rows
    out_up[size:] = packed(turned(v[width:2 * width], 1), width // GROUP)
    out_down[size:] = packed(v[:width], width // GROUP)


def fetch(source, count, rows, target, places, sem):
    def one(j, carry):
        pltpu.make_async_copy(source.at[pl.ds(rows(j), 1)], target.at[pl.ds(places(j), 1)], sem).start()
        return carry

    lax.fori_loop(0, count, one, 0, unroll=8)


def rows_kernel(pos, face, prim, slot, k_ref, f_ref, facev, primv, slotv, *rest):
    pieces, (spans, edge, places, ks, right_side, sem) = rest[:GROUP], rest[GROUP:]
    width, count, order, columns = face.shape[1], prim.shape[1], ks.shape[1], f_ref.shape[1]
    side = 2 * width
    fetch(k_ref, count, lambda j: prim[0, j], ks, lambda j: side + slot[0, j], sem)
    fetch(k_ref, side, lambda j: face[j // width, j % width], ks, lambda j: j, sem)

    def indicator(row):
        place = lax.broadcasted_iota(jnp.int32, (order, row.shape[1]), 0).astype(F32)
        return jnp.where(place == row, 1.0, 0.0).astype(BF16)

    slots = jnp.broadcast_to(slotv[...].astype(F32), (count, count)).T
    prims = jnp.broadcast_to(primv[...].astype(F32), (count, count)).T
    wanted = lax.broadcasted_iota(jnp.int32, (count, count), 1).astype(F32)
    by_slot = jnp.sum(jnp.where(slots == wanted, prims, 0.0), axis=0, keepdims=True)
    right_side[:, :width] = indicator(facev[0:1].astype(F32))
    right_side[:, width:side] = indicator(facev[1:2].astype(F32))
    right_side[:, side:side + count] = indicator(by_slot)
    right_side[:, side + count:side + width] = jnp.zeros((order, width - count), BF16)
    right_side[:, side + width:] = beside(f_ref[...])
    places[...] = right_side[:, :side + width]
    pltpu.make_async_copy(k_ref.at[pl.ds(0, ks.shape[0])], ks, sem).wait()

    at = side + width
    high, low = halves(ks[...])
    both = dot(high, right_side[...])
    part = dot(low, right_side[:, :at + columns])
    cut(both[:, at:at + columns] + both[:, at + columns:] + part[:, at:], pos[0], pieces)
    block = both[:, :at] + part[:, :at]
    rows = side + count
    for i in range(3):
        kept = side if i == 2 else rows
        spans[i * rows:i * rows + kept] = block[:kept, i * width:(i + 1) * width]
    edge[...] = jnp.where(pos[0] == GROUP - 1, block[width:side, side:], block[:width, side:])


GOT = (-1, None, 5, 4)
GOT_NEXT = (5, 4, -1, None)


GOT = (-1, None, 5, 4)
GOT_NEXT = (5, 4, -1, None)


def solver_kernel(pos, mine, next_mine, got, next_got, theirs, out):
    owned = mine.shape[0]
    half = out.shape[0] // 2
    other = [theirs[i * owned:(i + 1) * owned] for i in range(4)]
    for m in range(GROUP):

        @pl.when(pos[0] == m)
        def _():
            p = m ^ 1
            held = [(m, mine[...]), (m ^ 2, next_mine[...]), (GOT[m], got[...]), (GOT_NEXT[m], next_got[...])]
            held += list(zip((p, p ^ 2, GOT[p], GOT_NEXT[p]), other))
            for block, values in held:
                if block is not None:
                    at = (block + 1) * owned
                    high, low = halves(values)
                    out[at:at + owned] = high
                    out[half + at:half + at + owned] = low


def blocks_kernel(width, pos, s0, s2, came, came_next, theirs, cross, own, edge_up, edge_down):
    side, size = 2 * width, s0.shape[0]
    kept = (size - side) // 2
    other, at = [], 0
    for rows in (size, size, width, width):
        other.append(theirs.at[at:at + rows])
        at += rows
    for k, ref in enumerate((s0, other[0], s2, other[1])):
        own[:, k * side:k * side + width] = stacked(ref[:kept])
        own[:, k * side + width:(k + 1) * side] = stacked(ref[kept:2 * kept])
        cross[:, k * width:(k + 1) * width] = stacked(ref[2 * kept:])
    for m in range(GROUP):

        @pl.when(pos[0] == m)
        def _():
            held = {GOT[m]: came, GOT_NEXT[m]: came_next}
            for block, ref in zip((GOT[m ^ 1], GOT_NEXT[m ^ 1]), other[2:]):
                held.setdefault(block, ref)
            edge_up[...] = stacked(held[-1][...])
            edge_down[...] = stacked(held[4][...])


def start_kernel(pos, p0, p1, p2, p3, v_ref, *pays):
    v = joined([p0[...], p1[...], p2[...], p3[...]], pos[0])
    v_ref[...] = v
    payload(v, v.shape[1], *pays)


def shared(x, member):
    block = lane_block(x.shape[0])
    high, low = halves(x)
    high, low = high.astype(F32), low.astype(F32)
    out = []
    for k in range(GROUP):
        mine = block == (member ^ k)
        pair = [jnp.where(mine, half, 0.0).astype(BF16) for half in (high, low)]
        out.append(jnp.concatenate(pair, axis=1))
    return jnp.concatenate(out, axis=0)


def turn_kernel(kind, groups, pos, *refs):
    pays, (solver, cross, own, edge_up, edge_down, v0), refs = refs[:groups], refs[groups:groups + 6], refs[groups + 6:]
    if kind == "first":
        now = v0
    else:
        (now, left_ref, right_ref), refs = refs[:3], refs[3:]
    outs, stack = refs[:-1], refs[-1]
    member, group = pos[0], pos[1]
    width = edge_down.shape[1]
    owned = (v0.shape[0] - 2 * width) // 2
    size = owned + chunk_of(owned)
    first = lane_block(owned) == 0

    for k in range(groups):
        h = lax.rem(group - k + groups, groups)
        extra = unpacked(pays[(k + 1) % groups][owned:size, :], -(-owned // chunk_of(owned)))[:owned]
        whole = pays[k][:owned, :] + jnp.where(first, extra, 0.0)
        for i in range(GROUP):
            place = pl.multiple_of((h * GROUP + i) * owned, 16)
            stack[pl.ds(place, owned), :] = beside(turned(whole, -i))

    w = combined(dot(solver[...], stack[...]), LANES)
    pair = lane_block(2 * owned)
    q = w[owned:3 * owned]
    for i in range(1, GROUP):
        q = jnp.where(pair == i, turned(w[(i + 1) * owned:(i + 3) * owned], i), q)
    filler = jnp.zeros((width - 2 * owned, LANES), F32)

    def padded(x):
        return jnp.concatenate([x, filler], axis=0)

    faces = now[:2 * width] - combined(dot(cross[...], shared(padded(q), member)), LANES)
    left, right = faces[:width], faces[width:]
    before, after = beside(padded(w[:2 * owned])), beside(padded(w[(GROUP + 1) * owned:]))
    halo_up, halo_down = pays[1][size:, :], pays[groups - 1][size:, :]
    right_before = unpacked(halo_up, GROUP) - combined(dot(edge_up[...], before), LANES)
    left_after = unpacked(halo_down, GROUP) - combined(dot(edge_down[...], after), LANES)
    block = lane_block(width)
    beyond = jnp.where(block == GROUP - 1, turned(left_after, GROUP - 1), turned(left, -1))
    behind = jnp.where(block == 0, right_before, turned(right, 1))
    lam_right = DAMPING * (right - beyond)
    lam_left = DAMPING * (behind - left)
    if kind != "first":
        lam_right = lam_right + right_ref[...]
        lam_left = lam_left + left_ref[...]
    if kind == "last":
        cut(jnp.concatenate([q, lam_right, left_ref[...], right_ref[...]], axis=0), member, outs)
        return
    v_ref, left_out, right_out = outs[:3]
    left_out[...] = lam_left
    right_out[...] = lam_right
    lam = jnp.concatenate([lam_left, -lam_right], axis=0)
    v = v0[...] + combined(dot(own[...], shared(lam, member)), LANES)
    v_ref[...] = v
    payload(v, width, *outs[3:])


def final_kernel(count, pos, p0, p1, p2, p3, f_ref, places, k_ref, out, lam_ref):
    x = joined([p0[...], p1[...], p2[...], p3[...]], pos[0])
    width = lam_ref.shape[0]
    lam_ref[...] = x[count:count + width]
    at = count + width
    filler = jnp.zeros((width - count, LANES), F32)
    change = beside(jnp.concatenate([x[at:at + width], -x[at + width:], -x[:count], filler], axis=0))
    both = dot(places[...], change)
    loads = beside(f_ref[...] + both[:, :LANES] + both[:, LANES:])
    order = k_ref.shape[0]
    rows = 256 if order % 256 == 0 else order
    for at in range(0, order, rows):
        high, low = halves(k_ref[at:at + rows])
        part = dot(high, loads)
        out[at:at + rows] = part[:, :LANES] + part[:, LANES:] + dot(low, loads[:, :LANES])


def local(condensed, eigen_loads, coarse_inverse, face_rows, primal_rows, primal_slot):
    order, columns = eigen_loads.shape
    owned, coarse = coarse_inverse.shape
    width = face_rows.shape[2]
    side, count = 2 * width, 2 * owned
    kept = side + count
    total = lax.axis_size("sub")
    groups = total // GROUP
    me = lax.axis_index("sub")
    pos = jnp.stack([me % GROUP, me // GROUP]).astype(jnp.int32)
    faces = face_rows[0]

    def mate(x, k):
        return lax.ppermute(x, "sub", [(s, s ^ k) for s in range(total)])

    def crossing(x, pairs):
        pairs = [(g * GROUP + a, (g * GROUP + b) % total) for g in range(groups) for a, b in pairs]
        return lax.ppermute(x, "sub", pairs)

    def traded(pieces):
        return [pieces[0]] + [mate(pieces[k], k) for k in range(1, GROUP)]

    def planes(x, by):
        return lax.ppermute(x, "sub", [(s, (s + by * GROUP) % total) for s in range(total)])

    def along(pay, up, down):
        return [pay, planes(up, 1)] + [planes(pay, k) for k in range(2, groups - 1)] + [planes(down, -1)]

    def after(x, other):
        return lax.optimization_barrier((x, other))[0]

    c_next = mate(coarse_inverse, 2)
    got = crossing(coarse_inverse, [(GROUP - 1, GROUP), (0, -1), (1, -2)])
    got_next = crossing(coarse_inverse, [(GROUP - 1, GROUP + 2), (0, -3), (1, -4)])

    *pieces, spans, edge, places = call(
        rows_kernel,
        [(kept // GROUP, LANES)] * GROUP
        + [(2 * kept + side, width), (width, width), ((order, side + width), BF16)],
        (pos, faces, primal_rows, primal_slot, condensed, eigen_loads, faces, primal_rows, primal_slot),
        smem=4,
        hbm=(4,),
        scratch=[
            pltpu.VMEM((kept, order), F32),
            pltpu.VMEM((order, side + width + 2 * columns), BF16),
            pltpu.SemaphoreType.DMA,
        ],
        vmem=52,
    )
    spans_next = mate(spans, 2)
    *pieces, c_next, got, got_next = lax.optimization_barrier((*pieces, c_next, got, got_next))
    pieces = traded(pieces)
    came = crossing(edge, [(GROUP - 1, GROUP), (0, -1)])
    came_next = crossing(after(edge, pieces), [(GROUP - 1, GROUP + 2), (0, -3)])
    theirs_c = mate(after(jnp.concatenate([coarse_inverse, c_next, got, got_next], axis=0), pieces), 1)
    size = owned + chunk_of(owned)
    pay_shapes = [(size, LANES)] + [(size + width // GROUP, LANES)] * 2
    v0, *pays = call(start_kernel, [(kept, LANES), *pay_shapes], (pos, *pieces))
    pays = along(*pays)
    (solver,) = call(
        solver_kernel,
        [((2 * (GROUP + 3) * owned, coarse), BF16)],
        (pos, coarse_inverse, c_next, got, got_next, theirs_c),
    )
    *pays, spans_next, came, came_next = lax.optimization_barrier((*pays, spans_next, came, came_next))
    theirs = mate(jnp.concatenate([spans, spans_next, came, came_next], axis=0), 1)
    blocks = call(
        functools.partial(blocks_kernel, width),
        [
            ((2 * side, GROUP * width), BF16),
            ((2 * kept, GROUP * side), BF16),
            ((side, width), BF16),
            ((side, width), BF16),
        ],
        (pos, spans, spans_next, came, came_next, theirs),
    )

    state = ()
    for step in range(ITERS):
        kind = "first" if step == 0 else "last" if step == ITERS - 1 else "middle"
        shapes = [(kept, LANES), (width, LANES), (width, LANES), *pay_shapes]
        if kind == "last":
            shapes = [((count + 3 * width) // GROUP, LANES)] * GROUP
        outs = call(
            functools.partial(turn_kernel, kind, groups),
            shapes,
            (pos, *pays, solver, *blocks, v0, *state),
            scratch=[pltpu.VMEM((coarse, 2 * LANES), BF16)],
        )
        if kind != "last":
            state = outs[:3]
            pays = along(*outs[3:])
    displaced, multipliers = call(
        functools.partial(final_kernel, count),
        [(order, columns), (width, columns)],
        (pos, *traded(outs), eigen_loads, places, condensed),
    )
    return displaced, multipliers


def solution(mesh):
    placed = (
        P(("rve", "sub"), None),
        P(("rve", "sub"), None),
        P(("rve", "sub"), None),
        P("sub", None, None),
        P("sub", None),
        P("sub", None),
    )
    return jax.shard_map(
        local,
        mesh=mesh,
        in_specs=placed,
        out_specs=(P(("rve", "sub"), None), P(("rve", "sub"), None)),
        check_vma=False,
    )
```

time: 121 us -> 94 us (0.78)
  blocking collectives: 35.6 us -> 0 us
  local copies, waits for them, and re-layouts: 30.7 us -> 3.15 us
  waiting for transfers between devices: 3.82 us -> 28.6 us
  starting transfers between devices: 19 us -> 37.6 us
  Pallas kernels: 30 us -> 23.3 us
    all_to_all x3 -> x0, blocking collectives: 35.6 us -> none  [the longest x2 21 us: along(): return lax.all_to_all(x, 'sub', 0, 0, axis_index_groups=lines)]
    unnamed x54 -> x20, local copies, waits for them, and re-layouts: 30.1 us -> 3.15 us
    ppermute x0 -> x9, waiting for transfers between devices: none -> 14.4 us  [planes(): lax.ppermute(x, 'sub', [(s, (s + by * GROUP) % total) for s in range(tota...]
    ppermute x0 -> x9, starting transfers between devices: none -> 11.6 us  [planes(): lax.ppermute(x, 'sub', [(s, (s + by * GROUP) % total) for s in range(tota...]
    ppermute x2 -> x4, starting transfers between devices: 7.3 us -> 17.7 us  [crossing(): return lax.ppermute(x, 'sub', pairs)]
    ppermute x3 -> x10, waiting for transfers between devices: 3.81 us -> 14.1 us  [mate(): return lax.ppermute(x, 'sub', [(s, s ^ k) for s in range(total)])]
    all_to_all x2 -> x0, starting transfers between devices: 8.6 us -> none  [the longest x1 4.87 us: along(): return lax.all_to_all(x, 'sub', 0, 0, axis_index_groups=lines)]
    pallas_call x11 -> x8, Pallas kernels: 30 us -> 23.3 us  [call(): pl.pallas_call(kernel, out_shape=[jax.ShapeDtypeStruct(s, d) for s, d in...]
  transfers between devices with their start and end apart: 7 -> 23, of which waited for: 1 -> 7; matrix products, arithmetic and copies ran while one was open for 1% -> 0% of each run, Pallas kernels for 15% -> 2%
where the time goes in v4:
time: 94 us; the launch traced here: 93.7 us
  starting transfers between devices  37.6 us (40%)
  waiting for transfers between devices  28.6 us (30%)
  Pallas kernels  23.3 us (25%)
  local copies, waits for them, and re-layouts  3.15 us (3%)
    pallas_call x8, Pallas kernels, call(): pl.pallas_call(kernel, out_shape=[jax.ShapeDtypeStruct(s, d) for s, d in...  23.3 us
    ppermute x4, starting transfers between devices, crossing(): return lax.ppermute(x, 'sub', pairs)  17.7 us
    ppermute x9, waiting for transfers between devices, planes(): lax.ppermute(x, 'sub', [(s, (s + by * GROUP) % total) for s in range(tota...  14.4 us
    ppermute x10, waiting for transfers between devices, mate(): return lax.ppermute(x, 'sub', [(s, s ^ k) for s in range(total)])  14.1 us
    ppermute x9, starting transfers between devices, planes(): lax.ppermute(x, 'sub', [(s, (s + by * GROUP) % total) for s in range(tota...  11.6 us
    ppermute x10, starting transfers between devices, mate(): return lax.ppermute(x, 'sub', [(s, s ^ k) for s in range(total)])  8.3 us
    unnamed x20, local copies, waits for them, and re-layouts  3.15 us
  transfers between devices with their start and end apart: 23, of which 7 were waited for; matrix products, arithmetic and copies ran while one was open for 0% of the time, Pallas kernels for 2%

profile of v4, /device:TPU:0, one launch (start us, length us, event | category | flops | bytes accessed | tf_op | source)
XLA Modules:
  0.0 93.7 jit_solution(6298485913824908729)
XLA Ops:
  0.6 0.1 pad_add_fusion.pos
  0.7 1.1 %copy-done = f32[1536,128]{1,0:T(8,128)S(1)} copy-done((f32[1536,128]{1,0:T(8,128)S(1)}, f32[1536,128]{1,0:T(8,128)}, u32[]{:S(2)}) %copy-start) | copy-done | bytes 786456
  1.9 0.7 copy-done.4
  2.5 0.7 copy-done.5
  3.2 0.7 copy-done.6
  3.9 7.7 %shard_map.77 = (f32[88,128]{1,0:T(8,128)S(1)}, f32[88,128]{1,0:T(8,128)S(1)}, f32[88,128]{1,0:T(8,128)S(1)}, f32[88,128]{1,0:T(8,128)S(1)}, f32[960,128]{1,0:T(...) custom-call(s32[2]{0:T(128)S(1)} %pad_add_fusion.pos, s32[2,128]{1,0:T(2,128)S(1)} %bitcast.5, ...), custom_call_target="tpu_custom_call" | custom-call | tf_op jit(solution)/shard_map/pallas_call | solution.py:24
  11.5 3.0 %collective-permute-start.9 = (f32[960,128]{1,0:T(8,128)S(1)}, f32[960,128]{1,0:T(8,128)S(1)}, u32[]{:S(2)}, u32[]{:S(2)}) collective-permute-start(f32[960,128]{1,0:T(8,128)S(1)} %get-tuple-element.60.s0), channel_id=1, source_target_pairs={{0,2},{1,3},{2,0},{3,1},{4,6},{5,7},{6,4},{7,5},{8,10},{9,11},{10,... | collective-permute-start | bytes 1474568 | tf_op jit(solution)/shard_map/ppermute | solution.py:329
  14.6 0.0 copy-done.3
  14.6 0.1 collective-permute-start
  14.6 5.8 %collective-permute-start.1 = (f32[48,768]{1,0:T(8,128)S(1)}, f32[48,768]{1,0:T(8,128)S(1)}, u32[]{:S(2)}, u32[]{:S(2)}) collective-permute-start(f32[48,768]{1,0:T(8,128)S(1)} %copy-done.3), channel_id=1, source_target_pairs={{3,4},{0,15},{1,14},{7,8},{4,3},{5,2},{11,12},{8,7},{9,6},{15,0},{... | collective-permute-start | bytes 442376 | tf_op jit(solution)/shard_map/ppermute | solution.py:333
  20.4 3.2 %collective-permute-start.2 = (f32[48,768]{1,0:T(8,128)S(1)}, f32[48,768]{1,0:T(8,128)S(1)}, u32[]{:S(2)}, u32[]{:S(2)}) collective-permute-start(f32[48,768]{1,0:T(8,128)S(1)} %copy-done.3), channel_id=1, source_target_pairs={{3,6},{0,13},{1,12},{7,10},{4,1},{5,0},{11,14},{8,5},{9,4},{15,2},... | collective-permute-start | bytes 442376 | tf_op jit(solution)/shard_map/ppermute | solution.py:333
  23.6 7.7 %collective-permute-done.next_mine = f32[48,768]{1,0:T(8,128)S(1)} collective-permute-done((f32[48,768]{1,0:T(8,128)S(1)}, f32[48,768]{1,0:T(8,128)S(1)}, u32[]{:S(2)}, u32[]{:S(2)}) %collective-permute-start) | collective-permute-done | bytes 147488 | tf_op jit(solution)/shard_map/ppermute | solution.py:329
  31.4 0.0 collective-permute-done.1.got
  31.4 0.0 collective-permute-done.2.next_got
  31.4 0.0 collective-permute-start.3
  31.4 2.5 %collective-permute-start.4 = (f32[88,128]{1,0:T(8,128)S(1)}, f32[88,128]{1,0:T(8,128)S(1)}, u32[]{:S(2)}, u32[]{:S(2)}) collective-permute-start(f32[88,128]{1,0:T(8,128)S(1)} %get-tuple-element.55), channel_id=1, source_target_pairs={{0,2},{1,3},{2,0},{3,1},{4,6},{5,7},{6,4},{7,5},{8,10},{9,11},{10,... | collective-permute-start | bytes 135176 | tf_op jit(solution)/shard_map/ppermute | solution.py:329
  33.9 0.1 collective-permute-start.5
  34.0 6.6 %collective-permute-start.10 = (f32[128,128]{1,0:T(8,128)S(1)}, f32[128,128]{1,0:T(8,128)S(1)}, u32[]{:S(2)}, u32[]{:S(2)}) collective-permute-start(f32[128,128]{1,0:T(8,128)S(1)} %get-tuple-element.62), channel_id=1, source_target_pairs={{3,4},{0,15},{7,8},{4,3},{11,12},{8,7},{15,0},{12,11},{19,20},{16,... | collective-permute-start | bytes 196616 | tf_op jit(solution)/shard_map/ppermute | solution.py:333
  40.6 0.0 collective-permute-done.3.p1
  40.6 0.0 collective-permute-done.4.p2
  40.6 0.0 collective-permute-done.5.p3
  40.6 2.2 %collective-permute-start.11 = (f32[128,128]{1,0:T(8,128)S(1)}, f32[128,128]{1,0:T(8,128)S(1)}, u32[]{:S(2)}, u32[]{:S(2)}) collective-permute-start(f32[128,128]{1,0:T(8,128)S(1)} %get-tuple-element.62), channel_id=1, source_target_pairs={{3,6},{0,13},{7,10},{4,1},{11,14},{8,5},{15,2},{12,9},{19,22},{16,... | collective-permute-start | bytes 196616 | tf_op jit(solution)/shard_map/ppermute | solution.py:333
  42.8 0.9 shard_map.78
  43.7 0.1 collective-permute-start.6
  43.8 3.8 %collective-permute-start.8 = (f32[96,128]{1,0:T(8,128)S(1)}, f32[96,128]{1,0:T(8,128)S(1)}, u32[]{:S(2)}, u32[]{:S(2)}) collective-permute-start(f32[96,128]{1,0:T(8,128)S(1)} %get-tuple-element.59), channel_id=1, source_target_pairs={{0,12},{1,13},{2,14},{3,15},{4,0},{5,1},{6,2},{7,3},{8,4},{9,5},{1... | collective-permute-start | bytes 147464 | tf_op jit(solution)/shard_map/ppermute | solution.py:339
  47.6 0.0 collective-permute-done.10.came
  47.6 0.0 collective-permute-start.7
  47.6 4.8 %collective-permute-done.7.refs_2_ = f32[64,128]{1,0:T(8,128)S(1)} collective-permute-done((f32[64,128]{1,0:T(8,128)S(1)}, f32[64,128]{1,0:T(8,128)S(1)}, u32[]{:S(2)}, u32[]{:S(2)}) %collective-permute-start.7) | collective-permute-done | bytes 32800 | tf_op jit(solution)/shard_map/ppermute | solution.py:339
  52.4 0.0 collective-permute-done.6.refs_1_
  52.4 0.0 collective-permute-done.8.refs_3_
  52.4 0.0 collective-permute-done.11.came_next
  52.4 0.0 collective-permute-done.9.s2
  52.5 0.1 pad_maximum_fusion
  52.5 0.1 collective-permute-start.13
  52.7 0.6 collective-permute-start.12
  53.2 3.0 %collective-permute-done.12.theirs = f32[192,768]{1,0:T(8,128)S(1)} collective-permute-done((f32[192,768]{1,0:T(8,128)S(1)}, f32[192,768]{1,0:T(8,128)S(1)}, u32[]{:S(2)}, u32[]{:S(2)}) %collective-permute-start.12) | collective-permute-done | bytes 589856 | tf_op jit(solution)/shard_map/ppermute | solution.py:329
  56.2 0.7 shard_map.79.refs_4_
  56.9 0.0 collective-permute-done.13.theirs
  56.9 1.1 %shard_map.80 = (bf16[512,512]{1,0:T(8,128)(2,1)S(1)}, bf16[704,1024]{1,0:T(8,128)(2,1)S(1)}, bf16[256,128]{1,0:T(8,128)(2,1)S(1)}, bf16[256,128]{1,0:T(8,128)(2,1)S(1)}) custom-call(s32[2]{0:T(128)S(1)} %pad_add_fusion.pos, f32[960,128]{1,0:T(8,128)S(1)} %get-tuple-element.60.s0, f32[960,128]{1,0:T(8,128)S(1)} %collective-permute-done.9.s2, ...), custom_call_target="tpu_custom_call" | custom-call | tf_op jit(solution)/shard_map/pallas_call | solution.py:24
  58.0 0.0 slice-start.2
  58.0 2.8 %shard_map.81 = (f32[352,128]{1,0:T(8,128)S(1)}, f32[128,128]{1,0:T(8,128)S(1)}, f32[128,128]{1,0:T(8,128)S(1)}, f32[64,128]{1,0:T(8,128)S(1)}, f32[96,128]{1,0:T(8,128)S(1)}, /*index=5*/f32[96,128]{1,0:T(8,128)S(1)}) custom-call(s32[2]{0:T(128)S(1)} %pad_add_fusion.pos, f32[64,128]{1,0:T(8,128)S(1)} %get-tuple-element.63.refs_0_, ...), custom_call_target="tpu_custom_call" | custom-call | tf_op jit(solution)/shard_map/pallas_call | solution.py:24
  60.8 0.0 collective-permute-start.14
  60.9 3.8 %collective-permute-start.16 = (f32[96,128]{1,0:T(8,128)S(1)}, f32[96,128]{1,0:T(8,128)S(1)}, u32[]{:S(2)}, u32[]{:S(2)}) collective-permute-start(f32[96,128]{1,0:T(8,128)S(1)} %get-tuple-element.81), channel_id=1, source_target_pairs={{0,12},{1,13},{2,14},{3,15},{4,0},{5,1},{6,2},{7,3},{8,4},{9,5},{1... | collective-permute-start | bytes 147464 | tf_op jit(solution)/shard_map/ppermute | solution.py:339
  64.7 0.0 collective-permute-start.15
  64.7 4.8 %collective-permute-done.15.refs_2_ = f32[64,128]{1,0:T(8,128)S(1)} collective-permute-done((f32[64,128]{1,0:T(8,128)S(1)}, f32[64,128]{1,0:T(8,128)S(1)}, u32[]{:S(2)}, u32[]{:S(2)}) %collective-permute-start.15) | collective-permute-done | bytes 32800 | tf_op jit(solution)/shard_map/ppermute | solution.py:339
  69.5 0.0 collective-permute-done.14.refs_1_
  69.5 0.0 collective-permute-done.16.refs_3_
  69.5 2.8 %shard_map.82 = (f32[352,128]{1,0:T(8,128)S(1)}, f32[128,128]{1,0:T(8,128)S(1)}, f32[128,128]{1,0:T(8,128)S(1)}, f32[64,128]{1,0:T(8,128)S(1)}, f32[96,128]{1,0:T(8,128)S(1)}, /*index=5*/f32[96,128]{1,0:T(8,128)S(1)}) custom-call(s32[2]{0:T(128)S(1)} %pad_add_fusion.pos, f32[64,128]{1,0:T(8,128)S(1)} %get-tuple-element.79.refs_0_, ...), custom_call_target="tpu_custom_call" | custom-call | tf_op jit(solution)/shard_map/pallas_call | solution.py:24
  72.3 0.0 collective-permute-start.17
  72.4 3.8 %collective-permute-start.19 = (f32[96,128]{1,0:T(8,128)S(1)}, f32[96,128]{1,0:T(8,128)S(1)}, u32[]{:S(2)}, u32[]{:S(2)}) collective-permute-start(f32[96,128]{1,0:T(8,128)S(1)} %get-tuple-element.87), channel_id=1, source_target_pairs={{0,12},{1,13},{2,14},{3,15},{4,0},{5,1},{6,2},{7,3},{8,4},{9,5},{1... | collective-permute-start | bytes 147464 | tf_op jit(solution)/shard_map/ppermute | solution.py:339
  76.2 0.0 collective-permute-start.18
  76.2 4.8 %collective-permute-done.18.refs_2_ = f32[64,128]{1,0:T(8,128)S(1)} collective-permute-done((f32[64,128]{1,0:T(8,128)S(1)}, f32[64,128]{1,0:T(8,128)S(1)}, u32[]{:S(2)}, u32[]{:S(2)}) %collective-permute-start.18) | collective-permute-done | bytes 32800 | tf_op jit(solution)/shard_map/ppermute | solution.py:339
  81.0 0.0 collective-permute-done.17.refs_1_
  81.0 0.0 collective-permute-done.19.refs_3_
  81.0 0.0 copy-start.2
  81.0 2.0 %shard_map.83 = (f32[120,128]{1,0:T(8,128)S(1)}, f32[120,128]{1,0:T(8,128)S(1)}, f32[120,128]{1,0:T(8,128)S(1)}, f32[120,128]{1,0:T(8,128)S(1)}) custom-call(s32[2]{0:T(128)S(1)} %pad_add_fusion.pos, f32[64,128]{1,0:T(8,128)S(1)} %get-tuple-element.85.refs_0_, f32[96,128]{1,0:T(8,128)S(1)} %collective-permute-done.17.refs_1_, ...), custom_call_target="tpu_custom_call" | custom-call | tf_op jit(solution)/shard_map/pallas_call | solution.py:24
  83.1 0.1 collective-permute-start.20
  83.2 0.1 collective-permute-start.21
  83.2 1.8 %collective-permute-start.22 = (f32[120,128]{1,0:T(8,128)S(1)}, f32[120,128]{1,0:T(8,128)S(1)}, u32[]{:S(2)}, u32[]{:S(2)}) collective-permute-start(f32[120,128]{1,0:T(8,128)S(1)} %get-tuple-element.94), channel_id=1, source_target_pairs={{0,3},{1,2},{2,1},{3,0},{4,7},{5,6},{6,5},{7,4},{8,11},{9,10},{10,... | collective-permute-start | bytes 184328 | tf_op jit(solution)/shard_map/ppermute | solution.py:329
  85.0 0.0 collective-permute-done.20.p1
  85.0 3.0 %collective-permute-done.21.p2 = f32[120,128]{1,0:T(8,128)S(1)} collective-permute-done((f32[120,128]{1,0:T(8,128)S(1)}, f32[120,128]{1,0:T(8,128)S(1)}, u32[]{:S(2)}, u32[]{:S(2)}) %collective-permute-start.21) | collective-permute-done | bytes 61472 | tf_op jit(solution)/shard_map/ppermute | solution.py:329
  88.0 0.4 collective-permute-done.22.p3
  88.4 0.0 slice-done.1
  88.5 5.3 %shard_map.84 = (f32[1536,128]{1,0:T(8,128)}, f32[128,128]{1,0:T(8,128)}) custom-call(s32[2]{0:T(128)S(1)} %pad_add_fusion.pos, f32[120,128]{1,0:T(8,128)S(1)} %get-tuple-element.91.p0, f32[120,128]{1,0:T(8,128)S(1)} %collective-permute-done.20.p1, f32[120,128]{1,0:T(8,128)S(1)} %collective-permute-done.21.p2, f32[120,128]{1,0:T(8,128)S(1)} %collective-permute-done.22.p3, ...), custom_call_target="tpu_custom_call" | custom-call | tf_op jit(solution)/shard_map/pallas_call | solution.py:24
  (14 shorter events, 0.1 us)
Async XLA Ops:
  0.7 1.1 %copy-start = (f32[1536,128]{1,0:T(8,128)S(1)}, f32[1536,128]{1,0:T(8,128)}, u32[]{:S(2)}) copy-start(f32[1536,128]{1,0:T(8,128)} %f_ref.3) | copy-start | bytes 2359300
  1.9 0.7 copy-start.4
  2.5 0.7 copy-start.5
  3.2 0.7 copy-start.6
  3.9 10.7 %copy-start.3 = (f32[48,768]{1,0:T(8,128)S(1)}, f32[48,768]{1,0:T(8,128)}, u32[]{:S(2)}) copy-start(f32[48,768]{1,0:T(8,128)} %mine.1) | copy-start | bytes 442372
  3.9 84.6 %slice-start = ((s8[9437184]{0:T(1024)(128)(4,1)}), s8[1048576]{0:T(1024)(128)(4,1)S(1)}, s32[]{:S(2)}) async-start(s8[9437184]{0:T(1024)(128)(4,1)} %bitcast.3), calls=%async_computation | async-start | bytes 2097152
  3.9 84.6 %slice-start.1 = ((s8[9437184]{0:T(1024)(128)(4,1)}), s8[4194304]{0:T(1024)(128)(4,1)S(1)}, s32[]{:S(2)}) async-start(s8[9437184]{0:T(1024)(128)(4,1)} %bitcast.3), calls=%async_computation.1 | async-start | bytes 8388608
  11.5 40.9 %collective-permute-start.9 = (f32[960,128]{1,0:T(8,128)S(1)}, f32[960,128]{1,0:T(8,128)S(1)}, u32[]{:S(2)}, u32[]{:S(2)}) collective-permute-start(f32[960,128]{1,0:T(8,128)S(1)} %get-tuple-element.60.s0), channel_id=1, source_target_pairs={{0,2},{1,3},{2,0},{3,1},{4,6},{5,7},{6,4},{7,5},{8,10},{9,11},{10,... | collective-permute-start | bytes 1474568 | tf_op jit(solution)/shard_map/ppermute | solution.py:329
  14.6 16.8 %collective-permute-start = (f32[48,768]{1,0:T(8,128)S(1)}, f32[48,768]{1,0:T(8,128)S(1)}, u32[]{:S(2)}, u32[]{:S(2)}) collective-permute-start(f32[48,768]{1,0:T(8,128)S(1)} %copy-done.3), channel_id=1, source_target_pairs={{0,2},{1,3},{2,0},{3,1},{4,6},{5,7},{6,4},{7,5},{8,10},{9,11},{10,... | collective-permute-start | bytes 442376 | tf_op jit(solution)/shard_map/ppermute | solution.py:329
  14.6 16.7 %collective-permute-start.1 = (f32[48,768]{1,0:T(8,128)S(1)}, f32[48,768]{1,0:T(8,128)S(1)}, u32[]{:S(2)}, u32[]{:S(2)}) collective-permute-start(f32[48,768]{1,0:T(8,128)S(1)} %copy-done.3), channel_id=1, source_target_pairs={{3,4},{0,15},{1,14},{7,8},{4,3},{5,2},{11,12},{8,7},{9,6},{15,0},{... | collective-permute-start | bytes 442376 | tf_op jit(solution)/shard_map/ppermute | solution.py:333
  20.4 11.0 %collective-permute-start.2 = (f32[48,768]{1,0:T(8,128)S(1)}, f32[48,768]{1,0:T(8,128)S(1)}, u32[]{:S(2)}, u32[]{:S(2)}) collective-permute-start(f32[48,768]{1,0:T(8,128)S(1)} %copy-done.3), channel_id=1, source_target_pairs={{3,6},{0,13},{1,12},{7,10},{4,1},{5,0},{11,14},{8,5},{9,4},{15,2},... | collective-permute-start | bytes 442376 | tf_op jit(solution)/shard_map/ppermute | solution.py:333
  31.4 9.2 %collective-permute-start.3 = (f32[88,128]{1,0:T(8,128)S(1)}, f32[88,128]{1,0:T(8,128)S(1)}, u32[]{:S(2)}, u32[]{:S(2)}) collective-permute-start(f32[88,128]{1,0:T(8,128)S(1)} %get-tuple-element.54), channel_id=1, source_target_pairs={{0,1},{1,0},{2,3},{3,2},{4,5},{5,4},{6,7},{7,6},{8,9},{9,8},{10,11... | collective-permute-start | bytes 135176 | tf_op jit(solution)/shard_map/ppermute | solution.py:329
  31.4 9.3 %collective-permute-start.4 = (f32[88,128]{1,0:T(8,128)S(1)}, f32[88,128]{1,0:T(8,128)S(1)}, u32[]{:S(2)}, u32[]{:S(2)}) collective-permute-start(f32[88,128]{1,0:T(8,128)S(1)} %get-tuple-element.55), channel_id=1, source_target_pairs={{0,2},{1,3},{2,0},{3,1},{4,6},{5,7},{6,4},{7,5},{8,10},{9,11},{10,... | collective-permute-start | bytes 135176 | tf_op jit(solution)/shard_map/ppermute | solution.py:329
  33.9 6.7 %collective-permute-start.5 = (f32[88,128]{1,0:T(8,128)S(1)}, f32[88,128]{1,0:T(8,128)S(1)}, u32[]{:S(2)}, u32[]{:S(2)}) collective-permute-start(f32[88,128]{1,0:T(8,128)S(1)} %get-tuple-element.56), channel_id=1, source_target_pairs={{0,3},{1,2},{2,1},{3,0},{4,7},{5,6},{6,5},{7,4},{8,11},{9,10},{10,... | collective-permute-start | bytes 135176 | tf_op jit(solution)/shard_map/ppermute | solution.py:329
  34.0 13.6 %collective-permute-start.10 = (f32[128,128]{1,0:T(8,128)S(1)}, f32[128,128]{1,0:T(8,128)S(1)}, u32[]{:S(2)}, u32[]{:S(2)}) collective-permute-start(f32[128,128]{1,0:T(8,128)S(1)} %get-tuple-element.62), channel_id=1, source_target_pairs={{3,4},{0,15},{7,8},{4,3},{11,12},{8,7},{15,0},{12,11},{19,20},{16,... | collective-permute-start | bytes 196616 | tf_op jit(solution)/shard_map/ppermute | solution.py:333
  40.6 11.8 %collective-permute-start.11 = (f32[128,128]{1,0:T(8,128)S(1)}, f32[128,128]{1,0:T(8,128)S(1)}, u32[]{:S(2)}, u32[]{:S(2)}) collective-permute-start(f32[128,128]{1,0:T(8,128)S(1)} %get-tuple-element.62), channel_id=1, source_target_pairs={{3,6},{0,13},{7,10},{4,1},{11,14},{8,5},{15,2},{12,9},{19,22},{16,... | collective-permute-start | bytes 196616 | tf_op jit(solution)/shard_map/ppermute | solution.py:333
  43.7 8.7 %collective-permute-start.6 = (f32[96,128]{1,0:T(8,128)S(1)}, f32[96,128]{1,0:T(8,128)S(1)}, u32[]{:S(2)}, u32[]{:S(2)}) collective-permute-start(f32[96,128]{1,0:T(8,128)S(1)} %get-tuple-element.58), channel_id=1, source_target_pairs={{0,4},{1,5},{2,6},{3,7},{4,8},{5,9},{6,10},{7,11},{8,12},{9,13},{1... | collective-permute-start | bytes 147464 | tf_op jit(solution)/shard_map/ppermute | solution.py:339
  43.8 8.6 %collective-permute-start.8 = (f32[96,128]{1,0:T(8,128)S(1)}, f32[96,128]{1,0:T(8,128)S(1)}, u32[]{:S(2)}, u32[]{:S(2)}) collective-permute-start(f32[96,128]{1,0:T(8,128)S(1)} %get-tuple-element.59), channel_id=1, source_target_pairs={{0,12},{1,13},{2,14},{3,15},{4,0},{5,1},{6,2},{7,3},{8,4},{9,5},{1... | collective-permute-start | bytes 147464 | tf_op jit(solution)/shard_map/ppermute | solution.py:339
  47.6 4.8 %collective-permute-start.7 = (f32[64,128]{1,0:T(8,128)S(1)}, f32[64,128]{1,0:T(8,128)S(1)}, u32[]{:S(2)}, u32[]{:S(2)}) collective-permute-start(f32[64,128]{1,0:T(8,128)S(1)} %get-tuple-element.63.refs_0_), channel_id=1, source_target_pairs={{0,8},{1,9},{2,10},{3,11},{4,12},{5,13},{6,14},{7,15},{8,0},{9,1},... | collective-permute-start | bytes 98312 | tf_op jit(solution)/shard_map/ppermute | solution.py:339
  52.5 4.4 %collective-permute-start.13 = (f32[2176,128]{1,0:T(8,128)S(1)}, f32[2176,128]{1,0:T(8,128)S(1)}, u32[]{:S(2)}, u32[]{:S(2)}) collective-permute-start(f32[2176,128]{1,0:T(8,128)S(1)} %pad_maximum_fusion), channel_id=1, source_target_pairs={{0,1},{1,0},{2,3},{3,2},{4,5},{5,4},{6,7},{7,6},{8,9},{9,8},{10,11... | collective-permute-start | bytes 3342344 | tf_op jit(solution)/shard_map/ppermute | solution.py:329
  52.7 3.5 %collective-permute-start.12 = (f32[192,768]{1,0:T(8,128)S(1)}, f32[192,768]{1,0:T(8,128)S(1)}, u32[]{:S(2)}, u32[]{:S(2)}) collective-permute-start(f32[192,768]{1,0:T(8,128)S(1)} %pad_maximum_fusion.1), channel_id=1, source_target_pairs={{0,1},{1,0},{2,3},{3,2},{4,5},{5,4},{6,7},{7,6},{8,9},{9,8},{10,11... | collective-permute-start | bytes 1769480 | tf_op jit(solution)/shard_map/ppermute | solution.py:329
  58.0 30.4 %slice-start.2 = ((s8[9437184]{0:T(1024)(128)(4,1)}), s8[4194304]{0:T(1024)(128)(4,1)S(1)}, s32[]{:S(2)}) async-start(s8[9437184]{0:T(1024)(128)(4,1)} %bitcast.3), calls=%async_computation.2 | async-start | bytes 8388608
  60.8 8.7 %collective-permute-start.14 = (f32[96,128]{1,0:T(8,128)S(1)}, f32[96,128]{1,0:T(8,128)S(1)}, u32[]{:S(2)}, u32[]{:S(2)}) collective-permute-start(f32[96,128]{1,0:T(8,128)S(1)} %get-tuple-element.80), channel_id=1, source_target_pairs={{0,4},{1,5},{2,6},{3,7},{4,8},{5,9},{6,10},{7,11},{8,12},{9,13},{1... | collective-permute-start | bytes 147464 | tf_op jit(solution)/shard_map/ppermute | solution.py:339
  60.9 8.6 %collective-permute-start.16 = (f32[96,128]{1,0:T(8,128)S(1)}, f32[96,128]{1,0:T(8,128)S(1)}, u32[]{:S(2)}, u32[]{:S(2)}) collective-permute-start(f32[96,128]{1,0:T(8,128)S(1)} %get-tuple-element.81), channel_id=1, source_target_pairs={{0,12},{1,13},{2,14},{3,15},{4,0},{5,1},{6,2},{7,3},{8,4},{9,5},{1... | collective-permute-start | bytes 147464 | tf_op jit(solution)/shard_map/ppermute | solution.py:339
  64.7 4.8 %collective-permute-start.15 = (f32[64,128]{1,0:T(8,128)S(1)}, f32[64,128]{1,0:T(8,128)S(1)}, u32[]{:S(2)}, u32[]{:S(2)}) collective-permute-start(f32[64,128]{1,0:T(8,128)S(1)} %get-tuple-element.79.refs_0_), channel_id=1, source_target_pairs={{0,8},{1,9},{2,10},{3,11},{4,12},{5,13},{6,14},{7,15},{8,0},{9,1},... | collective-permute-start | bytes 98312 | tf_op jit(solution)/shard_map/ppermute | solution.py:339
  72.3 8.7 %collective-permute-start.17 = (f32[96,128]{1,0:T(8,128)S(1)}, f32[96,128]{1,0:T(8,128)S(1)}, u32[]{:S(2)}, u32[]{:S(2)}) collective-permute-start(f32[96,128]{1,0:T(8,128)S(1)} %get-tuple-element.86), channel_id=1, source_target_pairs={{0,4},{1,5},{2,6},{3,7},{4,8},{5,9},{6,10},{7,11},{8,12},{9,13},{1... | collective-permute-start | bytes 147464 | tf_op jit(solution)/shard_map/ppermute | solution.py:339
  72.4 8.6 %collective-permute-start.19 = (f32[96,128]{1,0:T(8,128)S(1)}, f32[96,128]{1,0:T(8,128)S(1)}, u32[]{:S(2)}, u32[]{:S(2)}) collective-permute-start(f32[96,128]{1,0:T(8,128)S(1)} %get-tuple-element.87), channel_id=1, source_target_pairs={{0,12},{1,13},{2,14},{3,15},{4,0},{5,1},{6,2},{7,3},{8,4},{9,5},{1... | collective-permute-start | bytes 147464 | tf_op jit(solution)/shard_map/ppermute | solution.py:339
  76.2 4.8 %collective-permute-start.18 = (f32[64,128]{1,0:T(8,128)S(1)}, f32[64,128]{1,0:T(8,128)S(1)}, u32[]{:S(2)}, u32[]{:S(2)}) collective-permute-start(f32[64,128]{1,0:T(8,128)S(1)} %get-tuple-element.85.refs_0_), channel_id=1, source_target_pairs={{0,8},{1,9},{2,10},{3,11},{4,12},{5,13},{6,14},{7,15},{8,0},{9,1},... | collective-permute-start | bytes 98312 | tf_op jit(solution)/shard_map/ppermute | solution.py:339
  81.0 7.4 %copy-start.1 = (f32[1536,128]{1,0:T(8,128)S(1)}, f32[1536,128]{1,0:T(8,128)}, u32[]{:S(2)}) copy-start(f32[1536,128]{1,0:T(8,128)} %f_ref.3) | copy-start | bytes 2359300
  81.0 7.4 %copy-start.2 = (bf16[1536,384]{1,0:T(8,128)(2,1)S(1)}, bf16[1536,384]{1,0:T(8,128)(2,1)}, u32[]{:S(2)}) copy-start(bf16[1536,384]{1,0:T(8,128)(2,1)} %get-tuple-element.95.places) | copy-start | bytes 3538948
  83.1 1.9 %collective-permute-start.20 = (f32[120,128]{1,0:T(8,128)S(1)}, f32[120,128]{1,0:T(8,128)S(1)}, u32[]{:S(2)}, u32[]{:S(2)}) collective-permute-start(f32[120,128]{1,0:T(8,128)S(1)} %get-tuple-element.92), channel_id=1, source_target_pairs={{0,1},{1,0},{2,3},{3,2},{4,5},{5,4},{6,7},{7,6},{8,9},{9,8},{10,11... | collective-permute-start | bytes 184328 | tf_op jit(solution)/shard_map/ppermute | solution.py:329
  83.2 4.9 %collective-permute-start.21 = (f32[120,128]{1,0:T(8,128)S(1)}, f32[120,128]{1,0:T(8,128)S(1)}, u32[]{:S(2)}, u32[]{:S(2)}) collective-permute-start(f32[120,128]{1,0:T(8,128)S(1)} %get-tuple-element.93), channel_id=1, source_target_pairs={{0,2},{1,3},{2,0},{3,1},{4,6},{5,7},{6,4},{7,5},{8,10},{9,11},{10,... | collective-permute-start | bytes 184328 | tf_op jit(solution)/shard_map/ppermute | solution.py:329
  83.2 5.2 %collective-permute-start.22 = (f32[120,128]{1,0:T(8,128)S(1)}, f32[120,128]{1,0:T(8,128)S(1)}, u32[]{:S(2)}, u32[]{:S(2)}) collective-permute-start(f32[120,128]{1,0:T(8,128)S(1)} %get-tuple-element.94), channel_id=1, source_target_pairs={{0,3},{1,2},{2,1},{3,0},{4,7},{5,6},{6,5},{7,4},{8,11},{9,10},{10,... | collective-permute-start | bytes 184328 | tf_op jit(solution)/shard_map/ppermute | solution.py:329

commit v5 on v4

--- a/solution.py
+++ b/solution.py
@@ -15,7 +15,7 @@
 F32 = jnp.float32
 
 
-def call(kernel, outs, args, smem=1, hbm=(), scratch=(), vmem=24):
+def call(kernel, outs, args, micros, smem=1, hbm=(), scratch=(), vmem=24):
     in_specs = [
         pl.BlockSpec(memory_space=pltpu.SMEM if i < smem else pltpu.HBM if i in hbm else pltpu.VMEM)
         for i in range(len(args))
@@ -28,6 +28,7 @@
         out_specs=[pl.BlockSpec(memory_space=pltpu.VMEM)] * len(shapes),
         scratch_shapes=list(scratch),
         compiler_params=pltpu.CompilerParams(vmem_limit_bytes=vmem * 1024 * 1024),
+        cost_estimate=pl.CostEstimate(flops=int(micros * 1e9), bytes_accessed=0, transcendentals=0),
     )(*args)
 
 
@@ -136,23 +137,23 @@
     lax.fori_loop(0, count, one, 0, unroll=8)
 
 
-def rows_kernel(pos, face, prim, slot, k_ref, f_ref, facev, primv, slotv, *rest):
+def rows_kernel(count, table, k_ref, f_ref, tablev, *rest):
     pieces, (spans, edge, places, ks, right_side, sem) = rest[:GROUP], rest[GROUP:]
-    width, count, order, columns = face.shape[1], prim.shape[1], ks.shape[1], f_ref.shape[1]
+    width, order, columns = edge.shape[1], ks.shape[1], f_ref.shape[1]
     side = 2 * width
-    fetch(k_ref, count, lambda j: prim[0, j], ks, lambda j: side + slot[0, j], sem)
-    fetch(k_ref, side, lambda j: face[j // width, j % width], ks, lambda j: j, sem)
+    fetch(k_ref, count, lambda j: table[2, j], ks, lambda j: side + table[3, j], sem)
+    fetch(k_ref, side, lambda j: table[j // width, j % width], ks, lambda j: j, sem)
 
     def indicator(row):
         place = lax.broadcasted_iota(jnp.int32, (order, row.shape[1]), 0).astype(F32)
         return jnp.where(place == row, 1.0, 0.0).astype(BF16)
 
-    slots = jnp.broadcast_to(slotv[...].astype(F32), (count, count)).T
-    prims = jnp.broadcast_to(primv[...].astype(F32), (count, count)).T
+    slots = jnp.broadcast_to(tablev[3:4, :count].astype(F32), (count, count)).T
+    prims = jnp.broadcast_to(tablev[2:3, :count].astype(F32), (count, count)).T
     wanted = lax.broadcasted_iota(jnp.int32, (count, count), 1).astype(F32)
     by_slot = jnp.sum(jnp.where(slots == wanted, prims, 0.0), axis=0, keepdims=True)
-    right_side[:, :width] = indicator(facev[0:1].astype(F32))
-    right_side[:, width:side] = indicator(facev[1:2].astype(F32))
+    right_side[:, :width] = indicator(tablev[0:1].astype(F32))
+    right_side[:, width:side] = indicator(tablev[1:2].astype(F32))
     right_side[:, side:side + count] = indicator(by_slot)
     right_side[:, side + count:side + width] = jnp.zeros((order, width - count), BF16)
     right_side[:, side + width:] = beside(f_ref[...])
@@ -163,13 +164,13 @@
     high, low = halves(ks[...])
     both = dot(high, right_side[...])
     part = dot(low, right_side[:, :at + columns])
-    cut(both[:, at:at + columns] + both[:, at + columns:] + part[:, at:], pos[0], pieces)
+    cut(both[:, at:at + columns] + both[:, at + columns:] + part[:, at:], table[4, 0], pieces)
     block = both[:, :at] + part[:, :at]
     rows = side + count
     for i in range(3):
         kept = side if i == 2 else rows
         spans[i * rows:i * rows + kept] = block[:kept, i * width:(i + 1) * width]
-    edge[...] = jnp.where(pos[0] == GROUP - 1, block[width:side, side:], block[:width, side:])
+    edge[...] = jnp.where(table[4, 0] == GROUP - 1, block[width:side, side:], block[:width, side:])
 
 
 GOT = (-1, None, 5, 4)
@@ -323,7 +324,11 @@
     groups = total // GROUP
     me = lax.axis_index("sub")
     pos = jnp.stack([me % GROUP, me // GROUP]).astype(jnp.int32)
-    faces = face_rows[0]
+
+    def row(x):
+        return jnp.pad(x[None], ((0, 0), (0, width - x.shape[0])))
+
+    table = jnp.concatenate([face_rows[0], row(primal_rows[0]), row(primal_slot[0]), row(pos)], axis=0)
 
     def mate(x, k):
         return lax.ppermute(x, "sub", [(s, s ^ k) for s in range(total)])
@@ -349,12 +354,12 @@
     got_next = crossing(coarse_inverse, [(GROUP - 1, GROUP + 2), (0, -3), (1, -4)])
 
     *pieces, spans, edge, places = call(
-        rows_kernel,
+        functools.partial(rows_kernel, count),
         [(kept // GROUP, LANES)] * GROUP
         + [(2 * kept + side, width), (width, width), ((order, side + width), BF16)],
-        (pos, faces, primal_rows, primal_slot, condensed, eigen_loads, faces, primal_rows, primal_slot),
-        smem=4,
-        hbm=(4,),
+        (table, condensed, eigen_loads, table),
+        7.5,
+        hbm=(1,),
         scratch=[
             pltpu.VMEM((kept, order), F32),
             pltpu.VMEM((order, side + width + 2 * columns), BF16),
@@ -362,20 +367,21 @@
         ],
         vmem=52,
     )
-    spans_next = mate(spans, 2)
+    spans_next = mate(after(spans, (c_next, got, got_next)), 2)
     *pieces, c_next, got, got_next = lax.optimization_barrier((*pieces, c_next, got, got_next))
     pieces = traded(pieces)
-    came = crossing(edge, [(GROUP - 1, GROUP), (0, -1)])
-    came_next = crossing(after(edge, pieces), [(GROUP - 1, GROUP + 2), (0, -3)])
+    came = crossing(after(edge, pieces), [(GROUP - 1, GROUP), (0, -1)])
     theirs_c = mate(after(jnp.concatenate([coarse_inverse, c_next, got, got_next], axis=0), pieces), 1)
     size = owned + chunk_of(owned)
     pay_shapes = [(size, LANES)] + [(size + width // GROUP, LANES)] * 2
-    v0, *pays = call(start_kernel, [(kept, LANES), *pay_shapes], (pos, *pieces))
+    v0, *pays = call(start_kernel, [(kept, LANES), *pay_shapes], (pos, *pieces), 0.9)
+    came_next = crossing(after(edge, pays), [(GROUP - 1, GROUP + 2), (0, -3)])
     pays = along(*pays)
     (solver,) = call(
         solver_kernel,
         [((2 * (GROUP + 3) * owned, coarse), BF16)],
         (pos, coarse_inverse, c_next, got, got_next, theirs_c),
+        0.7,
     )
     *pays, spans_next, came, came_next = lax.optimization_barrier((*pays, spans_next, came, came_next))
     theirs = mate(jnp.concatenate([spans, spans_next, came, came_next], axis=0), 1)
@@ -388,6 +394,7 @@
             ((side, width), BF16),
         ],
         (pos, spans, spans_next, came, came_next, theirs),
+        1,
     )
 
     state = ()
@@ -400,6 +407,7 @@
             functools.partial(turn_kernel, kind, groups),
             shapes,
             (pos, *pays, solver, *blocks, v0, *state),
+            2.8,
             scratch=[pltpu.VMEM((coarse, 2 * LANES), BF16)],
         )
         if kind != "last":
@@ -409,6 +417,7 @@
         functools.partial(final_kernel, count),
         [(order, columns), (width, columns)],
         (pos, *traded(outs), eigen_loads, places, condensed),
+        5.3,
     )
     return displaced, multipliers
 

time: 94 us -> 92 us (0.979)
  starting transfers between devices: 37.6 us -> 34.7 us
  local copies, waits for them, and re-layouts: 3.15 us -> 1.16 us
  waiting for transfers between devices: 28.6 us -> 30.2 us
    ppermute x10, waiting for transfers between devices: 14.1 us -> 18.7 us  [mate(): return lax.ppermute(x, 'sub', [(s, s ^ k) for s in range(total)])]
    ppermute x9, waiting for transfers between devices: 14.4 us -> 11.3 us  [planes(): lax.ppermute(x, 'sub', [(s, (s + by * GROUP) % total) for s in range(tota...]
    ppermute x4, starting transfers between devices: 17.7 us -> 14.8 us  [crossing(): return lax.ppermute(x, 'sub', pairs)]
    unnamed x20 -> x12, local copies, waits for them, and re-layouts: 3.15 us -> 1.16 us
  transfers between devices with their start and end apart: 23 -> 23, of which waited for: 7 -> 8; matrix products, arithmetic and copies ran while one was open for 0% -> 1% of each run, Pallas kernels for 2% -> 10%
where the time goes in v5:
time: 92 us; the launch traced here: 91.7 us
  starting transfers between devices  34.7 us (38%)
  waiting for transfers between devices  30.2 us (33%)
  Pallas kernels  23.8 us (26%)
  local copies, waits for them, and re-layouts  1.16 us (1%)
  other arithmetic  0.99 us (1%)
    pallas_call x8, Pallas kernels, call(): pl.pallas_call(kernel, out_shape=[jax.ShapeDtypeStruct(s, d) for s, d in...  23.8 us
    ppermute x10, waiting for transfers between devices, mate(): return lax.ppermute(x, 'sub', [(s, s ^ k) for s in range(total)])  18.7 us
    ppermute x4, starting transfers between devices, crossing(): return lax.ppermute(x, 'sub', pairs)  14.8 us
    ppermute x9, starting transfers between devices, planes(): lax.ppermute(x, 'sub', [(s, (s + by * GROUP) % total) for s in range(tota...  12.1 us
    ppermute x9, waiting for transfers between devices, planes(): lax.ppermute(x, 'sub', [(s, (s + by * GROUP) % total) for s in range(tota...  11.3 us
    ppermute x10, starting transfers between devices, mate(): return lax.ppermute(x, 'sub', [(s, s ^ k) for s in range(total)])  7.82 us
  transfers between devices with their start and end apart: 23, of which 8 were waited for; matrix products, arithmetic and copies ran while one was open for 1% of the time, Pallas kernels for 10%

profile of v5, /device:TPU:0, one launch (start us, length us, event | category | flops | bytes accessed | tf_op | source)
XLA Modules:
  0.0 91.7 jit_solution(13354881359739922195)
XLA Ops:
  0.6 3.0 %collective-permute-start = (f32[48,768]{1,0:T(8,128)}, f32[48,768]{1,0:T(8,128)S(1)}, u32[]{:S(2)}, u32[]{:S(2)}) collective-permute-start(f32[48,768]{1,0:T(8,128)} %mine.1), channel_id=1, source_target_pairs={{0,2},{1,3},{2,0},{3,1},{4,6},{5,7},{6,4},{7,5},{8,10},{9,11},{10,... | collective-permute-start | bytes 442376 | tf_op jit(solution)/shard_map/ppermute | solution.py:334
  3.7 4.6 %collective-permute-start.1 = (f32[48,768]{1,0:T(8,128)}, f32[48,768]{1,0:T(8,128)S(1)}, u32[]{:S(2)}, u32[]{:S(2)}) collective-permute-start(f32[48,768]{1,0:T(8,128)} %mine.1), channel_id=1, source_target_pairs={{3,4},{0,15},{1,14},{7,8},{4,3},{5,2},{11,12},{8,7},{9,6},{15,0},{... | collective-permute-start | bytes 442376 | tf_op jit(solution)/shard_map/ppermute | solution.py:338
  8.3 2.9 %collective-permute-start.2 = (f32[48,768]{1,0:T(8,128)}, f32[48,768]{1,0:T(8,128)S(1)}, u32[]{:S(2)}, u32[]{:S(2)}) collective-permute-start(f32[48,768]{1,0:T(8,128)} %mine.1), channel_id=1, source_target_pairs={{3,6},{0,13},{1,12},{7,10},{4,1},{5,0},{11,14},{8,5},{9,4},{15,2},... | collective-permute-start | bytes 442376 | tf_op jit(solution)/shard_map/ppermute | solution.py:338
  11.2 0.1 fusion
  11.3 0.7 pad_add_fusion.table.tablev
  12.0 1.1 %copy-done.1 = f32[1536,128]{1,0:T(8,128)S(1)} copy-done((f32[1536,128]{1,0:T(8,128)S(1)}, f32[1536,128]{1,0:T(8,128)}, u32[]{:S(2)}) %copy-start.1) | copy-done | bytes 786456
  13.2 7.9 %shard_map.77 = (f32[88,128]{1,0:T(8,128)S(1)}, f32[88,128]{1,0:T(8,128)S(1)}, f32[88,128]{1,0:T(8,128)S(1)}, f32[88,128]{1,0:T(8,128)S(1)}, f32[960,128]{1,0:T(...) custom-call(s32[5,128]{1,0:T(8,128)S(1)} %pad_add_fusion.table.tablev, f32[1536,1536]{1,0:T(8,128)} %k_ref.3, ...), custom_call_target="tpu_custom_call" | custom-call | flops 7500000256 | tf_op jit(solution)/shard_map/pallas_call | solution.py:24
  21.1 0.0 collective-permute-done.next_mine
  21.1 0.0 collective-permute-done.1.got
  21.1 0.0 collective-permute-done.2.next_got
  21.1 0.1 collective-permute-start.9
  21.2 0.1 collective-permute-start.3
  21.2 1.9 %collective-permute-start.4 = (f32[88,128]{1,0:T(8,128)S(1)}, f32[88,128]{1,0:T(8,128)S(1)}, u32[]{:S(2)}, u32[]{:S(2)}) collective-permute-start(f32[88,128]{1,0:T(8,128)S(1)} %get-tuple-element.57), channel_id=1, source_target_pairs={{0,2},{1,3},{2,0},{3,1},{4,6},{5,7},{6,4},{7,5},{8,10},{9,11},{10,... | collective-permute-start | bytes 135176 | tf_op jit(solution)/shard_map/ppermute | solution.py:334
  23.2 0.1 collective-permute-start.5
  23.3 0.1 pad_add_fusion.3.pos
  23.4 0.0 collective-permute-done.3.p1
  23.4 12.3 %collective-permute-done.4.p2 = f32[88,128]{1,0:T(8,128)S(1)} collective-permute-done((f32[88,128]{1,0:T(8,128)S(1)}, f32[88,128]{1,0:T(8,128)S(1)}, u32[]{:S(2)}, u32[]{:S(2)}) %collective-permute-start.4) | collective-permute-done | bytes 45088 | tf_op jit(solution)/shard_map/ppermute | solution.py:334
  35.7 0.0 collective-permute-done.5.p3
  35.7 0.9 shard_map.78
  36.7 0.1 collective-permute-start.7
  36.7 0.0 copy-start
  36.8 5.1 %collective-permute-start.11 = (f32[128,128]{1,0:T(8,128)S(1)}, f32[128,128]{1,0:T(8,128)S(1)}, u32[]{:S(2)}, u32[]{:S(2)}) collective-permute-start(f32[128,128]{1,0:T(8,128)S(1)} %get-tuple-element.66), channel_id=1, source_target_pairs={{3,6},{0,13},{7,10},{4,1},{11,14},{8,5},{15,2},{12,9},{19,22},{16,... | collective-permute-start | bytes 196616 | tf_op jit(solution)/shard_map/ppermute | solution.py:338
  41.9 2.2 %collective-permute-start.10 = (f32[128,128]{1,0:T(8,128)S(1)}, f32[128,128]{1,0:T(8,128)S(1)}, u32[]{:S(2)}, u32[]{:S(2)}) collective-permute-start(f32[128,128]{1,0:T(8,128)S(1)} %get-tuple-element.66), channel_id=1, source_target_pairs={{3,4},{0,15},{7,8},{4,3},{11,12},{8,7},{15,0},{12,11},{19,20},{16,... | collective-permute-start | bytes 196616 | tf_op jit(solution)/shard_map/ppermute | solution.py:338
  44.1 0.1 collective-permute-start.6
  44.1 0.0 collective-permute-done.7.refs_2_
  44.1 3.8 %collective-permute-start.8 = (f32[96,128]{1,0:T(8,128)S(1)}, f32[96,128]{1,0:T(8,128)S(1)}, u32[]{:S(2)}, u32[]{:S(2)}) collective-permute-start(f32[96,128]{1,0:T(8,128)S(1)} %get-tuple-element.61), channel_id=1, source_target_pairs={{0,12},{1,13},{2,14},{3,15},{4,0},{5,1},{6,2},{7,3},{8,4},{9,5},{1... | collective-permute-start | bytes 147464 | tf_op jit(solution)/shard_map/ppermute | solution.py:344
  48.0 2.1 %collective-permute-done.6.refs_1_ = f32[96,128]{1,0:T(8,128)S(1)} collective-permute-done((f32[96,128]{1,0:T(8,128)S(1)}, f32[96,128]{1,0:T(8,128)S(1)}, u32[]{:S(2)}, u32[]{:S(2)}) %collective-permute-start.6) | collective-permute-done | bytes 49184 | tf_op jit(solution)/shard_map/ppermute | solution.py:344
  50.0 0.0 collective-permute-done.8.refs_3_
  50.0 0.0 collective-permute-done.11.came_next
  50.0 0.2 collective-permute-done.10.came
  50.2 0.0 collective-permute-done.9.s2
  50.2 0.1 pad_maximum_fusion
  50.3 0.1 collective-permute-start.13
  50.3 0.0 copy-done
  50.4 0.6 collective-permute-start.12
  51.0 3.0 %collective-permute-done.12.theirs = f32[192,768]{1,0:T(8,128)S(1)} collective-permute-done((f32[192,768]{1,0:T(8,128)S(1)}, f32[192,768]{1,0:T(8,128)S(1)}, u32[]{:S(2)}, u32[]{:S(2)}) %collective-permute-start.12) | collective-permute-done | bytes 589856 | tf_op jit(solution)/shard_map/ppermute | solution.py:334
  53.9 0.7 shard_map.79.refs_4_
  54.7 0.0 collective-permute-done.13.theirs
  54.7 1.1 %shard_map.80 = (bf16[512,512]{1,0:T(8,128)(2,1)S(1)}, bf16[704,1024]{1,0:T(8,128)(2,1)S(1)}, bf16[256,128]{1,0:T(8,128)(2,1)S(1)}, bf16[256,128]{1,0:T(8,128)(2,1)S(1)}) custom-call(s32[2]{0:T(128)S(1)} %pad_add_fusion.3.pos, f32[960,128]{1,0:T(8,128)S(1)} %get-tuple-element.63.s0, f32[960,128]{1,0:T(8,128)S(1)} %collective-permute-done.9.s2, ...), custom_call_target="tpu_custom_call" | custom-call | flops 1000000000 | tf_op jit(solution)/shard_map/pallas_call | solution.py:24
  55.7 2.8 %shard_map.81 = (f32[352,128]{1,0:T(8,128)S(1)}, f32[128,128]{1,0:T(8,128)S(1)}, f32[128,128]{1,0:T(8,128)S(1)}, f32[64,128]{1,0:T(8,128)S(1)}, f32[96,128]{1,0:T(8,128)S(1)}, /*index=5*/f32[96,128]{1,0:T(8,128)S(1)}) custom-call(s32[2]{0:T(128)S(1)} %pad_add_fusion.3.pos, f32[64,128]{1,0:T(8,128)S(1)} %get-tuple-element.67.refs_0_, ...), custom_call_target="tpu_custom_call" | custom-call | flops 2800000000 | tf_op jit(solution)/shard_map/pallas_call | solution.py:24
  58.6 0.0 collective-permute-start.14
  58.6 3.8 %collective-permute-start.16 = (f32[96,128]{1,0:T(8,128)S(1)}, f32[96,128]{1,0:T(8,128)S(1)}, u32[]{:S(2)}, u32[]{:S(2)}) collective-permute-start(f32[96,128]{1,0:T(8,128)S(1)} %get-tuple-element.85), channel_id=1, source_target_pairs={{0,12},{1,13},{2,14},{3,15},{4,0},{5,1},{6,2},{7,3},{8,4},{9,5},{1... | collective-permute-start | bytes 147464 | tf_op jit(solution)/shard_map/ppermute | solution.py:344
  62.4 0.4 collective-permute-start.15
  62.8 4.4 %collective-permute-done.15.refs_2_ = f32[64,128]{1,0:T(8,128)S(1)} collective-permute-done((f32[64,128]{1,0:T(8,128)S(1)}, f32[64,128]{1,0:T(8,128)S(1)}, u32[]{:S(2)}, u32[]{:S(2)}) %collective-permute-start.15) | collective-permute-done | bytes 32800 | tf_op jit(solution)/shard_map/ppermute | solution.py:344
  67.2 0.0 collective-permute-done.14.refs_1_
  67.2 0.0 collective-permute-done.16.refs_3_
  67.2 0.0 slice-start.1
  67.3 2.8 %shard_map.82 = (f32[352,128]{1,0:T(8,128)S(1)}, f32[128,128]{1,0:T(8,128)S(1)}, f32[128,128]{1,0:T(8,128)S(1)}, f32[64,128]{1,0:T(8,128)S(1)}, f32[96,128]{1,0:T(8,128)S(1)}, /*index=5*/f32[96,128]{1,0:T(8,128)S(1)}) custom-call(s32[2]{0:T(128)S(1)} %pad_add_fusion.3.pos, f32[64,128]{1,0:T(8,128)S(1)} %get-tuple-element.83.refs_0_, ...), custom_call_target="tpu_custom_call" | custom-call | flops 2800000000 | tf_op jit(solution)/shard_map/pallas_call | solution.py:24
  70.1 0.1 collective-permute-start.17
  70.2 3.8 %collective-permute-start.19 = (f32[96,128]{1,0:T(8,128)S(1)}, f32[96,128]{1,0:T(8,128)S(1)}, u32[]{:S(2)}, u32[]{:S(2)}) collective-permute-start(f32[96,128]{1,0:T(8,128)S(1)} %get-tuple-element.91), channel_id=1, source_target_pairs={{0,12},{1,13},{2,14},{3,15},{4,0},{5,1},{6,2},{7,3},{8,4},{9,5},{1... | collective-permute-start | bytes 147464 | tf_op jit(solution)/shard_map/ppermute | solution.py:344
  73.9 0.0 collective-permute-start.18
  73.9 4.8 %collective-permute-done.18.refs_2_ = f32[64,128]{1,0:T(8,128)S(1)} collective-permute-done((f32[64,128]{1,0:T(8,128)S(1)}, f32[64,128]{1,0:T(8,128)S(1)}, u32[]{:S(2)}, u32[]{:S(2)}) %collective-permute-start.18) | collective-permute-done | bytes 32800 | tf_op jit(solution)/shard_map/ppermute | solution.py:344
  78.8 0.0 collective-permute-done.17.refs_1_
  78.8 0.0 collective-permute-done.19.refs_3_
  78.8 0.0 copy-start.2
  78.8 2.0 %shard_map.83 = (f32[120,128]{1,0:T(8,128)S(1)}, f32[120,128]{1,0:T(8,128)S(1)}, f32[120,128]{1,0:T(8,128)S(1)}, f32[120,128]{1,0:T(8,128)S(1)}) custom-call(s32[2]{0:T(128)S(1)} %pad_add_fusion.3.pos, f32[64,128]{1,0:T(8,128)S(1)} %get-tuple-element.89.refs_0_, f32[96,128]{1,0:T(8,128)S(1)} %collective-permute-done.17.refs_1_, ...), custom_call_target="tpu_custom_call" | custom-call | flops 2800000000 | tf_op jit(solution)/shard_map/pallas_call | solution.py:24
  80.8 0.1 collective-permute-start.20
  80.9 0.7 collective-permute-start.21
  81.6 1.2 %collective-permute-start.22 = (f32[120,128]{1,0:T(8,128)S(1)}, f32[120,128]{1,0:T(8,128)S(1)}, u32[]{:S(2)}, u32[]{:S(2)}) collective-permute-start(f32[120,128]{1,0:T(8,128)S(1)} %get-tuple-element.98), channel_id=1, source_target_pairs={{0,3},{1,2},{2,1},{3,0},{4,7},{5,6},{6,5},{7,4},{8,11},{9,10},{10,... | collective-permute-start | bytes 184328 | tf_op jit(solution)/shard_map/ppermute | solution.py:334
  82.8 0.0 collective-permute-done.20.p1
  82.8 3.0 %collective-permute-done.21.p2 = f32[120,128]{1,0:T(8,128)S(1)} collective-permute-done((f32[120,128]{1,0:T(8,128)S(1)}, f32[120,128]{1,0:T(8,128)S(1)}, u32[]{:S(2)}, u32[]{:S(2)}) %collective-permute-start.21) | collective-permute-done | bytes 61472 | tf_op jit(solution)/shard_map/ppermute | solution.py:334
  85.8 0.4 collective-permute-done.22.p3
  86.2 0.0 copy-done.2
  86.2 5.5 %shard_map.84 = (f32[1536,128]{1,0:T(8,128)}, f32[128,128]{1,0:T(8,128)}) custom-call(s32[2]{0:T(128)S(1)} %pad_add_fusion.3.pos, f32[120,128]{1,0:T(8,128)S(1)} %get-tuple-element.95.p0, f32[120,128]{1,0:T(8,128)S(1)} %collective-permute-done.20.p1, f32[120,128]{1,0:T(8,128)S(1)} %collective-permute-done.21.p2, f32[120,128]{1,0:T(8,128)S(1)} %collective-permute-done.22.p3, ...), custom_call_target="tpu_custom_call" | custom-call | flops 5299999744 | tf_op jit(solution)/shard_map/pallas_call | solution.py:24
  (8 shorter events, 0.1 us)
Async XLA Ops:
  0.6 20.4 %collective-permute-start = (f32[48,768]{1,0:T(8,128)}, f32[48,768]{1,0:T(8,128)S(1)}, u32[]{:S(2)}, u32[]{:S(2)}) collective-permute-start(f32[48,768]{1,0:T(8,128)} %mine.1), channel_id=1, source_target_pairs={{0,2},{1,3},{2,0},{3,1},{4,6},{5,7},{6,4},{7,5},{8,10},{9,11},{10,... | collective-permute-start | bytes 442376 | tf_op jit(solution)/shard_map/ppermute | solution.py:334
  3.7 17.4 %collective-permute-start.1 = (f32[48,768]{1,0:T(8,128)}, f32[48,768]{1,0:T(8,128)S(1)}, u32[]{:S(2)}, u32[]{:S(2)}) collective-permute-start(f32[48,768]{1,0:T(8,128)} %mine.1), channel_id=1, source_target_pairs={{3,4},{0,15},{1,14},{7,8},{4,3},{5,2},{11,12},{8,7},{9,6},{15,0},{... | collective-permute-start | bytes 442376 | tf_op jit(solution)/shard_map/ppermute | solution.py:338
  8.3 12.8 %collective-permute-start.2 = (f32[48,768]{1,0:T(8,128)}, f32[48,768]{1,0:T(8,128)S(1)}, u32[]{:S(2)}, u32[]{:S(2)}) collective-permute-start(f32[48,768]{1,0:T(8,128)} %mine.1), channel_id=1, source_target_pairs={{3,6},{0,13},{1,12},{7,10},{4,1},{5,0},{11,14},{8,5},{9,4},{15,2},... | collective-permute-start | bytes 442376 | tf_op jit(solution)/shard_map/ppermute | solution.py:338
  12.0 1.1 %copy-start.1 = (f32[1536,128]{1,0:T(8,128)S(1)}, f32[1536,128]{1,0:T(8,128)}, u32[]{:S(2)}) copy-start(f32[1536,128]{1,0:T(8,128)} %f_ref.3) | copy-start | bytes 2359300
  21.1 29.1 %collective-permute-start.9 = (f32[960,128]{1,0:T(8,128)S(1)}, f32[960,128]{1,0:T(8,128)S(1)}, u32[]{:S(2)}, u32[]{:S(2)}) collective-permute-start(f32[960,128]{1,0:T(8,128)S(1)} %get-tuple-element.63.s0), channel_id=1, source_target_pairs={{0,2},{1,3},{2,0},{3,1},{4,6},{5,7},{6,4},{7,5},{8,10},{9,11},{10,... | collective-permute-start | bytes 1474568 | tf_op jit(solution)/shard_map/ppermute | solution.py:334
  21.2 2.2 %collective-permute-start.3 = (f32[88,128]{1,0:T(8,128)S(1)}, f32[88,128]{1,0:T(8,128)S(1)}, u32[]{:S(2)}, u32[]{:S(2)}) collective-permute-start(f32[88,128]{1,0:T(8,128)S(1)} %get-tuple-element.56), channel_id=1, source_target_pairs={{0,1},{1,0},{2,3},{3,2},{4,5},{5,4},{6,7},{7,6},{8,9},{9,8},{10,11... | collective-permute-start | bytes 135176 | tf_op jit(solution)/shard_map/ppermute | solution.py:334
  21.2 14.5 %collective-permute-start.4 = (f32[88,128]{1,0:T(8,128)S(1)}, f32[88,128]{1,0:T(8,128)S(1)}, u32[]{:S(2)}, u32[]{:S(2)}) collective-permute-start(f32[88,128]{1,0:T(8,128)S(1)} %get-tuple-element.57), channel_id=1, source_target_pairs={{0,2},{1,3},{2,0},{3,1},{4,6},{5,7},{6,4},{7,5},{8,10},{9,11},{10,... | collective-permute-start | bytes 135176 | tf_op jit(solution)/shard_map/ppermute | solution.py:334
  23.2 12.6 %collective-permute-start.5 = (f32[88,128]{1,0:T(8,128)S(1)}, f32[88,128]{1,0:T(8,128)S(1)}, u32[]{:S(2)}, u32[]{:S(2)}) collective-permute-start(f32[88,128]{1,0:T(8,128)S(1)} %get-tuple-element.58), channel_id=1, source_target_pairs={{0,3},{1,2},{2,1},{3,0},{4,7},{5,6},{6,5},{7,4},{8,11},{9,10},{10,... | collective-permute-start | bytes 135176 | tf_op jit(solution)/shard_map/ppermute | solution.py:334
  36.7 7.5 %collective-permute-start.7 = (f32[64,128]{1,0:T(8,128)S(1)}, f32[64,128]{1,0:T(8,128)S(1)}, u32[]{:S(2)}, u32[]{:S(2)}) collective-permute-start(f32[64,128]{1,0:T(8,128)S(1)} %get-tuple-element.67.refs_0_), channel_id=1, source_target_pairs={{0,8},{1,9},{2,10},{3,11},{4,12},{5,13},{6,14},{7,15},{8,0},{9,1},... | collective-permute-start | bytes 98312 | tf_op jit(solution)/shard_map/ppermute | solution.py:344
  36.7 13.6 %copy-start = (f32[48,768]{1,0:T(8,128)S(1)}, f32[48,768]{1,0:T(8,128)}, u32[]{:S(2)}) copy-start(f32[48,768]{1,0:T(8,128)} %mine.1) | copy-start | bytes 442372
  36.8 13.3 %collective-permute-start.11 = (f32[128,128]{1,0:T(8,128)S(1)}, f32[128,128]{1,0:T(8,128)S(1)}, u32[]{:S(2)}, u32[]{:S(2)}) collective-permute-start(f32[128,128]{1,0:T(8,128)S(1)} %get-tuple-element.66), channel_id=1, source_target_pairs={{3,6},{0,13},{7,10},{4,1},{11,14},{8,5},{15,2},{12,9},{19,22},{16,... | collective-permute-start | bytes 196616 | tf_op jit(solution)/shard_map/ppermute | solution.py:338
  41.9 8.3 %collective-permute-start.10 = (f32[128,128]{1,0:T(8,128)S(1)}, f32[128,128]{1,0:T(8,128)S(1)}, u32[]{:S(2)}, u32[]{:S(2)}) collective-permute-start(f32[128,128]{1,0:T(8,128)S(1)} %get-tuple-element.66), channel_id=1, source_target_pairs={{3,4},{0,15},{7,8},{4,3},{11,12},{8,7},{15,0},{12,11},{19,20},{16,... | collective-permute-start | bytes 196616 | tf_op jit(solution)/shard_map/ppermute | solution.py:338
  44.1 5.9 %collective-permute-start.6 = (f32[96,128]{1,0:T(8,128)S(1)}, f32[96,128]{1,0:T(8,128)S(1)}, u32[]{:S(2)}, u32[]{:S(2)}) collective-permute-start(f32[96,128]{1,0:T(8,128)S(1)} %get-tuple-element.60), channel_id=1, source_target_pairs={{0,4},{1,5},{2,6},{3,7},{4,8},{5,9},{6,10},{7,11},{8,12},{9,13},{1... | collective-permute-start | bytes 147464 | tf_op jit(solution)/shard_map/ppermute | solution.py:344
  44.1 5.9 %collective-permute-start.8 = (f32[96,128]{1,0:T(8,128)S(1)}, f32[96,128]{1,0:T(8,128)S(1)}, u32[]{:S(2)}, u32[]{:S(2)}) collective-permute-start(f32[96,128]{1,0:T(8,128)S(1)} %get-tuple-element.61), channel_id=1, source_target_pairs={{0,12},{1,13},{2,14},{3,15},{4,0},{5,1},{6,2},{7,3},{8,4},{9,5},{1... | collective-permute-start | bytes 147464 | tf_op jit(solution)/shard_map/ppermute | solution.py:344
  50.3 4.4 %collective-permute-start.13 = (f32[2176,128]{1,0:T(8,128)S(1)}, f32[2176,128]{1,0:T(8,128)S(1)}, u32[]{:S(2)}, u32[]{:S(2)}) collective-permute-start(f32[2176,128]{1,0:T(8,128)S(1)} %pad_maximum_fusion), channel_id=1, source_target_pairs={{0,1},{1,0},{2,3},{3,2},{4,5},{5,4},{6,7},{7,6},{8,9},{9,8},{10,11... | collective-permute-start | bytes 3342344 | tf_op jit(solution)/shard_map/ppermute | solution.py:334
  50.4 3.5 %collective-permute-start.12 = (f32[192,768]{1,0:T(8,128)S(1)}, f32[192,768]{1,0:T(8,128)S(1)}, u32[]{:S(2)}, u32[]{:S(2)}) collective-permute-start(f32[192,768]{1,0:T(8,128)S(1)} %pad_maximum_fusion.1), channel_id=1, source_target_pairs={{0,1},{1,0},{2,3},{3,2},{4,5},{5,4},{6,7},{7,6},{8,9},{9,8},{10,11... | collective-permute-start | bytes 1769480 | tf_op jit(solution)/shard_map/ppermute | solution.py:334
  58.6 8.7 %collective-permute-start.14 = (f32[96,128]{1,0:T(8,128)S(1)}, f32[96,128]{1,0:T(8,128)S(1)}, u32[]{:S(2)}, u32[]{:S(2)}) collective-permute-start(f32[96,128]{1,0:T(8,128)S(1)} %get-tuple-element.84), channel_id=1, source_target_pairs={{0,4},{1,5},{2,6},{3,7},{4,8},{5,9},{6,10},{7,11},{8,12},{9,13},{1... | collective-permute-start | bytes 147464 | tf_op jit(solution)/shard_map/ppermute | solution.py:344
  58.6 8.6 %collective-permute-start.16 = (f32[96,128]{1,0:T(8,128)S(1)}, f32[96,128]{1,0:T(8,128)S(1)}, u32[]{:S(2)}, u32[]{:S(2)}) collective-permute-start(f32[96,128]{1,0:T(8,128)S(1)} %get-tuple-element.85), channel_id=1, source_target_pairs={{0,12},{1,13},{2,14},{3,15},{4,0},{5,1},{6,2},{7,3},{8,4},{9,5},{1... | collective-permute-start | bytes 147464 | tf_op jit(solution)/shard_map/ppermute | solution.py:344
  62.4 4.8 %collective-permute-start.15 = (f32[64,128]{1,0:T(8,128)S(1)}, f32[64,128]{1,0:T(8,128)S(1)}, u32[]{:S(2)}, u32[]{:S(2)}) collective-permute-start(f32[64,128]{1,0:T(8,128)S(1)} %get-tuple-element.83.refs_0_), channel_id=1, source_target_pairs={{0,8},{1,9},{2,10},{3,11},{4,12},{5,13},{6,14},{7,15},{8,0},{9,1},... | collective-permute-start | bytes 98312 | tf_op jit(solution)/shard_map/ppermute | solution.py:344
  67.2 18.9 %slice-start = ((s8[9437184]{0:T(1024)(128)(4,1)}), s8[4194304]{0:T(1024)(128)(4,1)S(1)}, s32[]{:S(2)}) async-start(s8[9437184]{0:T(1024)(128)(4,1)} %bitcast.5), calls=%async_computation | async-start | bytes 8388608
  67.2 18.9 %slice-start.1 = ((s8[9437184]{0:T(1024)(128)(4,1)}), s8[4194304]{0:T(1024)(128)(4,1)S(1)}, s32[]{:S(2)}) async-start(s8[9437184]{0:T(1024)(128)(4,1)} %bitcast.5), calls=%async_computation.1 | async-start | bytes 8388608
  70.1 8.7 %collective-permute-start.17 = (f32[96,128]{1,0:T(8,128)S(1)}, f32[96,128]{1,0:T(8,128)S(1)}, u32[]{:S(2)}, u32[]{:S(2)}) collective-permute-start(f32[96,128]{1,0:T(8,128)S(1)} %get-tuple-element.90), channel_id=1, source_target_pairs={{0,4},{1,5},{2,6},{3,7},{4,8},{5,9},{6,10},{7,11},{8,12},{9,13},{1... | collective-permute-start | bytes 147464 | tf_op jit(solution)/shard_map/ppermute | solution.py:344
  70.2 8.6 %collective-permute-start.19 = (f32[96,128]{1,0:T(8,128)S(1)}, f32[96,128]{1,0:T(8,128)S(1)}, u32[]{:S(2)}, u32[]{:S(2)}) collective-permute-start(f32[96,128]{1,0:T(8,128)S(1)} %get-tuple-element.91), channel_id=1, source_target_pairs={{0,12},{1,13},{2,14},{3,15},{4,0},{5,1},{6,2},{7,3},{8,4},{9,5},{1... | collective-permute-start | bytes 147464 | tf_op jit(solution)/shard_map/ppermute | solution.py:344
  73.9 4.8 %collective-permute-start.18 = (f32[64,128]{1,0:T(8,128)S(1)}, f32[64,128]{1,0:T(8,128)S(1)}, u32[]{:S(2)}, u32[]{:S(2)}) collective-permute-start(f32[64,128]{1,0:T(8,128)S(1)} %get-tuple-element.89.refs_0_), channel_id=1, source_target_pairs={{0,8},{1,9},{2,10},{3,11},{4,12},{5,13},{6,14},{7,15},{8,0},{9,1},... | collective-permute-start | bytes 98312 | tf_op jit(solution)/shard_map/ppermute | solution.py:344
  78.8 7.4 %slice-start.2 = ((s8[9437184]{0:T(1024)(128)(4,1)}), s8[1048576]{0:T(1024)(128)(4,1)S(1)}, s32[]{:S(2)}) async-start(s8[9437184]{0:T(1024)(128)(4,1)} %bitcast.5), calls=%async_computation.2 | async-start | bytes 2097152
  78.8 7.4 %copy-start.2 = (bf16[1536,384]{1,0:T(8,128)(2,1)S(1)}, bf16[1536,384]{1,0:T(8,128)(2,1)}, u32[]{:S(2)}) copy-start(bf16[1536,384]{1,0:T(8,128)(2,1)} %get-tuple-element.99.places) | copy-start | bytes 3538948
  80.8 1.9 %collective-permute-start.20 = (f32[120,128]{1,0:T(8,128)S(1)}, f32[120,128]{1,0:T(8,128)S(1)}, u32[]{:S(2)}, u32[]{:S(2)}) collective-permute-start(f32[120,128]{1,0:T(8,128)S(1)} %get-tuple-element.96), channel_id=1, source_target_pairs={{0,1},{1,0},{2,3},{3,2},{4,5},{5,4},{6,7},{7,6},{8,9},{9,8},{10,11... | collective-permute-start | bytes 184328 | tf_op jit(solution)/shard_map/ppermute | solution.py:334
  80.9 4.9 %collective-permute-start.21 = (f32[120,128]{1,0:T(8,128)S(1)}, f32[120,128]{1,0:T(8,128)S(1)}, u32[]{:S(2)}, u32[]{:S(2)}) collective-permute-start(f32[120,128]{1,0:T(8,128)S(1)} %get-tuple-element.97), channel_id=1, source_target_pairs={{0,2},{1,3},{2,0},{3,1},{4,6},{5,7},{6,4},{7,5},{8,10},{9,11},{10,... | collective-permute-start | bytes 184328 | tf_op jit(solution)/shard_map/ppermute | solution.py:334
  81.6 4.6 %collective-permute-start.22 = (f32[120,128]{1,0:T(8,128)S(1)}, f32[120,128]{1,0:T(8,128)S(1)}, u32[]{:S(2)}, u32[]{:S(2)}) collective-permute-start(f32[120,128]{1,0:T(8,128)S(1)} %get-tuple-element.98), channel_id=1, source_target_pairs={{0,3},{1,2},{2,1},{3,0},{4,7},{5,6},{6,5},{7,4},{8,11},{9,10},{10,... | collective-permute-start | bytes 184328 | tf_op jit(solution)/shard_map/ppermute | solution.py:334

commit v6 on v5

--- a/solution.py
+++ b/solution.py
@@ -10,6 +10,7 @@
 ITERS = 3
 DAMPING = 0.5
 GROUP = 4
+PAIRED = 4
 LANES = 128
 BF16 = jnp.bfloat16
 F32 = jnp.float32
@@ -116,17 +117,21 @@
     return p[:m, :n] + p[:m, n:] + p[m:, :n]
 
 
-def payload(v, width, out, out_up, out_down):
+def payload(v, width, paired, odd, out, out_a, out_b):
     coarse = v[2 * width:]
     owned = coarse.shape[0] // 2
     below = turned(coarse[owned:], 1)
     own = coarse[:owned] + jnp.where(lane_block(owned) == 0, 0.0, below)
     rows = jnp.concatenate([own, packed(below, chunk_of(owned))], axis=0)
     size = rows.shape[0]
-    for ref in (out, out_up, out_down):
+    for ref in (out, out_a, out_b):
         ref[:size] = rows
-    out_up[size:] = packed(turned(v[width:2 * width], 1), width // GROUP)
-    out_down[size:] = packed(v[:width], width // GROUP)
+    up = packed(turned(v[width:2 * width], 1), width // GROUP)
+    down = packed(v[:width], width // GROUP)
+    if paired:
+        up, down = jnp.where(odd, down, up), jnp.where(odd, up, down)
+    out_a[size:] = up
+    out_b[size:] = down
 
 
 def fetch(source, count, rows, target, places, sem):
@@ -137,9 +142,10 @@
     lax.fori_loop(0, count, one, 0, unroll=8)
 
 
-def rows_kernel(count, table, k_ref, f_ref, tablev, *rest):
+def rows_kernel(count, table, k_ref, f_ref, c_ref, tablev, *rest):
     pieces, (spans, edge, places, ks, right_side, sem) = rest[:GROUP], rest[GROUP:]
     width, order, columns = edge.shape[1], ks.shape[1], f_ref.shape[1]
+    owned = c_ref.shape[0]
     side = 2 * width
     fetch(k_ref, count, lambda j: table[2, j], ks, lambda j: side + table[3, j], sem)
     fetch(k_ref, side, lambda j: table[j // width, j % width], ks, lambda j: j, sem)
@@ -158,6 +164,9 @@
     right_side[:, side + count:side + width] = jnp.zeros((order, width - count), BF16)
     right_side[:, side + width:] = beside(f_ref[...])
     places[...] = right_side[:, :side + width]
+    for i in range(c_ref.shape[1] // LANES):
+        at = width + i * owned
+        edge[at:at + owned] = c_ref[:, i * LANES:(i + 1) * LANES]
     pltpu.make_async_copy(k_ref.at[pl.ds(0, ks.shape[0])], ks, sem).wait()
 
     at = side + width
@@ -170,7 +179,7 @@
     for i in range(3):
         kept = side if i == 2 else rows
         spans[i * rows:i * rows + kept] = block[:kept, i * width:(i + 1) * width]
-    edge[...] = jnp.where(table[4, 0] == GROUP - 1, block[width:side, side:], block[:width, side:])
+    edge[:width] = jnp.where(table[4, 0] == GROUP - 1, block[width:side, side:], block[:width, side:])
 
 
 GOT = (-1, None, 5, 4)
@@ -181,51 +190,51 @@
 GOT_NEXT = (5, 4, -1, None)
 
 
-def solver_kernel(pos, mine, next_mine, got, next_got, theirs, out):
-    owned = mine.shape[0]
-    half = out.shape[0] // 2
-    other = [theirs[i * owned:(i + 1) * owned] for i in range(4)]
-    for m in range(GROUP):
-
-        @pl.when(pos[0] == m)
-        def _():
-            p = m ^ 1
-            held = [(m, mine[...]), (m ^ 2, next_mine[...]), (GOT[m], got[...]), (GOT_NEXT[m], next_got[...])]
-            held += list(zip((p, p ^ 2, GOT[p], GOT_NEXT[p]), other))
-            for block, values in held:
-                if block is not None:
-                    at = (block + 1) * owned
-                    high, low = halves(values)
-                    out[at:at + owned] = high
-                    out[half + at:half + at + owned] = low
-
-
-def blocks_kernel(width, pos, s0, s2, came, came_next, theirs, cross, own, edge_up, edge_down):
-    side, size = 2 * width, s0.shape[0]
+def blocks_kernel(width, pos, c0, c2, c_other, s0, s2, came, came_next, theirs, solver, cross, own, edge_up, edge_down):
+    side, size, edge_size = 2 * width, s0.shape[0], came.shape[0]
     kept = (size - side) // 2
+    owned, tall = c0.shape[0], c0.shape[1] // LANES
+    half = solver.shape[0] // 2
     other, at = [], 0
-    for rows in (size, size, width, width):
+    for rows in (size, size, edge_size, edge_size):
         other.append(theirs.at[at:at + rows])
         at += rows
     for k, ref in enumerate((s0, other[0], s2, other[1])):
         own[:, k * side:k * side + width] = stacked(ref[:kept])
         own[:, k * side + width:(k + 1) * side] = stacked(ref[kept:2 * kept])
         cross[:, k * width:(k + 1) * width] = stacked(ref[2 * kept:])
+
+    def placed(block, values, columns):
+        at = (block + 1) * owned
+        high, low = halves(values)
+        solver[at:at + owned, columns] = high
+        solver[half + at:half + at + owned, columns] = low
+
     for m in range(GROUP):
 
         @pl.when(pos[0] == m)
         def _():
+            p = m ^ 1
+            everything = slice(None)
+            placed(m, c0[...], everything)
+            placed(m ^ 2, c2[...], everything)
+            placed(p, c_other[:owned], everything)
+            placed(p ^ 2, c_other[owned:], everything)
             held = {GOT[m]: came, GOT_NEXT[m]: came_next}
-            for block, ref in zip((GOT[m ^ 1], GOT_NEXT[m ^ 1]), other[2:]):
+            for block, ref in zip((GOT[p], GOT_NEXT[p]), other[2:]):
                 held.setdefault(block, ref)
-            edge_up[...] = stacked(held[-1][...])
-            edge_down[...] = stacked(held[4][...])
-
-
-def start_kernel(pos, p0, p1, p2, p3, v_ref, *pays):
+            for block in (-1, 4, 5):
+                for i in range(tall):
+                    at = width + i * owned
+                    placed(block, held[block][at:at + owned], slice(i * LANES, (i + 1) * LANES))
+            edge_up[...] = stacked(held[-1][:width])
+            edge_down[...] = stacked(held[4][:width])
+
+
+def start_kernel(paired, pos, p0, p1, p2, p3, v_ref, *pays):
     v = joined([p0[...], p1[...], p2[...], p3[...]], pos[0])
     v_ref[...] = v
-    payload(v, v.shape[1], *pays)
+    payload(v, v.shape[1], paired, pos[1] % 2 == 1, *pays)
 
 
 def shared(x, member):
@@ -246,7 +255,8 @@
         now = v0
     else:
         (now, left_ref, right_ref), refs = refs[:3], refs[3:]
-    outs, stack = refs[:-1], refs[-1]
+    outs, (held, stack) = refs[:-2], refs[-2:]
+    paired = groups == PAIRED
     member, group = pos[0], pos[1]
     width = edge_down.shape[1]
     owned = (v0.shape[0] - 2 * width) // 2
@@ -254,12 +264,13 @@
     first = lane_block(owned) == 0
 
     for k in range(groups):
-        h = lax.rem(group - k + groups, groups)
-        extra = unpacked(pays[(k + 1) % groups][owned:size, :], -(-owned // chunk_of(owned)))[:owned]
-        whole = pays[k][:owned, :] + jnp.where(first, extra, 0.0)
+        held[group ^ k if paired else lax.rem(group - k + groups, groups)] = pays[k][:size, :]
+    for h in range(groups):
+        extra = unpacked(held[(h - 1) % groups, owned:], -(-owned // chunk_of(owned)))[:owned]
+        whole = held[h, :owned] + jnp.where(first, extra, 0.0)
         for i in range(GROUP):
-            place = pl.multiple_of((h * GROUP + i) * owned, 16)
-            stack[pl.ds(place, owned), :] = beside(turned(whole, -i))
+            place = (h * GROUP + i) * owned
+            stack[place:place + owned, :] = beside(turned(whole, -i))
 
     w = combined(dot(solver[...], stack[...]), LANES)
     pair = lane_block(2 * owned)
@@ -275,6 +286,9 @@
     left, right = faces[:width], faces[width:]
     before, after = beside(padded(w[:2 * owned])), beside(padded(w[(GROUP + 1) * owned:]))
     halo_up, halo_down = pays[1][size:, :], pays[groups - 1][size:, :]
+    if paired:
+        odd = group % 2 == 1
+        halo_up, halo_down = jnp.where(odd, halo_up, halo_down), jnp.where(odd, halo_down, halo_up)
     right_before = unpacked(halo_up, GROUP) - combined(dot(edge_up[...], before), LANES)
     left_after = unpacked(halo_down, GROUP) - combined(dot(edge_down[...], after), LANES)
     block = lane_block(width)
@@ -294,7 +308,7 @@
     lam = jnp.concatenate([lam_left, -lam_right], axis=0)
     v = v0[...] + combined(dot(own[...], shared(lam, member)), LANES)
     v_ref[...] = v
-    payload(v, width, *outs[3:])
+    payload(v, width, paired, group % 2 == 1, *outs[3:])
 
 
 def final_kernel(count, pos, p0, p1, p2, p3, f_ref, places, k_ref, out, lam_ref):
@@ -343,21 +357,24 @@
     def planes(x, by):
         return lax.ppermute(x, "sub", [(s, (s + by * GROUP) % total) for s in range(total)])
 
-    def along(pay, up, down):
-        return [pay, planes(up, 1)] + [planes(pay, k) for k in range(2, groups - 1)] + [planes(down, -1)]
+    def along(pay, a, b):
+        if groups == PAIRED:
+            last = mate(b, 3 * GROUP)
+            middle = mate(pay, 2 * GROUP)
+            return [pay, mate(a, GROUP), middle, last]
+        return [pay, planes(a, 1)] + [planes(pay, k) for k in range(2, groups - 1)] + [planes(b, -1)]
 
     def after(x, other):
         return lax.optimization_barrier((x, other))[0]
 
     c_next = mate(coarse_inverse, 2)
-    got = crossing(coarse_inverse, [(GROUP - 1, GROUP), (0, -1), (1, -2)])
-    got_next = crossing(coarse_inverse, [(GROUP - 1, GROUP + 2), (0, -3), (1, -4)])
+    tall = owned * coarse // LANES
 
     *pieces, spans, edge, places = call(
         functools.partial(rows_kernel, count),
         [(kept // GROUP, LANES)] * GROUP
-        + [(2 * kept + side, width), (width, width), ((order, side + width), BF16)],
-        (table, condensed, eigen_loads, table),
+        + [(2 * kept + side, width), (width + tall, width), ((order, side + width), BF16)],
+        (table, condensed, eigen_loads, coarse_inverse, table),
         7.5,
         hbm=(1,),
         scratch=[
@@ -367,34 +384,36 @@
         ],
         vmem=52,
     )
-    spans_next = mate(after(spans, (c_next, got, got_next)), 2)
-    *pieces, c_next, got, got_next = lax.optimization_barrier((*pieces, c_next, got, got_next))
+    *pieces, c_next = lax.optimization_barrier((*pieces, c_next))
     pieces = traded(pieces)
-    came = crossing(after(edge, pieces), [(GROUP - 1, GROUP), (0, -1)])
-    theirs_c = mate(after(jnp.concatenate([coarse_inverse, c_next, got, got_next], axis=0), pieces), 1)
+    c_other = mate(jnp.concatenate([coarse_inverse, c_next], axis=0), 1)
+    spans_next = mate(after(spans, pieces), 2)
+    edge = after(edge, pieces)
+    came = crossing(edge, [(GROUP - 1, GROUP), (0, -1), (1, -2)])
+    came_next = crossing(edge, [(GROUP - 1, GROUP + 2), (0, -3), (1, -4)])
+    pieces[0] = after(pieces[0], c_other)
     size = owned + chunk_of(owned)
     pay_shapes = [(size, LANES)] + [(size + width // GROUP, LANES)] * 2
-    v0, *pays = call(start_kernel, [(kept, LANES), *pay_shapes], (pos, *pieces), 0.9)
-    came_next = crossing(after(edge, pays), [(GROUP - 1, GROUP + 2), (0, -3)])
+    v0, *pays = call(
+        functools.partial(start_kernel, groups == PAIRED),
+        [(kept, LANES), *pay_shapes],
+        (pos, *pieces),
+        0.9,
+    )
     pays = along(*pays)
-    (solver,) = call(
-        solver_kernel,
-        [((2 * (GROUP + 3) * owned, coarse), BF16)],
-        (pos, coarse_inverse, c_next, got, got_next, theirs_c),
-        0.7,
-    )
     *pays, spans_next, came, came_next = lax.optimization_barrier((*pays, spans_next, came, came_next))
     theirs = mate(jnp.concatenate([spans, spans_next, came, came_next], axis=0), 1)
     blocks = call(
         functools.partial(blocks_kernel, width),
         [
+            ((2 * (GROUP + 3) * owned, coarse), BF16),
             ((2 * side, GROUP * width), BF16),
             ((2 * kept, GROUP * side), BF16),
             ((side, width), BF16),
             ((side, width), BF16),
         ],
-        (pos, spans, spans_next, came, came_next, theirs),
-        1,
+        (pos, coarse_inverse, c_next, c_other, spans, spans_next, came, came_next, theirs),
+        1.7,
     )
 
     state = ()
@@ -406,9 +425,9 @@
         outs = call(
             functools.partial(turn_kernel, kind, groups),
             shapes,
-            (pos, *pays, solver, *blocks, v0, *state),
+            (pos, *pays, *blocks, v0, *state),
             2.8,
-            scratch=[pltpu.VMEM((coarse, 2 * LANES), BF16)],
+            scratch=[pltpu.VMEM((groups, size, LANES), F32), pltpu.VMEM((coarse, 2 * LANES), BF16)],
         )
         if kind != "last":
             state = outs[:3]

time: 92 us -> 79.4 us (0.86)
  starting transfers between devices: 34.7 us -> 27.8 us
  waiting for transfers between devices: 30.2 us -> 24.2 us
    ppermute x10 -> x19, starting transfers between devices: 7.82 us -> 20.1 us  [mate(): return lax.ppermute(x, 'sub', [(s, s ^ k) for s in range(total)])]
    ppermute x9 -> x0, starting transfers between devices: 12.1 us -> none  [planes(): lax.ppermute(x, 'sub', [(s, (s + by * GROUP) % total) for s in range(tota...]
    ppermute x9 -> x0, waiting for transfers between devices: 11.3 us -> none  [planes(): lax.ppermute(x, 'sub', [(s, (s + by * GROUP) % total) for s in range(tota...]
    ppermute x4 -> x2, starting transfers between devices: 14.8 us -> 7.71 us  [crossing(): return lax.ppermute(x, 'sub', pairs)]
    ppermute x4 -> x2, waiting for transfers between devices: 0.18 us -> 3.82 us  [crossing(): return lax.ppermute(x, 'sub', pairs)]
    ppermute x10 -> x19, waiting for transfers between devices: 18.7 us -> 20.3 us  [mate(): return lax.ppermute(x, 'sub', [(s, s ^ k) for s in range(total)])]
    pallas_call x8 -> x7, Pallas kernels: 23.8 us -> 23.3 us  [call(): pl.pallas_call(kernel, out_shape=[jax.ShapeDtypeStruct(s, d) for s, d in...]
  transfers between devices with their start and end apart: 23 -> 21, of which waited for: 8 -> 11; matrix products, arithmetic and copies ran while one was open for 1% -> 1% of each run, Pallas kernels for 10% -> 11%
where the time goes in v6:
time: 79.4 us; the launch traced here: 79.1 us
  starting transfers between devices  27.8 us (35%)
  waiting for transfers between devices  24.2 us (30%)
  Pallas kernels  23.3 us (29%)
  local copies, waits for them, and re-layouts  2.06 us (3%)
  other arithmetic  0.99 us (1%)
  between operations  0.8 us (1%)
    pallas_call x7, Pallas kernels, call(): pl.pallas_call(kernel, out_shape=[jax.ShapeDtypeStruct(s, d) for s, d in...  23.3 us
    ppermute x19, waiting for transfers between devices, mate(): return lax.ppermute(x, 'sub', [(s, s ^ k) for s in range(total)])  20.3 us
    ppermute x19, starting transfers between devices, mate(): return lax.ppermute(x, 'sub', [(s, s ^ k) for s in range(total)])  20.1 us
    ppermute x2, starting transfers between devices, crossing(): return lax.ppermute(x, 'sub', pairs)  7.71 us
    ppermute x2, waiting for transfers between devices, crossing(): return lax.ppermute(x, 'sub', pairs)  3.82 us
    unnamed x12, local copies, waits for them, and re-layouts  2.06 us
  transfers between devices with their start and end apart: 21, of which 11 were waited for; matrix products, arithmetic and copies ran while one was open for 1% of the time, Pallas kernels for 11%

profile of v6, /device:TPU:0, one launch (start us, length us, event | category | flops | bytes accessed | tf_op | source)
XLA Modules:
  0.0 79.1 jit_solution(6899944142111632908)
XLA Ops:
  0.6 3.0 %collective-permute-start = (f32[48,768]{1,0:T(8,128)}, f32[48,768]{1,0:T(8,128)S(1)}, u32[]{:S(2)}, u32[]{:S(2)}) collective-permute-start(f32[48,768]{1,0:T(8,128)} %c0.1), channel_id=1, source_target_pairs={{0,2},{1,3},{2,0},{3,1},{4,6},{5,7},{6,4},{7,5},{8,10},{9,11},{10,... | collective-permute-start | bytes 442376 | tf_op jit(solution)/shard_map/ppermute | solution.py:348
  3.7 0.1 fusion
  3.7 0.7 pad_add_fusion.table.tablev
  4.5 0.0 copy-start
  4.5 0.9 %copy-done = f32[48,768]{1,0:T(8,128)S(1)} copy-done((f32[48,768]{1,0:T(8,128)S(1)}, f32[48,768]{1,0:T(8,128)}, u32[]{:S(2)}) %copy-start) | copy-done | bytes 147480
  5.4 0.0 copy-start.1
  5.4 1.1 %copy-done.1 = f32[1536,128]{1,0:T(8,128)S(1)} copy-done((f32[1536,128]{1,0:T(8,128)S(1)}, f32[1536,128]{1,0:T(8,128)}, u32[]{:S(2)}) %copy-start.1) | copy-done | bytes 786456
  6.5 7.9 %shard_map.77 = (f32[88,128]{1,0:T(8,128)S(1)}, f32[88,128]{1,0:T(8,128)S(1)}, f32[88,128]{1,0:T(8,128)S(1)}, f32[88,128]{1,0:T(8,128)S(1)}, f32[960,128]{1,0:T(...) custom-call(s32[5,128]{1,0:T(8,128)S(1)} %pad_add_fusion.table.tablev, f32[1536,1536]{1,0:T(8,128)} %k_ref.3, ...), custom_call_target="tpu_custom_call" | custom-call | flops 7500000256 | tf_op jit(solution)/shard_map/pallas_call | solution.py:25
  14.4 0.0 collective-permute-done.c2
  14.4 0.1 collective-permute-start.2
  14.5 0.1 collective-permute-start.3
  14.6 1.8 %collective-permute-start.4 = (f32[88,128]{1,0:T(8,128)S(1)}, f32[88,128]{1,0:T(8,128)S(1)}, u32[]{:S(2)}, u32[]{:S(2)}) collective-permute-start(f32[88,128]{1,0:T(8,128)S(1)} %get-tuple-element.58), channel_id=1, source_target_pairs={{0,3},{1,2},{2,1},{3,0},{4,7},{5,6},{6,5},{7,4},{8,11},{9,10},{10,... | collective-permute-start | bytes 135176 | tf_op jit(solution)/shard_map/ppermute | solution.py:348
  16.4 0.0 collective-permute-done.2.p1
  16.4 2.7 %collective-permute-done.3.p2 = f32[88,128]{1,0:T(8,128)S(1)} collective-permute-done((f32[88,128]{1,0:T(8,128)S(1)}, f32[88,128]{1,0:T(8,128)S(1)}, u32[]{:S(2)}, u32[]{:S(2)}) %collective-permute-start.3) | collective-permute-done | bytes 45088 | tf_op jit(solution)/shard_map/ppermute | solution.py:348
  19.0 0.1 collective-permute-done.4.p3
  19.1 1.1 %collective-permute-start.8 = (f32[960,128]{1,0:T(8,128)S(1)}, f32[960,128]{1,0:T(8,128)S(1)}, u32[]{:S(2)}, u32[]{:S(2)}) collective-permute-start(f32[960,128]{1,0:T(8,128)S(1)} %get-tuple-element.63.s0), channel_id=1, source_target_pairs={{0,2},{1,3},{2,0},{3,1},{4,6},{5,7},{6,4},{7,5},{8,10},{9,11},{10,... | collective-permute-start | bytes 1474568 | tf_op jit(solution)/shard_map/ppermute | solution.py:348
  20.2 0.1 collective-permute-start.1
  20.3 5.6 %collective-permute-start.10 = (f32[416,128]{1,0:T(8,128)S(1)}, f32[416,128]{1,0:T(8,128)S(1)}, u32[]{:S(2)}, u32[]{:S(2)}) collective-permute-start(f32[416,128]{1,0:T(8,128)S(1)} %get-tuple-element.65), channel_id=1, source_target_pairs={{3,6},{0,13},{1,12},{7,10},{4,1},{5,0},{11,14},{8,5},{9,4},{15,2},... | collective-permute-start | bytes 638984 | tf_op jit(solution)/shard_map/ppermute | solution.py:352
  25.9 2.1 %collective-permute-start.9 = (f32[416,128]{1,0:T(8,128)S(1)}, f32[416,128]{1,0:T(8,128)S(1)}, u32[]{:S(2)}, u32[]{:S(2)}) collective-permute-start(f32[416,128]{1,0:T(8,128)S(1)} %get-tuple-element.65), channel_id=1, source_target_pairs={{3,4},{0,15},{1,14},{7,8},{4,3},{5,2},{11,12},{8,7},{9,6},{15,0},{... | collective-permute-start | bytes 638984 | tf_op jit(solution)/shard_map/ppermute | solution.py:352
  28.0 0.1 pad_add_fusion.3.pos
  28.1 0.0 collective-permute-done.1.c_other
  28.1 0.9 %shard_map.78 = (f32[352,128]{1,0:T(8,128)S(1)}, f32[64,128]{1,0:T(8,128)S(1)}, f32[96,128]{1,0:T(8,128)S(1)}, f32[96,128]{1,0:T(8,128)S(1)}) custom-call(s32[2]{0:T(128)S(1)} %pad_add_fusion.3.pos, f32[88,128]{1,0:T(8,128)S(1)} %get-tuple-element.55.p0, f32[88,128]{1,0:T(8,128)S(1)} %collective-permute-done.2.p1, f32[88,128]{1,0:T(8,128)S(1)} %collective-permute-done.3.p2, ...), custom_call_target="tpu_custom_call" | custom-call | flops 900000000 | tf_op jit(solution)/shard_map/pallas_call | solution.py:25
  29.0 0.1 collective-permute-start.5
  29.1 2.2 %collective-permute-start.7 = (f32[96,128]{1,0:T(8,128)S(1)}, f32[96,128]{1,0:T(8,128)S(1)}, u32[]{:S(2)}, u32[]{:S(2)}) collective-permute-start(f32[96,128]{1,0:T(8,128)S(1)} %get-tuple-element.61), channel_id=1, source_target_pairs={{0,12},{1,13},{2,14},{3,15},{4,8},{5,9},{6,10},{7,11},{8,4},{9,5},... | collective-permute-start | bytes 147464 | tf_op jit(solution)/shard_map/ppermute | solution.py:348
  31.3 0.2 collective-permute-done.10.came_next
  31.6 1.0 %collective-permute-start.6 = (f32[64,128]{1,0:T(8,128)S(1)}, f32[64,128]{1,0:T(8,128)S(1)}, u32[]{:S(2)}, u32[]{:S(2)}) collective-permute-start(f32[64,128]{1,0:T(8,128)S(1)} %get-tuple-element.66.refs_0_), channel_id=1, source_target_pairs={{0,8},{1,9},{2,10},{3,11},{4,12},{5,13},{6,14},{7,15},{8,0},{9,1},... | collective-permute-start | bytes 98312 | tf_op jit(solution)/shard_map/ppermute | solution.py:348
  32.6 3.6 %collective-permute-done.9.came = f32[416,128]{1,0:T(8,128)S(1)} collective-permute-done((f32[416,128]{1,0:T(8,128)S(1)}, f32[416,128]{1,0:T(8,128)S(1)}, u32[]{:S(2)}, u32[]{:S(2)}) %collective-permute-start.9) | collective-permute-done | bytes 213024 | tf_op jit(solution)/shard_map/ppermute | solution.py:352
  36.2 2.2 %collective-permute-done.6.refs_2_ = f32[64,128]{1,0:T(8,128)S(1)} collective-permute-done((f32[64,128]{1,0:T(8,128)S(1)}, f32[64,128]{1,0:T(8,128)S(1)}, u32[]{:S(2)}, u32[]{:S(2)}) %collective-permute-start.6) | collective-permute-done | bytes 32800 | tf_op jit(solution)/shard_map/ppermute | solution.py:348
  38.4 0.0 collective-permute-done.5.refs_1_
  38.4 0.5 collective-permute-done.7.refs_3_
  38.8 0.0 collective-permute-done.8.s2
  38.8 0.1 pad_maximum_fusion
  38.9 0.1 collective-permute-start.11
  39.0 3.2 %collective-permute-done.11.theirs = f32[2752,128]{1,0:T(8,128)S(1)} collective-permute-done((f32[2752,128]{1,0:T(8,128)S(1)}, f32[2752,128]{1,0:T(8,128)S(1)}, u32[]{:S(2)}, u32[]{:S(2)}) %collective-permute-start.11) | collective-permute-done | bytes 1409056 | tf_op jit(solution)/shard_map/ppermute | solution.py:348
  42.2 1.4 %shard_map.79 = (bf16[672,768]{1,0:T(8,128)(2,1)S(1)}, bf16[512,512]{1,0:T(8,128)(2,1)S(1)}, bf16[704,1024]{1,0:T(8,128)(2,1)S(1)}, bf16[256,128]{1,0:T(8,128)(2,1)S(1)}, bf16[256,128]{1,0:T(8,128)(2,1)S(1)}) custom-call(s32[2]{0:T(128)S(1)} %pad_add_fusion.3.pos, f32[48,768]{1,0:T(8,128)S(1)} %copy-done, f32[48,768]{1,0:T(8,128)S(1)} %collective-permute-done.c2, ...), custom_call_target="tpu_custom_call" | custom-call | flops 1700000000 | tf_op jit(solution)/shard_map/pallas_call | solution.py:25
  43.6 2.8 %shard_map.80 = (f32[352,128]{1,0:T(8,128)S(1)}, f32[128,128]{1,0:T(8,128)S(1)}, f32[128,128]{1,0:T(8,128)S(1)}, f32[64,128]{1,0:T(8,128)S(1)}, f32[96,128]{1,0:T(8,128)S(1)}, /*index=5*/f32[96,128]{1,0:T(8,128)S(1)}) custom-call(s32[2]{0:T(128)S(1)} %pad_add_fusion.3.pos, f32[64,128]{1,0:T(8,128)S(1)} %get-tuple-element.66.refs_0_, ...), custom_call_target="tpu_custom_call" | custom-call | flops 2800000000 | tf_op jit(solution)/shard_map/pallas_call | solution.py:25
  46.3 1.6 %collective-permute-start.12 = (f32[96,128]{1,0:T(8,128)S(1)}, f32[96,128]{1,0:T(8,128)S(1)}, u32[]{:S(2)}, u32[]{:S(2)}) collective-permute-start(f32[96,128]{1,0:T(8,128)S(1)} %get-tuple-element.80), channel_id=1, source_target_pairs={{0,4},{1,5},{2,6},{3,7},{4,0},{5,1},{6,2},{7,3},{8,12},{9,13},{10,... | collective-permute-start | bytes 147464 | tf_op jit(solution)/shard_map/ppermute | solution.py:348
  48.0 2.9 %collective-permute-start.14 = (f32[96,128]{1,0:T(8,128)S(1)}, f32[96,128]{1,0:T(8,128)S(1)}, u32[]{:S(2)}, u32[]{:S(2)}) collective-permute-start(f32[96,128]{1,0:T(8,128)S(1)} %get-tuple-element.81), channel_id=1, source_target_pairs={{0,12},{1,13},{2,14},{3,15},{4,8},{5,9},{6,10},{7,11},{8,4},{9,5},... | collective-permute-start | bytes 147464 | tf_op jit(solution)/shard_map/ppermute | solution.py:348
  50.9 0.5 collective-permute-start.13
  51.4 4.3 %collective-permute-done.13.refs_2_ = f32[64,128]{1,0:T(8,128)S(1)} collective-permute-done((f32[64,128]{1,0:T(8,128)S(1)}, f32[64,128]{1,0:T(8,128)S(1)}, u32[]{:S(2)}, u32[]{:S(2)}) %collective-permute-start.13) | collective-permute-done | bytes 32800 | tf_op jit(solution)/shard_map/ppermute | solution.py:348
  55.7 0.0 collective-permute-done.12.refs_1_
  55.7 0.0 collective-permute-done.14.refs_3_
  55.7 0.0 slice-start
  55.7 0.0 slice-start.1
  55.8 2.8 %shard_map.81 = (f32[352,128]{1,0:T(8,128)S(1)}, f32[128,128]{1,0:T(8,128)S(1)}, f32[128,128]{1,0:T(8,128)S(1)}, f32[64,128]{1,0:T(8,128)S(1)}, f32[96,128]{1,0:T(8,128)S(1)}, /*index=5*/f32[96,128]{1,0:T(8,128)S(1)}) custom-call(s32[2]{0:T(128)S(1)} %pad_add_fusion.3.pos, f32[64,128]{1,0:T(8,128)S(1)} %get-tuple-element.79.refs_0_, ...), custom_call_target="tpu_custom_call" | custom-call | flops 2800000000 | tf_op jit(solution)/shard_map/pallas_call | solution.py:25
  58.5 1.1 %collective-permute-start.15 = (f32[96,128]{1,0:T(8,128)S(1)}, f32[96,128]{1,0:T(8,128)S(1)}, u32[]{:S(2)}, u32[]{:S(2)}) collective-permute-start(f32[96,128]{1,0:T(8,128)S(1)} %get-tuple-element.86), channel_id=1, source_target_pairs={{0,4},{1,5},{2,6},{3,7},{4,0},{5,1},{6,2},{7,3},{8,12},{9,13},{10,... | collective-permute-start | bytes 147464 | tf_op jit(solution)/shard_map/ppermute | solution.py:348
  59.6 1.7 %collective-permute-start.17 = (f32[96,128]{1,0:T(8,128)S(1)}, f32[96,128]{1,0:T(8,128)S(1)}, u32[]{:S(2)}, u32[]{:S(2)}) collective-permute-start(f32[96,128]{1,0:T(8,128)S(1)} %get-tuple-element.87), channel_id=1, source_target_pairs={{0,12},{1,13},{2,14},{3,15},{4,8},{5,9},{6,10},{7,11},{8,4},{9,5},... | collective-permute-start | bytes 147464 | tf_op jit(solution)/shard_map/ppermute | solution.py:348
  61.3 0.8 collective-permute-start.16
  62.1 4.0 %collective-permute-done.16.refs_2_ = f32[64,128]{1,0:T(8,128)S(1)} collective-permute-done((f32[64,128]{1,0:T(8,128)S(1)}, f32[64,128]{1,0:T(8,128)S(1)}, u32[]{:S(2)}, u32[]{:S(2)}) %collective-permute-start.16) | collective-permute-done | bytes 32800 | tf_op jit(solution)/shard_map/ppermute | solution.py:348
  66.1 0.0 collective-permute-done.15.refs_1_
  66.1 0.0 collective-permute-done.17.refs_3_
  66.1 0.0 copy-start.2
  66.1 2.0 %shard_map.82 = (f32[120,128]{1,0:T(8,128)S(1)}, f32[120,128]{1,0:T(8,128)S(1)}, f32[120,128]{1,0:T(8,128)S(1)}, f32[120,128]{1,0:T(8,128)S(1)}) custom-call(s32[2]{0:T(128)S(1)} %pad_add_fusion.3.pos, f32[64,128]{1,0:T(8,128)S(1)} %get-tuple-element.85.refs_0_, f32[96,128]{1,0:T(8,128)S(1)} %collective-permute-done.15.refs_1_, ...), custom_call_target="tpu_custom_call" | custom-call | flops 2800000000 | tf_op jit(solution)/shard_map/pallas_call | solution.py:25
  68.2 0.1 collective-permute-start.18
  68.2 0.1 collective-permute-start.19
  68.3 1.8 %collective-permute-start.20 = (f32[120,128]{1,0:T(8,128)S(1)}, f32[120,128]{1,0:T(8,128)S(1)}, u32[]{:S(2)}, u32[]{:S(2)}) collective-permute-start(f32[120,128]{1,0:T(8,128)S(1)} %get-tuple-element.94), channel_id=1, source_target_pairs={{0,3},{1,2},{2,1},{3,0},{4,7},{5,6},{6,5},{7,4},{8,11},{9,10},{10,... | collective-permute-start | bytes 184328 | tf_op jit(solution)/shard_map/ppermute | solution.py:348
  70.1 0.0 collective-permute-done.18.p1
  70.1 3.0 %collective-permute-done.19.p2 = f32[120,128]{1,0:T(8,128)S(1)} collective-permute-done((f32[120,128]{1,0:T(8,128)S(1)}, f32[120,128]{1,0:T(8,128)S(1)}, u32[]{:S(2)}, u32[]{:S(2)}) %collective-permute-start.19) | collective-permute-done | bytes 61472 | tf_op jit(solution)/shard_map/ppermute | solution.py:348
  73.1 0.4 collective-permute-done.20.p3
  73.5 0.0 slice-done
  73.5 0.0 slice-done.1
  73.5 0.0 slice-done.2
  73.5 0.0 copy-done.2
  73.6 5.5 %shard_map.83 = (f32[1536,128]{1,0:T(8,128)}, f32[128,128]{1,0:T(8,128)}) custom-call(s32[2]{0:T(128)S(1)} %pad_add_fusion.3.pos, f32[120,128]{1,0:T(8,128)S(1)} %get-tuple-element.91.p0, f32[120,128]{1,0:T(8,128)S(1)} %collective-permute-done.18.p1, f32[120,128]{1,0:T(8,128)S(1)} %collective-permute-done.19.p2, f32[120,128]{1,0:T(8,128)S(1)} %collective-permute-done.20.p3, ...), custom_call_target="tpu_custom_call" | custom-call | flops 5299999744 | tf_op jit(solution)/shard_map/pallas_call | solution.py:25
  (3 shorter events, 0.0 us)
Async XLA Ops:
  0.6 13.8 %collective-permute-start = (f32[48,768]{1,0:T(8,128)}, f32[48,768]{1,0:T(8,128)S(1)}, u32[]{:S(2)}, u32[]{:S(2)}) collective-permute-start(f32[48,768]{1,0:T(8,128)} %c0.1), channel_id=1, source_target_pairs={{0,2},{1,3},{2,0},{3,1},{4,6},{5,7},{6,4},{7,5},{8,10},{9,11},{10,... | collective-permute-start | bytes 442376 | tf_op jit(solution)/shard_map/ppermute | solution.py:348
  4.5 0.9 %copy-start = (f32[48,768]{1,0:T(8,128)S(1)}, f32[48,768]{1,0:T(8,128)}, u32[]{:S(2)}) copy-start(f32[48,768]{1,0:T(8,128)} %c0.1) | copy-start | bytes 442372
  5.4 1.1 %copy-start.1 = (f32[1536,128]{1,0:T(8,128)S(1)}, f32[1536,128]{1,0:T(8,128)}, u32[]{:S(2)}) copy-start(f32[1536,128]{1,0:T(8,128)} %f_ref.3) | copy-start | bytes 2359300
  14.4 1.9 %collective-permute-start.2 = (f32[88,128]{1,0:T(8,128)S(1)}, f32[88,128]{1,0:T(8,128)S(1)}, u32[]{:S(2)}, u32[]{:S(2)}) collective-permute-start(f32[88,128]{1,0:T(8,128)S(1)} %get-tuple-element.56), channel_id=1, source_target_pairs={{0,1},{1,0},{2,3},{3,2},{4,5},{5,4},{6,7},{7,6},{8,9},{9,8},{10,11... | collective-permute-start | bytes 135176 | tf_op jit(solution)/shard_map/ppermute | solution.py:348
  14.5 4.5 %collective-permute-start.3 = (f32[88,128]{1,0:T(8,128)S(1)}, f32[88,128]{1,0:T(8,128)S(1)}, u32[]{:S(2)}, u32[]{:S(2)}) collective-permute-start(f32[88,128]{1,0:T(8,128)S(1)} %get-tuple-element.57), channel_id=1, source_target_pairs={{0,2},{1,3},{2,0},{3,1},{4,6},{5,7},{6,4},{7,5},{8,10},{9,11},{10,... | collective-permute-start | bytes 135176 | tf_op jit(solution)/shard_map/ppermute | solution.py:348
  14.6 4.5 %collective-permute-start.4 = (f32[88,128]{1,0:T(8,128)S(1)}, f32[88,128]{1,0:T(8,128)S(1)}, u32[]{:S(2)}, u32[]{:S(2)}) collective-permute-start(f32[88,128]{1,0:T(8,128)S(1)} %get-tuple-element.58), channel_id=1, source_target_pairs={{0,3},{1,2},{2,1},{3,0},{4,7},{5,6},{6,5},{7,4},{8,11},{9,10},{10,... | collective-permute-start | bytes 135176 | tf_op jit(solution)/shard_map/ppermute | solution.py:348
  19.1 19.8 %collective-permute-start.8 = (f32[960,128]{1,0:T(8,128)S(1)}, f32[960,128]{1,0:T(8,128)S(1)}, u32[]{:S(2)}, u32[]{:S(2)}) collective-permute-start(f32[960,128]{1,0:T(8,128)S(1)} %get-tuple-element.63.s0), channel_id=1, source_target_pairs={{0,2},{1,3},{2,0},{3,1},{4,6},{5,7},{6,4},{7,5},{8,10},{9,11},{10,... | collective-permute-start | bytes 1474568 | tf_op jit(solution)/shard_map/ppermute | solution.py:348
  20.2 7.9 %collective-permute-start.1 = (f32[96,768]{1,0:T(8,128)S(1)}, f32[96,768]{1,0:T(8,128)S(1)}, u32[]{:S(2)}, u32[]{:S(2)}) collective-permute-start(f32[96,768]{1,0:T(8,128)S(1)} %pad_maximum_fusion.1), channel_id=1, source_target_pairs={{0,1},{1,0},{2,3},{3,2},{4,5},{5,4},{6,7},{7,6},{8,9},{9,8},{10,11... | collective-permute-start | bytes 884744 | tf_op jit(solution)/shard_map/ppermute | solution.py:348
  20.3 11.3 %collective-permute-start.10 = (f32[416,128]{1,0:T(8,128)S(1)}, f32[416,128]{1,0:T(8,128)S(1)}, u32[]{:S(2)}, u32[]{:S(2)}) collective-permute-start(f32[416,128]{1,0:T(8,128)S(1)} %get-tuple-element.65), channel_id=1, source_target_pairs={{3,6},{0,13},{1,12},{7,10},{4,1},{5,0},{11,14},{8,5},{9,4},{15,2},... | collective-permute-start | bytes 638984 | tf_op jit(solution)/shard_map/ppermute | solution.py:352
  25.9 10.3 %collective-permute-start.9 = (f32[416,128]{1,0:T(8,128)S(1)}, f32[416,128]{1,0:T(8,128)S(1)}, u32[]{:S(2)}, u32[]{:S(2)}) collective-permute-start(f32[416,128]{1,0:T(8,128)S(1)} %get-tuple-element.65), channel_id=1, source_target_pairs={{3,4},{0,15},{1,14},{7,8},{4,3},{5,2},{11,12},{8,7},{9,6},{15,0},{... | collective-permute-start | bytes 638984 | tf_op jit(solution)/shard_map/ppermute | solution.py:352
  29.0 9.4 %collective-permute-start.5 = (f32[96,128]{1,0:T(8,128)S(1)}, f32[96,128]{1,0:T(8,128)S(1)}, u32[]{:S(2)}, u32[]{:S(2)}) collective-permute-start(f32[96,128]{1,0:T(8,128)S(1)} %get-tuple-element.60), channel_id=1, source_target_pairs={{0,4},{1,5},{2,6},{3,7},{4,0},{5,1},{6,2},{7,3},{8,12},{9,13},{10,... | collective-permute-start | bytes 147464 | tf_op jit(solution)/shard_map/ppermute | solution.py:348
  29.1 9.7 %collective-permute-start.7 = (f32[96,128]{1,0:T(8,128)S(1)}, f32[96,128]{1,0:T(8,128)S(1)}, u32[]{:S(2)}, u32[]{:S(2)}) collective-permute-start(f32[96,128]{1,0:T(8,128)S(1)} %get-tuple-element.61), channel_id=1, source_target_pairs={{0,12},{1,13},{2,14},{3,15},{4,8},{5,9},{6,10},{7,11},{8,4},{9,5},... | collective-permute-start | bytes 147464 | tf_op jit(solution)/shard_map/ppermute | solution.py:348
  31.6 6.8 %collective-permute-start.6 = (f32[64,128]{1,0:T(8,128)S(1)}, f32[64,128]{1,0:T(8,128)S(1)}, u32[]{:S(2)}, u32[]{:S(2)}) collective-permute-start(f32[64,128]{1,0:T(8,128)S(1)} %get-tuple-element.66.refs_0_), channel_id=1, source_target_pairs={{0,8},{1,9},{2,10},{3,11},{4,12},{5,13},{6,14},{7,15},{8,0},{9,1},... | collective-permute-start | bytes 98312 | tf_op jit(solution)/shard_map/ppermute | solution.py:348
  38.9 3.2 %collective-permute-start.11 = (f32[2752,128]{1,0:T(8,128)S(1)}, f32[2752,128]{1,0:T(8,128)S(1)}, u32[]{:S(2)}, u32[]{:S(2)}) collective-permute-start(f32[2752,128]{1,0:T(8,128)S(1)} %pad_maximum_fusion), channel_id=1, source_target_pairs={{0,1},{1,0},{2,3},{3,2},{4,5},{5,4},{6,7},{7,6},{8,9},{9,8},{10,11... | collective-permute-start | bytes 4227080 | tf_op jit(solution)/shard_map/ppermute | solution.py:348
  46.3 9.4 %collective-permute-start.12 = (f32[96,128]{1,0:T(8,128)S(1)}, f32[96,128]{1,0:T(8,128)S(1)}, u32[]{:S(2)}, u32[]{:S(2)}) collective-permute-start(f32[96,128]{1,0:T(8,128)S(1)} %get-tuple-element.80), channel_id=1, source_target_pairs={{0,4},{1,5},{2,6},{3,7},{4,0},{5,1},{6,2},{7,3},{8,12},{9,13},{10,... | collective-permute-start | bytes 147464 | tf_op jit(solution)/shard_map/ppermute | solution.py:348
  48.0 7.8 %collective-permute-start.14 = (f32[96,128]{1,0:T(8,128)S(1)}, f32[96,128]{1,0:T(8,128)S(1)}, u32[]{:S(2)}, u32[]{:S(2)}) collective-permute-start(f32[96,128]{1,0:T(8,128)S(1)} %get-tuple-element.81), channel_id=1, source_target_pairs={{0,12},{1,13},{2,14},{3,15},{4,8},{5,9},{6,10},{7,11},{8,4},{9,5},... | collective-permute-start | bytes 147464 | tf_op jit(solution)/shard_map/ppermute | solution.py:348
  50.9 4.8 %collective-permute-start.13 = (f32[64,128]{1,0:T(8,128)S(1)}, f32[64,128]{1,0:T(8,128)S(1)}, u32[]{:S(2)}, u32[]{:S(2)}) collective-permute-start(f32[64,128]{1,0:T(8,128)S(1)} %get-tuple-element.79.refs_0_), channel_id=1, source_target_pairs={{0,8},{1,9},{2,10},{3,11},{4,12},{5,13},{6,14},{7,15},{8,0},{9,1},... | collective-permute-start | bytes 98312 | tf_op jit(solution)/shard_map/ppermute | solution.py:348
  55.7 17.8 %slice-start = ((s8[9437184]{0:T(1024)(128)(4,1)}), s8[4194304]{0:T(1024)(128)(4,1)S(1)}, s32[]{:S(2)}) async-start(s8[9437184]{0:T(1024)(128)(4,1)} %bitcast.5), calls=%async_computation | async-start | bytes 8388608
  55.7 17.8 %slice-start.1 = ((s8[9437184]{0:T(1024)(128)(4,1)}), s8[4194304]{0:T(1024)(128)(4,1)S(1)}, s32[]{:S(2)}) async-start(s8[9437184]{0:T(1024)(128)(4,1)} %bitcast.5), calls=%async_computation.1 | async-start | bytes 8388608
  58.5 7.6 %collective-permute-start.15 = (f32[96,128]{1,0:T(8,128)S(1)}, f32[96,128]{1,0:T(8,128)S(1)}, u32[]{:S(2)}, u32[]{:S(2)}) collective-permute-start(f32[96,128]{1,0:T(8,128)S(1)} %get-tuple-element.86), channel_id=1, source_target_pairs={{0,4},{1,5},{2,6},{3,7},{4,0},{5,1},{6,2},{7,3},{8,12},{9,13},{10,... | collective-permute-start | bytes 147464 | tf_op jit(solution)/shard_map/ppermute | solution.py:348
  59.6 6.5 %collective-permute-start.17 = (f32[96,128]{1,0:T(8,128)S(1)}, f32[96,128]{1,0:T(8,128)S(1)}, u32[]{:S(2)}, u32[]{:S(2)}) collective-permute-start(f32[96,128]{1,0:T(8,128)S(1)} %get-tuple-element.87), channel_id=1, source_target_pairs={{0,12},{1,13},{2,14},{3,15},{4,8},{5,9},{6,10},{7,11},{8,4},{9,5},... | collective-permute-start | bytes 147464 | tf_op jit(solution)/shard_map/ppermute | solution.py:348
  61.3 4.8 %collective-permute-start.16 = (f32[64,128]{1,0:T(8,128)S(1)}, f32[64,128]{1,0:T(8,128)S(1)}, u32[]{:S(2)}, u32[]{:S(2)}) collective-permute-start(f32[64,128]{1,0:T(8,128)S(1)} %get-tuple-element.85.refs_0_), channel_id=1, source_target_pairs={{0,8},{1,9},{2,10},{3,11},{4,12},{5,13},{6,14},{7,15},{8,0},{9,1},... | collective-permute-start | bytes 98312 | tf_op jit(solution)/shard_map/ppermute | solution.py:348
  66.1 7.4 %slice-start.2 = ((s8[9437184]{0:T(1024)(128)(4,1)}), s8[1048576]{0:T(1024)(128)(4,1)S(1)}, s32[]{:S(2)}) async-start(s8[9437184]{0:T(1024)(128)(4,1)} %bitcast.5), calls=%async_computation.2 | async-start | bytes 2097152
  66.1 7.4 %copy-start.2 = (bf16[1536,384]{1,0:T(8,128)(2,1)S(1)}, bf16[1536,384]{1,0:T(8,128)(2,1)}, u32[]{:S(2)}) copy-start(bf16[1536,384]{1,0:T(8,128)(2,1)} %get-tuple-element.95.places) | copy-start | bytes 3538948
  68.2 1.9 %collective-permute-start.18 = (f32[120,128]{1,0:T(8,128)S(1)}, f32[120,128]{1,0:T(8,128)S(1)}, u32[]{:S(2)}, u32[]{:S(2)}) collective-permute-start(f32[120,128]{1,0:T(8,128)S(1)} %get-tuple-element.92), channel_id=1, source_target_pairs={{0,1},{1,0},{2,3},{3,2},{4,5},{5,4},{6,7},{7,6},{8,9},{9,8},{10,11... | collective-permute-start | bytes 184328 | tf_op jit(solution)/shard_map/ppermute | solution.py:348
  68.2 4.9 %collective-permute-start.19 = (f32[120,128]{1,0:T(8,128)S(1)}, f32[120,128]{1,0:T(8,128)S(1)}, u32[]{:S(2)}, u32[]{:S(2)}) collective-permute-start(f32[120,128]{1,0:T(8,128)S(1)} %get-tuple-element.93), channel_id=1, source_target_pairs={{0,2},{1,3},{2,0},{3,1},{4,6},{5,7},{6,4},{7,5},{8,10},{9,11},{10,... | collective-permute-start | bytes 184328 | tf_op jit(solution)/shard_map/ppermute | solution.py:348
  68.3 5.2 %collective-permute-start.20 = (f32[120,128]{1,0:T(8,128)S(1)}, f32[120,128]{1,0:T(8,128)S(1)}, u32[]{:S(2)}, u32[]{:S(2)}) collective-permute-start(f32[120,128]{1,0:T(8,128)S(1)} %get-tuple-element.94), channel_id=1, source_target_pairs={{0,3},{1,2},{2,1},{3,0},{4,7},{5,6},{6,5},{7,4},{8,11},{9,10},{10,... | collective-permute-start | bytes 184328 | tf_op jit(solution)/shard_map/ppermute | solution.py:348

commit v7 on v6

--- a/solution.py
+++ b/solution.py
@@ -143,12 +143,13 @@
 
 
 def rows_kernel(count, table, k_ref, f_ref, c_ref, tablev, *rest):
-    pieces, (spans, edge, places, ks, right_side, sem) = rest[:GROUP], rest[GROUP:]
+    pieces, (spans, edge, right_side, ks, sems) = rest[:GROUP], rest[GROUP:]
     width, order, columns = edge.shape[1], ks.shape[1], f_ref.shape[1]
     owned = c_ref.shape[0]
     side = 2 * width
-    fetch(k_ref, count, lambda j: table[2, j], ks, lambda j: side + table[3, j], sem)
-    fetch(k_ref, side, lambda j: table[j // width, j % width], ks, lambda j: j, sem)
+    fetch(k_ref, count, lambda j: table[2, j], ks, lambda j: side + table[3, j], sems.at[0])
+    fetch(k_ref, width, lambda j: table[0, j], ks, lambda j: j, sems.at[1])
+    fetch(k_ref, width, lambda j: table[1, j], ks, lambda j: width + j, sems.at[2])
 
     def indicator(row):
         place = lax.broadcasted_iota(jnp.int32, (order, row.shape[1]), 0).astype(F32)
@@ -163,23 +164,30 @@
     right_side[:, side:side + count] = indicator(by_slot)
     right_side[:, side + count:side + width] = jnp.zeros((order, width - count), BF16)
     right_side[:, side + width:] = beside(f_ref[...])
-    places[...] = right_side[:, :side + width]
     for i in range(c_ref.shape[1] // LANES):
         at = width + i * owned
         edge[at:at + owned] = c_ref[:, i * LANES:(i + 1) * LANES]
-    pltpu.make_async_copy(k_ref.at[pl.ds(0, ks.shape[0])], ks, sem).wait()
-
-    at = side + width
-    high, low = halves(ks[...])
-    both = dot(high, right_side[...])
-    part = dot(low, right_side[:, :at + columns])
-    cut(both[:, at:at + columns] + both[:, at + columns:] + part[:, at:], table[4, 0], pieces)
-    block = both[:, :at] + part[:, :at]
-    rows = side + count
-    for i in range(3):
-        kept = side if i == 2 else rows
-        spans[i * rows:i * rows + kept] = block[:kept, i * width:(i + 1) * width]
-    edge[:width] = jnp.where(table[4, 0] == GROUP - 1, block[width:side, side:], block[:width, side:])
+
+    at, rows = side + width, side + count
+    v = []
+    for i, (first, size) in enumerate(((side, count), (0, width), (width, width))):
+        part = ks.at[first:first + size]
+        pltpu.make_async_copy(k_ref.at[pl.ds(0, size)], part, sems.at[i]).wait()
+        high, low = halves(part[...])
+        both = dot(high, right_side[...])
+        rest = dot(low, right_side[:, :at + columns])
+        v.append(both[:, at:at + columns] + both[:, at + columns:] + rest[:, at:])
+        block = both[:, :at] + rest[:, :at]
+        spans[first:first + size] = block[:, :width]
+        spans[rows + first:rows + first + size] = block[:, width:side]
+        if first < side:
+            spans[2 * rows + first:2 * rows + first + size] = block[:, side:]
+
+            @pl.when((table[4, 0] == GROUP - 1) == (first > 0))
+            def _():
+                edge[:width] = block[:, side:]
+
+    cut(jnp.concatenate(v[1:] + v[:1], axis=0), table[4, 0], pieces)
 
 
 GOT = (-1, None, 5, 4)
@@ -311,21 +319,30 @@
     payload(v, width, paired, group % 2 == 1, *outs[3:])
 
 
-def final_kernel(count, pos, p0, p1, p2, p3, f_ref, places, k_ref, out, lam_ref):
+def sweep_kernel(first, pos, right_side, k_ref, u_ref, ks_ref):
+    rows, columns = u_ref.shape
+    at = right_side.shape[1] - 2 * columns
+    high, low = halves(k_ref[first:first + rows])
+    both = dot(high, right_side[...])
+    part = dot(low, right_side[:, :at + columns])
+    u_ref[...] = both[:, at:at + columns] + both[:, at + columns:] + part[:, at:]
+    ks_ref[...] = both[:, :at] + part[:, :at]
+
+
+def final_kernel(parts, count, pos, p0, p1, p2, p3, *refs):
     x = joined([p0[...], p1[...], p2[...], p3[...]], pos[0])
+    us, kss, (out, lam_ref) = refs[:parts], refs[parts:2 * parts], refs[2 * parts:]
     width = lam_ref.shape[0]
     lam_ref[...] = x[count:count + width]
     at = count + width
     filler = jnp.zeros((width - count, LANES), F32)
     change = beside(jnp.concatenate([x[at:at + width], -x[at + width:], -x[:count], filler], axis=0))
-    both = dot(places[...], change)
-    loads = beside(f_ref[...] + both[:, :LANES] + both[:, LANES:])
-    order = k_ref.shape[0]
-    rows = 256 if order % 256 == 0 else order
-    for at in range(0, order, rows):
-        high, low = halves(k_ref[at:at + rows])
-        part = dot(high, loads)
-        out[at:at + rows] = part[:, :LANES] + part[:, LANES:] + dot(low, loads[:, :LANES])
+    at = 0
+    for u, ks in zip(us, kss):
+        high, low = halves(ks[...])
+        part = dot(high, change)
+        out[at:at + u.shape[0]] = u[...] + part[:, :LANES] + part[:, LANES:] + dot(low, change[:, :LANES])
+        at += u.shape[0]
 
 
 def local(condensed, eigen_loads, coarse_inverse, face_rows, primal_rows, primal_slot):
@@ -370,17 +387,16 @@
     c_next = mate(coarse_inverse, 2)
     tall = owned * coarse // LANES
 
-    *pieces, spans, edge, places = call(
+    *pieces, spans, edge, right_side = call(
         functools.partial(rows_kernel, count),
         [(kept // GROUP, LANES)] * GROUP
-        + [(2 * kept + side, width), (width + tall, width), ((order, side + width), BF16)],
+        + [(2 * kept + side, width), (width + tall, width), ((order, side + width + 2 * columns), BF16)],
         (table, condensed, eigen_loads, coarse_inverse, table),
         7.5,
         hbm=(1,),
         scratch=[
             pltpu.VMEM((kept, order), F32),
-            pltpu.VMEM((order, side + width + 2 * columns), BF16),
-            pltpu.SemaphoreType.DMA,
+            pltpu.SemaphoreType.DMA((3,)),
         ],
         vmem=52,
     )
@@ -391,6 +407,19 @@
     edge = after(edge, pieces)
     came = crossing(edge, [(GROUP - 1, GROUP), (0, -1), (1, -2)])
     came_next = crossing(edge, [(GROUP - 1, GROUP + 2), (0, -3), (1, -4)])
+    parts = 4 if order % 64 == 0 else 1
+    block = order // parts
+    sweeps = []
+
+    def sweep(other):
+        if len(sweeps) < parts:
+            first = len(sweeps) * block
+            shapes = [(block, columns), (block, side + width)]
+            kernel = functools.partial(sweep_kernel, first)
+            sweeps.append(call(kernel, shapes, (pos, after(right_side, other), condensed), 2.3))
+            return sweeps[-1]
+        return other
+
     pieces[0] = after(pieces[0], c_other)
     size = owned + chunk_of(owned)
     pay_shapes = [(size, LANES)] + [(size + width // GROUP, LANES)] * 2
@@ -400,9 +429,11 @@
         (pos, *pieces),
         0.9,
     )
+    swept = sweep(pays)
     pays = along(*pays)
-    *pays, spans_next, came, came_next = lax.optimization_barrier((*pays, spans_next, came, came_next))
+    *pays, spans_next, came, came_next, _ = lax.optimization_barrier((*pays, spans_next, came, came_next, swept))
     theirs = mate(jnp.concatenate([spans, spans_next, came, came_next], axis=0), 1)
+    pays[0] = after(pays[0], sweep((spans_next, swept)))
     blocks = call(
         functools.partial(blocks_kernel, width),
         [
@@ -431,12 +462,14 @@
         )
         if kind != "last":
             state = outs[:3]
+            swept = sweep(outs)
             pays = along(*outs[3:])
+            pays[0] = after(pays[0], swept)
     displaced, multipliers = call(
-        functools.partial(final_kernel, count),
+        functools.partial(final_kernel, parts, count),
         [(order, columns), (width, columns)],
-        (pos, *traded(outs), eigen_loads, places, condensed),
-        5.3,
+        (pos, *traded(outs), *[x[0] for x in sweeps], *[x[1] for x in sweeps]),
+        2.6,
     )
     return displaced, multipliers
 

time: 79.4 us -> 76.3 us (0.961)
  waiting for transfers between devices: 24.2 us -> 15 us
  Pallas kernels: 23.3 us -> 28.6 us
    ppermute x19, waiting for transfers between devices: 20.3 us -> 13.9 us  [mate(): return lax.ppermute(x, 'sub', [(s, s ^ k) for s in range(total)])]
    pallas_call x7 -> x11, Pallas kernels: 23.3 us -> 28.6 us  [call(): pl.pallas_call(kernel, out_shape=[jax.ShapeDtypeStruct(s, d) for s, d in...]
    ppermute x2, waiting for transfers between devices: 3.82 us -> 1.16 us  [crossing(): return lax.ppermute(x, 'sub', pairs)]
    ppermute x19, starting transfers between devices: 20.1 us -> 21.4 us  [mate(): return lax.ppermute(x, 'sub', [(s, s ^ k) for s in range(total)])]
    unnamed x12 -> x8, local copies, waits for them, and re-layouts: 2.06 us -> 2.05 us
  transfers between devices with their start and end apart: 21 -> 21, of which waited for: 11 -> 9; matrix products, arithmetic and copies ran while one was open for 1% -> 1% of each run, Pallas kernels for 11% -> 23%
where the time goes in v7:
time: 76.3 us; the launch traced here: 76 us
  Pallas kernels  28.6 us (37%)
  starting transfers between devices  28.5 us (37%)
  waiting for transfers between devices  15 us (20%)
  local copies, waits for them, and re-layouts  2.05 us (3%)
  other arithmetic  0.99 us (1%)
  between operations  0.79 us (1%)
    pallas_call x11, Pallas kernels, call(): pl.pallas_call(kernel, out_shape=[jax.ShapeDtypeStruct(s, d) for s, d in...  28.6 us
    ppermute x19, starting transfers between devices, mate(): return lax.ppermute(x, 'sub', [(s, s ^ k) for s in range(total)])  21.4 us
    ppermute x19, waiting for transfers between devices, mate(): return lax.ppermute(x, 'sub', [(s, s ^ k) for s in range(total)])  13.9 us
    ppermute x2, starting transfers between devices, crossing(): return lax.ppermute(x, 'sub', pairs)  7.1 us
    unnamed x8, local copies, waits for them, and re-layouts  2.05 us
  transfers between devices with their start and end apart: 21, of which 9 were waited for; matrix products, arithmetic and copies ran while one was open for 1% of the time, Pallas kernels for 23%

profile of v7, /device:TPU:0, one launch (start us, length us, event | category | flops | bytes accessed | tf_op | source)
XLA Modules:
  0.0 76.0 jit_solution(10599829351300614141)
XLA Ops:
  0.6 3.0 %collective-permute-start = (f32[48,768]{1,0:T(8,128)}, f32[48,768]{1,0:T(8,128)S(1)}, u32[]{:S(2)}, u32[]{:S(2)}) collective-permute-start(f32[48,768]{1,0:T(8,128)} %c0.1), channel_id=1, source_target_pairs={{0,2},{1,3},{2,0},{3,1},{4,6},{5,7},{6,4},{7,5},{8,10},{9,11},{10,... | collective-permute-start | bytes 442376 | tf_op jit(solution)/shard_map/ppermute | solution.py:365
  3.7 0.1 fusion
  3.7 0.7 pad_add_fusion.table.tablev
  4.5 0.9 %copy-done.2 = f32[48,768]{1,0:T(8,128)S(1)} copy-done((f32[48,768]{1,0:T(8,128)S(1)}, f32[48,768]{1,0:T(8,128)}, u32[]{:S(2)}) %copy-start.2) | copy-done | bytes 147480
  5.4 0.0 copy-start.3
  5.4 1.1 %copy-done.3 = f32[1536,128]{1,0:T(8,128)S(1)} copy-done((f32[1536,128]{1,0:T(8,128)S(1)}, f32[1536,128]{1,0:T(8,128)}, u32[]{:S(2)}) %copy-start.3) | copy-done | bytes 786456
  6.5 0.0 copy-start
  6.5 7.2 %shard_map.77 = (f32[88,128]{1,0:T(8,128)S(1)}, f32[88,128]{1,0:T(8,128)S(1)}, f32[88,128]{1,0:T(8,128)S(1)}, f32[88,128]{1,0:T(8,128)S(1)}, f32[960,128]{1,0:T(...) custom-call(s32[5,128]{1,0:T(8,128)S(1)} %pad_add_fusion.table.tablev, f32[1536,1536]{1,0:T(8,128)} %k_ref.9, ...), custom_call_target="tpu_custom_call" | custom-call | flops 7500000256 | tf_op jit(solution)/shard_map/pallas_call | solution.py:25
  13.7 0.0 collective-permute-done.c2
  13.8 0.1 collective-permute-start.1
  13.8 0.5 collective-permute-start.2
  14.3 0.0 collective-permute-start.3
  14.4 1.4 %collective-permute-start.4 = (f32[88,128]{1,0:T(8,128)S(1)}, f32[88,128]{1,0:T(8,128)S(1)}, u32[]{:S(2)}, u32[]{:S(2)}) collective-permute-start(f32[88,128]{1,0:T(8,128)S(1)} %get-tuple-element.73), channel_id=1, source_target_pairs={{0,3},{1,2},{2,1},{3,0},{4,7},{5,6},{6,5},{7,4},{8,11},{9,10},{10,... | collective-permute-start | bytes 135176 | tf_op jit(solution)/shard_map/ppermute | solution.py:365
  15.8 0.0 collective-permute-done.2.p1
  15.8 2.7 %collective-permute-done.3.p2 = f32[88,128]{1,0:T(8,128)S(1)} collective-permute-done((f32[88,128]{1,0:T(8,128)S(1)}, f32[88,128]{1,0:T(8,128)S(1)}, u32[]{:S(2)}, u32[]{:S(2)}) %collective-permute-start.3) | collective-permute-done | bytes 45088 | tf_op jit(solution)/shard_map/ppermute | solution.py:365
  18.5 0.0 collective-permute-done.4.p3
  18.5 1.8 %collective-permute-start.8 = (f32[960,128]{1,0:T(8,128)S(1)}, f32[960,128]{1,0:T(8,128)S(1)}, u32[]{:S(2)}, u32[]{:S(2)}) collective-permute-start(f32[960,128]{1,0:T(8,128)S(1)} %get-tuple-element.78.s0), channel_id=1, source_target_pairs={{0,2},{1,3},{2,0},{3,1},{4,6},{5,7},{6,4},{7,5},{8,10},{9,11},{10,... | collective-permute-start | bytes 1474568 | tf_op jit(solution)/shard_map/ppermute | solution.py:365
  20.3 4.9 %collective-permute-start.10 = (f32[416,128]{1,0:T(8,128)S(1)}, f32[416,128]{1,0:T(8,128)S(1)}, u32[]{:S(2)}, u32[]{:S(2)}) collective-permute-start(f32[416,128]{1,0:T(8,128)S(1)} %get-tuple-element.80), channel_id=1, source_target_pairs={{3,6},{0,13},{1,12},{7,10},{4,1},{5,0},{11,14},{8,5},{9,4},{15,2},... | collective-permute-start | bytes 638984 | tf_op jit(solution)/shard_map/ppermute | solution.py:369
  25.2 0.1 pad_add_fusion.3.pos
  25.3 0.0 copy-start.1
  25.3 2.2 %collective-permute-start.9 = (f32[416,128]{1,0:T(8,128)S(1)}, f32[416,128]{1,0:T(8,128)S(1)}, u32[]{:S(2)}, u32[]{:S(2)}) collective-permute-start(f32[416,128]{1,0:T(8,128)S(1)} %get-tuple-element.80), channel_id=1, source_target_pairs={{3,4},{0,15},{1,14},{7,8},{4,3},{5,2},{11,12},{8,7},{9,6},{15,0},{... | collective-permute-start | bytes 638984 | tf_op jit(solution)/shard_map/ppermute | solution.py:369
  27.5 0.0 collective-permute-done.1.c_other
  27.5 0.9 %shard_map.78 = (f32[352,128]{1,0:T(8,128)S(1)}, f32[64,128]{1,0:T(8,128)S(1)}, f32[96,128]{1,0:T(8,128)S(1)}, f32[96,128]{1,0:T(8,128)S(1)}) custom-call(s32[2]{0:T(128)S(1)} %pad_add_fusion.3.pos, f32[88,128]{1,0:T(8,128)S(1)} %get-tuple-element.70.p0, f32[88,128]{1,0:T(8,128)S(1)} %collective-permute-done.2.p1, f32[88,128]{1,0:T(8,128)S(1)} %collective-permute-done.3.p2, ...), custom_call_target="tpu_custom_call" | custom-call | flops 900000000 | tf_op jit(solution)/shard_map/pallas_call | solution.py:25
  28.4 0.2 collective-permute-start.5
  28.6 2.5 %collective-permute-start.7 = (f32[96,128]{1,0:T(8,128)S(1)}, f32[96,128]{1,0:T(8,128)S(1)}, u32[]{:S(2)}, u32[]{:S(2)}) collective-permute-start(f32[96,128]{1,0:T(8,128)S(1)} %get-tuple-element.76), channel_id=1, source_target_pairs={{0,12},{1,13},{2,14},{3,15},{4,8},{5,9},{6,10},{7,11},{8,4},{9,5},... | collective-permute-start | bytes 147464 | tf_op jit(solution)/shard_map/ppermute | solution.py:365
  31.1 0.0 collective-permute-done.10.came_next
  31.1 1.1 %collective-permute-start.6 = (f32[64,128]{1,0:T(8,128)S(1)}, f32[64,128]{1,0:T(8,128)S(1)}, u32[]{:S(2)}, u32[]{:S(2)}) collective-permute-start(f32[64,128]{1,0:T(8,128)S(1)} %get-tuple-element.90.refs_0_), channel_id=1, source_target_pairs={{0,8},{1,9},{2,10},{3,11},{4,12},{5,13},{6,14},{7,15},{8,0},{9,1},... | collective-permute-start | bytes 98312 | tf_op jit(solution)/shard_map/ppermute | solution.py:365
  32.2 0.0 copy-done
  32.2 0.0 copy-done.1
  32.2 2.3 %shard_map.79 = (f32[384,128]{1,0:T(8,128)S(1)}, f32[384,384]{1,0:T(8,128)S(1)}) custom-call(s32[2]{0:T(128)S(1)} %pad_add_fusion.3.pos, bf16[1536,640]{1,0:T(8,128)(2,1)S(1)} %copy-done.1, f32[1536,1536]{1,0:T(8,128)S(1)} %copy-done), custom_call_target="tpu_custom_call" | custom-call | flops 2300000000 | tf_op jit(solution)/shard_map/pallas_call | solution.py:25
  34.5 1.2 %collective-permute-done.9.came = f32[416,128]{1,0:T(8,128)S(1)} collective-permute-done((f32[416,128]{1,0:T(8,128)S(1)}, f32[416,128]{1,0:T(8,128)S(1)}, u32[]{:S(2)}, u32[]{:S(2)}) %collective-permute-start.9) | collective-permute-done | bytes 213024 | tf_op jit(solution)/shard_map/ppermute | solution.py:369
  35.6 2.7 %collective-permute-done.6.refs_2_ = f32[64,128]{1,0:T(8,128)S(1)} collective-permute-done((f32[64,128]{1,0:T(8,128)S(1)}, f32[64,128]{1,0:T(8,128)S(1)}, u32[]{:S(2)}, u32[]{:S(2)}) %collective-permute-start.6) | collective-permute-done | bytes 32800 | tf_op jit(solution)/shard_map/ppermute | solution.py:365
  38.4 0.0 collective-permute-done.5.refs_1_
  38.4 0.2 collective-permute-done.7.refs_3_
  38.6 0.0 collective-permute-done.8.s2
  38.6 0.1 pad_maximum_fusion
  38.7 0.1 collective-permute-start.11
  38.8 2.3 %shard_map.80 = (f32[384,128]{1,0:T(8,128)S(1)}, f32[384,384]{1,0:T(8,128)S(1)}) custom-call(s32[2]{0:T(128)S(1)} %pad_add_fusion.3.pos, bf16[1536,640]{1,0:T(8,128)(2,1)S(1)} %copy-done.1, f32[1536,1536]{1,0:T(8,128)S(1)} %copy-done), custom_call_target="tpu_custom_call" | custom-call | flops 2300000000 | tf_op jit(solution)/shard_map/pallas_call | solution.py:25
  41.0 0.9 %collective-permute-done.11.theirs = f32[2752,128]{1,0:T(8,128)S(1)} collective-permute-done((f32[2752,128]{1,0:T(8,128)S(1)}, f32[2752,128]{1,0:T(8,128)S(1)}, u32[]{:S(2)}, u32[]{:S(2)}) %collective-permute-start.11) | collective-permute-done | bytes 1409056 | tf_op jit(solution)/shard_map/ppermute | solution.py:365
  41.9 1.4 %shard_map.81 = (bf16[672,768]{1,0:T(8,128)(2,1)S(1)}, bf16[512,512]{1,0:T(8,128)(2,1)S(1)}, bf16[704,1024]{1,0:T(8,128)(2,1)S(1)}, bf16[256,128]{1,0:T(8,128)(2,1)S(1)}, bf16[256,128]{1,0:T(8,128)(2,1)S(1)}) custom-call(s32[2]{0:T(128)S(1)} %pad_add_fusion.3.pos, f32[48,768]{1,0:T(8,128)S(1)} %copy-done.2, f32[48,768]{1,0:T(8,128)S(1)} %collective-permute-done.c2, ...), custom_call_target="tpu_custom_call" | custom-call | flops 1700000000 | tf_op jit(solution)/shard_map/pallas_call | solution.py:25
  43.3 2.8 %shard_map.82 = (f32[352,128]{1,0:T(8,128)S(1)}, f32[128,128]{1,0:T(8,128)S(1)}, f32[128,128]{1,0:T(8,128)S(1)}, f32[64,128]{1,0:T(8,128)S(1)}, f32[96,128]{1,0:T(8,128)S(1)}, /*index=5*/f32[96,128]{1,0:T(8,128)S(1)}) custom-call(s32[2]{0:T(128)S(1)} %pad_add_fusion.3.pos, f32[64,128]{1,0:T(8,128)S(1)} %get-tuple-element.90.refs_0_, ...), custom_call_target="tpu_custom_call" | custom-call | flops 2800000000 | tf_op jit(solution)/shard_map/pallas_call | solution.py:25
  46.1 1.9 %collective-permute-start.12 = (f32[96,128]{1,0:T(8,128)S(1)}, f32[96,128]{1,0:T(8,128)S(1)}, u32[]{:S(2)}, u32[]{:S(2)}) collective-permute-start(f32[96,128]{1,0:T(8,128)S(1)} %get-tuple-element.106), channel_id=1, source_target_pairs={{0,4},{1,5},{2,6},{3,7},{4,0},{5,1},{6,2},{7,3},{8,12},{9,13},{10,... | collective-permute-start | bytes 147464 | tf_op jit(solution)/shard_map/ppermute | solution.py:365
  48.0 2.9 %collective-permute-start.14 = (f32[96,128]{1,0:T(8,128)S(1)}, f32[96,128]{1,0:T(8,128)S(1)}, u32[]{:S(2)}, u32[]{:S(2)}) collective-permute-start(f32[96,128]{1,0:T(8,128)S(1)} %get-tuple-element.107), channel_id=1, source_target_pairs={{0,12},{1,13},{2,14},{3,15},{4,8},{5,9},{6,10},{7,11},{8,4},{9,5},... | collective-permute-start | bytes 147464 | tf_op jit(solution)/shard_map/ppermute | solution.py:365
  50.9 0.5 collective-permute-start.13
  51.4 2.3 %shard_map.83 = (f32[384,128]{1,0:T(8,128)S(1)}, f32[384,384]{1,0:T(8,128)S(1)}) custom-call(s32[2]{0:T(128)S(1)} %pad_add_fusion.3.pos, bf16[1536,640]{1,0:T(8,128)(2,1)S(1)} %copy-done.1, f32[1536,1536]{1,0:T(8,128)S(1)} %copy-done), custom_call_target="tpu_custom_call" | custom-call | flops 2300000000 | tf_op jit(solution)/shard_map/pallas_call | solution.py:25
  53.6 2.1 %collective-permute-done.13.refs_2_ = f32[64,128]{1,0:T(8,128)S(1)} collective-permute-done((f32[64,128]{1,0:T(8,128)S(1)}, f32[64,128]{1,0:T(8,128)S(1)}, u32[]{:S(2)}, u32[]{:S(2)}) %collective-permute-start.13) | collective-permute-done | bytes 32800 | tf_op jit(solution)/shard_map/ppermute | solution.py:365
  55.7 0.0 collective-permute-done.12.refs_1_
  55.7 0.0 collective-permute-done.14.refs_3_
  55.7 2.8 %shard_map.84 = (f32[352,128]{1,0:T(8,128)S(1)}, f32[128,128]{1,0:T(8,128)S(1)}, f32[128,128]{1,0:T(8,128)S(1)}, f32[64,128]{1,0:T(8,128)S(1)}, f32[96,128]{1,0:T(8,128)S(1)}, /*index=5*/f32[96,128]{1,0:T(8,128)S(1)}) custom-call(s32[2]{0:T(128)S(1)} %pad_add_fusion.3.pos, f32[64,128]{1,0:T(8,128)S(1)} %get-tuple-element.111.refs_0_, ...), custom_call_target="tpu_custom_call" | custom-call | flops 2800000000 | tf_op jit(solution)/shard_map/pallas_call | solution.py:25
  58.5 1.1 %collective-permute-start.15 = (f32[96,128]{1,0:T(8,128)S(1)}, f32[96,128]{1,0:T(8,128)S(1)}, u32[]{:S(2)}, u32[]{:S(2)}) collective-permute-start(f32[96,128]{1,0:T(8,128)S(1)} %get-tuple-element.116), channel_id=1, source_target_pairs={{0,4},{1,5},{2,6},{3,7},{4,0},{5,1},{6,2},{7,3},{8,12},{9,13},{10,... | collective-permute-start | bytes 147464 | tf_op jit(solution)/shard_map/ppermute | solution.py:365
  59.6 1.7 %collective-permute-start.17 = (f32[96,128]{1,0:T(8,128)S(1)}, f32[96,128]{1,0:T(8,128)S(1)}, u32[]{:S(2)}, u32[]{:S(2)}) collective-permute-start(f32[96,128]{1,0:T(8,128)S(1)} %get-tuple-element.117), channel_id=1, source_target_pairs={{0,12},{1,13},{2,14},{3,15},{4,8},{5,9},{6,10},{7,11},{8,4},{9,5},... | collective-permute-start | bytes 147464 | tf_op jit(solution)/shard_map/ppermute | solution.py:365
  61.3 0.8 %collective-permute-start.16 = (f32[64,128]{1,0:T(8,128)S(1)}, f32[64,128]{1,0:T(8,128)S(1)}, u32[]{:S(2)}, u32[]{:S(2)}) collective-permute-start(f32[64,128]{1,0:T(8,128)S(1)} %get-tuple-element.121.refs_0_), channel_id=1, source_target_pairs={{0,8},{1,9},{2,10},{3,11},{4,12},{5,13},{6,14},{7,15},{8,0},{9,1},... | collective-permute-start | bytes 98312 | tf_op jit(solution)/shard_map/ppermute | solution.py:365
  62.0 2.3 %shard_map.85 = (f32[384,128]{1,0:T(8,128)S(1)}, f32[384,384]{1,0:T(8,128)S(1)}) custom-call(s32[2]{0:T(128)S(1)} %pad_add_fusion.3.pos, bf16[1536,640]{1,0:T(8,128)(2,1)S(1)} %copy-done.1, f32[1536,1536]{1,0:T(8,128)S(1)} %copy-done), custom_call_target="tpu_custom_call" | custom-call | flops 2300000000 | tf_op jit(solution)/shard_map/pallas_call | solution.py:25
  64.3 1.8 %collective-permute-done.16.refs_2_ = f32[64,128]{1,0:T(8,128)S(1)} collective-permute-done((f32[64,128]{1,0:T(8,128)S(1)}, f32[64,128]{1,0:T(8,128)S(1)}, u32[]{:S(2)}, u32[]{:S(2)}) %collective-permute-start.16) | collective-permute-done | bytes 32800 | tf_op jit(solution)/shard_map/ppermute | solution.py:365
  66.1 0.0 collective-permute-done.15.refs_1_
  66.1 0.0 collective-permute-done.17.refs_3_
  66.1 2.0 %shard_map.86 = (f32[120,128]{1,0:T(8,128)S(1)}, f32[120,128]{1,0:T(8,128)S(1)}, f32[120,128]{1,0:T(8,128)S(1)}, f32[120,128]{1,0:T(8,128)S(1)}) custom-call(s32[2]{0:T(128)S(1)} %pad_add_fusion.3.pos, f32[64,128]{1,0:T(8,128)S(1)} %get-tuple-element.121.refs_0_, f32[96,128]{1,0:T(8,128)S(1)} %collective-permute-done.15.refs_1_, ...), custom_call_target="tpu_custom_call" | custom-call | flops 2800000000 | tf_op jit(solution)/shard_map/pallas_call | solution.py:25
  68.1 0.1 collective-permute-start.18
  68.2 0.1 collective-permute-start.19
  68.3 1.8 %collective-permute-start.20 = (f32[120,128]{1,0:T(8,128)S(1)}, f32[120,128]{1,0:T(8,128)S(1)}, u32[]{:S(2)}, u32[]{:S(2)}) collective-permute-start(f32[120,128]{1,0:T(8,128)S(1)} %get-tuple-element.125), channel_id=1, source_target_pairs={{0,3},{1,2},{2,1},{3,0},{4,7},{5,6},{6,5},{7,4},{8,11},{9,10},{10,... | collective-permute-start | bytes 184328 | tf_op jit(solution)/shard_map/ppermute | solution.py:365
  70.1 0.0 collective-permute-done.18.p1
  70.1 3.0 %collective-permute-done.19.p2 = f32[120,128]{1,0:T(8,128)S(1)} collective-permute-done((f32[120,128]{1,0:T(8,128)S(1)}, f32[120,128]{1,0:T(8,128)S(1)}, u32[]{:S(2)}, u32[]{:S(2)}) %collective-permute-start.19) | collective-permute-done | bytes 61472 | tf_op jit(solution)/shard_map/ppermute | solution.py:365
  73.1 0.4 collective-permute-done.20.p3
  73.5 2.5 %shard_map.87 = (f32[1536,128]{1,0:T(8,128)}, f32[128,128]{1,0:T(8,128)}) custom-call(s32[2]{0:T(128)S(1)} %pad_add_fusion.3.pos, f32[120,128]{1,0:T(8,128)S(1)} %get-tuple-element.122.p0, f32[120,128]{1,0:T(8,128)S(1)} %collective-permute-done.18.p1, f32[120,128]{1,0:T(8,128)S(1)} %collective-permute-done.19.p2, f32[120,128]{1,0:T(8,128)S(1)} %collective-permute-done.20.p3, ...), custom_call_target="tpu_custom_call" | custom-call | flops 2600000000 | tf_op jit(solution)/shard_map/pallas_call | solution.py:25
  (2 shorter events, 0.0 us)
Async XLA Ops:
  0.6 13.1 %collective-permute-start = (f32[48,768]{1,0:T(8,128)}, f32[48,768]{1,0:T(8,128)S(1)}, u32[]{:S(2)}, u32[]{:S(2)}) collective-permute-start(f32[48,768]{1,0:T(8,128)} %c0.1), channel_id=1, source_target_pairs={{0,2},{1,3},{2,0},{3,1},{4,6},{5,7},{6,4},{7,5},{8,10},{9,11},{10,... | collective-permute-start | bytes 442376 | tf_op jit(solution)/shard_map/ppermute | solution.py:365
  4.5 0.9 %copy-start.2 = (f32[48,768]{1,0:T(8,128)S(1)}, f32[48,768]{1,0:T(8,128)}, u32[]{:S(2)}) copy-start(f32[48,768]{1,0:T(8,128)} %c0.1) | copy-start | bytes 442372
  5.4 1.1 %copy-start.3 = (f32[1536,128]{1,0:T(8,128)S(1)}, f32[1536,128]{1,0:T(8,128)}, u32[]{:S(2)}) copy-start(f32[1536,128]{1,0:T(8,128)} %f_ref.1) | copy-start | bytes 2359300
  6.5 25.7 %copy-start = (f32[1536,1536]{1,0:T(8,128)S(1)}, f32[1536,1536]{1,0:T(8,128)}, u32[]{:S(2)}) copy-start(f32[1536,1536]{1,0:T(8,128)} %k_ref.9) | copy-start | bytes 28311556
  13.8 13.7 %collective-permute-start.1 = (f32[96,768]{1,0:T(8,128)S(1)}, f32[96,768]{1,0:T(8,128)S(1)}, u32[]{:S(2)}, u32[]{:S(2)}) collective-permute-start(f32[96,768]{1,0:T(8,128)S(1)} %pad_maximum_fusion.1), channel_id=1, source_target_pairs={{0,1},{1,0},{2,3},{3,2},{4,5},{5,4},{6,7},{7,6},{8,9},{9,8},{10,11... | collective-permute-start | bytes 884744 | tf_op jit(solution)/shard_map/ppermute | solution.py:365
  13.8 1.9 %collective-permute-start.2 = (f32[88,128]{1,0:T(8,128)S(1)}, f32[88,128]{1,0:T(8,128)S(1)}, u32[]{:S(2)}, u32[]{:S(2)}) collective-permute-start(f32[88,128]{1,0:T(8,128)S(1)} %get-tuple-element.71), channel_id=1, source_target_pairs={{0,1},{1,0},{2,3},{3,2},{4,5},{5,4},{6,7},{7,6},{8,9},{9,8},{10,11... | collective-permute-start | bytes 135176 | tf_op jit(solution)/shard_map/ppermute | solution.py:365
  14.3 4.1 %collective-permute-start.3 = (f32[88,128]{1,0:T(8,128)S(1)}, f32[88,128]{1,0:T(8,128)S(1)}, u32[]{:S(2)}, u32[]{:S(2)}) collective-permute-start(f32[88,128]{1,0:T(8,128)S(1)} %get-tuple-element.72), channel_id=1, source_target_pairs={{0,2},{1,3},{2,0},{3,1},{4,6},{5,7},{6,4},{7,5},{8,10},{9,11},{10,... | collective-permute-start | bytes 135176 | tf_op jit(solution)/shard_map/ppermute | solution.py:365
  14.4 4.1 %collective-permute-start.4 = (f32[88,128]{1,0:T(8,128)S(1)}, f32[88,128]{1,0:T(8,128)S(1)}, u32[]{:S(2)}, u32[]{:S(2)}) collective-permute-start(f32[88,128]{1,0:T(8,128)S(1)} %get-tuple-element.73), channel_id=1, source_target_pairs={{0,3},{1,2},{2,1},{3,0},{4,7},{5,6},{6,5},{7,4},{8,11},{9,10},{10,... | collective-permute-start | bytes 135176 | tf_op jit(solution)/shard_map/ppermute | solution.py:365
  18.5 20.1 %collective-permute-start.8 = (f32[960,128]{1,0:T(8,128)S(1)}, f32[960,128]{1,0:T(8,128)S(1)}, u32[]{:S(2)}, u32[]{:S(2)}) collective-permute-start(f32[960,128]{1,0:T(8,128)S(1)} %get-tuple-element.78.s0), channel_id=1, source_target_pairs={{0,2},{1,3},{2,0},{3,1},{4,6},{5,7},{6,4},{7,5},{8,10},{9,11},{10,... | collective-permute-start | bytes 1474568 | tf_op jit(solution)/shard_map/ppermute | solution.py:365
  20.3 10.8 %collective-permute-start.10 = (f32[416,128]{1,0:T(8,128)S(1)}, f32[416,128]{1,0:T(8,128)S(1)}, u32[]{:S(2)}, u32[]{:S(2)}) collective-permute-start(f32[416,128]{1,0:T(8,128)S(1)} %get-tuple-element.80), channel_id=1, source_target_pairs={{3,6},{0,13},{1,12},{7,10},{4,1},{5,0},{11,14},{8,5},{9,4},{15,2},... | collective-permute-start | bytes 638984 | tf_op jit(solution)/shard_map/ppermute | solution.py:369
  25.3 6.9 %copy-start.1 = (bf16[1536,640]{1,0:T(8,128)(2,1)S(1)}, bf16[1536,640]{1,0:T(8,128)(2,1)}, u32[]{:S(2)}) copy-start(bf16[1536,640]{1,0:T(8,128)(2,1)} %get-tuple-element.118.right_side) | copy-start | bytes 5898244
  25.3 10.3 %collective-permute-start.9 = (f32[416,128]{1,0:T(8,128)S(1)}, f32[416,128]{1,0:T(8,128)S(1)}, u32[]{:S(2)}, u32[]{:S(2)}) collective-permute-start(f32[416,128]{1,0:T(8,128)S(1)} %get-tuple-element.80), channel_id=1, source_target_pairs={{3,4},{0,15},{1,14},{7,8},{4,3},{5,2},{11,12},{8,7},{9,6},{15,0},{... | collective-permute-start | bytes 638984 | tf_op jit(solution)/shard_map/ppermute | solution.py:369
  28.4 9.9 %collective-permute-start.5 = (f32[96,128]{1,0:T(8,128)S(1)}, f32[96,128]{1,0:T(8,128)S(1)}, u32[]{:S(2)}, u32[]{:S(2)}) collective-permute-start(f32[96,128]{1,0:T(8,128)S(1)} %get-tuple-element.75), channel_id=1, source_target_pairs={{0,4},{1,5},{2,6},{3,7},{4,0},{5,1},{6,2},{7,3},{8,12},{9,13},{10,... | collective-permute-start | bytes 147464 | tf_op jit(solution)/shard_map/ppermute | solution.py:365
  28.6 10.0 %collective-permute-start.7 = (f32[96,128]{1,0:T(8,128)S(1)}, f32[96,128]{1,0:T(8,128)S(1)}, u32[]{:S(2)}, u32[]{:S(2)}) collective-permute-start(f32[96,128]{1,0:T(8,128)S(1)} %get-tuple-element.76), channel_id=1, source_target_pairs={{0,12},{1,13},{2,14},{3,15},{4,8},{5,9},{6,10},{7,11},{8,4},{9,5},... | collective-permute-start | bytes 147464 | tf_op jit(solution)/shard_map/ppermute | solution.py:365
  31.1 7.3 %collective-permute-start.6 = (f32[64,128]{1,0:T(8,128)S(1)}, f32[64,128]{1,0:T(8,128)S(1)}, u32[]{:S(2)}, u32[]{:S(2)}) collective-permute-start(f32[64,128]{1,0:T(8,128)S(1)} %get-tuple-element.90.refs_0_), channel_id=1, source_target_pairs={{0,8},{1,9},{2,10},{3,11},{4,12},{5,13},{6,14},{7,15},{8,0},{9,1},... | collective-permute-start | bytes 98312 | tf_op jit(solution)/shard_map/ppermute | solution.py:365
  38.7 3.2 %collective-permute-start.11 = (f32[2752,128]{1,0:T(8,128)S(1)}, f32[2752,128]{1,0:T(8,128)S(1)}, u32[]{:S(2)}, u32[]{:S(2)}) collective-permute-start(f32[2752,128]{1,0:T(8,128)S(1)} %pad_maximum_fusion), channel_id=1, source_target_pairs={{0,1},{1,0},{2,3},{3,2},{4,5},{5,4},{6,7},{7,6},{8,9},{9,8},{10,11... | collective-permute-start | bytes 4227080 | tf_op jit(solution)/shard_map/ppermute | solution.py:365
  46.1 9.6 %collective-permute-start.12 = (f32[96,128]{1,0:T(8,128)S(1)}, f32[96,128]{1,0:T(8,128)S(1)}, u32[]{:S(2)}, u32[]{:S(2)}) collective-permute-start(f32[96,128]{1,0:T(8,128)S(1)} %get-tuple-element.106), channel_id=1, source_target_pairs={{0,4},{1,5},{2,6},{3,7},{4,0},{5,1},{6,2},{7,3},{8,12},{9,13},{10,... | collective-permute-start | bytes 147464 | tf_op jit(solution)/shard_map/ppermute | solution.py:365
  48.0 7.7 %collective-permute-start.14 = (f32[96,128]{1,0:T(8,128)S(1)}, f32[96,128]{1,0:T(8,128)S(1)}, u32[]{:S(2)}, u32[]{:S(2)}) collective-permute-start(f32[96,128]{1,0:T(8,128)S(1)} %get-tuple-element.107), channel_id=1, source_target_pairs={{0,12},{1,13},{2,14},{3,15},{4,8},{5,9},{6,10},{7,11},{8,4},{9,5},... | collective-permute-start | bytes 147464 | tf_op jit(solution)/shard_map/ppermute | solution.py:365
  50.9 4.8 %collective-permute-start.13 = (f32[64,128]{1,0:T(8,128)S(1)}, f32[64,128]{1,0:T(8,128)S(1)}, u32[]{:S(2)}, u32[]{:S(2)}) collective-permute-start(f32[64,128]{1,0:T(8,128)S(1)} %get-tuple-element.111.refs_0_), channel_id=1, source_target_pairs={{0,8},{1,9},{2,10},{3,11},{4,12},{5,13},{6,14},{7,15},{8,0},{9,1},... | collective-permute-start | bytes 98312 | tf_op jit(solution)/shard_map/ppermute | solution.py:365
  58.5 7.6 %collective-permute-start.15 = (f32[96,128]{1,0:T(8,128)S(1)}, f32[96,128]{1,0:T(8,128)S(1)}, u32[]{:S(2)}, u32[]{:S(2)}) collective-permute-start(f32[96,128]{1,0:T(8,128)S(1)} %get-tuple-element.116), channel_id=1, source_target_pairs={{0,4},{1,5},{2,6},{3,7},{4,0},{5,1},{6,2},{7,3},{8,12},{9,13},{10,... | collective-permute-start | bytes 147464 | tf_op jit(solution)/shard_map/ppermute | solution.py:365
  59.6 6.5 %collective-permute-start.17 = (f32[96,128]{1,0:T(8,128)S(1)}, f32[96,128]{1,0:T(8,128)S(1)}, u32[]{:S(2)}, u32[]{:S(2)}) collective-permute-start(f32[96,128]{1,0:T(8,128)S(1)} %get-tuple-element.117), channel_id=1, source_target_pairs={{0,12},{1,13},{2,14},{3,15},{4,8},{5,9},{6,10},{7,11},{8,4},{9,5},... | collective-permute-start | bytes 147464 | tf_op jit(solution)/shard_map/ppermute | solution.py:365
  61.3 4.8 %collective-permute-start.16 = (f32[64,128]{1,0:T(8,128)S(1)}, f32[64,128]{1,0:T(8,128)S(1)}, u32[]{:S(2)}, u32[]{:S(2)}) collective-permute-start(f32[64,128]{1,0:T(8,128)S(1)} %get-tuple-element.121.refs_0_), channel_id=1, source_target_pairs={{0,8},{1,9},{2,10},{3,11},{4,12},{5,13},{6,14},{7,15},{8,0},{9,1},... | collective-permute-start | bytes 98312 | tf_op jit(solution)/shard_map/ppermute | solution.py:365
  68.1 1.9 %collective-permute-start.18 = (f32[120,128]{1,0:T(8,128)S(1)}, f32[120,128]{1,0:T(8,128)S(1)}, u32[]{:S(2)}, u32[]{:S(2)}) collective-permute-start(f32[120,128]{1,0:T(8,128)S(1)} %get-tuple-element.123), channel_id=1, source_target_pairs={{0,1},{1,0},{2,3},{3,2},{4,5},{5,4},{6,7},{7,6},{8,9},{9,8},{10,11... | collective-permute-start | bytes 184328 | tf_op jit(solution)/shard_map/ppermute | solution.py:365
  68.2 4.9 %collective-permute-start.19 = (f32[120,128]{1,0:T(8,128)S(1)}, f32[120,128]{1,0:T(8,128)S(1)}, u32[]{:S(2)}, u32[]{:S(2)}) collective-permute-start(f32[120,128]{1,0:T(8,128)S(1)} %get-tuple-element.124), channel_id=1, source_target_pairs={{0,2},{1,3},{2,0},{3,1},{4,6},{5,7},{6,4},{7,5},{8,10},{9,11},{10,... | collective-permute-start | bytes 184328 | tf_op jit(solution)/shard_map/ppermute | solution.py:365
  68.3 5.2 %collective-permute-start.20 = (f32[120,128]{1,0:T(8,128)S(1)}, f32[120,128]{1,0:T(8,128)S(1)}, u32[]{:S(2)}, u32[]{:S(2)}) collective-permute-start(f32[120,128]{1,0:T(8,128)S(1)} %get-tuple-element.125), channel_id=1, source_target_pairs={{0,3},{1,2},{2,1},{3,0},{4,7},{5,6},{6,5},{7,4},{8,11},{9,10},{10,... | collective-permute-start | bytes 184328 | tf_op jit(solution)/shard_map/ppermute | solution.py:365

commit v8 on v7

--- a/solution.py
+++ b/solution.py
@@ -142,14 +142,27 @@
     lax.fori_loop(0, count, one, 0, unroll=8)
 
 
-def rows_kernel(count, table, k_ref, f_ref, c_ref, tablev, *rest):
-    pieces, (spans, edge, right_side, ks, sems) = rest[:GROUP], rest[GROUP:]
-    width, order, columns = edge.shape[1], ks.shape[1], f_ref.shape[1]
-    owned = c_ref.shape[0]
+def rows_kernel(count, table, k_ref, f_ref, *rest):
+    pieces, (ks, sems) = rest[:GROUP], rest[GROUP:]
+    width, columns = table.shape[1], f_ref.shape[1]
     side = 2 * width
-    fetch(k_ref, count, lambda j: table[2, j], ks, lambda j: side + table[3, j], sems.at[0])
-    fetch(k_ref, width, lambda j: table[0, j], ks, lambda j: j, sems.at[1])
-    fetch(k_ref, width, lambda j: table[1, j], ks, lambda j: width + j, sems.at[2])
+    fetch(k_ref, width, lambda j: table[0, j], ks, lambda j: j, sems.at[0])
+    fetch(k_ref, width, lambda j: table[1, j], ks, lambda j: width + j, sems.at[1])
+    fetch(k_ref, count, lambda j: table[2, j], ks, lambda j: side + table[3, j], sems.at[2])
+    loads = beside(f_ref[...])
+    v = []
+    for i, (first, size) in enumerate(((0, width), (width, width), (side, count))):
+        part = ks.at[first:first + size]
+        pltpu.make_async_copy(k_ref.at[pl.ds(0, size)], part, sems.at[i]).wait()
+        high, low = halves(part[...])
+        both = dot(high, loads)
+        v.append(both[:, :columns] + both[:, columns:] + dot(low, loads[:, :columns]))
+    cut(jnp.concatenate(v, axis=0), table[4, 0], pieces)
+
+
+def near_kernel(count, table, ks, f_ref, c_ref, tablev, spans, edge, right_side):
+    width, order, owned = table.shape[1], ks.shape[1], c_ref.shape[0]
+    side = 2 * width
 
     def indicator(row):
         place = lax.broadcasted_iota(jnp.int32, (order, row.shape[1]), 0).astype(F32)
@@ -167,27 +180,13 @@
     for i in range(c_ref.shape[1] // LANES):
         at = width + i * owned
         edge[at:at + owned] = c_ref[:, i * LANES:(i + 1) * LANES]
-
+    high, low = halves(ks[...])
     at, rows = side + width, side + count
-    v = []
-    for i, (first, size) in enumerate(((side, count), (0, width), (width, width))):
-        part = ks.at[first:first + size]
-        pltpu.make_async_copy(k_ref.at[pl.ds(0, size)], part, sems.at[i]).wait()
-        high, low = halves(part[...])
-        both = dot(high, right_side[...])
-        rest = dot(low, right_side[:, :at + columns])
-        v.append(both[:, at:at + columns] + both[:, at + columns:] + rest[:, at:])
-        block = both[:, :at] + rest[:, :at]
-        spans[first:first + size] = block[:, :width]
-        spans[rows + first:rows + first + size] = block[:, width:side]
-        if first < side:
-            spans[2 * rows + first:2 * rows + first + size] = block[:, side:]
-
-            @pl.when((table[4, 0] == GROUP - 1) == (first > 0))
-            def _():
-                edge[:width] = block[:, side:]
-
-    cut(jnp.concatenate(v[1:] + v[:1], axis=0), table[4, 0], pieces)
+    block = dot(high, right_side[:, :at]) + dot(low, right_side[:, :at])
+    spans[:rows] = block[:, :width]
+    spans[rows:2 * rows] = block[:, width:side]
+    spans[2 * rows:] = block[:side, side:]
+    edge[:width] = jnp.where(table[4, 0] == GROUP - 1, block[width:side, side:], block[:width, side:])
 
 
 GOT = (-1, None, 5, 4)
@@ -387,18 +386,20 @@
     c_next = mate(coarse_inverse, 2)
     tall = owned * coarse // LANES
 
-    *pieces, spans, edge, right_side = call(
+    *pieces, ks = call(
         functools.partial(rows_kernel, count),
-        [(kept // GROUP, LANES)] * GROUP
-        + [(2 * kept + side, width), (width + tall, width), ((order, side + width + 2 * columns), BF16)],
-        (table, condensed, eigen_loads, coarse_inverse, table),
-        7.5,
+        [(kept // GROUP, LANES)] * GROUP + [(kept, order)],
+        (table, condensed, eigen_loads),
+        5.3,
         hbm=(1,),
-        scratch=[
-            pltpu.VMEM((kept, order), F32),
-            pltpu.SemaphoreType.DMA((3,)),
-        ],
-        vmem=52,
+        scratch=[pltpu.SemaphoreType.DMA((3,))],
+        vmem=50,
+    )
+    spans, edge, right_side = call(
+        functools.partial(near_kernel, count),
+        [(2 * kept + side, width), (width + tall, width), ((order, side + width + 2 * columns), BF16)],
+        (table, ks, eigen_loads, coarse_inverse, table),
+        2,
     )
     *pieces, c_next = lax.optimization_barrier((*pieces, c_next))
     pieces = traded(pieces)

time: 76.3 us -> 72.6 us (0.952)
  waiting for transfers between devices: 15 us -> 12.7 us
  local copies, waits for them, and re-layouts: 2.05 us -> 1.15 us
    ppermute x19, waiting for transfers between devices: 13.9 us -> 11.5 us  [mate(): return lax.ppermute(x, 'sub', [(s, s ^ k) for s in range(total)])]
    unnamed x8 -> x12, local copies, waits for them, and re-layouts: 2.05 us -> 1.15 us
    pallas_call x11 -> x12, Pallas kernels: 28.6 us -> 28.2 us  [call(): pl.pallas_call(kernel, out_shape=[jax.ShapeDtypeStruct(s, d) for s, d in...]
where the time goes in v8:
time: 72.6 us; the launch traced here: 72.4 us
  starting transfers between devices  28.5 us (39%)
  Pallas kernels  28.2 us (39%)
  waiting for transfers between devices  12.7 us (17%)
  local copies, waits for them, and re-layouts  1.15 us (2%)
  other arithmetic  0.99 us (1%)
  between operations  0.82 us (1%)
    pallas_call x12, Pallas kernels, call(): pl.pallas_call(kernel, out_shape=[jax.ShapeDtypeStruct(s, d) for s, d in...  28.2 us
    ppermute x19, starting transfers between devices, mate(): return lax.ppermute(x, 'sub', [(s, s ^ k) for s in range(total)])  21.5 us
    ppermute x19, waiting for transfers between devices, mate(): return lax.ppermute(x, 'sub', [(s, s ^ k) for s in range(total)])  11.5 us
    ppermute x2, starting transfers between devices, crossing(): return lax.ppermute(x, 'sub', pairs)  6.97 us
  transfers between devices with their start and end apart: 21, of which 9 were waited for; matrix products, arithmetic and copies ran while one was open for 1% of the time, Pallas kernels for 23%

profile of v8, /device:TPU:0, one launch (start us, length us, event | category | flops | bytes accessed | tf_op | source)
XLA Modules:
  0.0 72.4 jit_solution(16299899183279569851)
XLA Ops:
  0.6 3.0 %collective-permute-start = (f32[48,768]{1,0:T(8,128)}, f32[48,768]{1,0:T(8,128)S(1)}, u32[]{:S(2)}, u32[]{:S(2)}) collective-permute-start(f32[48,768]{1,0:T(8,128)} %c0.1), channel_id=1, source_target_pairs={{0,2},{1,3},{2,0},{3,1},{4,6},{5,7},{6,4},{7,5},{8,10},{9,11},{10,... | collective-permute-start | bytes 442376 | tf_op jit(solution)/shard_map/ppermute | solution.py:364
  3.7 0.1 fusion
  3.7 0.7 pad_add_fusion.table.tablev
  4.5 1.1 %copy-done.1 = f32[1536,128]{1,0:T(8,128)S(1)} copy-done((f32[1536,128]{1,0:T(8,128)S(1)}, f32[1536,128]{1,0:T(8,128)}, u32[]{:S(2)}) %copy-start.1) | copy-done | bytes 786456
  5.6 4.4 %shard_map.77 = (f32[88,128]{1,0:T(8,128)S(1)}, f32[88,128]{1,0:T(8,128)S(1)}, f32[88,128]{1,0:T(8,128)S(1)}, f32[88,128]{1,0:T(8,128)S(1)}, f32[352,1536]{1,0:T(8,128)S(1)}) custom-call(s32[5,128]{1,0:T(8,128)S(1)} %pad_add_fusion.table.tablev, f32[1536,1536]{1,0:T(8,128)} %k_ref.9, f32[1536,128]{1,0:T(8,128)S(1)} %copy-done.1), custom_call_target="tpu_custom_call" | custom-call | flops 5299999744 | tf_op jit(solution)/shard_map/pallas_call | solution.py:25
  10.0 0.0 collective-permute-done.c2
  10.0 0.0 copy-done
  10.1 0.1 collective-permute-start.1
  10.2 0.5 collective-permute-start.2
  10.7 0.0 collective-permute-start.3
  10.7 1.4 %collective-permute-start.4 = (f32[88,128]{1,0:T(8,128)S(1)}, f32[88,128]{1,0:T(8,128)S(1)}, u32[]{:S(2)}, u32[]{:S(2)}) collective-permute-start(f32[88,128]{1,0:T(8,128)S(1)} %get-tuple-element.74), channel_id=1, source_target_pairs={{0,3},{1,2},{2,1},{3,0},{4,7},{5,6},{6,5},{7,4},{8,11},{9,10},{10,... | collective-permute-start | bytes 135176 | tf_op jit(solution)/shard_map/ppermute | solution.py:364
  12.1 0.0 copy-done.2
  12.1 2.3 %shard_map.79 = (f32[960,128]{1,0:T(8,128)S(1)}, f32[416,128]{1,0:T(8,128)S(1)}, bf16[1536,640]{1,0:T(8,128)(2,1)S(1)}) custom-call(s32[5,128]{1,0:T(8,128)S(1)} %pad_add_fusion.table.tablev, f32[352,1536]{1,0:T(8,128)S(1)} %get-tuple-element.78.ks, f32[1536,128]{1,0:T(8,128)S(1)} %copy-done.2, f32[48,768]{1,0:T(8,128)S(1)} %copy-done, ...), custom_call_target="tpu_custom_call" | custom-call | flops 2000000000 | tf_op jit(solution)/shard_map/pallas_call | solution.py:25
  14.4 0.0 collective-permute-done.2.p1
  14.4 0.3 collective-permute-done.3.p2
  14.8 0.0 collective-permute-done.4.p3
  14.8 1.8 %collective-permute-start.8 = (f32[960,128]{1,0:T(8,128)S(1)}, f32[960,128]{1,0:T(8,128)S(1)}, u32[]{:S(2)}, u32[]{:S(2)}) collective-permute-start(f32[960,128]{1,0:T(8,128)S(1)} %get-tuple-element.80.s0), channel_id=1, source_target_pairs={{0,2},{1,3},{2,0},{3,1},{4,6},{5,7},{6,4},{7,5},{8,10},{9,11},{10,... | collective-permute-start | bytes 1474568 | tf_op jit(solution)/shard_map/ppermute | solution.py:364
  16.6 4.9 %collective-permute-start.10 = (f32[416,128]{1,0:T(8,128)S(1)}, f32[416,128]{1,0:T(8,128)S(1)}, u32[]{:S(2)}, u32[]{:S(2)}) collective-permute-start(f32[416,128]{1,0:T(8,128)S(1)} %get-tuple-element.82), channel_id=1, source_target_pairs={{3,6},{0,13},{1,12},{7,10},{4,1},{5,0},{11,14},{8,5},{9,4},{15,2},... | collective-permute-start | bytes 638984 | tf_op jit(solution)/shard_map/ppermute | solution.py:368
  21.5 0.1 pad_add_fusion.3.pos
  21.6 2.1 %collective-permute-start.9 = (f32[416,128]{1,0:T(8,128)S(1)}, f32[416,128]{1,0:T(8,128)S(1)}, u32[]{:S(2)}, u32[]{:S(2)}) collective-permute-start(f32[416,128]{1,0:T(8,128)S(1)} %get-tuple-element.82), channel_id=1, source_target_pairs={{3,4},{0,15},{1,14},{7,8},{4,3},{5,2},{11,12},{8,7},{9,6},{15,0},{... | collective-permute-start | bytes 638984 | tf_op jit(solution)/shard_map/ppermute | solution.py:368
  23.7 0.0 collective-permute-done.1.c_other
  23.7 0.9 %shard_map.78 = (f32[352,128]{1,0:T(8,128)S(1)}, f32[64,128]{1,0:T(8,128)S(1)}, f32[96,128]{1,0:T(8,128)S(1)}, f32[96,128]{1,0:T(8,128)S(1)}) custom-call(s32[2]{0:T(128)S(1)} %pad_add_fusion.3.pos, f32[88,128]{1,0:T(8,128)S(1)} %get-tuple-element.71.p0, f32[88,128]{1,0:T(8,128)S(1)} %collective-permute-done.2.p1, f32[88,128]{1,0:T(8,128)S(1)} %collective-permute-done.3.p2, ...), custom_call_target="tpu_custom_call" | custom-call | flops 900000000 | tf_op jit(solution)/shard_map/pallas_call | solution.py:25
  24.6 0.2 collective-permute-start.5
  24.8 2.5 %collective-permute-start.7 = (f32[96,128]{1,0:T(8,128)S(1)}, f32[96,128]{1,0:T(8,128)S(1)}, u32[]{:S(2)}, u32[]{:S(2)}) collective-permute-start(f32[96,128]{1,0:T(8,128)S(1)} %get-tuple-element.77), channel_id=1, source_target_pairs={{0,12},{1,13},{2,14},{3,15},{4,8},{5,9},{6,10},{7,11},{8,4},{9,5},... | collective-permute-start | bytes 147464 | tf_op jit(solution)/shard_map/ppermute | solution.py:364
  27.3 0.0 collective-permute-done.10.came_next
  27.3 1.2 %collective-permute-start.6 = (f32[64,128]{1,0:T(8,128)S(1)}, f32[64,128]{1,0:T(8,128)S(1)}, u32[]{:S(2)}, u32[]{:S(2)}) collective-permute-start(f32[64,128]{1,0:T(8,128)S(1)} %get-tuple-element.92.refs_0_), channel_id=1, source_target_pairs={{0,8},{1,9},{2,10},{3,11},{4,12},{5,13},{6,14},{7,15},{8,0},{9,1},... | collective-permute-start | bytes 98312 | tf_op jit(solution)/shard_map/ppermute | solution.py:364
  28.5 0.0 slice-done
  28.5 0.0 slice-done.1
  28.5 0.0 slice-done.2
  28.5 2.3 %shard_map.80 = (f32[384,128]{1,0:T(8,128)S(1)}, f32[384,384]{1,0:T(8,128)S(1)}) custom-call(s32[2]{0:T(128)S(1)} %pad_add_fusion.3.pos, bf16[1536,640]{1,0:T(8,128)(2,1)S(1)} %get-tuple-element.120.right_side, f32[1536,1536]{1,0:T(8,128)S(1)} %bitcast.6), custom_call_target="tpu_custom_call" | custom-call | flops 2300000000 | tf_op jit(solution)/shard_map/pallas_call | solution.py:25
  30.8 1.2 %collective-permute-done.9.came = f32[416,128]{1,0:T(8,128)S(1)} collective-permute-done((f32[416,128]{1,0:T(8,128)S(1)}, f32[416,128]{1,0:T(8,128)S(1)}, u32[]{:S(2)}, u32[]{:S(2)}) %collective-permute-start.9) | collective-permute-done | bytes 213024 | tf_op jit(solution)/shard_map/ppermute | solution.py:368
  31.9 2.8 %collective-permute-done.6.refs_2_ = f32[64,128]{1,0:T(8,128)S(1)} collective-permute-done((f32[64,128]{1,0:T(8,128)S(1)}, f32[64,128]{1,0:T(8,128)S(1)}, u32[]{:S(2)}, u32[]{:S(2)}) %collective-permute-start.6) | collective-permute-done | bytes 32800 | tf_op jit(solution)/shard_map/ppermute | solution.py:364
  34.7 0.0 collective-permute-done.5.refs_1_
  34.7 0.2 collective-permute-done.7.refs_3_
  34.9 0.0 collective-permute-done.8.s2
  34.9 0.1 pad_maximum_fusion
  35.0 0.1 collective-permute-start.11
  35.1 2.3 %shard_map.81 = (f32[384,128]{1,0:T(8,128)S(1)}, f32[384,384]{1,0:T(8,128)S(1)}) custom-call(s32[2]{0:T(128)S(1)} %pad_add_fusion.3.pos, bf16[1536,640]{1,0:T(8,128)(2,1)S(1)} %get-tuple-element.120.right_side, f32[1536,1536]{1,0:T(8,128)S(1)} %bitcast.6), custom_call_target="tpu_custom_call" | custom-call | flops 2300000000 | tf_op jit(solution)/shard_map/pallas_call | solution.py:25
  37.4 0.9 %collective-permute-done.11.theirs = f32[2752,128]{1,0:T(8,128)S(1)} collective-permute-done((f32[2752,128]{1,0:T(8,128)S(1)}, f32[2752,128]{1,0:T(8,128)S(1)}, u32[]{:S(2)}, u32[]{:S(2)}) %collective-permute-start.11) | collective-permute-done | bytes 1409056 | tf_op jit(solution)/shard_map/ppermute | solution.py:364
  38.3 1.4 %shard_map.82 = (bf16[672,768]{1,0:T(8,128)(2,1)S(1)}, bf16[512,512]{1,0:T(8,128)(2,1)S(1)}, bf16[704,1024]{1,0:T(8,128)(2,1)S(1)}, bf16[256,128]{1,0:T(8,128)(2,1)S(1)}, bf16[256,128]{1,0:T(8,128)(2,1)S(1)}) custom-call(s32[2]{0:T(128)S(1)} %pad_add_fusion.3.pos, f32[48,768]{1,0:T(8,128)S(1)} %copy-done, f32[48,768]{1,0:T(8,128)S(1)} %collective-permute-done.c2, ...), custom_call_target="tpu_custom_call" | custom-call | flops 1700000000 | tf_op jit(solution)/shard_map/pallas_call | solution.py:25
  39.7 2.8 %shard_map.83 = (f32[352,128]{1,0:T(8,128)S(1)}, f32[128,128]{1,0:T(8,128)S(1)}, f32[128,128]{1,0:T(8,128)S(1)}, f32[64,128]{1,0:T(8,128)S(1)}, f32[96,128]{1,0:T(8,128)S(1)}, /*index=5*/f32[96,128]{1,0:T(8,128)S(1)}) custom-call(s32[2]{0:T(128)S(1)} %pad_add_fusion.3.pos, f32[64,128]{1,0:T(8,128)S(1)} %get-tuple-element.92.refs_0_, ...), custom_call_target="tpu_custom_call" | custom-call | flops 2800000000 | tf_op jit(solution)/shard_map/pallas_call | solution.py:25
  42.5 1.9 %collective-permute-start.12 = (f32[96,128]{1,0:T(8,128)S(1)}, f32[96,128]{1,0:T(8,128)S(1)}, u32[]{:S(2)}, u32[]{:S(2)}) collective-permute-start(f32[96,128]{1,0:T(8,128)S(1)} %get-tuple-element.108), channel_id=1, source_target_pairs={{0,4},{1,5},{2,6},{3,7},{4,0},{5,1},{6,2},{7,3},{8,12},{9,13},{10,... | collective-permute-start | bytes 147464 | tf_op jit(solution)/shard_map/ppermute | solution.py:364
  44.4 2.9 %collective-permute-start.14 = (f32[96,128]{1,0:T(8,128)S(1)}, f32[96,128]{1,0:T(8,128)S(1)}, u32[]{:S(2)}, u32[]{:S(2)}) collective-permute-start(f32[96,128]{1,0:T(8,128)S(1)} %get-tuple-element.109), channel_id=1, source_target_pairs={{0,12},{1,13},{2,14},{3,15},{4,8},{5,9},{6,10},{7,11},{8,4},{9,5},... | collective-permute-start | bytes 147464 | tf_op jit(solution)/shard_map/ppermute | solution.py:364
  47.2 0.5 collective-permute-start.13
  47.7 2.3 %shard_map.84 = (f32[384,128]{1,0:T(8,128)S(1)}, f32[384,384]{1,0:T(8,128)S(1)}) custom-call(s32[2]{0:T(128)S(1)} %pad_add_fusion.3.pos, bf16[1536,640]{1,0:T(8,128)(2,1)S(1)} %get-tuple-element.120.right_side, f32[1536,1536]{1,0:T(8,128)S(1)} %bitcast.6), custom_call_target="tpu_custom_call" | custom-call | flops 2300000000 | tf_op jit(solution)/shard_map/pallas_call | solution.py:25
  50.0 2.1 %collective-permute-done.13.refs_2_ = f32[64,128]{1,0:T(8,128)S(1)} collective-permute-done((f32[64,128]{1,0:T(8,128)S(1)}, f32[64,128]{1,0:T(8,128)S(1)}, u32[]{:S(2)}, u32[]{:S(2)}) %collective-permute-start.13) | collective-permute-done | bytes 32800 | tf_op jit(solution)/shard_map/ppermute | solution.py:364
  52.0 0.0 collective-permute-done.12.refs_1_
  52.0 0.0 collective-permute-done.14.refs_3_
  52.0 2.8 %shard_map.85 = (f32[352,128]{1,0:T(8,128)S(1)}, f32[128,128]{1,0:T(8,128)S(1)}, f32[128,128]{1,0:T(8,128)S(1)}, f32[64,128]{1,0:T(8,128)S(1)}, f32[96,128]{1,0:T(8,128)S(1)}, /*index=5*/f32[96,128]{1,0:T(8,128)S(1)}) custom-call(s32[2]{0:T(128)S(1)} %pad_add_fusion.3.pos, f32[64,128]{1,0:T(8,128)S(1)} %get-tuple-element.113.refs_0_, ...), custom_call_target="tpu_custom_call" | custom-call | flops 2800000000 | tf_op jit(solution)/shard_map/pallas_call | solution.py:25
  54.8 1.1 %collective-permute-start.15 = (f32[96,128]{1,0:T(8,128)S(1)}, f32[96,128]{1,0:T(8,128)S(1)}, u32[]{:S(2)}, u32[]{:S(2)}) collective-permute-start(f32[96,128]{1,0:T(8,128)S(1)} %get-tuple-element.118), channel_id=1, source_target_pairs={{0,4},{1,5},{2,6},{3,7},{4,0},{5,1},{6,2},{7,3},{8,12},{9,13},{10,... | collective-permute-start | bytes 147464 | tf_op jit(solution)/shard_map/ppermute | solution.py:364
  55.9 1.7 %collective-permute-start.17 = (f32[96,128]{1,0:T(8,128)S(1)}, f32[96,128]{1,0:T(8,128)S(1)}, u32[]{:S(2)}, u32[]{:S(2)}) collective-permute-start(f32[96,128]{1,0:T(8,128)S(1)} %get-tuple-element.119), channel_id=1, source_target_pairs={{0,12},{1,13},{2,14},{3,15},{4,8},{5,9},{6,10},{7,11},{8,4},{9,5},... | collective-permute-start | bytes 147464 | tf_op jit(solution)/shard_map/ppermute | solution.py:364
  57.6 0.8 %collective-permute-start.16 = (f32[64,128]{1,0:T(8,128)S(1)}, f32[64,128]{1,0:T(8,128)S(1)}, u32[]{:S(2)}, u32[]{:S(2)}) collective-permute-start(f32[64,128]{1,0:T(8,128)S(1)} %get-tuple-element.123.refs_0_), channel_id=1, source_target_pairs={{0,8},{1,9},{2,10},{3,11},{4,12},{5,13},{6,14},{7,15},{8,0},{9,1},... | collective-permute-start | bytes 98312 | tf_op jit(solution)/shard_map/ppermute | solution.py:364
  58.4 2.3 %shard_map.86 = (f32[384,128]{1,0:T(8,128)S(1)}, f32[384,384]{1,0:T(8,128)S(1)}) custom-call(s32[2]{0:T(128)S(1)} %pad_add_fusion.3.pos, bf16[1536,640]{1,0:T(8,128)(2,1)S(1)} %get-tuple-element.120.right_side, f32[1536,1536]{1,0:T(8,128)S(1)} %bitcast.6), custom_call_target="tpu_custom_call" | custom-call | flops 2300000000 | tf_op jit(solution)/shard_map/pallas_call | solution.py:25
  60.6 1.8 %collective-permute-done.16.refs_2_ = f32[64,128]{1,0:T(8,128)S(1)} collective-permute-done((f32[64,128]{1,0:T(8,128)S(1)}, f32[64,128]{1,0:T(8,128)S(1)}, u32[]{:S(2)}, u32[]{:S(2)}) %collective-permute-start.16) | collective-permute-done | bytes 32800 | tf_op jit(solution)/shard_map/ppermute | solution.py:364
  62.4 0.0 collective-permute-done.15.refs_1_
  62.4 0.0 collective-permute-done.17.refs_3_
  62.4 2.0 %shard_map.87 = (f32[120,128]{1,0:T(8,128)S(1)}, f32[120,128]{1,0:T(8,128)S(1)}, f32[120,128]{1,0:T(8,128)S(1)}, f32[120,128]{1,0:T(8,128)S(1)}) custom-call(s32[2]{0:T(128)S(1)} %pad_add_fusion.3.pos, f32[64,128]{1,0:T(8,128)S(1)} %get-tuple-element.123.refs_0_, f32[96,128]{1,0:T(8,128)S(1)} %collective-permute-done.15.refs_1_, ...), custom_call_target="tpu_custom_call" | custom-call | flops 2800000000 | tf_op jit(solution)/shard_map/pallas_call | solution.py:25
  64.5 0.1 collective-permute-start.18
  64.5 0.1 collective-permute-start.19
  64.6 1.8 %collective-permute-start.20 = (f32[120,128]{1,0:T(8,128)S(1)}, f32[120,128]{1,0:T(8,128)S(1)}, u32[]{:S(2)}, u32[]{:S(2)}) collective-permute-start(f32[120,128]{1,0:T(8,128)S(1)} %get-tuple-element.127), channel_id=1, source_target_pairs={{0,3},{1,2},{2,1},{3,0},{4,7},{5,6},{6,5},{7,4},{8,11},{9,10},{10,... | collective-permute-start | bytes 184328 | tf_op jit(solution)/shard_map/ppermute | solution.py:364
  66.4 0.0 collective-permute-done.18.p1
  66.4 3.0 %collective-permute-done.19.p2 = f32[120,128]{1,0:T(8,128)S(1)} collective-permute-done((f32[120,128]{1,0:T(8,128)S(1)}, f32[120,128]{1,0:T(8,128)S(1)}, u32[]{:S(2)}, u32[]{:S(2)}) %collective-permute-start.19) | collective-permute-done | bytes 61472 | tf_op jit(solution)/shard_map/ppermute | solution.py:364
  69.4 0.4 collective-permute-done.20.p3
  69.8 2.5 %shard_map.88 = (f32[1536,128]{1,0:T(8,128)}, f32[128,128]{1,0:T(8,128)}) custom-call(s32[2]{0:T(128)S(1)} %pad_add_fusion.3.pos, f32[120,128]{1,0:T(8,128)S(1)} %get-tuple-element.124.p0, f32[120,128]{1,0:T(8,128)S(1)} %collective-permute-done.18.p1, f32[120,128]{1,0:T(8,128)S(1)} %collective-permute-done.19.p2, f32[120,128]{1,0:T(8,128)S(1)} %collective-permute-done.20.p3, ...), custom_call_target="tpu_custom_call" | custom-call | flops 2600000000 | tf_op jit(solution)/shard_map/pallas_call | solution.py:25
  (8 shorter events, 0.0 us)
Async XLA Ops:
  0.6 9.4 %collective-permute-start = (f32[48,768]{1,0:T(8,128)}, f32[48,768]{1,0:T(8,128)S(1)}, u32[]{:S(2)}, u32[]{:S(2)}) collective-permute-start(f32[48,768]{1,0:T(8,128)} %c0.1), channel_id=1, source_target_pairs={{0,2},{1,3},{2,0},{3,1},{4,6},{5,7},{6,4},{7,5},{8,10},{9,11},{10,... | collective-permute-start | bytes 442376 | tf_op jit(solution)/shard_map/ppermute | solution.py:364
  4.5 1.1 %copy-start.1 = (f32[1536,128]{1,0:T(8,128)S(1)}, f32[1536,128]{1,0:T(8,128)}, u32[]{:S(2)}) copy-start(f32[1536,128]{1,0:T(8,128)} %f_ref.3) | copy-start | bytes 2359300
  5.6 4.5 %copy-start = (f32[48,768]{1,0:T(8,128)S(1)}, f32[48,768]{1,0:T(8,128)}, u32[]{:S(2)}) copy-start(f32[48,768]{1,0:T(8,128)} %c0.1) | copy-start | bytes 442372
  5.6 6.5 %copy-start.2 = (f32[1536,128]{1,0:T(8,128)S(1)}, f32[1536,128]{1,0:T(8,128)}, u32[]{:S(2)}) copy-start(f32[1536,128]{1,0:T(8,128)} %f_ref.3) | copy-start | bytes 2359300
  5.6 22.9 %slice-start = ((s8[9437184]{0:T(1024)(128)(4,1)}), s8[1048576]{0:T(1024)(128)(4,1)S(1)}, s32[]{:S(2)}) async-start(s8[9437184]{0:T(1024)(128)(4,1)} %bitcast.5), calls=%async_computation | async-start | bytes 2097152
  5.6 22.9 %slice-start.1 = ((s8[9437184]{0:T(1024)(128)(4,1)}), s8[4194304]{0:T(1024)(128)(4,1)S(1)}, s32[]{:S(2)}) async-start(s8[9437184]{0:T(1024)(128)(4,1)} %bitcast.5), calls=%async_computation.1 | async-start | bytes 8388608
  10.1 13.6 %collective-permute-start.1 = (f32[96,768]{1,0:T(8,128)S(1)}, f32[96,768]{1,0:T(8,128)S(1)}, u32[]{:S(2)}, u32[]{:S(2)}) collective-permute-start(f32[96,768]{1,0:T(8,128)S(1)} %pad_maximum_fusion.1), channel_id=1, source_target_pairs={{0,1},{1,0},{2,3},{3,2},{4,5},{5,4},{6,7},{7,6},{8,9},{9,8},{10,11... | collective-permute-start | bytes 884744 | tf_op jit(solution)/shard_map/ppermute | solution.py:364
  10.2 4.3 %collective-permute-start.2 = (f32[88,128]{1,0:T(8,128)S(1)}, f32[88,128]{1,0:T(8,128)S(1)}, u32[]{:S(2)}, u32[]{:S(2)}) collective-permute-start(f32[88,128]{1,0:T(8,128)S(1)} %get-tuple-element.72), channel_id=1, source_target_pairs={{0,1},{1,0},{2,3},{3,2},{4,5},{5,4},{6,7},{7,6},{8,9},{9,8},{10,11... | collective-permute-start | bytes 135176 | tf_op jit(solution)/shard_map/ppermute | solution.py:364
  10.7 4.1 %collective-permute-start.3 = (f32[88,128]{1,0:T(8,128)S(1)}, f32[88,128]{1,0:T(8,128)S(1)}, u32[]{:S(2)}, u32[]{:S(2)}) collective-permute-start(f32[88,128]{1,0:T(8,128)S(1)} %get-tuple-element.73), channel_id=1, source_target_pairs={{0,2},{1,3},{2,0},{3,1},{4,6},{5,7},{6,4},{7,5},{8,10},{9,11},{10,... | collective-permute-start | bytes 135176 | tf_op jit(solution)/shard_map/ppermute | solution.py:364
  10.7 4.1 %collective-permute-start.4 = (f32[88,128]{1,0:T(8,128)S(1)}, f32[88,128]{1,0:T(8,128)S(1)}, u32[]{:S(2)}, u32[]{:S(2)}) collective-permute-start(f32[88,128]{1,0:T(8,128)S(1)} %get-tuple-element.74), channel_id=1, source_target_pairs={{0,3},{1,2},{2,1},{3,0},{4,7},{5,6},{6,5},{7,4},{8,11},{9,10},{10,... | collective-permute-start | bytes 135176 | tf_op jit(solution)/shard_map/ppermute | solution.py:364
  12.1 16.4 %slice-start.2 = ((s8[9437184]{0:T(1024)(128)(4,1)}), s8[4194304]{0:T(1024)(128)(4,1)S(1)}, s32[]{:S(2)}) async-start(s8[9437184]{0:T(1024)(128)(4,1)} %bitcast.5), calls=%async_computation.2 | async-start | bytes 8388608
  14.8 20.2 %collective-permute-start.8 = (f32[960,128]{1,0:T(8,128)S(1)}, f32[960,128]{1,0:T(8,128)S(1)}, u32[]{:S(2)}, u32[]{:S(2)}) collective-permute-start(f32[960,128]{1,0:T(8,128)S(1)} %get-tuple-element.80.s0), channel_id=1, source_target_pairs={{0,2},{1,3},{2,0},{3,1},{4,6},{5,7},{6,4},{7,5},{8,10},{9,11},{10,... | collective-permute-start | bytes 1474568 | tf_op jit(solution)/shard_map/ppermute | solution.py:364
  16.6 10.7 %collective-permute-start.10 = (f32[416,128]{1,0:T(8,128)S(1)}, f32[416,128]{1,0:T(8,128)S(1)}, u32[]{:S(2)}, u32[]{:S(2)}) collective-permute-start(f32[416,128]{1,0:T(8,128)S(1)} %get-tuple-element.82), channel_id=1, source_target_pairs={{3,6},{0,13},{1,12},{7,10},{4,1},{5,0},{11,14},{8,5},{9,4},{15,2},... | collective-permute-start | bytes 638984 | tf_op jit(solution)/shard_map/ppermute | solution.py:368
  21.6 10.3 %collective-permute-start.9 = (f32[416,128]{1,0:T(8,128)S(1)}, f32[416,128]{1,0:T(8,128)S(1)}, u32[]{:S(2)}, u32[]{:S(2)}) collective-permute-start(f32[416,128]{1,0:T(8,128)S(1)} %get-tuple-element.82), channel_id=1, source_target_pairs={{3,4},{0,15},{1,14},{7,8},{4,3},{5,2},{11,12},{8,7},{9,6},{15,0},{... | collective-permute-start | bytes 638984 | tf_op jit(solution)/shard_map/ppermute | solution.py:368
  24.6 10.1 %collective-permute-start.5 = (f32[96,128]{1,0:T(8,128)S(1)}, f32[96,128]{1,0:T(8,128)S(1)}, u32[]{:S(2)}, u32[]{:S(2)}) collective-permute-start(f32[96,128]{1,0:T(8,128)S(1)} %get-tuple-element.76), channel_id=1, source_target_pairs={{0,4},{1,5},{2,6},{3,7},{4,0},{5,1},{6,2},{7,3},{8,12},{9,13},{10,... | collective-permute-start | bytes 147464 | tf_op jit(solution)/shard_map/ppermute | solution.py:364
  24.8 10.1 %collective-permute-start.7 = (f32[96,128]{1,0:T(8,128)S(1)}, f32[96,128]{1,0:T(8,128)S(1)}, u32[]{:S(2)}, u32[]{:S(2)}) collective-permute-start(f32[96,128]{1,0:T(8,128)S(1)} %get-tuple-element.77), channel_id=1, source_target_pairs={{0,12},{1,13},{2,14},{3,15},{4,8},{5,9},{6,10},{7,11},{8,4},{9,5},... | collective-permute-start | bytes 147464 | tf_op jit(solution)/shard_map/ppermute | solution.py:364
  27.3 7.4 %collective-permute-start.6 = (f32[64,128]{1,0:T(8,128)S(1)}, f32[64,128]{1,0:T(8,128)S(1)}, u32[]{:S(2)}, u32[]{:S(2)}) collective-permute-start(f32[64,128]{1,0:T(8,128)S(1)} %get-tuple-element.92.refs_0_), channel_id=1, source_target_pairs={{0,8},{1,9},{2,10},{3,11},{4,12},{5,13},{6,14},{7,15},{8,0},{9,1},... | collective-permute-start | bytes 98312 | tf_op jit(solution)/shard_map/ppermute | solution.py:364
  35.0 3.2 %collective-permute-start.11 = (f32[2752,128]{1,0:T(8,128)S(1)}, f32[2752,128]{1,0:T(8,128)S(1)}, u32[]{:S(2)}, u32[]{:S(2)}) collective-permute-start(f32[2752,128]{1,0:T(8,128)S(1)} %pad_maximum_fusion), channel_id=1, source_target_pairs={{0,1},{1,0},{2,3},{3,2},{4,5},{5,4},{6,7},{7,6},{8,9},{9,8},{10,11... | collective-permute-start | bytes 4227080 | tf_op jit(solution)/shard_map/ppermute | solution.py:364
  42.5 9.6 %collective-permute-start.12 = (f32[96,128]{1,0:T(8,128)S(1)}, f32[96,128]{1,0:T(8,128)S(1)}, u32[]{:S(2)}, u32[]{:S(2)}) collective-permute-start(f32[96,128]{1,0:T(8,128)S(1)} %get-tuple-element.108), channel_id=1, source_target_pairs={{0,4},{1,5},{2,6},{3,7},{4,0},{5,1},{6,2},{7,3},{8,12},{9,13},{10,... | collective-permute-start | bytes 147464 | tf_op jit(solution)/shard_map/ppermute | solution.py:364
  44.4 7.7 %collective-permute-start.14 = (f32[96,128]{1,0:T(8,128)S(1)}, f32[96,128]{1,0:T(8,128)S(1)}, u32[]{:S(2)}, u32[]{:S(2)}) collective-permute-start(f32[96,128]{1,0:T(8,128)S(1)} %get-tuple-element.109), channel_id=1, source_target_pairs={{0,12},{1,13},{2,14},{3,15},{4,8},{5,9},{6,10},{7,11},{8,4},{9,5},... | collective-permute-start | bytes 147464 | tf_op jit(solution)/shard_map/ppermute | solution.py:364
  47.2 4.8 %collective-permute-start.13 = (f32[64,128]{1,0:T(8,128)S(1)}, f32[64,128]{1,0:T(8,128)S(1)}, u32[]{:S(2)}, u32[]{:S(2)}) collective-permute-start(f32[64,128]{1,0:T(8,128)S(1)} %get-tuple-element.113.refs_0_), channel_id=1, source_target_pairs={{0,8},{1,9},{2,10},{3,11},{4,12},{5,13},{6,14},{7,15},{8,0},{9,1},... | collective-permute-start | bytes 98312 | tf_op jit(solution)/shard_map/ppermute | solution.py:364
  54.8 7.6 %collective-permute-start.15 = (f32[96,128]{1,0:T(8,128)S(1)}, f32[96,128]{1,0:T(8,128)S(1)}, u32[]{:S(2)}, u32[]{:S(2)}) collective-permute-start(f32[96,128]{1,0:T(8,128)S(1)} %get-tuple-element.118), channel_id=1, source_target_pairs={{0,4},{1,5},{2,6},{3,7},{4,0},{5,1},{6,2},{7,3},{8,12},{9,13},{10,... | collective-permute-start | bytes 147464 | tf_op jit(solution)/shard_map/ppermute | solution.py:364
  55.9 6.5 %collective-permute-start.17 = (f32[96,128]{1,0:T(8,128)S(1)}, f32[96,128]{1,0:T(8,128)S(1)}, u32[]{:S(2)}, u32[]{:S(2)}) collective-permute-start(f32[96,128]{1,0:T(8,128)S(1)} %get-tuple-element.119), channel_id=1, source_target_pairs={{0,12},{1,13},{2,14},{3,15},{4,8},{5,9},{6,10},{7,11},{8,4},{9,5},... | collective-permute-start | bytes 147464 | tf_op jit(solution)/shard_map/ppermute | solution.py:364
  57.6 4.8 %collective-permute-start.16 = (f32[64,128]{1,0:T(8,128)S(1)}, f32[64,128]{1,0:T(8,128)S(1)}, u32[]{:S(2)}, u32[]{:S(2)}) collective-permute-start(f32[64,128]{1,0:T(8,128)S(1)} %get-tuple-element.123.refs_0_), channel_id=1, source_target_pairs={{0,8},{1,9},{2,10},{3,11},{4,12},{5,13},{6,14},{7,15},{8,0},{9,1},... | collective-permute-start | bytes 98312 | tf_op jit(solution)/shard_map/ppermute | solution.py:364
  64.5 1.9 %collective-permute-start.18 = (f32[120,128]{1,0:T(8,128)S(1)}, f32[120,128]{1,0:T(8,128)S(1)}, u32[]{:S(2)}, u32[]{:S(2)}) collective-permute-start(f32[120,128]{1,0:T(8,128)S(1)} %get-tuple-element.125), channel_id=1, source_target_pairs={{0,1},{1,0},{2,3},{3,2},{4,5},{5,4},{6,7},{7,6},{8,9},{9,8},{10,11... | collective-permute-start | bytes 184328 | tf_op jit(solution)/shard_map/ppermute | solution.py:364
  64.5 4.9 %collective-permute-start.19 = (f32[120,128]{1,0:T(8,128)S(1)}, f32[120,128]{1,0:T(8,128)S(1)}, u32[]{:S(2)}, u32[]{:S(2)}) collective-permute-start(f32[120,128]{1,0:T(8,128)S(1)} %get-tuple-element.126), channel_id=1, source_target_pairs={{0,2},{1,3},{2,0},{3,1},{4,6},{5,7},{6,4},{7,5},{8,10},{9,11},{10,... | collective-permute-start | bytes 184328 | tf_op jit(solution)/shard_map/ppermute | solution.py:364
  64.6 5.2 %collective-permute-start.20 = (f32[120,128]{1,0:T(8,128)S(1)}, f32[120,128]{1,0:T(8,128)S(1)}, u32[]{:S(2)}, u32[]{:S(2)}) collective-permute-start(f32[120,128]{1,0:T(8,128)S(1)} %get-tuple-element.127), channel_id=1, source_target_pairs={{0,3},{1,2},{2,1},{3,0},{4,7},{5,6},{6,5},{7,4},{8,11},{9,10},{10,... | collective-permute-start | bytes 184328 | tf_op jit(solution)/shard_map/ppermute | solution.py:364

commit v9 on v8

--- a/solution.py
+++ b/solution.py
@@ -307,7 +307,7 @@
         lam_right = lam_right + right_ref[...]
         lam_left = lam_left + left_ref[...]
     if kind == "last":
-        cut(jnp.concatenate([q, lam_right, left_ref[...], right_ref[...]], axis=0), member, outs)
+        cut(jnp.concatenate([q, lam_right], axis=0), member, outs)
         return
     v_ref, left_out, right_out = outs[:3]
     left_out[...] = lam_left
@@ -315,7 +315,9 @@
     lam = jnp.concatenate([lam_left, -lam_right], axis=0)
     v = v0[...] + combined(dot(own[...], shared(lam, member)), LANES)
     v_ref[...] = v
-    payload(v, width, paired, group % 2 == 1, *outs[3:])
+    payload(v, width, paired, group % 2 == 1, *outs[3:6])
+    if kind == "middle":
+        cut(jnp.concatenate([lam_left, -lam_right], axis=0), member, outs[6:])
 
 
 def sweep_kernel(first, pos, right_side, k_ref, u_ref, ks_ref):
@@ -328,20 +330,33 @@
     ks_ref[...] = both[:, :at] + part[:, :at]
 
 
-def final_kernel(parts, count, pos, p0, p1, p2, p3, *refs):
+def changed(u, ks, change):
+    high, low = halves(ks)
+    part = dot(high, change)
+    return u + part[:, :LANES] + part[:, LANES:] + dot(low, change[:, :LANES])
+
+
+def spread_kernel(parts, pos, p0, p1, p2, p3, *refs):
+    lam = joined([p0[...], p1[...], p2[...], p3[...]], pos[0])
+    us, kss, out = refs[:parts], refs[parts:2 * parts], refs[2 * parts]
+    side, at = lam.shape[0], 0
+    lam = beside(lam)
+    for u, ks in zip(us, kss):
+        out[at:at + u.shape[0]] = changed(u[...], ks[:, :side], lam)
+        at += u.shape[0]
+
+
+def final_kernel(parts, count, pos, p0, p1, p2, p3, u_ref, *refs):
     x = joined([p0[...], p1[...], p2[...], p3[...]], pos[0])
-    us, kss, (out, lam_ref) = refs[:parts], refs[parts:2 * parts], refs[2 * parts:]
+    kss, (out, lam_ref) = refs[:parts], refs[parts:]
     width = lam_ref.shape[0]
-    lam_ref[...] = x[count:count + width]
-    at = count + width
-    filler = jnp.zeros((width - count, LANES), F32)
-    change = beside(jnp.concatenate([x[at:at + width], -x[at + width:], -x[:count], filler], axis=0))
+    lam_ref[...] = x[count:]
+    change = beside(jnp.concatenate([-x[:count], jnp.zeros((width - count, LANES), F32)], axis=0))
     at = 0
-    for u, ks in zip(us, kss):
-        high, low = halves(ks[...])
-        part = dot(high, change)
-        out[at:at + u.shape[0]] = u[...] + part[:, :LANES] + part[:, LANES:] + dot(low, change[:, :LANES])
-        at += u.shape[0]
+    for ks in kss:
+        rows = slice(at, at + ks.shape[0])
+        out[rows] = changed(u_ref[rows], ks[:, 2 * width:], change)
+        at += ks.shape[0]
 
 
 def local(condensed, eigen_loads, coarse_inverse, face_rows, primal_rows, primal_slot):
@@ -452,8 +467,10 @@
     for step in range(ITERS):
         kind = "first" if step == 0 else "last" if step == ITERS - 1 else "middle"
         shapes = [(kept, LANES), (width, LANES), (width, LANES), *pay_shapes]
+        if kind == "middle":
+            shapes = shapes + [(side // GROUP, LANES)] * GROUP
         if kind == "last":
-            shapes = [((count + 3 * width) // GROUP, LANES)] * GROUP
+            shapes = [((count + width) // GROUP, LANES)] * GROUP
         outs = call(
             functools.partial(turn_kernel, kind, groups),
             shapes,
@@ -464,13 +481,23 @@
         if kind != "last":
             state = outs[:3]
             swept = sweep(outs)
-            pays = along(*outs[3:])
+            pays = along(*outs[3:6])
             pays[0] = after(pays[0], swept)
+        if kind == "middle":
+            lam_pieces = traded(after(outs[6:], swept))
+    us, kss = [x[0] for x in sweeps], [x[1] for x in sweeps]
+    traded_back = traded(outs)
+    (spread,) = call(
+        functools.partial(spread_kernel, parts),
+        [(order, columns)],
+        (pos, *after(lam_pieces, outs), *us, *kss),
+        1.3,
+    )
     displaced, multipliers = call(
         functools.partial(final_kernel, parts, count),
         [(order, columns), (width, columns)],
-        (pos, *traded(outs), *[x[0] for x in sweeps], *[x[1] for x in sweeps]),
-        2.6,
+        (pos, *traded_back, spread, *kss),
+        2,
     )
     return displaced, multipliers
 

time: 72.6 us -> 72.5 us (level)
  waiting for transfers between devices: 12.7 us -> 11.4 us
    ppermute x19 -> x22, waiting for transfers between devices: 11.5 us -> 10.2 us  [mate(): return lax.ppermute(x, 'sub', [(s, s ^ k) for s in range(total)])]
    pallas_call x12 -> x13, Pallas kernels: 28.2 us -> 28.9 us  [call(): pl.pallas_call(kernel, out_shape=[jax.ShapeDtypeStruct(s, d) for s, d in...]
    ppermute x19 -> x22, starting transfers between devices: 21.5 us -> 22 us  [mate(): return lax.ppermute(x, 'sub', [(s, s ^ k) for s in range(total)])]
  transfers between devices with their start and end apart: 21 -> 24, of which waited for: 9 -> 9; matrix products, arithmetic and copies ran while one was open for 1% -> 1% of each run, Pallas kernels for 23% -> 28%
where the time goes in v9:
time: 72.5 us; the launch traced here: 72.2 us
  starting transfers between devices  28.9 us (40%)
  Pallas kernels  28.9 us (40%)
  waiting for transfers between devices  11.4 us (16%)
  local copies, waits for them, and re-layouts  1.15 us (2%)
  other arithmetic  0.99 us (1%)
  between operations  0.85 us (1%)
    pallas_call x13, Pallas kernels, call(): pl.pallas_call(kernel, out_shape=[jax.ShapeDtypeStruct(s, d) for s, d in...  28.9 us
    ppermute x22, starting transfers between devices, mate(): return lax.ppermute(x, 'sub', [(s, s ^ k) for s in range(total)])  22 us
    ppermute x22, waiting for transfers between devices, mate(): return lax.ppermute(x, 'sub', [(s, s ^ k) for s in range(total)])  10.2 us
    ppermute x2, starting transfers between devices, crossing(): return lax.ppermute(x, 'sub', pairs)  6.97 us
  transfers between devices with their start and end apart: 24, of which 9 were waited for; matrix products, arithmetic and copies ran while one was open for 1% of the time, Pallas kernels for 28%

profile of v9, /device:TPU:0, one launch (start us, length us, event | category | flops | bytes accessed | tf_op | source)
XLA Modules:
  0.0 72.2 jit_solution(5433384383947039149)
XLA Ops:
  0.6 3.0 %collective-permute-start = (f32[48,768]{1,0:T(8,128)}, f32[48,768]{1,0:T(8,128)S(1)}, u32[]{:S(2)}, u32[]{:S(2)}) collective-permute-start(f32[48,768]{1,0:T(8,128)} %c0.1), channel_id=1, source_target_pairs={{0,2},{1,3},{2,0},{3,1},{4,6},{5,7},{6,4},{7,5},{8,10},{9,11},{10,... | collective-permute-start | bytes 442376 | tf_op jit(solution)/shard_map/ppermute | solution.py:379
  3.7 0.1 fusion
  3.7 0.7 pad_add_fusion.table.tablev
  4.5 1.1 %copy-done.1 = f32[1536,128]{1,0:T(8,128)S(1)} copy-done((f32[1536,128]{1,0:T(8,128)S(1)}, f32[1536,128]{1,0:T(8,128)}, u32[]{:S(2)}) %copy-start.1) | copy-done | bytes 786456
  5.6 4.4 %shard_map.77 = (f32[88,128]{1,0:T(8,128)S(1)}, f32[88,128]{1,0:T(8,128)S(1)}, f32[88,128]{1,0:T(8,128)S(1)}, f32[88,128]{1,0:T(8,128)S(1)}, f32[352,1536]{1,0:T(8,128)S(1)}) custom-call(s32[5,128]{1,0:T(8,128)S(1)} %pad_add_fusion.table.tablev, f32[1536,1536]{1,0:T(8,128)} %k_ref.9, f32[1536,128]{1,0:T(8,128)S(1)} %copy-done.1), custom_call_target="tpu_custom_call" | custom-call | flops 5299999744 | tf_op jit(solution)/shard_map/pallas_call | solution.py:25
  10.0 0.0 collective-permute-done.c2
  10.1 0.1 collective-permute-start.1
  10.2 0.5 collective-permute-start.2
  10.7 0.0 collective-permute-start.3
  10.7 1.4 %collective-permute-start.4 = (f32[88,128]{1,0:T(8,128)S(1)}, f32[88,128]{1,0:T(8,128)S(1)}, u32[]{:S(2)}, u32[]{:S(2)}) collective-permute-start(f32[88,128]{1,0:T(8,128)S(1)} %get-tuple-element.86), channel_id=1, source_target_pairs={{0,3},{1,2},{2,1},{3,0},{4,7},{5,6},{6,5},{7,4},{8,11},{9,10},{10,... | collective-permute-start | bytes 135176 | tf_op jit(solution)/shard_map/ppermute | solution.py:379
  12.1 2.3 %shard_map.79 = (f32[960,128]{1,0:T(8,128)S(1)}, f32[416,128]{1,0:T(8,128)S(1)}, bf16[1536,640]{1,0:T(8,128)(2,1)S(1)}) custom-call(s32[5,128]{1,0:T(8,128)S(1)} %pad_add_fusion.table.tablev, f32[352,1536]{1,0:T(8,128)S(1)} %get-tuple-element.90.ks, f32[1536,128]{1,0:T(8,128)S(1)} %copy-done.2, f32[48,768]{1,0:T(8,128)S(1)} %copy-done, ...), custom_call_target="tpu_custom_call" | custom-call | flops 2000000000 | tf_op jit(solution)/shard_map/pallas_call | solution.py:25
  14.4 0.0 collective-permute-done.2.p1
  14.4 0.3 collective-permute-done.3.p2
  14.8 0.0 collective-permute-done.4.p3
  14.8 1.8 %collective-permute-start.8 = (f32[960,128]{1,0:T(8,128)S(1)}, f32[960,128]{1,0:T(8,128)S(1)}, u32[]{:S(2)}, u32[]{:S(2)}) collective-permute-start(f32[960,128]{1,0:T(8,128)S(1)} %get-tuple-element.92.s0), channel_id=1, source_target_pairs={{0,2},{1,3},{2,0},{3,1},{4,6},{5,7},{6,4},{7,5},{8,10},{9,11},{10,... | collective-permute-start | bytes 1474568 | tf_op jit(solution)/shard_map/ppermute | solution.py:379
  16.6 4.9 %collective-permute-start.10 = (f32[416,128]{1,0:T(8,128)S(1)}, f32[416,128]{1,0:T(8,128)S(1)}, u32[]{:S(2)}, u32[]{:S(2)}) collective-permute-start(f32[416,128]{1,0:T(8,128)S(1)} %get-tuple-element.94), channel_id=1, source_target_pairs={{3,6},{0,13},{1,12},{7,10},{4,1},{5,0},{11,14},{8,5},{9,4},{15,2},... | collective-permute-start | bytes 638984 | tf_op jit(solution)/shard_map/ppermute | solution.py:383
  21.5 0.1 pad_add_fusion.3.pos
  21.6 2.1 %collective-permute-start.9 = (f32[416,128]{1,0:T(8,128)S(1)}, f32[416,128]{1,0:T(8,128)S(1)}, u32[]{:S(2)}, u32[]{:S(2)}) collective-permute-start(f32[416,128]{1,0:T(8,128)S(1)} %get-tuple-element.94), channel_id=1, source_target_pairs={{3,4},{0,15},{1,14},{7,8},{4,3},{5,2},{11,12},{8,7},{9,6},{15,0},{... | collective-permute-start | bytes 638984 | tf_op jit(solution)/shard_map/ppermute | solution.py:383
  23.7 0.0 collective-permute-done.1.c_other
  23.7 0.9 %shard_map.78 = (f32[352,128]{1,0:T(8,128)S(1)}, f32[64,128]{1,0:T(8,128)S(1)}, f32[96,128]{1,0:T(8,128)S(1)}, f32[96,128]{1,0:T(8,128)S(1)}) custom-call(s32[2]{0:T(128)S(1)} %pad_add_fusion.3.pos, f32[88,128]{1,0:T(8,128)S(1)} %get-tuple-element.83.p0, f32[88,128]{1,0:T(8,128)S(1)} %collective-permute-done.2.p1, f32[88,128]{1,0:T(8,128)S(1)} %collective-permute-done.3.p2, ...), custom_call_target="tpu_custom_call" | custom-call | flops 900000000 | tf_op jit(solution)/shard_map/pallas_call | solution.py:25
  24.6 0.2 collective-permute-start.5
  24.8 2.5 %collective-permute-start.7 = (f32[96,128]{1,0:T(8,128)S(1)}, f32[96,128]{1,0:T(8,128)S(1)}, u32[]{:S(2)}, u32[]{:S(2)}) collective-permute-start(f32[96,128]{1,0:T(8,128)S(1)} %get-tuple-element.89), channel_id=1, source_target_pairs={{0,12},{1,13},{2,14},{3,15},{4,8},{5,9},{6,10},{7,11},{8,4},{9,5},... | collective-permute-start | bytes 147464 | tf_op jit(solution)/shard_map/ppermute | solution.py:379
  27.3 0.0 collective-permute-done.10.came_next
  27.3 1.2 %collective-permute-start.6 = (f32[64,128]{1,0:T(8,128)S(1)}, f32[64,128]{1,0:T(8,128)S(1)}, u32[]{:S(2)}, u32[]{:S(2)}) collective-permute-start(f32[64,128]{1,0:T(8,128)S(1)} %get-tuple-element.104.refs_0_), channel_id=1, source_target_pairs={{0,8},{1,9},{2,10},{3,11},{4,12},{5,13},{6,14},{7,15},{8,0},{9,1},... | collective-permute-start | bytes 98312 | tf_op jit(solution)/shard_map/ppermute | solution.py:379
  28.5 2.3 %shard_map.80 = (f32[384,128]{1,0:T(8,128)S(1)}, f32[384,384]{1,0:T(8,128)S(1)}) custom-call(s32[2]{0:T(128)S(1)} %pad_add_fusion.3.pos, bf16[1536,640]{1,0:T(8,128)(2,1)S(1)} %get-tuple-element.136.right_side, f32[1536,1536]{1,0:T(8,128)S(1)} %bitcast.6), custom_call_target="tpu_custom_call" | custom-call | flops 2300000000 | tf_op jit(solution)/shard_map/pallas_call | solution.py:25
  30.8 1.2 %collective-permute-done.9.came = f32[416,128]{1,0:T(8,128)S(1)} collective-permute-done((f32[416,128]{1,0:T(8,128)S(1)}, f32[416,128]{1,0:T(8,128)S(1)}, u32[]{:S(2)}, u32[]{:S(2)}) %collective-permute-start.9) | collective-permute-done | bytes 213024 | tf_op jit(solution)/shard_map/ppermute | solution.py:383
  31.9 2.8 %collective-permute-done.6.refs_2_ = f32[64,128]{1,0:T(8,128)S(1)} collective-permute-done((f32[64,128]{1,0:T(8,128)S(1)}, f32[64,128]{1,0:T(8,128)S(1)}, u32[]{:S(2)}, u32[]{:S(2)}) %collective-permute-start.6) | collective-permute-done | bytes 32800 | tf_op jit(solution)/shard_map/ppermute | solution.py:379
  34.7 0.0 collective-permute-done.5.refs_1_
  34.7 0.2 collective-permute-done.7.refs_3_
  34.9 0.0 collective-permute-done.8.s2
  34.9 0.1 pad_maximum_fusion
  35.0 0.1 collective-permute-start.11
  35.1 2.3 %shard_map.81 = (f32[384,128]{1,0:T(8,128)S(1)}, f32[384,384]{1,0:T(8,128)S(1)}) custom-call(s32[2]{0:T(128)S(1)} %pad_add_fusion.3.pos, bf16[1536,640]{1,0:T(8,128)(2,1)S(1)} %get-tuple-element.136.right_side, f32[1536,1536]{1,0:T(8,128)S(1)} %bitcast.6), custom_call_target="tpu_custom_call" | custom-call | flops 2300000000 | tf_op jit(solution)/shard_map/pallas_call | solution.py:25
  37.4 0.9 %collective-permute-done.11.theirs = f32[2752,128]{1,0:T(8,128)S(1)} collective-permute-done((f32[2752,128]{1,0:T(8,128)S(1)}, f32[2752,128]{1,0:T(8,128)S(1)}, u32[]{:S(2)}, u32[]{:S(2)}) %collective-permute-start.11) | collective-permute-done | bytes 1409056 | tf_op jit(solution)/shard_map/ppermute | solution.py:379
  38.3 1.4 %shard_map.82 = (bf16[672,768]{1,0:T(8,128)(2,1)S(1)}, bf16[512,512]{1,0:T(8,128)(2,1)S(1)}, bf16[704,1024]{1,0:T(8,128)(2,1)S(1)}, bf16[256,128]{1,0:T(8,128)(2,1)S(1)}, bf16[256,128]{1,0:T(8,128)(2,1)S(1)}) custom-call(s32[2]{0:T(128)S(1)} %pad_add_fusion.3.pos, f32[48,768]{1,0:T(8,128)S(1)} %copy-done, f32[48,768]{1,0:T(8,128)S(1)} %collective-permute-done.c2, ...), custom_call_target="tpu_custom_call" | custom-call | flops 1700000000 | tf_op jit(solution)/shard_map/pallas_call | solution.py:25
  39.7 2.8 %shard_map.83 = (f32[352,128]{1,0:T(8,128)S(1)}, f32[128,128]{1,0:T(8,128)S(1)}, f32[128,128]{1,0:T(8,128)S(1)}, f32[64,128]{1,0:T(8,128)S(1)}, f32[96,128]{1,0:T(8,128)S(1)}, /*index=5*/f32[96,128]{1,0:T(8,128)S(1)}) custom-call(s32[2]{0:T(128)S(1)} %pad_add_fusion.3.pos, f32[64,128]{1,0:T(8,128)S(1)} %get-tuple-element.104.refs_0_, ...), custom_call_target="tpu_custom_call" | custom-call | flops 2800000000 | tf_op jit(solution)/shard_map/pallas_call | solution.py:25
  42.5 1.9 %collective-permute-start.12 = (f32[96,128]{1,0:T(8,128)S(1)}, f32[96,128]{1,0:T(8,128)S(1)}, u32[]{:S(2)}, u32[]{:S(2)}) collective-permute-start(f32[96,128]{1,0:T(8,128)S(1)} %get-tuple-element.120), channel_id=1, source_target_pairs={{0,4},{1,5},{2,6},{3,7},{4,0},{5,1},{6,2},{7,3},{8,12},{9,13},{10,... | collective-permute-start | bytes 147464 | tf_op jit(solution)/shard_map/ppermute | solution.py:379
  44.4 2.9 %collective-permute-start.14 = (f32[96,128]{1,0:T(8,128)S(1)}, f32[96,128]{1,0:T(8,128)S(1)}, u32[]{:S(2)}, u32[]{:S(2)}) collective-permute-start(f32[96,128]{1,0:T(8,128)S(1)} %get-tuple-element.121), channel_id=1, source_target_pairs={{0,12},{1,13},{2,14},{3,15},{4,8},{5,9},{6,10},{7,11},{8,4},{9,5},... | collective-permute-start | bytes 147464 | tf_op jit(solution)/shard_map/ppermute | solution.py:379
  47.2 0.5 collective-permute-start.13
  47.7 2.3 %shard_map.84 = (f32[384,128]{1,0:T(8,128)S(1)}, f32[384,384]{1,0:T(8,128)S(1)}) custom-call(s32[2]{0:T(128)S(1)} %pad_add_fusion.3.pos, bf16[1536,640]{1,0:T(8,128)(2,1)S(1)} %get-tuple-element.136.right_side, f32[1536,1536]{1,0:T(8,128)S(1)} %bitcast.6), custom_call_target="tpu_custom_call" | custom-call | flops 2300000000 | tf_op jit(solution)/shard_map/pallas_call | solution.py:25
  50.0 2.1 %collective-permute-done.13.refs_2_ = f32[64,128]{1,0:T(8,128)S(1)} collective-permute-done((f32[64,128]{1,0:T(8,128)S(1)}, f32[64,128]{1,0:T(8,128)S(1)}, u32[]{:S(2)}, u32[]{:S(2)}) %collective-permute-start.13) | collective-permute-done | bytes 32800 | tf_op jit(solution)/shard_map/ppermute | solution.py:379
  52.0 0.0 collective-permute-done.12.refs_1_
  52.0 0.0 collective-permute-done.14.refs_3_
  52.0 2.8 %shard_map.85 = (f32[352,128]{1,0:T(8,128)S(1)}, f32[128,128]{1,0:T(8,128)S(1)}, f32[128,128]{1,0:T(8,128)S(1)}, f32[64,128]{1,0:T(8,128)S(1)}, f32[96,128]{1,0:...) custom-call(s32[2]{0:T(128)S(1)} %pad_add_fusion.3.pos, ...), custom_call_target="tpu_custom_call" | custom-call | flops 2800000000 | tf_op jit(solution)/shard_map/pallas_call | solution.py:25
  54.8 1.1 %collective-permute-start.15 = (f32[96,128]{1,0:T(8,128)S(1)}, f32[96,128]{1,0:T(8,128)S(1)}, u32[]{:S(2)}, u32[]{:S(2)}) collective-permute-start(f32[96,128]{1,0:T(8,128)S(1)} %get-tuple-element.130), channel_id=1, source_target_pairs={{0,4},{1,5},{2,6},{3,7},{4,0},{5,1},{6,2},{7,3},{8,12},{9,13},{10,... | collective-permute-start | bytes 147464 | tf_op jit(solution)/shard_map/ppermute | solution.py:379
  55.9 1.7 %collective-permute-start.17 = (f32[96,128]{1,0:T(8,128)S(1)}, f32[96,128]{1,0:T(8,128)S(1)}, u32[]{:S(2)}, u32[]{:S(2)}) collective-permute-start(f32[96,128]{1,0:T(8,128)S(1)} %get-tuple-element.131), channel_id=1, source_target_pairs={{0,12},{1,13},{2,14},{3,15},{4,8},{5,9},{6,10},{7,11},{8,4},{9,5},... | collective-permute-start | bytes 147464 | tf_op jit(solution)/shard_map/ppermute | solution.py:379
  57.6 0.8 %collective-permute-start.16 = (f32[64,128]{1,0:T(8,128)S(1)}, f32[64,128]{1,0:T(8,128)S(1)}, u32[]{:S(2)}, u32[]{:S(2)}) collective-permute-start(f32[64,128]{1,0:T(8,128)S(1)} %get-tuple-element.139.refs_0_), channel_id=1, source_target_pairs={{0,8},{1,9},{2,10},{3,11},{4,12},{5,13},{6,14},{7,15},{8,0},{9,1},... | collective-permute-start | bytes 98312 | tf_op jit(solution)/shard_map/ppermute | solution.py:379
  58.4 2.3 %shard_map.86 = (f32[384,128]{1,0:T(8,128)S(1)}, f32[384,384]{1,0:T(8,128)S(1)}) custom-call(s32[2]{0:T(128)S(1)} %pad_add_fusion.3.pos, bf16[1536,640]{1,0:T(8,128)(2,1)S(1)} %get-tuple-element.136.right_side, f32[1536,1536]{1,0:T(8,128)S(1)} %bitcast.6), custom_call_target="tpu_custom_call" | custom-call | flops 2300000000 | tf_op jit(solution)/shard_map/pallas_call | solution.py:25
  60.6 0.1 collective-permute-start.21
  60.7 0.1 collective-permute-start.22
  60.8 1.6 %collective-permute-done.16.refs_2_ = f32[64,128]{1,0:T(8,128)S(1)} collective-permute-done((f32[64,128]{1,0:T(8,128)S(1)}, f32[64,128]{1,0:T(8,128)S(1)}, u32[]{:S(2)}, u32[]{:S(2)}) %collective-permute-start.16) | collective-permute-done | bytes 32800 | tf_op jit(solution)/shard_map/ppermute | solution.py:379
  62.4 0.2 collective-permute-start.23
  62.6 0.0 collective-permute-done.15.refs_1_
  62.6 0.0 collective-permute-done.17.refs_3_
  62.6 2.0 %shard_map.87 = (f32[56,128]{1,0:T(8,128)S(1)}, f32[56,128]{1,0:T(8,128)S(1)}, f32[56,128]{1,0:T(8,128)S(1)}, f32[56,128]{1,0:T(8,128)S(1)}) custom-call(s32[2]{0:T(128)S(1)} %pad_add_fusion.3.pos, f32[64,128]{1,0:T(8,128)S(1)} %get-tuple-element.139.refs_0_, f32[96,128]{1,0:T(8,128)S(1)} %collective-permute-done.15.refs_1_, ...), custom_call_target="tpu_custom_call" | custom-call | flops 2800000000 | tf_op jit(solution)/shard_map/pallas_call | solution.py:25
  64.6 0.4 collective-permute-start.18
  65.0 1.6 %collective-permute-start.19 = (f32[56,128]{1,0:T(8,128)S(1)}, f32[56,128]{1,0:T(8,128)S(1)}, u32[]{:S(2)}, u32[]{:S(2)}) collective-permute-start(f32[56,128]{1,0:T(8,128)S(1)} %get-tuple-element.142), channel_id=1, source_target_pairs={{0,2},{1,3},{2,0},{3,1},{4,6},{5,7},{6,4},{7,5},{8,10},{9,11},{10,... | collective-permute-start | bytes 86024 | tf_op jit(solution)/shard_map/ppermute | solution.py:379
  66.7 0.0 collective-permute-done.21.p1
  66.7 0.0 collective-permute-start.20
  66.7 0.0 collective-permute-done.23.p3
  66.7 1.3 %shard_map.88.u_ref = f32[1536,128]{1,0:T(8,128)S(1)} custom-call(s32[2]{0:T(128)S(1)} %pad_add_fusion.3.pos, f32[64,128]{1,0:T(8,128)S(1)} %get-tuple-element.148.p0, f32[64,128]{1,0:T(8,128)S(1)} %collective-permute-done.21.p1, f32[64,128]{1,0:T(8,128)S(1)} %collective-permute-done.22.p2, f32[64,128]{1,0:T(8,128)S(1)} %collective-permute-done.23.p3, ...), custom_call_target="tpu_custom_call" | custom-call | flops 1300000000 | tf_op jit(solution)/shard_map/pallas_call | solution.py:25
  68.0 0.9 %collective-permute-done.19.p2 = f32[56,128]{1,0:T(8,128)S(1)} collective-permute-done((f32[56,128]{1,0:T(8,128)S(1)}, f32[56,128]{1,0:T(8,128)S(1)}, u32[]{:S(2)}, u32[]{:S(2)}) %collective-permute-start.19) | collective-permute-done | bytes 28704 | tf_op jit(solution)/shard_map/ppermute | solution.py:379
  68.9 1.4 %collective-permute-done.20.p3 = f32[56,128]{1,0:T(8,128)S(1)} collective-permute-done((f32[56,128]{1,0:T(8,128)S(1)}, f32[56,128]{1,0:T(8,128)S(1)}, u32[]{:S(2)}, u32[]{:S(2)}) %collective-permute-start.20) | collective-permute-done | bytes 28704 | tf_op jit(solution)/shard_map/ppermute | solution.py:379
  70.2 2.0 %shard_map.89 = (f32[1536,128]{1,0:T(8,128)}, f32[128,128]{1,0:T(8,128)}) custom-call(s32[2]{0:T(128)S(1)} %pad_add_fusion.3.pos, f32[56,128]{1,0:T(8,128)S(1)} %get-tuple-element.140.p0, f32[56,128]{1,0:T(8,128)S(1)} %collective-permute-done.18.p1, f32[56,128]{1,0:T(8,128)S(1)} %collective-permute-done.19.p2, f32[56,128]{1,0:T(8,128)S(1)} %collective-permute-done.20.p3, ...), custom_call_target="tpu_custom_call" | custom-call | flops 2000000000 | tf_op jit(solution)/shard_map/pallas_call | solution.py:25
  (15 shorter events, 0.0 us)
Async XLA Ops:
  0.6 9.4 %collective-permute-start = (f32[48,768]{1,0:T(8,128)}, f32[48,768]{1,0:T(8,128)S(1)}, u32[]{:S(2)}, u32[]{:S(2)}) collective-permute-start(f32[48,768]{1,0:T(8,128)} %c0.1), channel_id=1, source_target_pairs={{0,2},{1,3},{2,0},{3,1},{4,6},{5,7},{6,4},{7,5},{8,10},{9,11},{10,... | collective-permute-start | bytes 442376 | tf_op jit(solution)/shard_map/ppermute | solution.py:379
  4.5 1.1 %copy-start.1 = (f32[1536,128]{1,0:T(8,128)S(1)}, f32[1536,128]{1,0:T(8,128)}, u32[]{:S(2)}) copy-start(f32[1536,128]{1,0:T(8,128)} %f_ref.3) | copy-start | bytes 2359300
  5.6 4.5 %copy-start = (f32[48,768]{1,0:T(8,128)S(1)}, f32[48,768]{1,0:T(8,128)}, u32[]{:S(2)}) copy-start(f32[48,768]{1,0:T(8,128)} %c0.1) | copy-start | bytes 442372
  5.6 6.5 %copy-start.2 = (f32[1536,128]{1,0:T(8,128)S(1)}, f32[1536,128]{1,0:T(8,128)}, u32[]{:S(2)}) copy-start(f32[1536,128]{1,0:T(8,128)} %f_ref.3) | copy-start | bytes 2359300
  5.6 22.9 %slice-start = ((s8[9437184]{0:T(1024)(128)(4,1)}), s8[1048576]{0:T(1024)(128)(4,1)S(1)}, s32[]{:S(2)}) async-start(s8[9437184]{0:T(1024)(128)(4,1)} %bitcast.5), calls=%async_computation | async-start | bytes 2097152
  5.6 22.9 %slice-start.1 = ((s8[9437184]{0:T(1024)(128)(4,1)}), s8[4194304]{0:T(1024)(128)(4,1)S(1)}, s32[]{:S(2)}) async-start(s8[9437184]{0:T(1024)(128)(4,1)} %bitcast.5), calls=%async_computation.1 | async-start | bytes 8388608
  10.1 13.6 %collective-permute-start.1 = (f32[96,768]{1,0:T(8,128)S(1)}, f32[96,768]{1,0:T(8,128)S(1)}, u32[]{:S(2)}, u32[]{:S(2)}) collective-permute-start(f32[96,768]{1,0:T(8,128)S(1)} %pad_maximum_fusion.1), channel_id=1, source_target_pairs={{0,1},{1,0},{2,3},{3,2},{4,5},{5,4},{6,7},{7,6},{8,9},{9,8},{10,11... | collective-permute-start | bytes 884744 | tf_op jit(solution)/shard_map/ppermute | solution.py:379
  10.2 4.3 %collective-permute-start.2 = (f32[88,128]{1,0:T(8,128)S(1)}, f32[88,128]{1,0:T(8,128)S(1)}, u32[]{:S(2)}, u32[]{:S(2)}) collective-permute-start(f32[88,128]{1,0:T(8,128)S(1)} %get-tuple-element.84), channel_id=1, source_target_pairs={{0,1},{1,0},{2,3},{3,2},{4,5},{5,4},{6,7},{7,6},{8,9},{9,8},{10,11... | collective-permute-start | bytes 135176 | tf_op jit(solution)/shard_map/ppermute | solution.py:379
  10.7 4.1 %collective-permute-start.3 = (f32[88,128]{1,0:T(8,128)S(1)}, f32[88,128]{1,0:T(8,128)S(1)}, u32[]{:S(2)}, u32[]{:S(2)}) collective-permute-start(f32[88,128]{1,0:T(8,128)S(1)} %get-tuple-element.85), channel_id=1, source_target_pairs={{0,2},{1,3},{2,0},{3,1},{4,6},{5,7},{6,4},{7,5},{8,10},{9,11},{10,... | collective-permute-start | bytes 135176 | tf_op jit(solution)/shard_map/ppermute | solution.py:379
  10.7 4.1 %collective-permute-start.4 = (f32[88,128]{1,0:T(8,128)S(1)}, f32[88,128]{1,0:T(8,128)S(1)}, u32[]{:S(2)}, u32[]{:S(2)}) collective-permute-start(f32[88,128]{1,0:T(8,128)S(1)} %get-tuple-element.86), channel_id=1, source_target_pairs={{0,3},{1,2},{2,1},{3,0},{4,7},{5,6},{6,5},{7,4},{8,11},{9,10},{10,... | collective-permute-start | bytes 135176 | tf_op jit(solution)/shard_map/ppermute | solution.py:379
  12.1 16.4 %slice-start.2 = ((s8[9437184]{0:T(1024)(128)(4,1)}), s8[4194304]{0:T(1024)(128)(4,1)S(1)}, s32[]{:S(2)}) async-start(s8[9437184]{0:T(1024)(128)(4,1)} %bitcast.5), calls=%async_computation.2 | async-start | bytes 8388608
  14.8 20.2 %collective-permute-start.8 = (f32[960,128]{1,0:T(8,128)S(1)}, f32[960,128]{1,0:T(8,128)S(1)}, u32[]{:S(2)}, u32[]{:S(2)}) collective-permute-start(f32[960,128]{1,0:T(8,128)S(1)} %get-tuple-element.92.s0), channel_id=1, source_target_pairs={{0,2},{1,3},{2,0},{3,1},{4,6},{5,7},{6,4},{7,5},{8,10},{9,11},{10,... | collective-permute-start | bytes 1474568 | tf_op jit(solution)/shard_map/ppermute | solution.py:379
  16.6 10.7 %collective-permute-start.10 = (f32[416,128]{1,0:T(8,128)S(1)}, f32[416,128]{1,0:T(8,128)S(1)}, u32[]{:S(2)}, u32[]{:S(2)}) collective-permute-start(f32[416,128]{1,0:T(8,128)S(1)} %get-tuple-element.94), channel_id=1, source_target_pairs={{3,6},{0,13},{1,12},{7,10},{4,1},{5,0},{11,14},{8,5},{9,4},{15,2},... | collective-permute-start | bytes 638984 | tf_op jit(solution)/shard_map/ppermute | solution.py:383
  21.6 10.3 %collective-permute-start.9 = (f32[416,128]{1,0:T(8,128)S(1)}, f32[416,128]{1,0:T(8,128)S(1)}, u32[]{:S(2)}, u32[]{:S(2)}) collective-permute-start(f32[416,128]{1,0:T(8,128)S(1)} %get-tuple-element.94), channel_id=1, source_target_pairs={{3,4},{0,15},{1,14},{7,8},{4,3},{5,2},{11,12},{8,7},{9,6},{15,0},{... | collective-permute-start | bytes 638984 | tf_op jit(solution)/shard_map/ppermute | solution.py:383
  24.6 10.1 %collective-permute-start.5 = (f32[96,128]{1,0:T(8,128)S(1)}, f32[96,128]{1,0:T(8,128)S(1)}, u32[]{:S(2)}, u32[]{:S(2)}) collective-permute-start(f32[96,128]{1,0:T(8,128)S(1)} %get-tuple-element.88), channel_id=1, source_target_pairs={{0,4},{1,5},{2,6},{3,7},{4,0},{5,1},{6,2},{7,3},{8,12},{9,13},{10,... | collective-permute-start | bytes 147464 | tf_op jit(solution)/shard_map/ppermute | solution.py:379
  24.8 10.1 %collective-permute-start.7 = (f32[96,128]{1,0:T(8,128)S(1)}, f32[96,128]{1,0:T(8,128)S(1)}, u32[]{:S(2)}, u32[]{:S(2)}) collective-permute-start(f32[96,128]{1,0:T(8,128)S(1)} %get-tuple-element.89), channel_id=1, source_target_pairs={{0,12},{1,13},{2,14},{3,15},{4,8},{5,9},{6,10},{7,11},{8,4},{9,5},... | collective-permute-start | bytes 147464 | tf_op jit(solution)/shard_map/ppermute | solution.py:379
  27.3 7.4 %collective-permute-start.6 = (f32[64,128]{1,0:T(8,128)S(1)}, f32[64,128]{1,0:T(8,128)S(1)}, u32[]{:S(2)}, u32[]{:S(2)}) collective-permute-start(f32[64,128]{1,0:T(8,128)S(1)} %get-tuple-element.104.refs_0_), channel_id=1, source_target_pairs={{0,8},{1,9},{2,10},{3,11},{4,12},{5,13},{6,14},{7,15},{8,0},{9,1},... | collective-permute-start | bytes 98312 | tf_op jit(solution)/shard_map/ppermute | solution.py:379
  35.0 3.2 %collective-permute-start.11 = (f32[2752,128]{1,0:T(8,128)S(1)}, f32[2752,128]{1,0:T(8,128)S(1)}, u32[]{:S(2)}, u32[]{:S(2)}) collective-permute-start(f32[2752,128]{1,0:T(8,128)S(1)} %pad_maximum_fusion), channel_id=1, source_target_pairs={{0,1},{1,0},{2,3},{3,2},{4,5},{5,4},{6,7},{7,6},{8,9},{9,8},{10,11... | collective-permute-start | bytes 4227080 | tf_op jit(solution)/shard_map/ppermute | solution.py:379
  42.5 9.6 %collective-permute-start.12 = (f32[96,128]{1,0:T(8,128)S(1)}, f32[96,128]{1,0:T(8,128)S(1)}, u32[]{:S(2)}, u32[]{:S(2)}) collective-permute-start(f32[96,128]{1,0:T(8,128)S(1)} %get-tuple-element.120), channel_id=1, source_target_pairs={{0,4},{1,5},{2,6},{3,7},{4,0},{5,1},{6,2},{7,3},{8,12},{9,13},{10,... | collective-permute-start | bytes 147464 | tf_op jit(solution)/shard_map/ppermute | solution.py:379
  44.4 7.7 %collective-permute-start.14 = (f32[96,128]{1,0:T(8,128)S(1)}, f32[96,128]{1,0:T(8,128)S(1)}, u32[]{:S(2)}, u32[]{:S(2)}) collective-permute-start(f32[96,128]{1,0:T(8,128)S(1)} %get-tuple-element.121), channel_id=1, source_target_pairs={{0,12},{1,13},{2,14},{3,15},{4,8},{5,9},{6,10},{7,11},{8,4},{9,5},... | collective-permute-start | bytes 147464 | tf_op jit(solution)/shard_map/ppermute | solution.py:379
  47.2 4.8 %collective-permute-start.13 = (f32[64,128]{1,0:T(8,128)S(1)}, f32[64,128]{1,0:T(8,128)S(1)}, u32[]{:S(2)}, u32[]{:S(2)}) collective-permute-start(f32[64,128]{1,0:T(8,128)S(1)} %get-tuple-element.125.refs_0_), channel_id=1, source_target_pairs={{0,8},{1,9},{2,10},{3,11},{4,12},{5,13},{6,14},{7,15},{8,0},{9,1},... | collective-permute-start | bytes 98312 | tf_op jit(solution)/shard_map/ppermute | solution.py:379
  54.8 7.7 %collective-permute-start.15 = (f32[96,128]{1,0:T(8,128)S(1)}, f32[96,128]{1,0:T(8,128)S(1)}, u32[]{:S(2)}, u32[]{:S(2)}) collective-permute-start(f32[96,128]{1,0:T(8,128)S(1)} %get-tuple-element.130), channel_id=1, source_target_pairs={{0,4},{1,5},{2,6},{3,7},{4,0},{5,1},{6,2},{7,3},{8,12},{9,13},{10,... | collective-permute-start | bytes 147464 | tf_op jit(solution)/shard_map/ppermute | solution.py:379
  55.9 6.7 %collective-permute-start.17 = (f32[96,128]{1,0:T(8,128)S(1)}, f32[96,128]{1,0:T(8,128)S(1)}, u32[]{:S(2)}, u32[]{:S(2)}) collective-permute-start(f32[96,128]{1,0:T(8,128)S(1)} %get-tuple-element.131), channel_id=1, source_target_pairs={{0,12},{1,13},{2,14},{3,15},{4,8},{5,9},{6,10},{7,11},{8,4},{9,5},... | collective-permute-start | bytes 147464 | tf_op jit(solution)/shard_map/ppermute | solution.py:379
  57.6 4.8 %collective-permute-start.16 = (f32[64,128]{1,0:T(8,128)S(1)}, f32[64,128]{1,0:T(8,128)S(1)}, u32[]{:S(2)}, u32[]{:S(2)}) collective-permute-start(f32[64,128]{1,0:T(8,128)S(1)} %get-tuple-element.139.refs_0_), channel_id=1, source_target_pairs={{0,8},{1,9},{2,10},{3,11},{4,12},{5,13},{6,14},{7,15},{8,0},{9,1},... | collective-permute-start | bytes 98312 | tf_op jit(solution)/shard_map/ppermute | solution.py:379
  60.6 6.0 %collective-permute-start.21 = (f32[64,128]{1,0:T(8,128)S(1)}, f32[64,128]{1,0:T(8,128)S(1)}, u32[]{:S(2)}, u32[]{:S(2)}) collective-permute-start(f32[64,128]{1,0:T(8,128)S(1)} %get-tuple-element.145), channel_id=1, source_target_pairs={{0,1},{1,0},{2,3},{3,2},{4,5},{5,4},{6,7},{7,6},{8,9},{9,8},{10,11... | collective-permute-start | bytes 98312 | tf_op jit(solution)/shard_map/ppermute | solution.py:379
  60.7 6.0 %collective-permute-start.22 = (f32[64,128]{1,0:T(8,128)S(1)}, f32[64,128]{1,0:T(8,128)S(1)}, u32[]{:S(2)}, u32[]{:S(2)}) collective-permute-start(f32[64,128]{1,0:T(8,128)S(1)} %get-tuple-element.146), channel_id=1, source_target_pairs={{0,2},{1,3},{2,0},{3,1},{4,6},{5,7},{6,4},{7,5},{8,10},{9,11},{10,... | collective-permute-start | bytes 98312 | tf_op jit(solution)/shard_map/ppermute | solution.py:379
  62.4 4.3 %collective-permute-start.23 = (f32[64,128]{1,0:T(8,128)S(1)}, f32[64,128]{1,0:T(8,128)S(1)}, u32[]{:S(2)}, u32[]{:S(2)}) collective-permute-start(f32[64,128]{1,0:T(8,128)S(1)} %get-tuple-element.147), channel_id=1, source_target_pairs={{0,3},{1,2},{2,1},{3,0},{4,7},{5,6},{6,5},{7,4},{8,11},{9,10},{10,... | collective-permute-start | bytes 98312 | tf_op jit(solution)/shard_map/ppermute | solution.py:379
  64.6 3.4 %collective-permute-start.18 = (f32[56,128]{1,0:T(8,128)S(1)}, f32[56,128]{1,0:T(8,128)S(1)}, u32[]{:S(2)}, u32[]{:S(2)}) collective-permute-start(f32[56,128]{1,0:T(8,128)S(1)} %get-tuple-element.141), channel_id=1, source_target_pairs={{0,1},{1,0},{2,3},{3,2},{4,5},{5,4},{6,7},{7,6},{8,9},{9,8},{10,11... | collective-permute-start | bytes 86024 | tf_op jit(solution)/shard_map/ppermute | solution.py:379
  65.0 3.9 %collective-permute-start.19 = (f32[56,128]{1,0:T(8,128)S(1)}, f32[56,128]{1,0:T(8,128)S(1)}, u32[]{:S(2)}, u32[]{:S(2)}) collective-permute-start(f32[56,128]{1,0:T(8,128)S(1)} %get-tuple-element.142), channel_id=1, source_target_pairs={{0,2},{1,3},{2,0},{3,1},{4,6},{5,7},{6,4},{7,5},{8,10},{9,11},{10,... | collective-permute-start | bytes 86024 | tf_op jit(solution)/shard_map/ppermute | solution.py:379
  66.7 3.6 %collective-permute-start.20 = (f32[56,128]{1,0:T(8,128)S(1)}, f32[56,128]{1,0:T(8,128)S(1)}, u32[]{:S(2)}, u32[]{:S(2)}) collective-permute-start(f32[56,128]{1,0:T(8,128)S(1)} %get-tuple-element.143), channel_id=1, source_target_pairs={{0,3},{1,2},{2,1},{3,0},{4,7},{5,6},{6,5},{7,4},{8,11},{9,10},{10,... | collective-permute-start | bytes 86024 | tf_op jit(solution)/shard_map/ppermute | solution.py:379

commit v10 on v9

--- a/solution.py
+++ b/solution.py
@@ -197,16 +197,16 @@
 GOT_NEXT = (5, 4, -1, None)
 
 
-def blocks_kernel(width, pos, c0, c2, c_other, s0, s2, came, came_next, theirs, solver, cross, own, edge_up, edge_down):
+def blocks_kernel(width, pos, c0, c2, c_other, s0, s1, s2, came, came_next, theirs, solver, cross, own, edge_up, edge_down):
     side, size, edge_size = 2 * width, s0.shape[0], came.shape[0]
     kept = (size - side) // 2
     owned, tall = c0.shape[0], c0.shape[1] // LANES
     half = solver.shape[0] // 2
     other, at = [], 0
-    for rows in (size, size, edge_size, edge_size):
+    for rows in (size, edge_size, edge_size):
         other.append(theirs.at[at:at + rows])
         at += rows
-    for k, ref in enumerate((s0, other[0], s2, other[1])):
+    for k, ref in enumerate((s0, s1, s2, other[0])):
         own[:, k * side:k * side + width] = stacked(ref[:kept])
         own[:, k * side + width:(k + 1) * side] = stacked(ref[kept:2 * kept])
         cross[:, k * width:(k + 1) * width] = stacked(ref[2 * kept:])
@@ -228,7 +228,7 @@
             placed(p, c_other[:owned], everything)
             placed(p ^ 2, c_other[owned:], everything)
             held = {GOT[m]: came, GOT_NEXT[m]: came_next}
-            for block, ref in zip((GOT[p], GOT_NEXT[p]), other[2:]):
+            for block, ref in zip((GOT[p], GOT_NEXT[p]), other[1:]):
                 held.setdefault(block, ref)
             for block in (-1, 4, 5):
                 for i in range(tall):
@@ -419,7 +419,9 @@
     *pieces, c_next = lax.optimization_barrier((*pieces, c_next))
     pieces = traded(pieces)
     c_other = mate(jnp.concatenate([coarse_inverse, c_next], axis=0), 1)
-    spans_next = mate(after(spans, pieces), 2)
+    tied = after(spans, pieces)
+    spans_next = mate(tied, 2)
+    spans_other = mate(tied, 1)
     edge = after(edge, pieces)
     came = crossing(edge, [(GROUP - 1, GROUP), (0, -1), (1, -2)])
     came_next = crossing(edge, [(GROUP - 1, GROUP + 2), (0, -3), (1, -4)])
@@ -436,7 +438,7 @@
             return sweeps[-1]
         return other
 
-    pieces[0] = after(pieces[0], c_other)
+    pieces[0] = after(pieces[0], (c_other, spans_other))
     size = owned + chunk_of(owned)
     pay_shapes = [(size, LANES)] + [(size + width // GROUP, LANES)] * 2
     v0, *pays = call(
@@ -448,7 +450,7 @@
     swept = sweep(pays)
     pays = along(*pays)
     *pays, spans_next, came, came_next, _ = lax.optimization_barrier((*pays, spans_next, came, came_next, swept))
-    theirs = mate(jnp.concatenate([spans, spans_next, came, came_next], axis=0), 1)
+    theirs = mate(jnp.concatenate([spans_next, came, came_next], axis=0), 1)
     pays[0] = after(pays[0], sweep((spans_next, swept)))
     blocks = call(
         functools.partial(blocks_kernel, width),
@@ -459,7 +461,7 @@
             ((side, width), BF16),
             ((side, width), BF16),
         ],
-        (pos, coarse_inverse, c_next, c_other, spans, spans_next, came, came_next, theirs),
+        (pos, coarse_inverse, c_next, c_other, spans, spans_other, spans_next, came, came_next, theirs),
         1.7,
     )
 

time: 72.5 us -> 72.1 us (level)
    ppermute x22 -> x23, starting transfers between devices: 22 us -> 20.9 us  [mate(): return lax.ppermute(x, 'sub', [(s, s ^ k) for s in range(total)])]
    ppermute x2, starting transfers between devices: 6.97 us -> 7.92 us  [crossing(): return lax.ppermute(x, 'sub', pairs)]
    ppermute x22 -> x23, waiting for transfers between devices: 10.2 us -> 9.61 us  [mate(): return lax.ppermute(x, 'sub', [(s, s ^ k) for s in range(total)])]
  transfers between devices with their start and end apart: 24 -> 25, of which waited for: 9 -> 11; matrix products, arithmetic and copies ran while one was open for 1% -> 1% of each run, Pallas kernels for 28% -> 28%
where the time goes in v10:
time: 72.1 us; the launch traced here: 71.9 us
  Pallas kernels  29 us (40%)
  starting transfers between devices  28.8 us (40%)
  waiting for transfers between devices  11.2 us (16%)
  local copies, waits for them, and re-layouts  1.15 us (2%)
  other arithmetic  0.96 us (1%)
  between operations  0.85 us (1%)
    pallas_call x13, Pallas kernels, call(): pl.pallas_call(kernel, out_shape=[jax.ShapeDtypeStruct(s, d) for s, d in...  29 us
    ppermute x23, starting transfers between devices, mate(): return lax.ppermute(x, 'sub', [(s, s ^ k) for s in range(total)])  20.9 us
    ppermute x23, waiting for transfers between devices, mate(): return lax.ppermute(x, 'sub', [(s, s ^ k) for s in range(total)])  9.61 us
    ppermute x2, starting transfers between devices, crossing(): return lax.ppermute(x, 'sub', pairs)  7.92 us
    ppermute x2, waiting for transfers between devices, crossing(): return lax.ppermute(x, 'sub', pairs)  1.57 us
  transfers between devices with their start and end apart: 25, of which 11 were waited for; matrix products, arithmetic and copies ran while one was open for 1% of the time, Pallas kernels for 28%

profile of v10, /device:TPU:0, one launch (start us, length us, event | category | flops | bytes accessed | tf_op | source)
XLA Modules:
  0.0 71.9 jit_solution(4951568838466812745)
XLA Ops:
  0.6 3.0 %collective-permute-start = (f32[48,768]{1,0:T(8,128)}, f32[48,768]{1,0:T(8,128)S(1)}, u32[]{:S(2)}, u32[]{:S(2)}) collective-permute-start(f32[48,768]{1,0:T(8,128)} %c0.1), channel_id=1, source_target_pairs={{0,2},{1,3},{2,0},{3,1},{4,6},{5,7},{6,4},{7,5},{8,10},{9,11},{10,... | collective-permute-start | bytes 442376 | tf_op jit(solution)/shard_map/ppermute | solution.py:379
  3.7 0.1 fusion
  3.7 0.7 %pad_add_fusion.table.tablev = s32[5,128]{1,0:T(8,128)S(1)} fusion(s32[1,2]{1,0:T(1,128)S(1)} %fusion, s32[1,96]{1,0:T(1,128)} %param.11, s32[1,96]{1,0:T(1,128)} %param.10, s32[2,128]{1,0:T(2,128)} %bitcast.7), kind=kLoop, calls=%fused_computation.2 | loop fusion | flops 1920 | bytes 4360 | tf_op jit(solution)/shard_map/concatenate | solution.py:376
  4.5 1.1 %copy-done.1 = f32[1536,128]{1,0:T(8,128)S(1)} copy-done((f32[1536,128]{1,0:T(8,128)S(1)}, f32[1536,128]{1,0:T(8,128)}, u32[]{:S(2)}) %copy-start.1) | copy-done | bytes 786456
  5.6 4.4 %shard_map.77 = (f32[88,128]{1,0:T(8,128)S(1)}, f32[88,128]{1,0:T(8,128)S(1)}, f32[88,128]{1,0:T(8,128)S(1)}, f32[88,128]{1,0:T(8,128)S(1)}, f32[352,1536]{1,0:T(8,128)S(1)}) custom-call(s32[5,128]{1,0:T(8,128)S(1)} %pad_add_fusion.table.tablev, f32[1536,1536]{1,0:T(8,128)} %k_ref.9, f32[1536,128]{1,0:T(8,128)S(1)} %copy-done.1), custom_call_target="tpu_custom_call" | custom-call | flops 5299999744 | tf_op jit(solution)/shard_map/pallas_call | solution.py:25
  10.0 0.0 collective-permute-done.c2
  10.0 0.1 collective-permute-start.2
  10.1 0.1 collective-permute-start.3
  10.2 1.8 %collective-permute-start.4 = (f32[88,128]{1,0:T(8,128)S(1)}, f32[88,128]{1,0:T(8,128)S(1)}, u32[]{:S(2)}, u32[]{:S(2)}) collective-permute-start(f32[88,128]{1,0:T(8,128)S(1)} %get-tuple-element.87), channel_id=1, source_target_pairs={{0,3},{1,2},{2,1},{3,0},{4,7},{5,6},{6,5},{7,4},{8,11},{9,10},{10,... | collective-permute-start | bytes 135176 | tf_op jit(solution)/shard_map/ppermute | solution.py:379
  12.0 2.3 %shard_map.78 = (f32[960,128]{1,0:T(8,128)S(1)}, f32[416,128]{1,0:T(8,128)S(1)}, bf16[1536,640]{1,0:T(8,128)(2,1)S(1)}) custom-call(s32[5,128]{1,0:T(8,128)S(1)} %pad_add_fusion.table.tablev, f32[352,1536]{1,0:T(8,128)S(1)} %get-tuple-element.83.ks, f32[1536,128]{1,0:T(8,128)S(1)} %copy-done.2, f32[48,768]{1,0:T(8,128)S(1)} %copy-done, ...), custom_call_target="tpu_custom_call" | custom-call | flops 2000000000 | tf_op jit(solution)/shard_map/pallas_call | solution.py:25
  14.3 0.0 collective-permute-done.2.p1
  14.3 0.3 collective-permute-done.3.p2
  14.6 0.1 collective-permute-done.4.p3
  14.7 0.3 collective-permute-start.5
  15.0 0.3 collective-permute-start.1
  15.3 1.1 %collective-permute-start.9 = (f32[960,128]{1,0:T(8,128)S(1)}, f32[960,128]{1,0:T(8,128)S(1)}, u32[]{:S(2)}, u32[]{:S(2)}) collective-permute-start(f32[960,128]{1,0:T(8,128)S(1)} %get-tuple-element.88.s0), channel_id=1, source_target_pairs={{0,2},{1,3},{2,0},{3,1},{4,6},{5,7},{6,4},{7,5},{8,10},{9,11},{10,... | collective-permute-start | bytes 1474568 | tf_op jit(solution)/shard_map/ppermute | solution.py:379
  16.4 5.5 %collective-permute-start.10 = (f32[416,128]{1,0:T(8,128)S(1)}, f32[416,128]{1,0:T(8,128)S(1)}, u32[]{:S(2)}, u32[]{:S(2)}) collective-permute-start(f32[416,128]{1,0:T(8,128)S(1)} %get-tuple-element.94), channel_id=1, source_target_pairs={{3,4},{0,15},{1,14},{7,8},{4,3},{5,2},{11,12},{8,7},{9,6},{15,0},{... | collective-permute-start | bytes 638984 | tf_op jit(solution)/shard_map/ppermute | solution.py:383
  21.9 0.1 pad_add_fusion.3.pos
  22.0 2.5 %collective-permute-start.11 = (f32[416,128]{1,0:T(8,128)S(1)}, f32[416,128]{1,0:T(8,128)S(1)}, u32[]{:S(2)}, u32[]{:S(2)}) collective-permute-start(f32[416,128]{1,0:T(8,128)S(1)} %get-tuple-element.94), channel_id=1, source_target_pairs={{3,6},{0,13},{1,12},{7,10},{4,1},{5,0},{11,14},{8,5},{9,4},{15,2},... | collective-permute-start | bytes 638984 | tf_op jit(solution)/shard_map/ppermute | solution.py:383
  24.4 0.0 collective-permute-done.1.c_other
  24.4 0.0 collective-permute-done.5.s1
  24.5 0.9 %shard_map.79 = (f32[352,128]{1,0:T(8,128)S(1)}, f32[64,128]{1,0:T(8,128)S(1)}, f32[96,128]{1,0:T(8,128)S(1)}, f32[96,128]{1,0:T(8,128)S(1)}) custom-call(s32[2]{0:T(128)S(1)} %pad_add_fusion.3.pos, f32[88,128]{1,0:T(8,128)S(1)} %get-tuple-element.89.p0, f32[88,128]{1,0:T(8,128)S(1)} %collective-permute-done.2.p1, f32[88,128]{1,0:T(8,128)S(1)} %collective-permute-done.3.p2, ...), custom_call_target="tpu_custom_call" | custom-call | flops 900000000 | tf_op jit(solution)/shard_map/pallas_call | solution.py:25
  25.4 1.6 %collective-permute-start.6 = (f32[96,128]{1,0:T(8,128)S(1)}, f32[96,128]{1,0:T(8,128)S(1)}, u32[]{:S(2)}, u32[]{:S(2)}) collective-permute-start(f32[96,128]{1,0:T(8,128)S(1)} %get-tuple-element.91), channel_id=1, source_target_pairs={{0,4},{1,5},{2,6},{3,7},{4,0},{5,1},{6,2},{7,3},{8,12},{9,13},{10,... | collective-permute-start | bytes 147464 | tf_op jit(solution)/shard_map/ppermute | solution.py:379
  27.0 0.0 collective-permute-start.8
  27.0 0.6 collective-permute-done.10.came
  27.6 1.3 %collective-permute-start.7 = (f32[64,128]{1,0:T(8,128)S(1)}, f32[64,128]{1,0:T(8,128)S(1)}, u32[]{:S(2)}, u32[]{:S(2)}) collective-permute-start(f32[64,128]{1,0:T(8,128)S(1)} %get-tuple-element.104.refs_0_), channel_id=1, source_target_pairs={{0,8},{1,9},{2,10},{3,11},{4,12},{5,13},{6,14},{7,15},{8,0},{9,1},... | collective-permute-start | bytes 98312 | tf_op jit(solution)/shard_map/ppermute | solution.py:379
  28.9 2.3 %shard_map.80 = (f32[384,128]{1,0:T(8,128)S(1)}, f32[384,384]{1,0:T(8,128)S(1)}) custom-call(s32[2]{0:T(128)S(1)} %pad_add_fusion.3.pos, bf16[1536,640]{1,0:T(8,128)(2,1)S(1)} %get-tuple-element.136.right_side, f32[1536,1536]{1,0:T(8,128)S(1)} %bitcast.6), custom_call_target="tpu_custom_call" | custom-call | flops 2300000000 | tf_op jit(solution)/shard_map/pallas_call | solution.py:25
  31.2 1.0 %collective-permute-done.11.came_next = f32[416,128]{1,0:T(8,128)S(1)} collective-permute-done((f32[416,128]{1,0:T(8,128)S(1)}, f32[416,128]{1,0:T(8,128)S(1)}, u32[]{:S(2)}, u32[]{:S(2)}) %collective-permute-start.11) | collective-permute-done | bytes 213024 | tf_op jit(solution)/shard_map/ppermute | solution.py:383
  32.2 2.7 %collective-permute-done.7.refs_2_ = f32[64,128]{1,0:T(8,128)S(1)} collective-permute-done((f32[64,128]{1,0:T(8,128)S(1)}, f32[64,128]{1,0:T(8,128)S(1)}, u32[]{:S(2)}, u32[]{:S(2)}) %collective-permute-start.7) | collective-permute-done | bytes 32800 | tf_op jit(solution)/shard_map/ppermute | solution.py:379
  34.9 0.2 collective-permute-done.8.refs_3_
  35.1 0.1 pad_maximum_fusion
  35.2 0.1 collective-permute-start.12
  35.3 2.3 %shard_map.81 = (f32[384,128]{1,0:T(8,128)S(1)}, f32[384,384]{1,0:T(8,128)S(1)}) custom-call(s32[2]{0:T(128)S(1)} %pad_add_fusion.3.pos, bf16[1536,640]{1,0:T(8,128)(2,1)S(1)} %get-tuple-element.136.right_side, f32[1536,1536]{1,0:T(8,128)S(1)} %bitcast.6), custom_call_target="tpu_custom_call" | custom-call | flops 2300000000 | tf_op jit(solution)/shard_map/pallas_call | solution.py:25
  37.5 0.2 collective-permute-done.12.theirs
  37.7 1.4 %shard_map.82 = (bf16[672,768]{1,0:T(8,128)(2,1)S(1)}, bf16[512,512]{1,0:T(8,128)(2,1)S(1)}, bf16[704,1024]{1,0:T(8,128)(2,1)S(1)}, bf16[256,128]{1,0:T(8,128)(2,1)S(1)}, bf16[256,128]{1,0:T(8,128)(2,1)S(1)}) custom-call(s32[2]{0:T(128)S(1)} %pad_add_fusion.3.pos, f32[48,768]{1,0:T(8,128)S(1)} %copy-done, f32[48,768]{1,0:T(8,128)S(1)} %collective-permute-done.c2, ...), custom_call_target="tpu_custom_call" | custom-call | flops 1700000000 | tf_op jit(solution)/shard_map/pallas_call | solution.py:25
  39.1 2.8 %shard_map.83 = (f32[352,128]{1,0:T(8,128)S(1)}, f32[128,128]{1,0:T(8,128)S(1)}, f32[128,128]{1,0:T(8,128)S(1)}, f32[64,128]{1,0:T(8,128)S(1)}, f32[96,128]{1,0:T(8,128)S(1)}, /*index=5*/f32[96,128]{1,0:T(8,128)S(1)}) custom-call(s32[2]{0:T(128)S(1)} %pad_add_fusion.3.pos, f32[64,128]{1,0:T(8,128)S(1)} %get-tuple-element.104.refs_0_, ...), custom_call_target="tpu_custom_call" | custom-call | flops 2800000000 | tf_op jit(solution)/shard_map/pallas_call | solution.py:25
  41.9 1.9 %collective-permute-start.13 = (f32[96,128]{1,0:T(8,128)S(1)}, f32[96,128]{1,0:T(8,128)S(1)}, u32[]{:S(2)}, u32[]{:S(2)}) collective-permute-start(f32[96,128]{1,0:T(8,128)S(1)} %get-tuple-element.120), channel_id=1, source_target_pairs={{0,4},{1,5},{2,6},{3,7},{4,0},{5,1},{6,2},{7,3},{8,12},{9,13},{10,... | collective-permute-start | bytes 147464 | tf_op jit(solution)/shard_map/ppermute | solution.py:379
  43.8 2.9 %collective-permute-start.15 = (f32[96,128]{1,0:T(8,128)S(1)}, f32[96,128]{1,0:T(8,128)S(1)}, u32[]{:S(2)}, u32[]{:S(2)}) collective-permute-start(f32[96,128]{1,0:T(8,128)S(1)} %get-tuple-element.121), channel_id=1, source_target_pairs={{0,12},{1,13},{2,14},{3,15},{4,8},{5,9},{6,10},{7,11},{8,4},{9,5},... | collective-permute-start | bytes 147464 | tf_op jit(solution)/shard_map/ppermute | solution.py:379
  46.7 0.5 collective-permute-start.14
  47.2 2.3 %shard_map.84 = (f32[384,128]{1,0:T(8,128)S(1)}, f32[384,384]{1,0:T(8,128)S(1)}) custom-call(s32[2]{0:T(128)S(1)} %pad_add_fusion.3.pos, bf16[1536,640]{1,0:T(8,128)(2,1)S(1)} %get-tuple-element.136.right_side, f32[1536,1536]{1,0:T(8,128)S(1)} %bitcast.6), custom_call_target="tpu_custom_call" | custom-call | flops 2300000000 | tf_op jit(solution)/shard_map/pallas_call | solution.py:25
  49.4 2.1 %collective-permute-done.14.refs_2_ = f32[64,128]{1,0:T(8,128)S(1)} collective-permute-done((f32[64,128]{1,0:T(8,128)S(1)}, f32[64,128]{1,0:T(8,128)S(1)}, u32[]{:S(2)}, u32[]{:S(2)}) %collective-permute-start.14) | collective-permute-done | bytes 32800 | tf_op jit(solution)/shard_map/ppermute | solution.py:379
  51.5 0.0 collective-permute-done.13.refs_1_
  51.5 0.0 collective-permute-done.15.refs_3_
  51.5 2.8 %shard_map.85 = (f32[352,128]{1,0:T(8,128)S(1)}, f32[128,128]{1,0:T(8,128)S(1)}, f32[128,128]{1,0:T(8,128)S(1)}, f32[64,128]{1,0:T(8,128)S(1)}, f32[96,128]{1,0:...) custom-call(s32[2]{0:T(128)S(1)} %pad_add_fusion.3.pos, ...), custom_call_target="tpu_custom_call" | custom-call | flops 2800000000 | tf_op jit(solution)/shard_map/pallas_call | solution.py:25
  54.3 1.1 %collective-permute-start.16 = (f32[96,128]{1,0:T(8,128)S(1)}, f32[96,128]{1,0:T(8,128)S(1)}, u32[]{:S(2)}, u32[]{:S(2)}) collective-permute-start(f32[96,128]{1,0:T(8,128)S(1)} %get-tuple-element.130), channel_id=1, source_target_pairs={{0,4},{1,5},{2,6},{3,7},{4,0},{5,1},{6,2},{7,3},{8,12},{9,13},{10,... | collective-permute-start | bytes 147464 | tf_op jit(solution)/shard_map/ppermute | solution.py:379
  55.4 1.9 %collective-permute-start.18 = (f32[96,128]{1,0:T(8,128)S(1)}, f32[96,128]{1,0:T(8,128)S(1)}, u32[]{:S(2)}, u32[]{:S(2)}) collective-permute-start(f32[96,128]{1,0:T(8,128)S(1)} %get-tuple-element.131), channel_id=1, source_target_pairs={{0,12},{1,13},{2,14},{3,15},{4,8},{5,9},{6,10},{7,11},{8,4},{9,5},... | collective-permute-start | bytes 147464 | tf_op jit(solution)/shard_map/ppermute | solution.py:379
  57.2 0.6 collective-permute-start.17
  57.8 2.3 %shard_map.86 = (f32[384,128]{1,0:T(8,128)S(1)}, f32[384,384]{1,0:T(8,128)S(1)}) custom-call(s32[2]{0:T(128)S(1)} %pad_add_fusion.3.pos, bf16[1536,640]{1,0:T(8,128)(2,1)S(1)} %get-tuple-element.136.right_side, f32[1536,1536]{1,0:T(8,128)S(1)} %bitcast.6), custom_call_target="tpu_custom_call" | custom-call | flops 2300000000 | tf_op jit(solution)/shard_map/pallas_call | solution.py:25
  60.1 0.1 collective-permute-start.22
  60.2 0.1 collective-permute-start.23
  60.3 1.8 %collective-permute-done.17.refs_2_ = f32[64,128]{1,0:T(8,128)S(1)} collective-permute-done((f32[64,128]{1,0:T(8,128)S(1)}, f32[64,128]{1,0:T(8,128)S(1)}, u32[]{:S(2)}, u32[]{:S(2)}) %collective-permute-start.17) | collective-permute-done | bytes 32800 | tf_op jit(solution)/shard_map/ppermute | solution.py:379
  62.1 0.0 collective-permute-start.24
  62.1 0.0 collective-permute-done.16.refs_1_
  62.1 0.0 collective-permute-done.18.refs_3_
  62.1 2.0 %shard_map.87 = (f32[56,128]{1,0:T(8,128)S(1)}, f32[56,128]{1,0:T(8,128)S(1)}, f32[56,128]{1,0:T(8,128)S(1)}, f32[56,128]{1,0:T(8,128)S(1)}) custom-call(s32[2]{0:T(128)S(1)} %pad_add_fusion.3.pos, f32[64,128]{1,0:T(8,128)S(1)} %get-tuple-element.139.refs_0_, f32[96,128]{1,0:T(8,128)S(1)} %collective-permute-done.16.refs_1_, ...), custom_call_target="tpu_custom_call" | custom-call | flops 2800000000 | tf_op jit(solution)/shard_map/pallas_call | solution.py:25
  64.1 0.4 collective-permute-start.19
  64.5 1.8 %collective-permute-start.20 = (f32[56,128]{1,0:T(8,128)S(1)}, f32[56,128]{1,0:T(8,128)S(1)}, u32[]{:S(2)}, u32[]{:S(2)}) collective-permute-start(f32[56,128]{1,0:T(8,128)S(1)} %get-tuple-element.142), channel_id=1, source_target_pairs={{0,2},{1,3},{2,0},{3,1},{4,6},{5,7},{6,4},{7,5},{8,10},{9,11},{10,... | collective-permute-start | bytes 86024 | tf_op jit(solution)/shard_map/ppermute | solution.py:379
  66.3 0.0 collective-permute-done.22.p1
  66.3 0.0 collective-permute-done.24.p3
  66.3 1.3 %shard_map.88.u_ref = f32[1536,128]{1,0:T(8,128)S(1)} custom-call(s32[2]{0:T(128)S(1)} %pad_add_fusion.3.pos, f32[64,128]{1,0:T(8,128)S(1)} %get-tuple-element.148.p0, f32[64,128]{1,0:T(8,128)S(1)} %collective-permute-done.22.p1, f32[64,128]{1,0:T(8,128)S(1)} %collective-permute-done.23.p2, f32[64,128]{1,0:T(8,128)S(1)} %collective-permute-done.24.p3, ...), custom_call_target="tpu_custom_call" | custom-call | flops 1300000000 | tf_op jit(solution)/shard_map/pallas_call | solution.py:25
  67.6 0.0 collective-permute-done.19.p1
  67.6 0.7 collective-permute-done.20.p2
  68.4 1.5 %collective-permute-done.21.p3 = f32[56,128]{1,0:T(8,128)S(1)} collective-permute-done((f32[56,128]{1,0:T(8,128)S(1)}, f32[56,128]{1,0:T(8,128)S(1)}, u32[]{:S(2)}, u32[]{:S(2)}) %collective-permute-start.21) | collective-permute-done | bytes 28704 | tf_op jit(solution)/shard_map/ppermute | solution.py:379
  69.9 2.0 %shard_map.89 = (f32[1536,128]{1,0:T(8,128)}, f32[128,128]{1,0:T(8,128)}) custom-call(s32[2]{0:T(128)S(1)} %pad_add_fusion.3.pos, f32[56,128]{1,0:T(8,128)S(1)} %get-tuple-element.140.p0, f32[56,128]{1,0:T(8,128)S(1)} %collective-permute-done.19.p1, f32[56,128]{1,0:T(8,128)S(1)} %collective-permute-done.20.p2, f32[56,128]{1,0:T(8,128)S(1)} %collective-permute-done.21.p3, ...), custom_call_target="tpu_custom_call" | custom-call | flops 2000000000 | tf_op jit(solution)/shard_map/pallas_call | solution.py:25
  (17 shorter events, 0.1 us)
Async XLA Ops:
  0.6 9.4 %collective-permute-start = (f32[48,768]{1,0:T(8,128)}, f32[48,768]{1,0:T(8,128)S(1)}, u32[]{:S(2)}, u32[]{:S(2)}) collective-permute-start(f32[48,768]{1,0:T(8,128)} %c0.1), channel_id=1, source_target_pairs={{0,2},{1,3},{2,0},{3,1},{4,6},{5,7},{6,4},{7,5},{8,10},{9,11},{10,... | collective-permute-start | bytes 442376 | tf_op jit(solution)/shard_map/ppermute | solution.py:379
  4.5 1.1 %copy-start.1 = (f32[1536,128]{1,0:T(8,128)S(1)}, f32[1536,128]{1,0:T(8,128)}, u32[]{:S(2)}) copy-start(f32[1536,128]{1,0:T(8,128)} %f_ref.3) | copy-start | bytes 2359300
  5.6 6.4 %copy-start = (f32[48,768]{1,0:T(8,128)S(1)}, f32[48,768]{1,0:T(8,128)}, u32[]{:S(2)}) copy-start(f32[48,768]{1,0:T(8,128)} %c0.1) | copy-start | bytes 442372
  5.6 6.4 %copy-start.2 = (f32[1536,128]{1,0:T(8,128)S(1)}, f32[1536,128]{1,0:T(8,128)}, u32[]{:S(2)}) copy-start(f32[1536,128]{1,0:T(8,128)} %f_ref.3) | copy-start | bytes 2359300
  5.6 23.3 %slice-start = ((s8[9437184]{0:T(1024)(128)(4,1)}), s8[1048576]{0:T(1024)(128)(4,1)S(1)}, s32[]{:S(2)}) async-start(s8[9437184]{0:T(1024)(128)(4,1)} %bitcast.5), calls=%async_computation | async-start | bytes 2097152
  5.6 23.3 %slice-start.1 = ((s8[9437184]{0:T(1024)(128)(4,1)}), s8[4194304]{0:T(1024)(128)(4,1)S(1)}, s32[]{:S(2)}) async-start(s8[9437184]{0:T(1024)(128)(4,1)} %bitcast.5), calls=%async_computation.1 | async-start | bytes 8388608
  10.0 4.3 %collective-permute-start.2 = (f32[88,128]{1,0:T(8,128)S(1)}, f32[88,128]{1,0:T(8,128)S(1)}, u32[]{:S(2)}, u32[]{:S(2)}) collective-permute-start(f32[88,128]{1,0:T(8,128)S(1)} %get-tuple-element.85), channel_id=1, source_target_pairs={{0,1},{1,0},{2,3},{3,2},{4,5},{5,4},{6,7},{7,6},{8,9},{9,8},{10,11... | collective-permute-start | bytes 135176 | tf_op jit(solution)/shard_map/ppermute | solution.py:379
  10.1 4.5 %collective-permute-start.3 = (f32[88,128]{1,0:T(8,128)S(1)}, f32[88,128]{1,0:T(8,128)S(1)}, u32[]{:S(2)}, u32[]{:S(2)}) collective-permute-start(f32[88,128]{1,0:T(8,128)S(1)} %get-tuple-element.86), channel_id=1, source_target_pairs={{0,2},{1,3},{2,0},{3,1},{4,6},{5,7},{6,4},{7,5},{8,10},{9,11},{10,... | collective-permute-start | bytes 135176 | tf_op jit(solution)/shard_map/ppermute | solution.py:379
  10.2 4.5 %collective-permute-start.4 = (f32[88,128]{1,0:T(8,128)S(1)}, f32[88,128]{1,0:T(8,128)S(1)}, u32[]{:S(2)}, u32[]{:S(2)}) collective-permute-start(f32[88,128]{1,0:T(8,128)S(1)} %get-tuple-element.87), channel_id=1, source_target_pairs={{0,3},{1,2},{2,1},{3,0},{4,7},{5,6},{6,5},{7,4},{8,11},{9,10},{10,... | collective-permute-start | bytes 135176 | tf_op jit(solution)/shard_map/ppermute | solution.py:379
  12.0 16.9 %slice-start.2 = ((s8[9437184]{0:T(1024)(128)(4,1)}), s8[4194304]{0:T(1024)(128)(4,1)S(1)}, s32[]{:S(2)}) async-start(s8[9437184]{0:T(1024)(128)(4,1)} %bitcast.5), calls=%async_computation.2 | async-start | bytes 8388608
  14.7 9.7 %collective-permute-start.5 = (f32[960,128]{1,0:T(8,128)S(1)}, f32[960,128]{1,0:T(8,128)S(1)}, u32[]{:S(2)}, u32[]{:S(2)}) collective-permute-start(f32[960,128]{1,0:T(8,128)S(1)} %get-tuple-element.88.s0), channel_id=1, source_target_pairs={{0,1},{1,0},{2,3},{3,2},{4,5},{5,4},{6,7},{7,6},{8,9},{9,8},{10,11... | collective-permute-start | bytes 1474568 | tf_op jit(solution)/shard_map/ppermute | solution.py:379
  15.0 9.4 %collective-permute-start.1 = (f32[96,768]{1,0:T(8,128)S(1)}, f32[96,768]{1,0:T(8,128)S(1)}, u32[]{:S(2)}, u32[]{:S(2)}) collective-permute-start(f32[96,768]{1,0:T(8,128)S(1)} %pad_maximum_fusion.1), channel_id=1, source_target_pairs={{0,1},{1,0},{2,3},{3,2},{4,5},{5,4},{6,7},{7,6},{8,9},{9,8},{10,11... | collective-permute-start | bytes 884744 | tf_op jit(solution)/shard_map/ppermute | solution.py:379
  15.3 16.9 %collective-permute-start.9 = (f32[960,128]{1,0:T(8,128)S(1)}, f32[960,128]{1,0:T(8,128)S(1)}, u32[]{:S(2)}, u32[]{:S(2)}) collective-permute-start(f32[960,128]{1,0:T(8,128)S(1)} %get-tuple-element.88.s0), channel_id=1, source_target_pairs={{0,2},{1,3},{2,0},{3,1},{4,6},{5,7},{6,4},{7,5},{8,10},{9,11},{10,... | collective-permute-start | bytes 1474568 | tf_op jit(solution)/shard_map/ppermute | solution.py:379
  16.4 11.2 %collective-permute-start.10 = (f32[416,128]{1,0:T(8,128)S(1)}, f32[416,128]{1,0:T(8,128)S(1)}, u32[]{:S(2)}, u32[]{:S(2)}) collective-permute-start(f32[416,128]{1,0:T(8,128)S(1)} %get-tuple-element.94), channel_id=1, source_target_pairs={{3,4},{0,15},{1,14},{7,8},{4,3},{5,2},{11,12},{8,7},{9,6},{15,0},{... | collective-permute-start | bytes 638984 | tf_op jit(solution)/shard_map/ppermute | solution.py:383
  22.0 10.2 %collective-permute-start.11 = (f32[416,128]{1,0:T(8,128)S(1)}, f32[416,128]{1,0:T(8,128)S(1)}, u32[]{:S(2)}, u32[]{:S(2)}) collective-permute-start(f32[416,128]{1,0:T(8,128)S(1)} %get-tuple-element.94), channel_id=1, source_target_pairs={{3,6},{0,13},{1,12},{7,10},{4,1},{5,0},{11,14},{8,5},{9,4},{15,2},... | collective-permute-start | bytes 638984 | tf_op jit(solution)/shard_map/ppermute | solution.py:383
  25.4 9.5 %collective-permute-start.6 = (f32[96,128]{1,0:T(8,128)S(1)}, f32[96,128]{1,0:T(8,128)S(1)}, u32[]{:S(2)}, u32[]{:S(2)}) collective-permute-start(f32[96,128]{1,0:T(8,128)S(1)} %get-tuple-element.91), channel_id=1, source_target_pairs={{0,4},{1,5},{2,6},{3,7},{4,0},{5,1},{6,2},{7,3},{8,12},{9,13},{10,... | collective-permute-start | bytes 147464 | tf_op jit(solution)/shard_map/ppermute | solution.py:379
  27.0 8.1 %collective-permute-start.8 = (f32[96,128]{1,0:T(8,128)S(1)}, f32[96,128]{1,0:T(8,128)S(1)}, u32[]{:S(2)}, u32[]{:S(2)}) collective-permute-start(f32[96,128]{1,0:T(8,128)S(1)} %get-tuple-element.92), channel_id=1, source_target_pairs={{0,12},{1,13},{2,14},{3,15},{4,8},{5,9},{6,10},{7,11},{8,4},{9,5},... | collective-permute-start | bytes 147464 | tf_op jit(solution)/shard_map/ppermute | solution.py:379
  27.6 7.3 %collective-permute-start.7 = (f32[64,128]{1,0:T(8,128)S(1)}, f32[64,128]{1,0:T(8,128)S(1)}, u32[]{:S(2)}, u32[]{:S(2)}) collective-permute-start(f32[64,128]{1,0:T(8,128)S(1)} %get-tuple-element.104.refs_0_), channel_id=1, source_target_pairs={{0,8},{1,9},{2,10},{3,11},{4,12},{5,13},{6,14},{7,15},{8,0},{9,1},... | collective-permute-start | bytes 98312 | tf_op jit(solution)/shard_map/ppermute | solution.py:379
  35.2 2.5 %collective-permute-start.12 = (f32[1792,128]{1,0:T(8,128)S(1)}, f32[1792,128]{1,0:T(8,128)S(1)}, u32[]{:S(2)}, u32[]{:S(2)}) collective-permute-start(f32[1792,128]{1,0:T(8,128)S(1)} %pad_maximum_fusion), channel_id=1, source_target_pairs={{0,1},{1,0},{2,3},{3,2},{4,5},{5,4},{6,7},{7,6},{8,9},{9,8},{10,11... | collective-permute-start | bytes 2752520 | tf_op jit(solution)/shard_map/ppermute | solution.py:379
  41.9 9.6 %collective-permute-start.13 = (f32[96,128]{1,0:T(8,128)S(1)}, f32[96,128]{1,0:T(8,128)S(1)}, u32[]{:S(2)}, u32[]{:S(2)}) collective-permute-start(f32[96,128]{1,0:T(8,128)S(1)} %get-tuple-element.120), channel_id=1, source_target_pairs={{0,4},{1,5},{2,6},{3,7},{4,0},{5,1},{6,2},{7,3},{8,12},{9,13},{10,... | collective-permute-start | bytes 147464 | tf_op jit(solution)/shard_map/ppermute | solution.py:379
  43.8 7.7 %collective-permute-start.15 = (f32[96,128]{1,0:T(8,128)S(1)}, f32[96,128]{1,0:T(8,128)S(1)}, u32[]{:S(2)}, u32[]{:S(2)}) collective-permute-start(f32[96,128]{1,0:T(8,128)S(1)} %get-tuple-element.121), channel_id=1, source_target_pairs={{0,12},{1,13},{2,14},{3,15},{4,8},{5,9},{6,10},{7,11},{8,4},{9,5},... | collective-permute-start | bytes 147464 | tf_op jit(solution)/shard_map/ppermute | solution.py:379
  46.7 4.8 %collective-permute-start.14 = (f32[64,128]{1,0:T(8,128)S(1)}, f32[64,128]{1,0:T(8,128)S(1)}, u32[]{:S(2)}, u32[]{:S(2)}) collective-permute-start(f32[64,128]{1,0:T(8,128)S(1)} %get-tuple-element.125.refs_0_), channel_id=1, source_target_pairs={{0,8},{1,9},{2,10},{3,11},{4,12},{5,13},{6,14},{7,15},{8,0},{9,1},... | collective-permute-start | bytes 98312 | tf_op jit(solution)/shard_map/ppermute | solution.py:379
  54.3 7.8 %collective-permute-start.16 = (f32[96,128]{1,0:T(8,128)S(1)}, f32[96,128]{1,0:T(8,128)S(1)}, u32[]{:S(2)}, u32[]{:S(2)}) collective-permute-start(f32[96,128]{1,0:T(8,128)S(1)} %get-tuple-element.130), channel_id=1, source_target_pairs={{0,4},{1,5},{2,6},{3,7},{4,0},{5,1},{6,2},{7,3},{8,12},{9,13},{10,... | collective-permute-start | bytes 147464 | tf_op jit(solution)/shard_map/ppermute | solution.py:379
  55.4 6.7 %collective-permute-start.18 = (f32[96,128]{1,0:T(8,128)S(1)}, f32[96,128]{1,0:T(8,128)S(1)}, u32[]{:S(2)}, u32[]{:S(2)}) collective-permute-start(f32[96,128]{1,0:T(8,128)S(1)} %get-tuple-element.131), channel_id=1, source_target_pairs={{0,12},{1,13},{2,14},{3,15},{4,8},{5,9},{6,10},{7,11},{8,4},{9,5},... | collective-permute-start | bytes 147464 | tf_op jit(solution)/shard_map/ppermute | solution.py:379
  57.2 4.8 %collective-permute-start.17 = (f32[64,128]{1,0:T(8,128)S(1)}, f32[64,128]{1,0:T(8,128)S(1)}, u32[]{:S(2)}, u32[]{:S(2)}) collective-permute-start(f32[64,128]{1,0:T(8,128)S(1)} %get-tuple-element.139.refs_0_), channel_id=1, source_target_pairs={{0,8},{1,9},{2,10},{3,11},{4,12},{5,13},{6,14},{7,15},{8,0},{9,1},... | collective-permute-start | bytes 98312 | tf_op jit(solution)/shard_map/ppermute | solution.py:379
  60.1 6.2 %collective-permute-start.22 = (f32[64,128]{1,0:T(8,128)S(1)}, f32[64,128]{1,0:T(8,128)S(1)}, u32[]{:S(2)}, u32[]{:S(2)}) collective-permute-start(f32[64,128]{1,0:T(8,128)S(1)} %get-tuple-element.145), channel_id=1, source_target_pairs={{0,1},{1,0},{2,3},{3,2},{4,5},{5,4},{6,7},{7,6},{8,9},{9,8},{10,11... | collective-permute-start | bytes 98312 | tf_op jit(solution)/shard_map/ppermute | solution.py:379
  60.2 6.1 %collective-permute-start.23 = (f32[64,128]{1,0:T(8,128)S(1)}, f32[64,128]{1,0:T(8,128)S(1)}, u32[]{:S(2)}, u32[]{:S(2)}) collective-permute-start(f32[64,128]{1,0:T(8,128)S(1)} %get-tuple-element.146), channel_id=1, source_target_pairs={{0,2},{1,3},{2,0},{3,1},{4,6},{5,7},{6,4},{7,5},{8,10},{9,11},{10,... | collective-permute-start | bytes 98312 | tf_op jit(solution)/shard_map/ppermute | solution.py:379
  62.1 4.3 %collective-permute-start.24 = (f32[64,128]{1,0:T(8,128)S(1)}, f32[64,128]{1,0:T(8,128)S(1)}, u32[]{:S(2)}, u32[]{:S(2)}) collective-permute-start(f32[64,128]{1,0:T(8,128)S(1)} %get-tuple-element.147), channel_id=1, source_target_pairs={{0,3},{1,2},{2,1},{3,0},{4,7},{5,6},{6,5},{7,4},{8,11},{9,10},{10,... | collective-permute-start | bytes 98312 | tf_op jit(solution)/shard_map/ppermute | solution.py:379
  64.1 3.5 %collective-permute-start.19 = (f32[56,128]{1,0:T(8,128)S(1)}, f32[56,128]{1,0:T(8,128)S(1)}, u32[]{:S(2)}, u32[]{:S(2)}) collective-permute-start(f32[56,128]{1,0:T(8,128)S(1)} %get-tuple-element.141), channel_id=1, source_target_pairs={{0,1},{1,0},{2,3},{3,2},{4,5},{5,4},{6,7},{7,6},{8,9},{9,8},{10,11... | collective-permute-start | bytes 86024 | tf_op jit(solution)/shard_map/ppermute | solution.py:379
  64.5 3.9 %collective-permute-start.20 = (f32[56,128]{1,0:T(8,128)S(1)}, f32[56,128]{1,0:T(8,128)S(1)}, u32[]{:S(2)}, u32[]{:S(2)}) collective-permute-start(f32[56,128]{1,0:T(8,128)S(1)} %get-tuple-element.142), channel_id=1, source_target_pairs={{0,2},{1,3},{2,0},{3,1},{4,6},{5,7},{6,4},{7,5},{8,10},{9,11},{10,... | collective-permute-start | bytes 86024 | tf_op jit(solution)/shard_map/ppermute | solution.py:379
  66.3 3.6 %collective-permute-start.21 = (f32[56,128]{1,0:T(8,128)S(1)}, f32[56,128]{1,0:T(8,128)S(1)}, u32[]{:S(2)}, u32[]{:S(2)}) collective-permute-start(f32[56,128]{1,0:T(8,128)S(1)} %get-tuple-element.143), channel_id=1, source_target_pairs={{0,3},{1,2},{2,1},{3,0},{4,7},{5,6},{6,5},{7,4},{8,11},{9,10},{10,... | collective-permute-start | bytes 86024 | tf_op jit(solution)/shard_map/ppermute | solution.py:379

commit v11 on v10

--- a/solution.py
+++ b/solution.py
@@ -264,6 +264,8 @@
         (now, left_ref, right_ref), refs = refs[:3], refs[3:]
     outs, (held, stack) = refs[:-2], refs[-2:]
     paired = groups == PAIRED
+    if paired:
+        pays = pays[:1] + pays[:0:-1]
     member, group = pos[0], pos[1]
     width = edge_down.shape[1]
     owned = (v0.shape[0] - 2 * width) // 2
@@ -392,7 +394,7 @@
         if groups == PAIRED:
             last = mate(b, 3 * GROUP)
             middle = mate(pay, 2 * GROUP)
-            return [pay, mate(a, GROUP), middle, last]
+            return [pay, last, middle, mate(a, GROUP)]
         return [pay, planes(a, 1)] + [planes(pay, k) for k in range(2, groups - 1)] + [planes(b, -1)]
 
     def after(x, other):

time: 72.1 us -> 71.7 us (level)
  waiting for transfers between devices: 11.2 us -> 6.99 us
  starting transfers between devices: 28.8 us -> 32.6 us
    ppermute x23, starting transfers between devices: 20.9 us -> 24.7 us  [mate(): return lax.ppermute(x, 'sub', [(s, s ^ k) for s in range(total)])]
    ppermute x23, waiting for transfers between devices: 9.61 us -> 6.53 us  [mate(): return lax.ppermute(x, 'sub', [(s, s ^ k) for s in range(total)])]
    ppermute x2, waiting for transfers between devices: 1.57 us -> 0.46 us  [crossing(): return lax.ppermute(x, 'sub', pairs)]
  transfers between devices with their start and end apart: 25 -> 25, of which waited for: 11 -> 8; matrix products, arithmetic and copies ran while one was open for 1% -> 1% of each run, Pallas kernels for 28% -> 28%
where the time goes in v11:
time: 71.7 us; the launch traced here: 71.4 us
  starting transfers between devices  32.6 us (45%)
  Pallas kernels  28.9 us (40%)
  waiting for transfers between devices  6.99 us (10%)
  local copies, waits for them, and re-layouts  1.15 us (2%)
  other arithmetic  0.96 us (1%)
  between operations  0.84 us (1%)
    pallas_call x13, Pallas kernels, call(): pl.pallas_call(kernel, out_shape=[jax.ShapeDtypeStruct(s, d) for s, d in...  28.9 us
    ppermute x23, starting transfers between devices, mate(): return lax.ppermute(x, 'sub', [(s, s ^ k) for s in range(total)])  24.7 us
    ppermute x2, starting transfers between devices, crossing(): return lax.ppermute(x, 'sub', pairs)  7.92 us
    ppermute x23, waiting for transfers between devices, mate(): return lax.ppermute(x, 'sub', [(s, s ^ k) for s in range(total)])  6.53 us
  transfers between devices with their start and end apart: 25, of which 8 were waited for; matrix products, arithmetic and copies ran while one was open for 1% of the time, Pallas kernels for 28%

profile of v11, /device:TPU:0, one launch (start us, length us, event | category | flops | bytes accessed | tf_op | source)
XLA Modules:
  0.0 71.4 jit_solution(17571492010610525901)
XLA Ops:
  0.6 3.0 %collective-permute-start = (f32[48,768]{1,0:T(8,128)}, f32[48,768]{1,0:T(8,128)S(1)}, u32[]{:S(2)}, u32[]{:S(2)}) collective-permute-start(f32[48,768]{1,0:T(8,128)} %c0.1), channel_id=1, source_target_pairs={{0,2},{1,3},{2,0},{3,1},{4,6},{5,7},{6,4},{7,5},{8,10},{9,11},{10,... | collective-permute-start | bytes 442376 | tf_op jit(solution)/shard_map/ppermute | solution.py:381
  3.7 0.1 fusion
  3.7 0.7 %pad_add_fusion.table.tablev = s32[5,128]{1,0:T(8,128)S(1)} fusion(s32[1,2]{1,0:T(1,128)S(1)} %fusion, s32[1,96]{1,0:T(1,128)} %param.11, s32[1,96]{1,0:T(1,128)} %param.10, s32[2,128]{1,0:T(2,128)} %bitcast.7), kind=kLoop, calls=%fused_computation.2 | loop fusion | flops 1920 | bytes 4360 | tf_op jit(solution)/shard_map/concatenate | solution.py:378
  4.5 1.1 %copy-done.1 = f32[1536,128]{1,0:T(8,128)S(1)} copy-done((f32[1536,128]{1,0:T(8,128)S(1)}, f32[1536,128]{1,0:T(8,128)}, u32[]{:S(2)}) %copy-start.1) | copy-done | bytes 786456
  5.6 4.4 %shard_map.77 = (f32[88,128]{1,0:T(8,128)S(1)}, f32[88,128]{1,0:T(8,128)S(1)}, f32[88,128]{1,0:T(8,128)S(1)}, f32[88,128]{1,0:T(8,128)S(1)}, f32[352,1536]{1,0:T(8,128)S(1)}) custom-call(s32[5,128]{1,0:T(8,128)S(1)} %pad_add_fusion.table.tablev, f32[1536,1536]{1,0:T(8,128)} %k_ref.9, f32[1536,128]{1,0:T(8,128)S(1)} %copy-done.1), custom_call_target="tpu_custom_call" | custom-call | flops 5299999744 | tf_op jit(solution)/shard_map/pallas_call | solution.py:25
  10.0 0.0 collective-permute-done.c2
  10.0 0.1 collective-permute-start.2
  10.1 0.1 collective-permute-start.3
  10.2 1.8 %collective-permute-start.4 = (f32[88,128]{1,0:T(8,128)S(1)}, f32[88,128]{1,0:T(8,128)S(1)}, u32[]{:S(2)}, u32[]{:S(2)}) collective-permute-start(f32[88,128]{1,0:T(8,128)S(1)} %get-tuple-element.87), channel_id=1, source_target_pairs={{0,3},{1,2},{2,1},{3,0},{4,7},{5,6},{6,5},{7,4},{8,11},{9,10},{10,... | collective-permute-start | bytes 135176 | tf_op jit(solution)/shard_map/ppermute | solution.py:381
  12.0 2.3 %shard_map.78 = (f32[960,128]{1,0:T(8,128)S(1)}, f32[416,128]{1,0:T(8,128)S(1)}, bf16[1536,640]{1,0:T(8,128)(2,1)S(1)}) custom-call(s32[5,128]{1,0:T(8,128)S(1)} %pad_add_fusion.table.tablev, f32[352,1536]{1,0:T(8,128)S(1)} %get-tuple-element.83.ks, f32[1536,128]{1,0:T(8,128)S(1)} %copy-done.2, f32[48,768]{1,0:T(8,128)S(1)} %copy-done, ...), custom_call_target="tpu_custom_call" | custom-call | flops 2000000000 | tf_op jit(solution)/shard_map/pallas_call | solution.py:25
  14.3 0.0 collective-permute-done.2.p1
  14.3 0.3 collective-permute-done.3.p2
  14.6 0.1 collective-permute-done.4.p3
  14.7 0.3 collective-permute-start.5
  15.0 0.3 collective-permute-start.1
  15.3 1.1 %collective-permute-start.9 = (f32[960,128]{1,0:T(8,128)S(1)}, f32[960,128]{1,0:T(8,128)S(1)}, u32[]{:S(2)}, u32[]{:S(2)}) collective-permute-start(f32[960,128]{1,0:T(8,128)S(1)} %get-tuple-element.88.s0), channel_id=1, source_target_pairs={{0,2},{1,3},{2,0},{3,1},{4,6},{5,7},{6,4},{7,5},{8,10},{9,11},{10,... | collective-permute-start | bytes 1474568 | tf_op jit(solution)/shard_map/ppermute | solution.py:381
  16.4 5.5 %collective-permute-start.10 = (f32[416,128]{1,0:T(8,128)S(1)}, f32[416,128]{1,0:T(8,128)S(1)}, u32[]{:S(2)}, u32[]{:S(2)}) collective-permute-start(f32[416,128]{1,0:T(8,128)S(1)} %get-tuple-element.94), channel_id=1, source_target_pairs={{3,4},{0,15},{1,14},{7,8},{4,3},{5,2},{11,12},{8,7},{9,6},{15,0},{... | collective-permute-start | bytes 638984 | tf_op jit(solution)/shard_map/ppermute | solution.py:385
  21.9 0.1 pad_add_fusion.3.pos
  22.0 2.5 %collective-permute-start.11 = (f32[416,128]{1,0:T(8,128)S(1)}, f32[416,128]{1,0:T(8,128)S(1)}, u32[]{:S(2)}, u32[]{:S(2)}) collective-permute-start(f32[416,128]{1,0:T(8,128)S(1)} %get-tuple-element.94), channel_id=1, source_target_pairs={{3,6},{0,13},{1,12},{7,10},{4,1},{5,0},{11,14},{8,5},{9,4},{15,2},... | collective-permute-start | bytes 638984 | tf_op jit(solution)/shard_map/ppermute | solution.py:385
  24.4 0.0 collective-permute-done.1.c_other
  24.4 0.0 collective-permute-done.5.s1
  24.5 0.9 %shard_map.79 = (f32[352,128]{1,0:T(8,128)S(1)}, f32[64,128]{1,0:T(8,128)S(1)}, f32[96,128]{1,0:T(8,128)S(1)}, f32[96,128]{1,0:T(8,128)S(1)}) custom-call(s32[2]{0:T(128)S(1)} %pad_add_fusion.3.pos, f32[88,128]{1,0:T(8,128)S(1)} %get-tuple-element.89.p0, f32[88,128]{1,0:T(8,128)S(1)} %collective-permute-done.2.p1, f32[88,128]{1,0:T(8,128)S(1)} %collective-permute-done.3.p2, ...), custom_call_target="tpu_custom_call" | custom-call | flops 900000000 | tf_op jit(solution)/shard_map/pallas_call | solution.py:25
  25.4 0.5 collective-permute-start.6
  25.9 1.2 %collective-permute-start.8 = (f32[96,128]{1,0:T(8,128)S(1)}, f32[96,128]{1,0:T(8,128)S(1)}, u32[]{:S(2)}, u32[]{:S(2)}) collective-permute-start(f32[96,128]{1,0:T(8,128)S(1)} %get-tuple-element.92), channel_id=1, source_target_pairs={{0,4},{1,5},{2,6},{3,7},{4,0},{5,1},{6,2},{7,3},{8,12},{9,13},{10,... | collective-permute-start | bytes 147464 | tf_op jit(solution)/shard_map/ppermute | solution.py:381
  27.1 0.4 collective-permute-done.10.came
  27.5 2.3 %collective-permute-start.7 = (f32[64,128]{1,0:T(8,128)S(1)}, f32[64,128]{1,0:T(8,128)S(1)}, u32[]{:S(2)}, u32[]{:S(2)}) collective-permute-start(f32[64,128]{1,0:T(8,128)S(1)} %get-tuple-element.104.refs_0_), channel_id=1, source_target_pairs={{0,8},{1,9},{2,10},{3,11},{4,12},{5,13},{6,14},{7,15},{8,0},{9,1},... | collective-permute-start | bytes 98312 | tf_op jit(solution)/shard_map/ppermute | solution.py:381
  29.8 2.3 %shard_map.80 = (f32[384,128]{1,0:T(8,128)S(1)}, f32[384,384]{1,0:T(8,128)S(1)}) custom-call(s32[2]{0:T(128)S(1)} %pad_add_fusion.3.pos, bf16[1536,640]{1,0:T(8,128)(2,1)S(1)} %get-tuple-element.136.right_side, f32[1536,1536]{1,0:T(8,128)S(1)} %bitcast.6), custom_call_target="tpu_custom_call" | custom-call | flops 2300000000 | tf_op jit(solution)/shard_map/pallas_call | solution.py:25
  32.1 0.1 collective-permute-done.11.came_next
  32.2 2.6 %collective-permute-done.7.refs_2_ = f32[64,128]{1,0:T(8,128)S(1)} collective-permute-done((f32[64,128]{1,0:T(8,128)S(1)}, f32[64,128]{1,0:T(8,128)S(1)}, u32[]{:S(2)}, u32[]{:S(2)}) %collective-permute-start.7) | collective-permute-done | bytes 32800 | tf_op jit(solution)/shard_map/ppermute | solution.py:381
  34.8 0.1 pad_maximum_fusion
  34.9 0.1 collective-permute-start.12
  34.9 2.3 %shard_map.81 = (f32[384,128]{1,0:T(8,128)S(1)}, f32[384,384]{1,0:T(8,128)S(1)}) custom-call(s32[2]{0:T(128)S(1)} %pad_add_fusion.3.pos, bf16[1536,640]{1,0:T(8,128)(2,1)S(1)} %get-tuple-element.136.right_side, f32[1536,1536]{1,0:T(8,128)S(1)} %bitcast.6), custom_call_target="tpu_custom_call" | custom-call | flops 2300000000 | tf_op jit(solution)/shard_map/pallas_call | solution.py:25
  37.2 0.2 collective-permute-done.12.theirs
  37.4 1.4 %shard_map.82 = (bf16[672,768]{1,0:T(8,128)(2,1)S(1)}, bf16[512,512]{1,0:T(8,128)(2,1)S(1)}, bf16[704,1024]{1,0:T(8,128)(2,1)S(1)}, bf16[256,128]{1,0:T(8,128)(2,1)S(1)}, bf16[256,128]{1,0:T(8,128)(2,1)S(1)}) custom-call(s32[2]{0:T(128)S(1)} %pad_add_fusion.3.pos, f32[48,768]{1,0:T(8,128)S(1)} %copy-done, f32[48,768]{1,0:T(8,128)S(1)} %collective-permute-done.c2, ...), custom_call_target="tpu_custom_call" | custom-call | flops 1700000000 | tf_op jit(solution)/shard_map/pallas_call | solution.py:25
  38.8 2.8 %shard_map.83 = (f32[352,128]{1,0:T(8,128)S(1)}, f32[128,128]{1,0:T(8,128)S(1)}, f32[128,128]{1,0:T(8,128)S(1)}, f32[64,128]{1,0:T(8,128)S(1)}, f32[96,128]{1,0:T(8,128)S(1)}, /*index=5*/f32[96,128]{1,0:T(8,128)S(1)}) custom-call(s32[2]{0:T(128)S(1)} %pad_add_fusion.3.pos, f32[64,128]{1,0:T(8,128)S(1)} %get-tuple-element.104.refs_0_, ...), custom_call_target="tpu_custom_call" | custom-call | flops 2800000000 | tf_op jit(solution)/shard_map/pallas_call | solution.py:25
  41.6 4.9 %collective-permute-start.13 = (f32[96,128]{1,0:T(8,128)S(1)}, f32[96,128]{1,0:T(8,128)S(1)}, u32[]{:S(2)}, u32[]{:S(2)}) collective-permute-start(f32[96,128]{1,0:T(8,128)S(1)} %get-tuple-element.121), channel_id=1, source_target_pairs={{0,12},{1,13},{2,14},{3,15},{4,8},{5,9},{6,10},{7,11},{8,4},{9,5},... | collective-permute-start | bytes 147464 | tf_op jit(solution)/shard_map/ppermute | solution.py:381
  46.5 0.0 collective-permute-start.15
  46.5 0.6 collective-permute-start.14
  47.2 2.3 %shard_map.84 = (f32[384,128]{1,0:T(8,128)S(1)}, f32[384,384]{1,0:T(8,128)S(1)}) custom-call(s32[2]{0:T(128)S(1)} %pad_add_fusion.3.pos, bf16[1536,640]{1,0:T(8,128)(2,1)S(1)} %get-tuple-element.136.right_side, f32[1536,1536]{1,0:T(8,128)S(1)} %bitcast.6), custom_call_target="tpu_custom_call" | custom-call | flops 2300000000 | tf_op jit(solution)/shard_map/pallas_call | solution.py:25
  49.4 2.3 %collective-permute-done.14.refs_2_ = f32[64,128]{1,0:T(8,128)S(1)} collective-permute-done((f32[64,128]{1,0:T(8,128)S(1)}, f32[64,128]{1,0:T(8,128)S(1)}, u32[]{:S(2)}, u32[]{:S(2)}) %collective-permute-start.14) | collective-permute-done | bytes 32800 | tf_op jit(solution)/shard_map/ppermute | solution.py:381
  51.7 0.0 collective-permute-done.13.refs_1_
  51.7 0.0 collective-permute-done.15.refs_3_
  51.7 2.8 %shard_map.85 = (f32[352,128]{1,0:T(8,128)S(1)}, f32[128,128]{1,0:T(8,128)S(1)}, f32[128,128]{1,0:T(8,128)S(1)}, f32[64,128]{1,0:T(8,128)S(1)}, f32[96,128]{1,0:...) custom-call(s32[2]{0:T(128)S(1)} %pad_add_fusion.3.pos, ...), custom_call_target="tpu_custom_call" | custom-call | flops 2800000000 | tf_op jit(solution)/shard_map/pallas_call | solution.py:25
  54.5 1.7 %collective-permute-start.16 = (f32[96,128]{1,0:T(8,128)S(1)}, f32[96,128]{1,0:T(8,128)S(1)}, u32[]{:S(2)}, u32[]{:S(2)}) collective-permute-start(f32[96,128]{1,0:T(8,128)S(1)} %get-tuple-element.131), channel_id=1, source_target_pairs={{0,12},{1,13},{2,14},{3,15},{4,8},{5,9},{6,10},{7,11},{8,4},{9,5},... | collective-permute-start | bytes 147464 | tf_op jit(solution)/shard_map/ppermute | solution.py:381
  56.2 0.4 collective-permute-start.18
  56.5 2.4 %collective-permute-start.17 = (f32[64,128]{1,0:T(8,128)S(1)}, f32[64,128]{1,0:T(8,128)S(1)}, u32[]{:S(2)}, u32[]{:S(2)}) collective-permute-start(f32[64,128]{1,0:T(8,128)S(1)} %get-tuple-element.139.refs_0_), channel_id=1, source_target_pairs={{0,8},{1,9},{2,10},{3,11},{4,12},{5,13},{6,14},{7,15},{8,0},{9,1},... | collective-permute-start | bytes 98312 | tf_op jit(solution)/shard_map/ppermute | solution.py:381
  58.9 2.3 %shard_map.86 = (f32[384,128]{1,0:T(8,128)S(1)}, f32[384,384]{1,0:T(8,128)S(1)}) custom-call(s32[2]{0:T(128)S(1)} %pad_add_fusion.3.pos, bf16[1536,640]{1,0:T(8,128)(2,1)S(1)} %get-tuple-element.136.right_side, f32[1536,1536]{1,0:T(8,128)S(1)} %bitcast.6), custom_call_target="tpu_custom_call" | custom-call | flops 2300000000 | tf_op jit(solution)/shard_map/pallas_call | solution.py:25
  61.2 0.1 collective-permute-start.22
  61.3 0.1 collective-permute-start.23
  61.3 0.0 collective-permute-done.17.refs_2_
  61.3 1.8 %collective-permute-start.24 = (f32[64,128]{1,0:T(8,128)S(1)}, f32[64,128]{1,0:T(8,128)S(1)}, u32[]{:S(2)}, u32[]{:S(2)}) collective-permute-start(f32[64,128]{1,0:T(8,128)S(1)} %get-tuple-element.147), channel_id=1, source_target_pairs={{0,3},{1,2},{2,1},{3,0},{4,7},{5,6},{6,5},{7,4},{8,11},{9,10},{10,... | collective-permute-start | bytes 98312 | tf_op jit(solution)/shard_map/ppermute | solution.py:381
  63.1 0.0 collective-permute-done.16.refs_1_
  63.1 2.0 %shard_map.87 = (f32[56,128]{1,0:T(8,128)S(1)}, f32[56,128]{1,0:T(8,128)S(1)}, f32[56,128]{1,0:T(8,128)S(1)}, f32[56,128]{1,0:T(8,128)S(1)}) custom-call(s32[2]{0:T(128)S(1)} %pad_add_fusion.3.pos, f32[64,128]{1,0:T(8,128)S(1)} %get-tuple-element.139.refs_0_, f32[96,128]{1,0:T(8,128)S(1)} %collective-permute-done.16.refs_1_, ...), custom_call_target="tpu_custom_call" | custom-call | flops 2800000000 | tf_op jit(solution)/shard_map/pallas_call | solution.py:25
  65.2 0.4 collective-permute-start.19
  65.6 0.1 collective-permute-start.20
  65.7 0.0 collective-permute-done.22.p1
  65.7 1.4 %collective-permute-start.21 = (f32[56,128]{1,0:T(8,128)S(1)}, f32[56,128]{1,0:T(8,128)S(1)}, u32[]{:S(2)}, u32[]{:S(2)}) collective-permute-start(f32[56,128]{1,0:T(8,128)S(1)} %get-tuple-element.143), channel_id=1, source_target_pairs={{0,3},{1,2},{2,1},{3,0},{4,7},{5,6},{6,5},{7,4},{8,11},{9,10},{10,... | collective-permute-start | bytes 86024 | tf_op jit(solution)/shard_map/ppermute | solution.py:381
  67.1 0.0 collective-permute-done.23.p2
  67.1 0.0 collective-permute-done.24.p3
  67.1 1.3 %shard_map.88.u_ref = f32[1536,128]{1,0:T(8,128)S(1)} custom-call(s32[2]{0:T(128)S(1)} %pad_add_fusion.3.pos, f32[64,128]{1,0:T(8,128)S(1)} %get-tuple-element.148.p0, f32[64,128]{1,0:T(8,128)S(1)} %collective-permute-done.22.p1, f32[64,128]{1,0:T(8,128)S(1)} %collective-permute-done.23.p2, f32[64,128]{1,0:T(8,128)S(1)} %collective-permute-done.24.p3, ...), custom_call_target="tpu_custom_call" | custom-call | flops 1300000000 | tf_op jit(solution)/shard_map/pallas_call | solution.py:25
  68.4 0.0 collective-permute-done.19.p1
  68.4 1.0 %collective-permute-done.20.p2 = f32[56,128]{1,0:T(8,128)S(1)} collective-permute-done((f32[56,128]{1,0:T(8,128)S(1)}, f32[56,128]{1,0:T(8,128)S(1)}, u32[]{:S(2)}, u32[]{:S(2)}) %collective-permute-start.20) | collective-permute-done | bytes 28704 | tf_op jit(solution)/shard_map/ppermute | solution.py:381
  69.4 0.0 collective-permute-done.21.p3
  69.4 2.0 %shard_map.89 = (f32[1536,128]{1,0:T(8,128)}, f32[128,128]{1,0:T(8,128)}) custom-call(s32[2]{0:T(128)S(1)} %pad_add_fusion.3.pos, f32[56,128]{1,0:T(8,128)S(1)} %get-tuple-element.140.p0, f32[56,128]{1,0:T(8,128)S(1)} %collective-permute-done.19.p1, f32[56,128]{1,0:T(8,128)S(1)} %collective-permute-done.20.p2, f32[56,128]{1,0:T(8,128)S(1)} %collective-permute-done.21.p3, ...), custom_call_target="tpu_custom_call" | custom-call | flops 2000000000 | tf_op jit(solution)/shard_map/pallas_call | solution.py:25
  (17 shorter events, 0.1 us)
Async XLA Ops:
  0.6 9.4 %collective-permute-start = (f32[48,768]{1,0:T(8,128)}, f32[48,768]{1,0:T(8,128)S(1)}, u32[]{:S(2)}, u32[]{:S(2)}) collective-permute-start(f32[48,768]{1,0:T(8,128)} %c0.1), channel_id=1, source_target_pairs={{0,2},{1,3},{2,0},{3,1},{4,6},{5,7},{6,4},{7,5},{8,10},{9,11},{10,... | collective-permute-start | bytes 442376 | tf_op jit(solution)/shard_map/ppermute | solution.py:381
  4.5 1.1 %copy-start.1 = (f32[1536,128]{1,0:T(8,128)S(1)}, f32[1536,128]{1,0:T(8,128)}, u32[]{:S(2)}) copy-start(f32[1536,128]{1,0:T(8,128)} %f_ref.3) | copy-start | bytes 2359300
  5.6 6.4 %copy-start = (f32[48,768]{1,0:T(8,128)S(1)}, f32[48,768]{1,0:T(8,128)}, u32[]{:S(2)}) copy-start(f32[48,768]{1,0:T(8,128)} %c0.1) | copy-start | bytes 442372
  5.6 6.4 %copy-start.2 = (f32[1536,128]{1,0:T(8,128)S(1)}, f32[1536,128]{1,0:T(8,128)}, u32[]{:S(2)}) copy-start(f32[1536,128]{1,0:T(8,128)} %f_ref.3) | copy-start | bytes 2359300
  5.6 24.2 %slice-start = ((s8[9437184]{0:T(1024)(128)(4,1)}), s8[1048576]{0:T(1024)(128)(4,1)S(1)}, s32[]{:S(2)}) async-start(s8[9437184]{0:T(1024)(128)(4,1)} %bitcast.5), calls=%async_computation | async-start | bytes 2097152
  5.6 24.2 %slice-start.1 = ((s8[9437184]{0:T(1024)(128)(4,1)}), s8[4194304]{0:T(1024)(128)(4,1)S(1)}, s32[]{:S(2)}) async-start(s8[9437184]{0:T(1024)(128)(4,1)} %bitcast.5), calls=%async_computation.1 | async-start | bytes 8388608
  10.0 4.3 %collective-permute-start.2 = (f32[88,128]{1,0:T(8,128)S(1)}, f32[88,128]{1,0:T(8,128)S(1)}, u32[]{:S(2)}, u32[]{:S(2)}) collective-permute-start(f32[88,128]{1,0:T(8,128)S(1)} %get-tuple-element.85), channel_id=1, source_target_pairs={{0,1},{1,0},{2,3},{3,2},{4,5},{5,4},{6,7},{7,6},{8,9},{9,8},{10,11... | collective-permute-start | bytes 135176 | tf_op jit(solution)/shard_map/ppermute | solution.py:381
  10.1 4.5 %collective-permute-start.3 = (f32[88,128]{1,0:T(8,128)S(1)}, f32[88,128]{1,0:T(8,128)S(1)}, u32[]{:S(2)}, u32[]{:S(2)}) collective-permute-start(f32[88,128]{1,0:T(8,128)S(1)} %get-tuple-element.86), channel_id=1, source_target_pairs={{0,2},{1,3},{2,0},{3,1},{4,6},{5,7},{6,4},{7,5},{8,10},{9,11},{10,... | collective-permute-start | bytes 135176 | tf_op jit(solution)/shard_map/ppermute | solution.py:381
  10.2 4.5 %collective-permute-start.4 = (f32[88,128]{1,0:T(8,128)S(1)}, f32[88,128]{1,0:T(8,128)S(1)}, u32[]{:S(2)}, u32[]{:S(2)}) collective-permute-start(f32[88,128]{1,0:T(8,128)S(1)} %get-tuple-element.87), channel_id=1, source_target_pairs={{0,3},{1,2},{2,1},{3,0},{4,7},{5,6},{6,5},{7,4},{8,11},{9,10},{10,... | collective-permute-start | bytes 135176 | tf_op jit(solution)/shard_map/ppermute | solution.py:381
  12.0 17.8 %slice-start.2 = ((s8[9437184]{0:T(1024)(128)(4,1)}), s8[4194304]{0:T(1024)(128)(4,1)S(1)}, s32[]{:S(2)}) async-start(s8[9437184]{0:T(1024)(128)(4,1)} %bitcast.5), calls=%async_computation.2 | async-start | bytes 8388608
  14.7 9.7 %collective-permute-start.5 = (f32[960,128]{1,0:T(8,128)S(1)}, f32[960,128]{1,0:T(8,128)S(1)}, u32[]{:S(2)}, u32[]{:S(2)}) collective-permute-start(f32[960,128]{1,0:T(8,128)S(1)} %get-tuple-element.88.s0), channel_id=1, source_target_pairs={{0,1},{1,0},{2,3},{3,2},{4,5},{5,4},{6,7},{7,6},{8,9},{9,8},{10,11... | collective-permute-start | bytes 1474568 | tf_op jit(solution)/shard_map/ppermute | solution.py:381
  15.0 9.4 %collective-permute-start.1 = (f32[96,768]{1,0:T(8,128)S(1)}, f32[96,768]{1,0:T(8,128)S(1)}, u32[]{:S(2)}, u32[]{:S(2)}) collective-permute-start(f32[96,768]{1,0:T(8,128)S(1)} %pad_maximum_fusion.1), channel_id=1, source_target_pairs={{0,1},{1,0},{2,3},{3,2},{4,5},{5,4},{6,7},{7,6},{8,9},{9,8},{10,11... | collective-permute-start | bytes 884744 | tf_op jit(solution)/shard_map/ppermute | solution.py:381
  15.3 16.9 %collective-permute-start.9 = (f32[960,128]{1,0:T(8,128)S(1)}, f32[960,128]{1,0:T(8,128)S(1)}, u32[]{:S(2)}, u32[]{:S(2)}) collective-permute-start(f32[960,128]{1,0:T(8,128)S(1)} %get-tuple-element.88.s0), channel_id=1, source_target_pairs={{0,2},{1,3},{2,0},{3,1},{4,6},{5,7},{6,4},{7,5},{8,10},{9,11},{10,... | collective-permute-start | bytes 1474568 | tf_op jit(solution)/shard_map/ppermute | solution.py:381
  16.4 11.1 %collective-permute-start.10 = (f32[416,128]{1,0:T(8,128)S(1)}, f32[416,128]{1,0:T(8,128)S(1)}, u32[]{:S(2)}, u32[]{:S(2)}) collective-permute-start(f32[416,128]{1,0:T(8,128)S(1)} %get-tuple-element.94), channel_id=1, source_target_pairs={{3,4},{0,15},{1,14},{7,8},{4,3},{5,2},{11,12},{8,7},{9,6},{15,0},{... | collective-permute-start | bytes 638984 | tf_op jit(solution)/shard_map/ppermute | solution.py:385
  22.0 10.2 %collective-permute-start.11 = (f32[416,128]{1,0:T(8,128)S(1)}, f32[416,128]{1,0:T(8,128)S(1)}, u32[]{:S(2)}, u32[]{:S(2)}) collective-permute-start(f32[416,128]{1,0:T(8,128)S(1)} %get-tuple-element.94), channel_id=1, source_target_pairs={{3,6},{0,13},{1,12},{7,10},{4,1},{5,0},{11,14},{8,5},{9,4},{15,2},... | collective-permute-start | bytes 638984 | tf_op jit(solution)/shard_map/ppermute | solution.py:385
  25.4 9.4 %collective-permute-start.6 = (f32[96,128]{1,0:T(8,128)S(1)}, f32[96,128]{1,0:T(8,128)S(1)}, u32[]{:S(2)}, u32[]{:S(2)}) collective-permute-start(f32[96,128]{1,0:T(8,128)S(1)} %get-tuple-element.91), channel_id=1, source_target_pairs={{0,12},{1,13},{2,14},{3,15},{4,8},{5,9},{6,10},{7,11},{8,4},{9,5},... | collective-permute-start | bytes 147464 | tf_op jit(solution)/shard_map/ppermute | solution.py:381
  25.9 8.9 %collective-permute-start.8 = (f32[96,128]{1,0:T(8,128)S(1)}, f32[96,128]{1,0:T(8,128)S(1)}, u32[]{:S(2)}, u32[]{:S(2)}) collective-permute-start(f32[96,128]{1,0:T(8,128)S(1)} %get-tuple-element.92), channel_id=1, source_target_pairs={{0,4},{1,5},{2,6},{3,7},{4,0},{5,1},{6,2},{7,3},{8,12},{9,13},{10,... | collective-permute-start | bytes 147464 | tf_op jit(solution)/shard_map/ppermute | solution.py:381
  27.5 7.3 %collective-permute-start.7 = (f32[64,128]{1,0:T(8,128)S(1)}, f32[64,128]{1,0:T(8,128)S(1)}, u32[]{:S(2)}, u32[]{:S(2)}) collective-permute-start(f32[64,128]{1,0:T(8,128)S(1)} %get-tuple-element.104.refs_0_), channel_id=1, source_target_pairs={{0,8},{1,9},{2,10},{3,11},{4,12},{5,13},{6,14},{7,15},{8,0},{9,1},... | collective-permute-start | bytes 98312 | tf_op jit(solution)/shard_map/ppermute | solution.py:381
  34.9 2.5 %collective-permute-start.12 = (f32[1792,128]{1,0:T(8,128)S(1)}, f32[1792,128]{1,0:T(8,128)S(1)}, u32[]{:S(2)}, u32[]{:S(2)}) collective-permute-start(f32[1792,128]{1,0:T(8,128)S(1)} %pad_maximum_fusion), channel_id=1, source_target_pairs={{0,1},{1,0},{2,3},{3,2},{4,5},{5,4},{6,7},{7,6},{8,9},{9,8},{10,11... | collective-permute-start | bytes 2752520 | tf_op jit(solution)/shard_map/ppermute | solution.py:381
  41.6 10.1 %collective-permute-start.13 = (f32[96,128]{1,0:T(8,128)S(1)}, f32[96,128]{1,0:T(8,128)S(1)}, u32[]{:S(2)}, u32[]{:S(2)}) collective-permute-start(f32[96,128]{1,0:T(8,128)S(1)} %get-tuple-element.121), channel_id=1, source_target_pairs={{0,12},{1,13},{2,14},{3,15},{4,8},{5,9},{6,10},{7,11},{8,4},{9,5},... | collective-permute-start | bytes 147464 | tf_op jit(solution)/shard_map/ppermute | solution.py:381
  46.5 5.2 %collective-permute-start.15 = (f32[96,128]{1,0:T(8,128)S(1)}, f32[96,128]{1,0:T(8,128)S(1)}, u32[]{:S(2)}, u32[]{:S(2)}) collective-permute-start(f32[96,128]{1,0:T(8,128)S(1)} %get-tuple-element.120), channel_id=1, source_target_pairs={{0,4},{1,5},{2,6},{3,7},{4,0},{5,1},{6,2},{7,3},{8,12},{9,13},{10,... | collective-permute-start | bytes 147464 | tf_op jit(solution)/shard_map/ppermute | solution.py:381
  46.5 5.2 %collective-permute-start.14 = (f32[64,128]{1,0:T(8,128)S(1)}, f32[64,128]{1,0:T(8,128)S(1)}, u32[]{:S(2)}, u32[]{:S(2)}) collective-permute-start(f32[64,128]{1,0:T(8,128)S(1)} %get-tuple-element.125.refs_0_), channel_id=1, source_target_pairs={{0,8},{1,9},{2,10},{3,11},{4,12},{5,13},{6,14},{7,15},{8,0},{9,1},... | collective-permute-start | bytes 98312 | tf_op jit(solution)/shard_map/ppermute | solution.py:381
  54.5 8.6 %collective-permute-start.16 = (f32[96,128]{1,0:T(8,128)S(1)}, f32[96,128]{1,0:T(8,128)S(1)}, u32[]{:S(2)}, u32[]{:S(2)}) collective-permute-start(f32[96,128]{1,0:T(8,128)S(1)} %get-tuple-element.131), channel_id=1, source_target_pairs={{0,12},{1,13},{2,14},{3,15},{4,8},{5,9},{6,10},{7,11},{8,4},{9,5},... | collective-permute-start | bytes 147464 | tf_op jit(solution)/shard_map/ppermute | solution.py:381
  56.2 7.0 %collective-permute-start.18 = (f32[96,128]{1,0:T(8,128)S(1)}, f32[96,128]{1,0:T(8,128)S(1)}, u32[]{:S(2)}, u32[]{:S(2)}) collective-permute-start(f32[96,128]{1,0:T(8,128)S(1)} %get-tuple-element.130), channel_id=1, source_target_pairs={{0,4},{1,5},{2,6},{3,7},{4,0},{5,1},{6,2},{7,3},{8,12},{9,13},{10,... | collective-permute-start | bytes 147464 | tf_op jit(solution)/shard_map/ppermute | solution.py:381
  56.5 4.8 %collective-permute-start.17 = (f32[64,128]{1,0:T(8,128)S(1)}, f32[64,128]{1,0:T(8,128)S(1)}, u32[]{:S(2)}, u32[]{:S(2)}) collective-permute-start(f32[64,128]{1,0:T(8,128)S(1)} %get-tuple-element.139.refs_0_), channel_id=1, source_target_pairs={{0,8},{1,9},{2,10},{3,11},{4,12},{5,13},{6,14},{7,15},{8,0},{9,1},... | collective-permute-start | bytes 98312 | tf_op jit(solution)/shard_map/ppermute | solution.py:381
  61.2 4.5 %collective-permute-start.22 = (f32[64,128]{1,0:T(8,128)S(1)}, f32[64,128]{1,0:T(8,128)S(1)}, u32[]{:S(2)}, u32[]{:S(2)}) collective-permute-start(f32[64,128]{1,0:T(8,128)S(1)} %get-tuple-element.145), channel_id=1, source_target_pairs={{0,1},{1,0},{2,3},{3,2},{4,5},{5,4},{6,7},{7,6},{8,9},{9,8},{10,11... | collective-permute-start | bytes 98312 | tf_op jit(solution)/shard_map/ppermute | solution.py:381
  61.3 5.8 %collective-permute-start.23 = (f32[64,128]{1,0:T(8,128)S(1)}, f32[64,128]{1,0:T(8,128)S(1)}, u32[]{:S(2)}, u32[]{:S(2)}) collective-permute-start(f32[64,128]{1,0:T(8,128)S(1)} %get-tuple-element.146), channel_id=1, source_target_pairs={{0,2},{1,3},{2,0},{3,1},{4,6},{5,7},{6,4},{7,5},{8,10},{9,11},{10,... | collective-permute-start | bytes 98312 | tf_op jit(solution)/shard_map/ppermute | solution.py:381
  61.3 5.7 %collective-permute-start.24 = (f32[64,128]{1,0:T(8,128)S(1)}, f32[64,128]{1,0:T(8,128)S(1)}, u32[]{:S(2)}, u32[]{:S(2)}) collective-permute-start(f32[64,128]{1,0:T(8,128)S(1)} %get-tuple-element.147), channel_id=1, source_target_pairs={{0,3},{1,2},{2,1},{3,0},{4,7},{5,6},{6,5},{7,4},{8,11},{9,10},{10,... | collective-permute-start | bytes 98312 | tf_op jit(solution)/shard_map/ppermute | solution.py:381
  65.2 3.2 %collective-permute-start.19 = (f32[56,128]{1,0:T(8,128)S(1)}, f32[56,128]{1,0:T(8,128)S(1)}, u32[]{:S(2)}, u32[]{:S(2)}) collective-permute-start(f32[56,128]{1,0:T(8,128)S(1)} %get-tuple-element.141), channel_id=1, source_target_pairs={{0,1},{1,0},{2,3},{3,2},{4,5},{5,4},{6,7},{7,6},{8,9},{9,8},{10,11... | collective-permute-start | bytes 86024 | tf_op jit(solution)/shard_map/ppermute | solution.py:381
  65.6 3.9 %collective-permute-start.20 = (f32[56,128]{1,0:T(8,128)S(1)}, f32[56,128]{1,0:T(8,128)S(1)}, u32[]{:S(2)}, u32[]{:S(2)}) collective-permute-start(f32[56,128]{1,0:T(8,128)S(1)} %get-tuple-element.142), channel_id=1, source_target_pairs={{0,2},{1,3},{2,0},{3,1},{4,6},{5,7},{6,4},{7,5},{8,10},{9,11},{10,... | collective-permute-start | bytes 86024 | tf_op jit(solution)/shard_map/ppermute | solution.py:381
  65.7 3.8 %collective-permute-start.21 = (f32[56,128]{1,0:T(8,128)S(1)}, f32[56,128]{1,0:T(8,128)S(1)}, u32[]{:S(2)}, u32[]{:S(2)}) collective-permute-start(f32[56,128]{1,0:T(8,128)S(1)} %get-tuple-element.143), channel_id=1, source_target_pairs={{0,3},{1,2},{2,1},{3,0},{4,7},{5,6},{6,5},{7,4},{8,11},{9,10},{10,... | collective-permute-start | bytes 86024 | tf_op jit(solution)/shard_map/ppermute | solution.py:381
